TPU v7x, 32 devices: a whole 2x2x4 slice. The times are simulated.
32 devices in a mesh: grp: 2 (over y), tile: 4 (over z), var: 4 (over x, core).
Axes of the slice: x: 2, y: 2, z: 4, core: 2. Of those that a mesh axis runs over, the one named last changes fastest.
Arguments:
- control: float32 [8, 128, 2048], P('var', ('grp', 'tile')), parts along dimension 1, may hold values from -6 to 6
- diffusivity: float32 [2, 128, 2048], P(None, ('grp', 'tile')), parts along dimension 1, may hold values from 0.05 to 0.95
- land_mask: int32 [128, 2048], P(('grp', 'tile')), parts along dimension 0, may hold values 0 or 1
- panel_tile: int32 [1024, 1], P(('grp', 'tile')), parts along dimension 0, may hold values from 0 to 3; in each aligned block of 128 rows (0 to 127, 128 to 255, ...) at most 64 rows name the same one
- panel_row: int32 [1024], P(('grp', 'tile')), parts along dimension 0, may hold values from 0 to 15
- panel_cols: int32 [1024, 128], P(('grp', 'tile')), parts along dimension 0, may hold values from 0 to 2047
- obs_values: float32 [1024, 128], P(('grp', 'tile')), parts along dimension 0, may hold values from -6 to 6
- obs_weights: float32 [1024, 128], P(('grp', 'tile')), parts along dimension 0, may hold values from 0.5 to 4
- panel_sensor: int32 [1024], P(('grp', 'tile')), parts along dimension 0, may hold values from 0 to 1
- sensitivity: float32 [2, 8], replicated, may hold values from 0.2 to 1
- cross_factor: float32 [8, 8], replicated, may hold values from -0.45 to 2
Outputs:
- gradient: float32 [8, 128, 2048], P('var', ('grp', 'tile')), parts along dimension 1
There are 2 independent parts, one for each index of `grp`. A program takes and returns all parts, laid end to end along the dimension named above; an argument that names none is the same for every part. Nothing has to cross between parts.
Inputs may be any that keep to these rules, and one draw needn't show every extreme that they name: `panel_tile`: among the 128 panels held by one tile index, at most 64 name the same tile.
All inputs are finite; a program needn't handle non-finite values. No bound on the sum of `land_mask` on one device may be relied on, other than what follows from the above.
Results may differ from a plain program's by a relative error of at most 0.00014.
Values sent between devices are 32-bit elements; how exact they have to be, the bound alone decides.
No kernel may reach another device: no remote copies, remote signals or barrier semaphores. Data moves between devices by JAX's collectives and lax.ppermute only.
A program may use at most 128 MiB of HBM per device.

v0:
```python
import functools

import jax
import jax.numpy as jnp
from jax import lax
from jax.experimental import pallas as pl
from jax.experimental.pallas import tpu as pltpu
from jax.sharding import PartitionSpec as P

PASSES = 10
LANES = 128
GROUP = 16
VMEM = pl.BlockSpec(memory_space=pltpu.VMEM)
SMEM = pl.BlockSpec(memory_space=pltpu.SMEM)
HBM = pl.BlockSpec(memory_space=pltpu.HBM)
AFTER = pl.BlockSpec(memory_space=pl.ANY)
F32 = jnp.float32


def in_hbm(values):
    return pltpu.with_memory_space_constraint(values, pltpu.HBM)


def call(body, outs, ins, scratch=(), limit=16, cost=None):
    return pl.pallas_call(
        body,
        out_shape=outs,
        in_specs=ins,
        out_specs=[VMEM] * len(outs),
        scratch_shapes=list(scratch),
        compiler_params=pltpu.CompilerParams(vmem_limit_bytes=limit << 20),
        cost_estimate=cost,
    )


def cost(cycles):
    return pl.CostEstimate(flops=cycles * 4096, bytes_accessed=cycles * 1024, transcendentals=0)


def response(sens_ref, factor_ref, sensor, variable):
    total = sens_ref[sensor, 0] * factor_ref[0, variable]
    for u in range(1, factor_ref.shape[0]):
        total = total + sens_ref[sensor, u] * factor_ref[u, variable]
    return total


def fetch(pairs, sems):
    copies = [pltpu.make_async_copy(src, dst, sems.at[i]) for i, (src, dst) in enumerate(pairs)]
    for copy in copies:
        copy.start()
    return copies


def window_of(chip, chips, blocks):
    own = blocks // chips
    size = min(own + 2, own + chips - 1)
    return jnp.clip(chip * own - 1, 0, blocks - size), size


def my_chip():
    return lax.axis_index("var") // 2


def chip_count():
    return lax.axis_size("var") // 2


def lanes(start, size):
    return pl.ds(pl.multiple_of(start * LANES, LANES), size * LANES)


def first_kernel(slots, margin, sens_hbm, factor_hbm, control_hbm, kappa_hbm, tile_hbm, row_hbm, sensor_hbm,
                 value_hbm, weight_hbm, cols_hbm, own_ref, other_ref, response_ref, kappa_ref, even_ref,
                 odd_ref, *refs):
    chunk_refs = refs[:-11]
    (sens_ref, factor_ref, control_ref, tile_ref, row_ref, sensor_ref, value_ref, weight_ref, cols_ref,
     send_ref, sems) = refs[-11:]
    window = lanes(*window_of(my_chip(), chip_count(), own_ref.shape[1] // LANES))
    pairs = (
        (sens_hbm, sens_ref), (factor_hbm, factor_ref), (control_hbm, control_ref),
        (kappa_hbm.at[:, :, window], kappa_ref), (tile_hbm, tile_ref), (row_hbm, row_ref), (sensor_hbm, sensor_ref),
        (value_hbm, value_ref), (weight_hbm, weight_ref), (cols_hbm, cols_ref),
    )
    copies = [pltpu.make_async_copy(src, dst, sems.at[i]) for i, (src, dst) in enumerate(pairs)]
    for copy in copies:
        copy.start()
    send_ref[...] = jnp.zeros(send_ref.shape, F32)
    turns = len(chunk_refs)
    for copy in copies:
        copy.wait()

    member, mine = lax.axis_index("var"), lax.axis_index("tile")
    core = member % 2
    var_dev = control_ref.shape[0]
    for which, (sensor, out_ref) in enumerate(((core, own_ref), (1 - core, other_ref))):
        total = None
        for v in range(var_dev):
            scale = response(sens_ref, factor_ref, sensor, member * var_dev + v)
            response_ref[which, v] = jnp.full(response_ref.shape[2:], scale, F32)
            term = scale * control_ref[v]
            total = term if total is None else total + term
        out_ref[...] = total

    for i in range(2):
        pack_edges(even_ref.at[i], odd_ref.at[i], kappa_ref[i], margin)

    panels = value_ref.shape[0]
    sub = lax.broadcasted_iota(jnp.int32, (8 * turns, LANES), 0)
    lane = lax.broadcasted_iota(jnp.int32, (8 * turns, LANES), 1)
    trash = 3 * slots + 7

    def place(p, carry):
        meta, counts = carry
        turn = (tile_ref[p] ^ mine) - core * turns
        keep = (turn >= 0) & (turn < turns)
        turn = jnp.where(keep, turn, 0)
        slot = counts[0]
        for i in range(1, turns):
            slot = jnp.where(turn == i, counts[i], slot)
        counts = [c + (keep & (turn == i)).astype(jnp.int32) for i, c in enumerate(counts)]
        rows = (value_ref[pl.ds(p, 1), :], weight_ref[pl.ds(p, 1), :], cols_ref[pl.ds(p, 1), :].astype(F32))
        for part, row in enumerate(rows):
            send_ref[turn, pl.ds(jnp.where(keep, part * slots + slot, trash), 1), :] = row
        facts = jnp.where(sub == 8 * turn, row_ref[p], sensor_ref[p]).astype(F32)
        here = (lane == jnp.where(keep, slot, LANES)) & (sub // 8 == turn)
        return jnp.where(here, facts, meta), counts

    none = jnp.zeros((8 * turns, LANES), F32), [jnp.int32(0)] * turns
    meta, counts = lax.fori_loop(0, panels, place, none, unroll=8)
    for turn, chunk_ref in enumerate(chunk_refs):
        chunk_ref[: 3 * slots] = send_ref[turn, : 3 * slots]
        facts = meta[8 * turn : 8 * turn + 8]
        chunk_ref[3 * slots :] = jnp.where(lane[:8] == slots, counts[turn].astype(F32), facts)


def pieces(values):
    top = values.astype(jnp.bfloat16).astype(F32)
    return top, values - top


def scatter_kernel(slots, blocks_all, after_ref, home_ref, *refs):
    got_refs, (own_ref, other_ref, first_ref, acc_ref, meta_ref, sems) = refs[:-6], refs[-6:]
    core = lax.axis_index("var") % 2
    first_ref[...] = jnp.where(core == 0, home_ref[...], got_refs[0][...])
    got_refs = (first_ref, *got_refs[1:])
    copies = [
        pltpu.make_async_copy(ref.at[pl.ds(3 * slots, 8)], meta_ref.at[pl.ds(8 * s, 8)], sems.at[s])
        for s, ref in enumerate(got_refs)
    ]
    for copy in copies:
        copy.start()
    rows = own_ref.shape[1]
    start, size = window_of(my_chip(), chip_count(), blocks_all)
    per_kind = padded_blocks(size)
    tall = 2 * per_kind
    acc_ref[...] = jnp.zeros(acc_ref.shape, F32)
    place = lax.broadcasted_iota(jnp.int32, (tall, LANES), 0)
    is_weight = place < per_kind
    place = jnp.where(is_weight, place, place - per_kind) + start
    lane_ids = lax.broadcasted_iota(jnp.int32, (LANES, LANES), 0).astype(F32).astype(jnp.bfloat16)
    one, zero = jnp.bfloat16(1), jnp.bfloat16(0)
    sub = lax.broadcasted_iota(jnp.int32, (GROUP, LANES), 0)
    blank = jnp.zeros((2 * tall, LANES), jnp.bfloat16)
    for copy in copies:
        copy.wait()

    def load(s, base):
        got_ref = got_refs[s]
        count = meta_ref[8 * s, slots].astype(jnp.int32)
        value = got_ref[pl.ds(base, GROUP), :]
        weight = got_ref[pl.ds(slots + base, GROUP), :]
        cell = got_ref[pl.ds(2 * slots + base, GROUP), :].astype(jnp.int32)
        weight = jnp.where(sub + base < count, weight, 0.0)
        return pieces(weight), pieces(weight * value), (cell % LANES).astype(F32), cell // LANES

    def one_hots(loaded, i):
        weights, values, low, high = loaded
        here = place == high[i : i + 1]
        rows_of = [
            jnp.where(here, jnp.where(is_weight, w[i : i + 1], v[i : i + 1]), 0.0)
            for w, v in zip(weights, values)
        ]
        left = jnp.concatenate(rows_of, axis=0).astype(jnp.bfloat16)
        column = jnp.broadcast_to(low[i : i + 1], (16, LANES)).astype(jnp.bfloat16)
        column = jnp.concatenate([column] * (LANES // 16), axis=0)
        return left, jnp.where(lane_ids == column, one, zero)

    def pair(s, g, carry):
        base = pl.multiple_of(g * GROUP, GROUP)
        loaded = [load(s + i, base) for i in (0, 1)]
        for k in range(GROUP):
            hots = [one_hots(loaded[i], k) for i in (0, 1)]
            left = jnp.concatenate(
                [
                    jnp.concatenate([hots[0][0], blank], axis=1),
                    jnp.concatenate([blank, hots[1][0]], axis=1),
                ],
                axis=0,
            )
            both = lax.dot_general(
                left, jnp.concatenate([hots[0][1], hots[1][1]], axis=1), (((1,), (1,)), ((), ())),
                preferred_element_type=F32,
            )
            for i in (0, 1):
                row = meta_ref[8 * (s + i), base + k].astype(jnp.int32)
                sensor = meta_ref[8 * (s + i) + 1, base + k].astype(jnp.int32)
                at = pl.multiple_of((sensor * rows + row) * tall, 8)
                mine = both[2 * i * tall : 2 * (i + 1) * tall]
                acc_ref[pl.ds(at, tall), :] += mine[:tall] + mine[tall:]
        return carry

    for s in range(0, len(got_refs), 2):
        most = jnp.maximum(meta_ref[8 * s, slots], meta_ref[8 * s + 8, slots]).astype(jnp.int32)
        lax.fori_loop(0, (most + GROUP - 1) // GROUP, functools.partial(pair, s), 0)
    for sensor, out_ref in ((core, own_ref), (1 - core, other_ref)):
        begin = sensor * rows * tall
        for kind in range(2):
            for b in range(size):
                out_ref[kind, :, b * LANES : (b + 1) * LANES] = acc_ref[
                    pl.ds(begin + kind * per_kind + b, rows, stride=tall), :
                ]


def padded_blocks(size):
    return -(-size // 4) * 4


def even_tile():
    return lax.axis_index("tile") % 2 == 0


def has_above():
    return lax.axis_index("tile") > 0


def has_below():
    return lax.axis_index("tile") + 1 < lax.axis_size("tile")


def pack_edges(even_ref, odd_ref, rows_value, margin):
    rows, width = rows_value.shape
    even = even_tile()
    for b in range(width // LANES):
        at = slice(b * LANES, (b + 1) * LANES)
        head, tail = rows_value[:margin, at], rows_value[rows - margin :, at]
        even_ref[b * margin : (b + 1) * margin] = jnp.where(even, tail, head)
        odd_ref[b * margin : (b + 1) * margin] = jnp.where(even, head, tail)


def cut_kernel(first_ref, second_ref, mine_ref, *out_refs):
    chip, chips, blocks = my_chip(), chip_count(), first_ref.shape[1] // LANES
    for d, out_ref in enumerate((mine_ref, *out_refs)):
        window = lanes(*window_of(chip ^ d, chips, blocks))
        out_ref[...] = first_ref[:, window] + second_ref[:, window]


def edges_kernel(margin, *refs):
    terms, (total_ref, even_ref, odd_ref) = refs[:-3], refs[-3:]
    total = terms[0][...]
    for term in terms[1:]:
        total = total + term[...]
    total_ref[...] = total
    pack_edges(even_ref, odd_ref, total, margin)


def ring_rows(rows, margin):
    return -(-(rows + 2 * margin) // 8) * 8


def lay_ring(ref, own, from_even, from_odd, margin):
    rows, total = own.shape[0], ref.shape[0]
    even = even_tile()
    ref[rows:total] = jnp.zeros((total - rows, ref.shape[1]), F32)
    ref[:rows] = own
    for b in range(ref.shape[1] // LANES):
        at = slice(b * LANES, (b + 1) * LANES)
        one, two = (m[b * margin : (b + 1) * margin] for m in (from_even, from_odd))
        ref[rows : rows + margin, at] = jnp.where(has_below(), jnp.where(even, one, two), 0.0)
        ref[total - margin :, at] = jnp.where(has_above(), jnp.where(even, two, one), 0.0)


def block(ref, j):
    return ref[:, j * LANES : (j + 1) * LANES]


def sideways(blocks):
    shape = blocks[0].shape
    lane = lax.broadcasted_iota(jnp.int32, shape, 1)
    zero = jnp.zeros(shape, F32)
    ahead = [pltpu.roll(x, 1, 1) for x in blocks]
    back = [pltpu.roll(x, LANES - 1, 1) for x in blocks]
    for j, here in enumerate(blocks):
        before = ahead[j - 1] if j else zero
        after = back[j + 1] if j + 1 < len(blocks) else zero
        yield here, jnp.where(lane == 0, before, ahead[j]), jnp.where(lane == LANES - 1, after, back[j])


def face_weights(coef_ref, row_ref, col_ref, rows, margin):
    total, width = row_ref.shape
    blocks = width // LANES
    r = lax.broadcasted_iota(jnp.int32, (total, LANES), 0)
    inside = (
        (r < rows)
        | ((r < rows + margin) & has_below())
        | ((r >= total - margin) & has_above())
    )
    scale = jnp.where(inside, 0.125, 0.0)
    unit = jnp.where(inside, 1.0, 0.0)
    columns = [block(col_ref, j) for j in range(blocks)]
    for j, (k_col, k_left, k_right) in enumerate(sideways(columns)):
        at = slice(j * LANES, (j + 1) * LANES)
        k_row = block(row_ref, j)
        up = scale * (k_row + pltpu.roll(k_row, 1, 0))
        down = scale * (k_row + pltpu.roll(k_row, total - 1, 0))
        left = scale * (k_col + k_left)
        right = scale * (k_col + k_right)
        coef_ref[0, :, at] = unit - up - down - left - right
        coef_ref[1, :, at] = up
        coef_ref[2, :, at] = down
        coef_ref[3, :, at] = left
        coef_ref[4, :, at] = right


def one_pass(fields, coef_ref, spans):
    def weights(i, at):
        got = [coef_ref[i, span, at] for span in spans]
        return jnp.concatenate(got, axis=0) if len(got) > 1 else got[0]

    total = fields[0].shape[0]
    out = []
    for j, (here, left, right) in enumerate(sideways(fields)):
        at = slice(j * LANES, (j + 1) * LANES)
        out.append(
            weights(0, at) * here
            + weights(1, at) * pltpu.roll(here, 1, 0)
            + weights(2, at) * pltpu.roll(here, total - 1, 0)
            + weights(3, at) * left
            + weights(4, at) * right
        )
    return out


def diffuse(ring_ref, coef_ref, rows, margin):
    total, width = ring_ref.shape
    inner = margin // 8 * 8
    wide = [slice(0, total)]
    narrow = [slice(0, rows + inner), slice(total - inner, total)]
    fields = [block(ring_ref, j) for j in range(width // LANES)]
    for _ in range(margin - inner):
        fields = one_pass(fields, coef_ref, wide)
    fields = [jnp.concatenate([f[span] for span in narrow], axis=0) for f in fields]
    for _ in range(inner):
        fields = one_pass(fields, coef_ref, narrow)
    return [f[:rows] for f in fields]


def faces_kernel(margin, even_ref, odd_ref, kappa_ref, sums_ref, *refs):
    coef_ref, sums_out, one_ref, two_ref = refs[-4:]
    sums_out[...] = sums_ref[...]
    rows = kappa_ref.shape[1]
    lay_ring(one_ref, kappa_ref[0], even_ref.at[0], odd_ref.at[0], margin)
    lay_ring(two_ref, kappa_ref[1], even_ref.at[1], odd_ref.at[1], margin)
    face_weights(coef_ref, one_ref, two_ref, rows, margin)


def smooth_kernel(margin, own_ref, even_ref, odd_ref, coef_ref, out_ref, ring_ref):
    rows = own_ref.shape[0]
    lay_ring(ring_ref, own_ref[...], even_ref, odd_ref, margin)
    for j, field in enumerate(diffuse(ring_ref, coef_ref, rows, margin)):
        out_ref[:, j * LANES : (j + 1) * LANES] = field


def adjoint_kernel(margin, smooth_ref, mask_ref, sums_ref, more_ref, adjoint_ref, even_ref, odd_ref):
    weight = sums_ref[0] + more_ref[0]
    value = sums_ref[1] + more_ref[1]
    window = lanes(*window_of(my_chip(), chip_count(), mask_ref.shape[1] // LANES))
    adjoint = mask_ref[:, window].astype(F32) * (weight * smooth_ref[...] - value)
    adjoint_ref[...] = adjoint
    pack_edges(even_ref, odd_ref, adjoint, margin)


def spread_kernel(margin, own_ref, even_ref, odd_ref, coef_ref, out_ref, ring_ref):
    rows = own_ref.shape[0]
    lay_ring(ring_ref, own_ref[...], even_ref, odd_ref, margin)
    for j, field in enumerate(diffuse(ring_ref, coef_ref, rows, margin)):
        ring_ref[:rows, j * LANES : (j + 1) * LANES] = field
    own = out_ref.shape[1] // LANES
    start = window_of(my_chip(), chip_count(), own * chip_count())[0]
    out_ref[...] = ring_ref[:rows, lanes(my_chip() * own - start, own)]


def result_kernel(response_ref, control_ref, *refs):
    own, out_ref = refs[0].shape[1] // LANES, refs[-1]
    for d in range(len(refs) // 2):
        window = lanes((my_chip() ^ d) * own, own)
        for v in range(control_ref.shape[0]):
            mine, theirs = (response_ref[i, v][:1, :1] for i in range(2))
            out_ref[v, :, window] = (
                control_ref[v, :, window] + mine * refs[2 * d][...] + theirs * refs[2 * d + 1][...]
            )


def swap(values, axis, bit):
    count = lax.axis_size(axis)
    return lax.ppermute(values, axis, [(i, i ^ bit) for i in range(count)])


def swap_edges(even, odd):
    tiles, members = lax.axis_size("tile"), lax.axis_size("var")
    pairs = []
    for t in range(tiles):
        other = t + 1 if t % 2 else t - 1
        for q in range(members):
            to = other * members + q if 0 <= other < tiles else t * members + (q ^ 1)
            pairs.append((t * members + q, to))
    return swap(even, "tile", 1), lax.ppermute(odd, ("tile", "var"), pairs)


def deliver(chunk, turn):
    tiles, members = lax.axis_size("tile"), lax.axis_size("var")
    pairs = []
    for t in range(tiles):
        for q in range(members):
            offset = (q % 2) * (tiles // 2) + turn
            to = (t ^ offset) * members + (q if offset else q ^ 2)
            pairs.append((t * members + q, to))
    return lax.ppermute(chunk, ("tile", "var"), pairs)


def local(control, diffusivity, land_mask, panel_tile, panel_row, panel_cols, obs_values,
          obs_weights, panel_sensor, sensitivity, cross_factor):
    rows, width = control.shape[1:]
    var_dev = control.shape[0]
    tiles, members = lax.axis_size("tile"), lax.axis_size("var")
    panels, panel_width = panel_cols.shape
    slots = 2 * panels // tiles
    turns = tiles // 2
    blocks = width // LANES
    margin = PASSES
    total = ring_rows(rows, margin)
    chips = members // 2
    size = window_of(0, chips, blocks)[1]
    field = jax.ShapeDtypeStruct((rows, width), F32)
    share = jax.ShapeDtypeStruct((rows, width // chips), F32)
    view = jax.ShapeDtypeStruct((rows, size * LANES), F32)
    view2 = jax.ShapeDtypeStruct((2, *view.shape), F32)
    edge = jax.ShapeDtypeStruct((margin * size, LANES), F32)
    edge2 = jax.ShapeDtypeStruct((2, *edge.shape), F32)
    chunk = jax.ShapeDtypeStruct((3 * slots + 8, panel_width), F32)
    ints = pltpu.SMEM((panels,), jnp.int32)

    own, other, responses, kappa, kappa_even, kappa_odd, *chunks = call(
        functools.partial(first_kernel, slots, margin),
        [field, field, jax.ShapeDtypeStruct((2, var_dev, 8, LANES), F32), view2, edge2, edge2]
        + [chunk] * turns,
        [HBM] * 10,
        [
            pltpu.SMEM(sensitivity.shape, F32),
            pltpu.SMEM(cross_factor.shape, F32),
            pltpu.VMEM(control.shape, F32),
            ints, ints, ints,
            pltpu.VMEM(obs_values.shape, F32),
            pltpu.VMEM(obs_weights.shape, F32),
            pltpu.VMEM(panel_cols.shape, jnp.int32),
            pltpu.VMEM((turns, *chunk.shape), F32),
            pltpu.SemaphoreType.DMA((10,)),
        ],
        cost=cost(3000),
    )(*(in_hbm(x) for x in (sensitivity, cross_factor, control, diffusivity, panel_tile.reshape(-1),
                            panel_row, panel_sensor, obs_values, obs_weights, panel_cols)))

    got = [deliver(c, turn) for turn, c in enumerate(chunks)]
    part, *parts = call(cut_kernel, [view] * chips, [VMEM] * 2, cost=cost(200))(
        own, swap(other, "var", 1)
    )
    parts = [swap(p, "var", 2 * (d + 1)) for d, p in enumerate(parts)]
    kappa_even, kappa_odd = swap_edges(kappa_even, kappa_odd)
    smooth_in, even, odd = call(
        functools.partial(edges_kernel, margin), [view, edge, edge], [VMEM] * chips, cost=cost(500)
    )(part, *parts)
    even, odd = swap_edges(even, odd)
    sums, sums_other = call(
        functools.partial(scatter_kernel, slots, blocks),
        [view2, view2],
        [AFTER] + [VMEM] * (turns + 1),
        [
            pltpu.VMEM(chunk.shape, F32),
            pltpu.VMEM((2 * rows * 2 * padded_blocks(size), LANES), F32),
            pltpu.SMEM((8 * turns, LANES), F32),
            pltpu.SemaphoreType.DMA((turns,)),
        ],
        cost=cost(100000),
    )(smooth_in, chunks[0], *got)
    ring = pltpu.VMEM((total, size * LANES), F32)
    coef, sums_other = call(
        functools.partial(faces_kernel, margin),
        [jax.ShapeDtypeStruct((5, total, size * LANES), F32), view2],
        [VMEM] * 4 + [AFTER] * 2,
        [ring, ring],
        cost=cost(1000),
    )(kappa_even, kappa_odd, kappa, sums_other, even, odd)
    more_sums = swap(sums_other, "var", 1)
    (smooth,) = call(
        functools.partial(smooth_kernel, margin),
        [view],
        [VMEM] * 4,
        [ring],
        cost=cost(4000),
    )(smooth_in, even, odd, coef)
    adjoint, even, odd = call(
        functools.partial(adjoint_kernel, margin), [view, edge, edge], [VMEM] * 4, cost=cost(500)
    )(smooth, land_mask, sums, more_sums)
    even, odd = swap_edges(even, odd)
    (mine,) = call(
        functools.partial(spread_kernel, margin),
        [share],
        [VMEM] * 4,
        [ring],
        cost=cost(4000),
    )(adjoint, even, odd, coef)
    shares = [mine] + [swap(mine, "var", d) for d in range(1, members)]
    (out,) = call(
        result_kernel,
        [jax.ShapeDtypeStruct(control.shape, F32)],
        [VMEM] * (2 + members),
        cost=cost(1000),
    )(responses, control, *shares)
    return out


def solution(mesh):
    return jax.shard_map(
        local,
        mesh=mesh,
        in_specs=(
            P("var", ("grp", "tile"), None),
            P(None, ("grp", "tile"), None),
            P(("grp", "tile"), None),
            P(("grp", "tile"), None),
            P(("grp", "tile")),
            P(("grp", "tile"), None),
            P(("grp", "tile"), None),
            P(("grp", "tile"), None),
            P(("grp", "tile")),
            P(),
            P(),
        ),
        out_specs=P("var", ("grp", "tile"), None),
        check_vma=False,
    )
```

profile of v0, /device:TPU:0, one launch (start us, length us, event | category | flops | bytes accessed | tf_op | source)
XLA Modules:
  0.0 30.9 jit_solution(3490111258510516162)
XLA Ops:
  0.0 3.0 %shard_map.109 = (f32[16,2048]{1,0:T(8,128)S(1)}, f32[16,2048]{1,0:T(8,128)S(1)}, f32[2,2,8,128]{3,2,1,0:T(8,128)S(1)}, f32[2,16,1152]{2,1,0:T(8,128)S(1)}, f32[...) custom-call(f32[2,8]{1,0:T(2,128)} %sens_hbm.1, ...), custom_call_target="tpu_custom_call" | custom-call | flops 12288000 | bytes 3072000 | tf_op jit(solution)/shard_map/pallas_call | solution.py:452
  3.0 0.5 %collective-permute-start = (f32[16,2048]{1,0:T(8,128)S(1)}, f32[16,2048]{1,0:T(8,128)S(1)}, u32[]{:S(2)}, u32[]{:S(2)}) collective-permute-start(f32[16,2048]{1,0:T(8,128)S(1)} %get-tuple-element.27), channel_id=1, source_target_pairs={{0,1},{1,0},{2,3},{3,2},{4,5},{5,4},{6,7},{7,6},{8,9},{9,8},{10,11... | collective-permute-start | bytes 393224 | tf_op jit(solution)/shard_map/ppermute | solution.py:405
  3.5 2.6 %collective-permute-start.7 = (f32[200,128]{1,0:T(8,128)S(1)}, f32[200,128]{1,0:T(8,128)S(1)}, u32[]{:S(2)}, u32[]{:S(2)}) collective-permute-start(f32[200,128]{1,0:T(8,128)S(1)} %get-tuple-element.37), channel_id=1, source_target_pairs={{0,4},{1,13},{2,6},{3,15},{4,0},{5,9},{6,2},{7,11},{8,12},{9,5},{1... | collective-permute-start | bytes 307208 | tf_op jit(solution)/shard_map/ppermute | solution.py:427
  6.2 1.5 %collective-permute-start.6 = (f32[200,128]{1,0:T(8,128)S(1)}, f32[200,128]{1,0:T(8,128)S(1)}, u32[]{:S(2)}, u32[]{:S(2)}) collective-permute-start(f32[200,128]{1,0:T(8,128)S(1)} %get-tuple-element.36.home_ref), channel_id=1, source_target_pairs={{0,2},{1,9},{2,0},{3,11},{4,6},{5,13},{6,4},{7,15},{8,10},{9,1},{1... | collective-permute-start | bytes 307208 | tf_op jit(solution)/shard_map/ppermute | solution.py:427
  7.7 0.0 collective-permute-done.second_ref
  7.7 0.6 %collective-permute-start.1 = (f32[16,1152]{1,0:T(8,128)S(1)}, f32[16,1152]{1,0:T(8,128)S(1)}, u32[]{:S(2)}, u32[]{:S(2)}) collective-permute-start(f32[16,1152]{1,0:T(8,128)S(1)} %get-tuple-element.29), channel_id=1, source_target_pairs={{0,2},{1,3},{2,0},{3,1},{4,6},{5,7},{6,4},{7,5},{8,10},{9,11},{10,... | collective-permute-start | bytes 221192 | tf_op jit(solution)/shard_map/ppermute | solution.py:405
  8.3 0.7 %collective-permute-start.4 = (f32[2,90,128]{2,1,0:T(8,128)S(1)}, f32[2,90,128]{2,1,0:T(8,128)S(1)}, u32[]{:S(2)}, u32[]{:S(2)}) collective-permute-start(f32[2,90,128]{2,1,0:T(8,128)S(1)} %get-tuple-element.33), channel_id=1, source_target_pairs={{0,4},{4,0},{8,12},{12,8},{1,5},{5,1},{9,13},{13,9},{2,6},{6,2},{1... | collective-permute-start | bytes 276488 | tf_op jit(solution)/shard_map/ppermute | solution.py:405
  9.0 0.9 %collective-permute-start.5 = (f32[2,90,128]{2,1,0:T(8,128)S(1)}, f32[2,90,128]{2,1,0:T(8,128)S(1)}, u32[]{:S(2)}, u32[]{:S(2)}) collective-permute-start(f32[2,90,128]{2,1,0:T(8,128)S(1)} %get-tuple-element.34), channel_id=1, source_target_pairs={{0,1},{1,0},{2,3},{3,2},{4,8},{5,9},{6,10},{7,11},{8,4},{9,5},{10,... | collective-permute-start | bytes 276488 | tf_op jit(solution)/shard_map/ppermute | solution.py:416
  9.9 2.7 %collective-permute-done.1.refs_1_ = f32[16,1152]{1,0:T(8,128)S(1)} collective-permute-done((f32[16,1152]{1,0:T(8,128)S(1)}, f32[16,1152]{1,0:T(8,128)S(1)}, u32[]{:S(2)}, u32[]{:S(2)}) %collective-permute-start.1) | collective-permute-done | bytes 73760 | tf_op jit(solution)/shard_map/ppermute | solution.py:405
  12.6 0.6 %collective-permute-start.2 = (f32[90,128]{1,0:T(8,128)S(1)}, f32[90,128]{1,0:T(8,128)S(1)}, u32[]{:S(2)}, u32[]{:S(2)}) collective-permute-start(f32[90,128]{1,0:T(8,128)S(1)} %get-tuple-element.31), channel_id=1, source_target_pairs={{0,4},{4,0},{8,12},{12,8},{1,5},{5,1},{9,13},{13,9},{2,6},{6,2},{1... | collective-permute-start | bytes 138248 | tf_op jit(solution)/shard_map/ppermute | solution.py:405
  13.3 0.0 collective-permute-start.3
  13.3 0.0 collective-permute-done.6.refs_0_
  13.3 1.8 %shard_map.112 = (f32[2,16,1152]{2,1,0:T(8,128)S(1)}, f32[2,16,1152]{2,1,0:T(8,128)S(1)}) custom-call(f32[16,1152]{1,0:T(8,128)S(1)} %get-tuple-element.30.after_ref.own_ref, f32[200,128]{1,0:T(8,128)S(1)} %get-tuple-element.36.home_ref, f32[200,128]{1,0:T(8,128)S(1)} %collective-permute-done.6.refs_0_, f32[200,128]{1,0:T(8,128)S(1)} %collective-permute-done.7.refs_1_), custom_call_target="tpu_custom_call" | custom-call | flops 409600000 | bytes 102400000 | tf_op jit(solution)/shard_map/pallas_call | solution.py:482
  15.1 0.0 collective-permute-done.5.odd_ref
  15.1 1.7 %collective-permute-done.2.refs_0_.even_ref = f32[90,128]{1,0:T(8,128)S(1)} collective-permute-done((f32[90,128]{1,0:T(8,128)S(1)}, f32[90,128]{1,0:T(8,128)S(1)}, u32[]{:S(2)}, u32[]{:S(2)}) %collective-permute-start.2) | collective-permute-done | bytes 46112 | tf_op jit(solution)/shard_map/ppermute | solution.py:405
  16.8 0.2 shard_map.113
  17.0 0.1 collective-permute-start.8
  17.1 0.0 copy-start.1
  17.1 1.3 %shard_map.114.smooth_ref = f32[16,1152]{1,0:T(8,128)S(1)} custom-call(f32[16,1152]{1,0:T(8,128)S(1)} %get-tuple-element.30.after_ref.own_ref, f32[90,128]{1,0:T(8,128)S(1)} %collective-permute-done.2.refs_0_.even_ref, f32[90,128]{1,0:T(8,128)S(1)} %collective-permute-done.3.refs_1_.odd_ref, f32[5,40,1152]{2,1,0:T(8,128)S(1)} %get-tuple-element.39.coef_ref), custom_call_target="tpu_custom_call" | custom-call | flops 16384000 | bytes 4096000 | tf_op jit(solution)/shard_map/pallas_call | solution.py:503
  18.4 0.1 collective-permute-done.8.more_ref
  18.5 2.2 %collective-permute-start.9 = (f32[90,128]{1,0:T(8,128)S(1)}, f32[90,128]{1,0:T(8,128)S(1)}, u32[]{:S(2)}, u32[]{:S(2)}) collective-permute-start(f32[90,128]{1,0:T(8,128)S(1)} %get-tuple-element.43), channel_id=1, source_target_pairs={{0,4},{4,0},{8,12},{12,8},{1,5},{5,1},{9,13},{13,9},{2,6},{6,2},{1... | collective-permute-start | bytes 138248 | tf_op jit(solution)/shard_map/ppermute | solution.py:405
  20.7 0.1 collective-permute-start.10
  20.8 2.2 %collective-permute-done.9.even_ref = f32[90,128]{1,0:T(8,128)S(1)} collective-permute-done((f32[90,128]{1,0:T(8,128)S(1)}, f32[90,128]{1,0:T(8,128)S(1)}, u32[]{:S(2)}, u32[]{:S(2)}) %collective-permute-start.9) | collective-permute-done | bytes 46112 | tf_op jit(solution)/shard_map/ppermute | solution.py:405
  23.0 0.0 collective-permute-done.10.odd_ref
  23.0 1.2 %shard_map.116.refs_0_ = f32[16,1024]{1,0:T(8,128)S(1)} custom-call(f32[16,1152]{1,0:T(8,128)S(1)} %get-tuple-element.42.own_ref, f32[90,128]{1,0:T(8,128)S(1)} %collective-permute-done.9.even_ref, f32[90,128]{1,0:T(8,128)S(1)} %collective-permute-done.10.odd_ref, f32[5,40,1152]{2,1,0:T(8,128)S(1)} %get-tuple-element.39.coef_ref), custom_call_target="tpu_custom_call" | custom-call | flops 16384000 | bytes 4096000 | tf_op jit(solution)/shard_map/pallas_call | solution.py:514
  24.3 1.0 %collective-permute-start.13 = (f32[16,1024]{1,0:T(8,128)S(1)}, f32[16,1024]{1,0:T(8,128)S(1)}, u32[]{:S(2)}, u32[]{:S(2)}) collective-permute-start(f32[16,1024]{1,0:T(8,128)S(1)} %shard_map.116.refs_0_), channel_id=1, source_target_pairs={{0,3},{1,2},{2,1},{3,0},{4,7},{5,6},{6,5},{7,4},{8,11},{9,10},{10,... | collective-permute-start | bytes 196616 | tf_op jit(solution)/shard_map/ppermute | solution.py:405
  25.3 0.6 %collective-permute-start.12 = (f32[16,1024]{1,0:T(8,128)S(1)}, f32[16,1024]{1,0:T(8,128)S(1)}, u32[]{:S(2)}, u32[]{:S(2)}) collective-permute-start(f32[16,1024]{1,0:T(8,128)S(1)} %shard_map.116.refs_0_), channel_id=1, source_target_pairs={{0,2},{1,3},{2,0},{3,1},{4,6},{5,7},{6,4},{7,5},{8,10},{9,11},{10,... | collective-permute-start | bytes 196616 | tf_op jit(solution)/shard_map/ppermute | solution.py:405
  25.9 0.3 collective-permute-start.11
  26.2 2.5 %collective-permute-done.13.refs_3_ = f32[16,1024]{1,0:T(8,128)S(1)} collective-permute-done((f32[16,1024]{1,0:T(8,128)S(1)}, f32[16,1024]{1,0:T(8,128)S(1)}, u32[]{:S(2)}, u32[]{:S(2)}) %collective-permute-start.13) | collective-permute-done | bytes 65568 | tf_op jit(solution)/shard_map/ppermute | solution.py:405
  28.7 1.5 %collective-permute-done.12.refs_2_ = f32[16,1024]{1,0:T(8,128)S(1)} collective-permute-done((f32[16,1024]{1,0:T(8,128)S(1)}, f32[16,1024]{1,0:T(8,128)S(1)}, u32[]{:S(2)}, u32[]{:S(2)}) %collective-permute-start.12) | collective-permute-done | bytes 65568 | tf_op jit(solution)/shard_map/ppermute | solution.py:405
  30.1 0.0 collective-permute-done.11.refs_1_
  30.1 0.8 %shard_map.117 = f32[2,16,2048]{2,1,0:T(8,128)} custom-call(f32[2,2,8,128]{3,2,1,0:T(8,128)S(1)} %get-tuple-element.25.response_ref, f32[2,16,2048]{2,1,0:T(8,128)S(1)} %copy-done, f32[16,1024]{1,0:T(8,128)S(1)} %shard_map.116.refs_0_, f32[16,1024]{1,0:T(8,128)S(1)} %collective-permute-done.11.refs_1_, f32[16,1024]{1,0:T(8,128)S(1)} %collective-permute-done.12.refs_2_, ...), custom_call_target="tpu_custom_call" | custom-call | flops 4096000 | bytes 1024000 | tf_op jit(solution)/shard_map/pallas_call | solution.py:522
  (9 shorter events, 0.1 us)
Async XLA Ops:
  3.0 4.7 %collective-permute-start = (f32[16,2048]{1,0:T(8,128)S(1)}, f32[16,2048]{1,0:T(8,128)S(1)}, u32[]{:S(2)}, u32[]{:S(2)}) collective-permute-start(f32[16,2048]{1,0:T(8,128)S(1)} %get-tuple-element.27), channel_id=1, source_target_pairs={{0,1},{1,0},{2,3},{3,2},{4,5},{5,4},{6,7},{7,6},{8,9},{9,8},{10,11... | collective-permute-start | bytes 393224 | tf_op jit(solution)/shard_map/ppermute | solution.py:405
  3.5 9.8 %collective-permute-start.7 = (f32[200,128]{1,0:T(8,128)S(1)}, f32[200,128]{1,0:T(8,128)S(1)}, u32[]{:S(2)}, u32[]{:S(2)}) collective-permute-start(f32[200,128]{1,0:T(8,128)S(1)} %get-tuple-element.37), channel_id=1, source_target_pairs={{0,4},{1,13},{2,6},{3,15},{4,0},{5,9},{6,2},{7,11},{8,12},{9,5},{1... | collective-permute-start | bytes 307208 | tf_op jit(solution)/shard_map/ppermute | solution.py:427
  6.2 7.1 %collective-permute-start.6 = (f32[200,128]{1,0:T(8,128)S(1)}, f32[200,128]{1,0:T(8,128)S(1)}, u32[]{:S(2)}, u32[]{:S(2)}) collective-permute-start(f32[200,128]{1,0:T(8,128)S(1)} %get-tuple-element.36.home_ref), channel_id=1, source_target_pairs={{0,2},{1,9},{2,0},{3,11},{4,6},{5,13},{6,4},{7,15},{8,10},{9,1},{1... | collective-permute-start | bytes 307208 | tf_op jit(solution)/shard_map/ppermute | solution.py:427
  7.7 4.9 %collective-permute-start.1 = (f32[16,1152]{1,0:T(8,128)S(1)}, f32[16,1152]{1,0:T(8,128)S(1)}, u32[]{:S(2)}, u32[]{:S(2)}) collective-permute-start(f32[16,1152]{1,0:T(8,128)S(1)} %get-tuple-element.29), channel_id=1, source_target_pairs={{0,2},{1,3},{2,0},{3,1},{4,6},{5,7},{6,4},{7,5},{8,10},{9,11},{10,... | collective-permute-start | bytes 221192 | tf_op jit(solution)/shard_map/ppermute | solution.py:405
  8.3 6.8 %collective-permute-start.4 = (f32[2,90,128]{2,1,0:T(8,128)S(1)}, f32[2,90,128]{2,1,0:T(8,128)S(1)}, u32[]{:S(2)}, u32[]{:S(2)}) collective-permute-start(f32[2,90,128]{2,1,0:T(8,128)S(1)} %get-tuple-element.33), channel_id=1, source_target_pairs={{0,4},{4,0},{8,12},{12,8},{1,5},{5,1},{9,13},{13,9},{2,6},{6,2},{1... | collective-permute-start | bytes 276488 | tf_op jit(solution)/shard_map/ppermute | solution.py:405
  9.0 6.1 %collective-permute-start.5 = (f32[2,90,128]{2,1,0:T(8,128)S(1)}, f32[2,90,128]{2,1,0:T(8,128)S(1)}, u32[]{:S(2)}, u32[]{:S(2)}) collective-permute-start(f32[2,90,128]{2,1,0:T(8,128)S(1)} %get-tuple-element.34), channel_id=1, source_target_pairs={{0,1},{1,0},{2,3},{3,2},{4,8},{5,9},{6,10},{7,11},{8,4},{9,5},{10,... | collective-permute-start | bytes 276488 | tf_op jit(solution)/shard_map/ppermute | solution.py:416
  12.6 4.2 %collective-permute-start.2 = (f32[90,128]{1,0:T(8,128)S(1)}, f32[90,128]{1,0:T(8,128)S(1)}, u32[]{:S(2)}, u32[]{:S(2)}) collective-permute-start(f32[90,128]{1,0:T(8,128)S(1)} %get-tuple-element.31), channel_id=1, source_target_pairs={{0,4},{4,0},{8,12},{12,8},{1,5},{5,1},{9,13},{13,9},{2,6},{6,2},{1... | collective-permute-start | bytes 138248 | tf_op jit(solution)/shard_map/ppermute | solution.py:405
  13.3 3.5 %collective-permute-start.3 = (f32[90,128]{1,0:T(8,128)S(1)}, f32[90,128]{1,0:T(8,128)S(1)}, u32[]{:S(2)}, u32[]{:S(2)}) collective-permute-start(f32[90,128]{1,0:T(8,128)S(1)} %get-tuple-element.32), channel_id=1, source_target_pairs={{0,1},{1,0},{2,3},{3,2},{4,8},{5,9},{6,10},{7,11},{8,4},{9,5},{10,... | collective-permute-start | bytes 138248 | tf_op jit(solution)/shard_map/ppermute | solution.py:416
  17.0 1.4 %collective-permute-start.8 = (f32[2,16,1152]{2,1,0:T(8,128)S(1)}, f32[2,16,1152]{2,1,0:T(8,128)S(1)}, u32[]{:S(2)}, u32[]{:S(2)}) collective-permute-start(f32[2,16,1152]{2,1,0:T(8,128)S(1)} %get-tuple-element.41), channel_id=1, source_target_pairs={{0,1},{1,0},{2,3},{3,2},{4,5},{5,4},{6,7},{7,6},{8,9},{9,8},{10,11... | collective-permute-start | bytes 442376 | tf_op jit(solution)/shard_map/ppermute | solution.py:405
  17.1 1.4 %copy-start.1 = (s32[16,2048]{1,0:T(8,128)S(1)}, s32[16,2048]{1,0:T(8,128)}, u32[]{:S(2)}) copy-start(s32[16,2048]{1,0:T(8,128)} %mask_ref.1) | copy-start | bytes 393220
  18.5 4.5 %collective-permute-start.9 = (f32[90,128]{1,0:T(8,128)S(1)}, f32[90,128]{1,0:T(8,128)S(1)}, u32[]{:S(2)}, u32[]{:S(2)}) collective-permute-start(f32[90,128]{1,0:T(8,128)S(1)} %get-tuple-element.43), channel_id=1, source_target_pairs={{0,4},{4,0},{8,12},{12,8},{1,5},{5,1},{9,13},{13,9},{2,6},{6,2},{1... | collective-permute-start | bytes 138248 | tf_op jit(solution)/shard_map/ppermute | solution.py:405
  20.7 2.3 %collective-permute-start.10 = (f32[90,128]{1,0:T(8,128)S(1)}, f32[90,128]{1,0:T(8,128)S(1)}, u32[]{:S(2)}, u32[]{:S(2)}) collective-permute-start(f32[90,128]{1,0:T(8,128)S(1)} %get-tuple-element.44), channel_id=1, source_target_pairs={{0,1},{1,0},{2,3},{3,2},{4,8},{5,9},{6,10},{7,11},{8,4},{9,5},{10,... | collective-permute-start | bytes 138248 | tf_op jit(solution)/shard_map/ppermute | solution.py:416
  23.0 7.1 %copy-start = (f32[2,16,2048]{2,1,0:T(8,128)S(1)}, f32[2,16,2048]{2,1,0:T(8,128)}, u32[]{:S(2)}) copy-start(f32[2,16,2048]{2,1,0:T(8,128)} %control_ref.1) | copy-start | bytes 786436
  24.3 4.4 %collective-permute-start.13 = (f32[16,1024]{1,0:T(8,128)S(1)}, f32[16,1024]{1,0:T(8,128)S(1)}, u32[]{:S(2)}, u32[]{:S(2)}) collective-permute-start(f32[16,1024]{1,0:T(8,128)S(1)} %shard_map.116.refs_0_), channel_id=1, source_target_pairs={{0,3},{1,2},{2,1},{3,0},{4,7},{5,6},{6,5},{7,4},{8,11},{9,10},{10,... | collective-permute-start | bytes 196616 | tf_op jit(solution)/shard_map/ppermute | solution.py:405
  25.3 4.9 %collective-permute-start.12 = (f32[16,1024]{1,0:T(8,128)S(1)}, f32[16,1024]{1,0:T(8,128)S(1)}, u32[]{:S(2)}, u32[]{:S(2)}) collective-permute-start(f32[16,1024]{1,0:T(8,128)S(1)} %shard_map.116.refs_0_), channel_id=1, source_target_pairs={{0,2},{1,3},{2,0},{3,1},{4,6},{5,7},{6,4},{7,5},{8,10},{9,11},{10,... | collective-permute-start | bytes 196616 | tf_op jit(solution)/shard_map/ppermute | solution.py:405
  25.9 4.2 %collective-permute-start.11 = (f32[16,1024]{1,0:T(8,128)S(1)}, f32[16,1024]{1,0:T(8,128)S(1)}, u32[]{:S(2)}, u32[]{:S(2)}) collective-permute-start(f32[16,1024]{1,0:T(8,128)S(1)} %shard_map.116.refs_0_), channel_id=1, source_target_pairs={{0,1},{1,0},{2,3},{3,2},{4,5},{5,4},{6,7},{7,6},{8,9},{9,8},{10,11... | collective-permute-start | bytes 196616 | tf_op jit(solution)/shard_map/ppermute | solution.py:405
where the time goes:
time: 31 us; the launch traced here: 30.9 us
  starting transfers between devices  11.9 us (38%)
  waiting for transfers between devices  10.6 us (34%)
  Pallas kernels  8.36 us (27%)
    ppermute x9, waiting for transfers between devices, swap(): return lax.ppermute(values, axis, [(i, i ^ bit) for i in range(count)])  10.6 us
    ppermute x9, starting transfers between devices, swap(): return lax.ppermute(values, axis, [(i, i ^ bit) for i in range(count)])  6.67 us
    ppermute x2, starting transfers between devices, deliver(): return lax.ppermute(chunk, ('tile', 'var'), pairs)  4.14 us
    pallas_call x1, Pallas kernels, local(): call(functools.partial(first_kernel, slots, margin), [field, field, jax.S...  2.99 us
    pallas_call x1, Pallas kernels, local(): call(functools.partial(scatter_kernel, slots, blocks), [view2, view2], [A...  1.8 us
    pallas_call x1, Pallas kernels, local(): call(functools.partial(smooth_kernel, margin), [view], [VMEM] * 4, [ring]...  1.25 us
    pallas_call x1, Pallas kernels, local(): call(functools.partial(spread_kernel, margin), [share], [VMEM] * 4, [ring...  1.25 us
    ppermute x3, starting transfers between devices, swap_edges(): return (swap(even, 'tile', 1), lax.ppermute(odd, ('tile', 'var'), pairs))  1.07 us
  transfers between devices with their start and end apart: 14, of which 6 were waited for; matrix products, arithmetic and copies ran while one was open for 0% of the time, Pallas kernels for 10%

commit v1 on v0

--- a/solution.py
+++ b/solution.py
@@ -72,9 +72,9 @@
 def first_kernel(slots, margin, sens_hbm, factor_hbm, control_hbm, kappa_hbm, tile_hbm, row_hbm, sensor_hbm,
                  value_hbm, weight_hbm, cols_hbm, own_ref, other_ref, response_ref, kappa_ref, even_ref,
                  odd_ref, *refs):
-    chunk_refs = refs[:-11]
+    chunk_refs = refs[:-12]
     (sens_ref, factor_ref, control_ref, tile_ref, row_ref, sensor_ref, value_ref, weight_ref, cols_ref,
-     send_ref, sems) = refs[-11:]
+     send_ref, count_ref, sems) = refs[-12:]
     window = lanes(*window_of(my_chip(), chip_count(), own_ref.shape[1] // LANES))
     pairs = (
         (sens_hbm, sens_ref), (factor_hbm, factor_ref), (control_hbm, control_ref),
@@ -86,6 +86,8 @@
         copy.start()
     send_ref[...] = jnp.zeros(send_ref.shape, F32)
     turns = len(chunk_refs)
+    for turn in range(turns):
+        count_ref[turn] = 0
     for copy in copies:
         copy.wait()
 
@@ -109,28 +111,24 @@
     lane = lax.broadcasted_iota(jnp.int32, (8 * turns, LANES), 1)
     trash = 3 * slots + 7
 
-    def place(p, carry):
-        meta, counts = carry
+    def place(p, meta):
         turn = (tile_ref[p] ^ mine) - core * turns
         keep = (turn >= 0) & (turn < turns)
         turn = jnp.where(keep, turn, 0)
-        slot = counts[0]
-        for i in range(1, turns):
-            slot = jnp.where(turn == i, counts[i], slot)
-        counts = [c + (keep & (turn == i)).astype(jnp.int32) for i, c in enumerate(counts)]
+        slot = count_ref[turn]
+        count_ref[turn] = slot + keep.astype(jnp.int32)
         rows = (value_ref[pl.ds(p, 1), :], weight_ref[pl.ds(p, 1), :], cols_ref[pl.ds(p, 1), :].astype(F32))
         for part, row in enumerate(rows):
             send_ref[turn, pl.ds(jnp.where(keep, part * slots + slot, trash), 1), :] = row
         facts = jnp.where(sub == 8 * turn, row_ref[p], sensor_ref[p]).astype(F32)
         here = (lane == jnp.where(keep, slot, LANES)) & (sub // 8 == turn)
-        return jnp.where(here, facts, meta), counts
-
-    none = jnp.zeros((8 * turns, LANES), F32), [jnp.int32(0)] * turns
-    meta, counts = lax.fori_loop(0, panels, place, none, unroll=8)
+        return jnp.where(here, facts, meta)
+
+    meta = lax.fori_loop(0, panels, place, jnp.zeros((8 * turns, LANES), F32), unroll=8)
     for turn, chunk_ref in enumerate(chunk_refs):
         chunk_ref[: 3 * slots] = send_ref[turn, : 3 * slots]
         facts = meta[8 * turn : 8 * turn + 8]
-        chunk_ref[3 * slots :] = jnp.where(lane[:8] == slots, counts[turn].astype(F32), facts)
+        chunk_ref[3 * slots :] = jnp.where(lane[:8] == slots, count_ref[turn].astype(F32), facts)
 
 
 def pieces(values):
@@ -422,8 +420,7 @@
     for t in range(tiles):
         for q in range(members):
             offset = (q % 2) * (tiles // 2) + turn
-            to = (t ^ offset) * members + (q if offset else q ^ 2)
-            pairs.append((t * members + q, to))
+            pairs.append((t * members + q, (t ^ max(offset, 1)) * members + q))
     return lax.ppermute(chunk, ("tile", "var"), pairs)
 
 
@@ -463,6 +460,7 @@
             pltpu.VMEM(obs_weights.shape, F32),
             pltpu.VMEM(panel_cols.shape, jnp.int32),
             pltpu.VMEM((turns, *chunk.shape), F32),
+            pltpu.SMEM((turns,), jnp.int32),
             pltpu.SemaphoreType.DMA((10,)),
         ],
         cost=cost(3000),

time: 31 us -> 30.4 us (0.981)
  starting transfers between devices: 11.9 us -> 14.5 us
  waiting for transfers between devices: 10.6 us -> 8.22 us
  Pallas kernels: 8.36 us -> 7.34 us
    ppermute x9, starting transfers between devices: 6.67 us -> 11.5 us  [swap(): return lax.ppermute(values, axis, [(i, i ^ bit) for i in range(count)])]
    ppermute x9, waiting for transfers between devices: 10.6 us -> 8.21 us  [swap(): return lax.ppermute(values, axis, [(i, i ^ bit) for i in range(count)])]
    ppermute x2, starting transfers between devices: 4.14 us -> 2.73 us  [deliver(): return lax.ppermute(chunk, ('tile', 'var'), pairs)]
    ppermute x3, starting transfers between devices: 1.07 us -> 0.31 us  [swap_edges(): return (swap(even, 'tile', 1), lax.ppermute(odd, ('tile', 'var'), pairs))]
    pallas_call x1, Pallas kernels: 2.99 us -> 2.48 us  [local(): call(functools.partial(first_kernel, slots, margin), [field, field, jax.S...]
    pallas_call x1, Pallas kernels: 1.8 us -> 1.29 us  [local(): call(functools.partial(scatter_kernel, slots, blocks), [view2, view2], [A...]
  transfers between devices with their start and end apart: 14 -> 14, of which waited for: 6 -> 6; matrix products, arithmetic and copies ran while one was open for 0% -> 0% of each run, Pallas kernels for 10% -> 9%
where the time goes in v1:
time: 30.4 us; the launch traced here: 30.2 us
  starting transfers between devices  14.5 us (48%)
  waiting for transfers between devices  8.22 us (27%)
  Pallas kernels  7.34 us (24%)
    ppermute x9, starting transfers between devices, swap(): return lax.ppermute(values, axis, [(i, i ^ bit) for i in range(count)])  11.5 us
    ppermute x9, waiting for transfers between devices, swap(): return lax.ppermute(values, axis, [(i, i ^ bit) for i in range(count)])  8.21 us
    ppermute x2, starting transfers between devices, deliver(): return lax.ppermute(chunk, ('tile', 'var'), pairs)  2.73 us
    pallas_call x1, Pallas kernels, local(): call(functools.partial(first_kernel, slots, margin), [field, field, jax.S...  2.48 us
    pallas_call x1, Pallas kernels, local(): call(functools.partial(scatter_kernel, slots, blocks), [view2, view2], [A...  1.29 us
    pallas_call x1, Pallas kernels, local(): call(functools.partial(smooth_kernel, margin), [view], [VMEM] * 4, [ring]...  1.25 us
    pallas_call x1, Pallas kernels, local(): call(functools.partial(spread_kernel, margin), [share], [VMEM] * 4, [ring...  1.25 us
    pallas_call x1, Pallas kernels, local(): call(result_kernel, [jax.ShapeDtypeStruct(control.shape, F32)], [VMEM] *...  0.78 us
  transfers between devices with their start and end apart: 14, of which 6 were waited for; matrix products, arithmetic and copies ran while one was open for 0% of the time, Pallas kernels for 9%

profile of v1, /device:TPU:0, one launch (start us, length us, event | category | flops | bytes accessed | tf_op | source)
XLA Modules:
  0.0 30.2 jit_solution(2189394411470316128)
XLA Ops:
  0.0 2.5 %shard_map.109 = (f32[16,2048]{1,0:T(8,128)S(1)}, f32[16,2048]{1,0:T(8,128)S(1)}, f32[2,2,8,128]{3,2,1,0:T(8,128)S(1)}, f32[2,16,1152]{2,1,0:T(8,128)S(1)}, f32[...) custom-call(f32[2,8]{1,0:T(2,128)} %sens_hbm.1, ...), custom_call_target="tpu_custom_call" | custom-call | flops 12288000 | bytes 3072000 | tf_op jit(solution)/shard_map/pallas_call | solution.py:449
  2.5 0.5 %collective-permute-start = (f32[16,2048]{1,0:T(8,128)S(1)}, f32[16,2048]{1,0:T(8,128)S(1)}, u32[]{:S(2)}, u32[]{:S(2)}) collective-permute-start(f32[16,2048]{1,0:T(8,128)S(1)} %get-tuple-element.27), channel_id=1, source_target_pairs={{0,1},{1,0},{2,3},{3,2},{4,5},{5,4},{6,7},{7,6},{8,9},{9,8},{10,11... | collective-permute-start | bytes 393224 | tf_op jit(solution)/shard_map/ppermute | solution.py:403
  3.0 2.6 %collective-permute-start.7 = (f32[200,128]{1,0:T(8,128)S(1)}, f32[200,128]{1,0:T(8,128)S(1)}, u32[]{:S(2)}, u32[]{:S(2)}) collective-permute-start(f32[200,128]{1,0:T(8,128)S(1)} %get-tuple-element.37), channel_id=1, source_target_pairs={{0,4},{1,13},{2,6},{3,15},{4,0},{5,9},{6,2},{7,11},{8,12},{9,5},{1... | collective-permute-start | bytes 307208 | tf_op jit(solution)/shard_map/ppermute | solution.py:424
  5.7 0.1 collective-permute-start.6
  5.7 0.0 collective-permute-done.second_ref
  5.8 1.9 %collective-permute-start.1 = (f32[16,1152]{1,0:T(8,128)S(1)}, f32[16,1152]{1,0:T(8,128)S(1)}, u32[]{:S(2)}, u32[]{:S(2)}) collective-permute-start(f32[16,1152]{1,0:T(8,128)S(1)} %get-tuple-element.29), channel_id=1, source_target_pairs={{0,2},{1,3},{2,0},{3,1},{4,6},{5,7},{6,4},{7,5},{8,10},{9,11},{10,... | collective-permute-start | bytes 221192 | tf_op jit(solution)/shard_map/ppermute | solution.py:403
  7.7 1.6 %collective-permute-start.4 = (f32[2,90,128]{2,1,0:T(8,128)S(1)}, f32[2,90,128]{2,1,0:T(8,128)S(1)}, u32[]{:S(2)}, u32[]{:S(2)}) collective-permute-start(f32[2,90,128]{2,1,0:T(8,128)S(1)} %get-tuple-element.33), channel_id=1, source_target_pairs={{0,4},{4,0},{8,12},{12,8},{1,5},{5,1},{9,13},{13,9},{2,6},{6,2},{1... | collective-permute-start | bytes 276488 | tf_op jit(solution)/shard_map/ppermute | solution.py:403
  9.3 0.2 collective-permute-start.5
  9.4 0.8 %collective-permute-done.1.refs_1_ = f32[16,1152]{1,0:T(8,128)S(1)} collective-permute-done((f32[16,1152]{1,0:T(8,128)S(1)}, f32[16,1152]{1,0:T(8,128)S(1)}, u32[]{:S(2)}, u32[]{:S(2)}) %collective-permute-start.1) | collective-permute-done | bytes 73760 | tf_op jit(solution)/shard_map/ppermute | solution.py:403
  10.2 2.5 %collective-permute-start.2 = (f32[90,128]{1,0:T(8,128)S(1)}, f32[90,128]{1,0:T(8,128)S(1)}, u32[]{:S(2)}, u32[]{:S(2)}) collective-permute-start(f32[90,128]{1,0:T(8,128)S(1)} %get-tuple-element.31), channel_id=1, source_target_pairs={{0,4},{4,0},{8,12},{12,8},{1,5},{5,1},{9,13},{13,9},{2,6},{6,2},{1... | collective-permute-start | bytes 138248 | tf_op jit(solution)/shard_map/ppermute | solution.py:403
  12.8 0.0 collective-permute-done.7.refs_1_
  12.8 0.0 collective-permute-start.3
  12.8 0.0 collective-permute-done.6.refs_0_
  12.8 1.3 %shard_map.112 = (f32[2,16,1152]{2,1,0:T(8,128)S(1)}, f32[2,16,1152]{2,1,0:T(8,128)S(1)}) custom-call(f32[16,1152]{1,0:T(8,128)S(1)} %get-tuple-element.30.after_ref.own_ref, f32[200,128]{1,0:T(8,128)S(1)} %get-tuple-element.36.home_ref, f32[200,128]{1,0:T(8,128)S(1)} %collective-permute-done.6.refs_0_, f32[200,128]{1,0:T(8,128)S(1)} %collective-permute-done.7.refs_1_), custom_call_target="tpu_custom_call" | custom-call | flops 409600000 | bytes 102400000 | tf_op jit(solution)/shard_map/pallas_call | solution.py:480
  14.1 0.1 collective-permute-done.4.even_ref
  14.1 0.0 collective-permute-done.5.odd_ref
  14.1 1.3 %collective-permute-done.2.refs_0_.even_ref = f32[90,128]{1,0:T(8,128)S(1)} collective-permute-done((f32[90,128]{1,0:T(8,128)S(1)}, f32[90,128]{1,0:T(8,128)S(1)}, u32[]{:S(2)}, u32[]{:S(2)}) %collective-permute-start.2) | collective-permute-done | bytes 46112 | tf_op jit(solution)/shard_map/ppermute | solution.py:403
  15.4 0.2 shard_map.113
  15.6 0.2 collective-permute-start.8
  15.8 1.2 %shard_map.114.smooth_ref = f32[16,1152]{1,0:T(8,128)S(1)} custom-call(f32[16,1152]{1,0:T(8,128)S(1)} %get-tuple-element.30.after_ref.own_ref, f32[90,128]{1,0:T(8,128)S(1)} %collective-permute-done.2.refs_0_.even_ref, f32[90,128]{1,0:T(8,128)S(1)} %collective-permute-done.3.refs_1_.odd_ref, f32[5,40,1152]{2,1,0:T(8,128)S(1)} %get-tuple-element.39.coef_ref), custom_call_target="tpu_custom_call" | custom-call | flops 16384000 | bytes 4096000 | tf_op jit(solution)/shard_map/pallas_call | solution.py:501
  17.1 2.8 %collective-permute-start.9 = (f32[90,128]{1,0:T(8,128)S(1)}, f32[90,128]{1,0:T(8,128)S(1)}, u32[]{:S(2)}, u32[]{:S(2)}) collective-permute-start(f32[90,128]{1,0:T(8,128)S(1)} %get-tuple-element.43), channel_id=1, source_target_pairs={{0,4},{4,0},{8,12},{12,8},{1,5},{5,1},{9,13},{13,9},{2,6},{6,2},{1... | collective-permute-start | bytes 138248 | tf_op jit(solution)/shard_map/ppermute | solution.py:403
  20.0 0.1 collective-permute-start.10
  20.1 2.2 %collective-permute-done.9.even_ref = f32[90,128]{1,0:T(8,128)S(1)} collective-permute-done((f32[90,128]{1,0:T(8,128)S(1)}, f32[90,128]{1,0:T(8,128)S(1)}, u32[]{:S(2)}, u32[]{:S(2)}) %collective-permute-start.9) | collective-permute-done | bytes 46112 | tf_op jit(solution)/shard_map/ppermute | solution.py:403
  22.3 0.0 collective-permute-done.10.odd_ref
  22.3 1.2 %shard_map.116.refs_0_ = f32[16,1024]{1,0:T(8,128)S(1)} custom-call(f32[16,1152]{1,0:T(8,128)S(1)} %get-tuple-element.42.own_ref, f32[90,128]{1,0:T(8,128)S(1)} %collective-permute-done.9.even_ref, f32[90,128]{1,0:T(8,128)S(1)} %collective-permute-done.10.odd_ref, f32[5,40,1152]{2,1,0:T(8,128)S(1)} %get-tuple-element.39.coef_ref), custom_call_target="tpu_custom_call" | custom-call | flops 16384000 | bytes 4096000 | tf_op jit(solution)/shard_map/pallas_call | solution.py:512
  23.5 1.0 %collective-permute-start.13 = (f32[16,1024]{1,0:T(8,128)S(1)}, f32[16,1024]{1,0:T(8,128)S(1)}, u32[]{:S(2)}, u32[]{:S(2)}) collective-permute-start(f32[16,1024]{1,0:T(8,128)S(1)} %shard_map.116.refs_0_), channel_id=1, source_target_pairs={{0,3},{1,2},{2,1},{3,0},{4,7},{5,6},{6,5},{7,4},{8,11},{9,10},{10,... | collective-permute-start | bytes 196616 | tf_op jit(solution)/shard_map/ppermute | solution.py:403
  24.5 0.6 %collective-permute-start.12 = (f32[16,1024]{1,0:T(8,128)S(1)}, f32[16,1024]{1,0:T(8,128)S(1)}, u32[]{:S(2)}, u32[]{:S(2)}) collective-permute-start(f32[16,1024]{1,0:T(8,128)S(1)} %shard_map.116.refs_0_), channel_id=1, source_target_pairs={{0,2},{1,3},{2,0},{3,1},{4,6},{5,7},{6,4},{7,5},{8,10},{9,11},{10,... | collective-permute-start | bytes 196616 | tf_op jit(solution)/shard_map/ppermute | solution.py:403
  25.2 0.3 collective-permute-start.11
  25.5 2.5 %collective-permute-done.13.refs_3_ = f32[16,1024]{1,0:T(8,128)S(1)} collective-permute-done((f32[16,1024]{1,0:T(8,128)S(1)}, f32[16,1024]{1,0:T(8,128)S(1)}, u32[]{:S(2)}, u32[]{:S(2)}) %collective-permute-start.13) | collective-permute-done | bytes 65568 | tf_op jit(solution)/shard_map/ppermute | solution.py:403
  28.0 1.4 %collective-permute-done.12.refs_2_ = f32[16,1024]{1,0:T(8,128)S(1)} collective-permute-done((f32[16,1024]{1,0:T(8,128)S(1)}, f32[16,1024]{1,0:T(8,128)S(1)}, u32[]{:S(2)}, u32[]{:S(2)}) %collective-permute-start.12) | collective-permute-done | bytes 65568 | tf_op jit(solution)/shard_map/ppermute | solution.py:403
  29.4 0.0 collective-permute-done.11.refs_1_
  29.4 0.8 %shard_map.117 = f32[2,16,2048]{2,1,0:T(8,128)} custom-call(f32[2,2,8,128]{3,2,1,0:T(8,128)S(1)} %get-tuple-element.25.response_ref, f32[2,16,2048]{2,1,0:T(8,128)S(1)} %copy-done, f32[16,1024]{1,0:T(8,128)S(1)} %shard_map.116.refs_0_, f32[16,1024]{1,0:T(8,128)S(1)} %collective-permute-done.11.refs_1_, f32[16,1024]{1,0:T(8,128)S(1)} %collective-permute-done.12.refs_2_, ...), custom_call_target="tpu_custom_call" | custom-call | flops 4096000 | bytes 1024000 | tf_op jit(solution)/shard_map/pallas_call | solution.py:520
  (9 shorter events, 0.1 us)
Async XLA Ops:
  2.5 3.2 %collective-permute-start = (f32[16,2048]{1,0:T(8,128)S(1)}, f32[16,2048]{1,0:T(8,128)S(1)}, u32[]{:S(2)}, u32[]{:S(2)}) collective-permute-start(f32[16,2048]{1,0:T(8,128)S(1)} %get-tuple-element.27), channel_id=1, source_target_pairs={{0,1},{1,0},{2,3},{3,2},{4,5},{5,4},{6,7},{7,6},{8,9},{9,8},{10,11... | collective-permute-start | bytes 393224 | tf_op jit(solution)/shard_map/ppermute | solution.py:403
  3.0 9.8 %collective-permute-start.7 = (f32[200,128]{1,0:T(8,128)S(1)}, f32[200,128]{1,0:T(8,128)S(1)}, u32[]{:S(2)}, u32[]{:S(2)}) collective-permute-start(f32[200,128]{1,0:T(8,128)S(1)} %get-tuple-element.37), channel_id=1, source_target_pairs={{0,4},{1,13},{2,6},{3,15},{4,0},{5,9},{6,2},{7,11},{8,12},{9,5},{1... | collective-permute-start | bytes 307208 | tf_op jit(solution)/shard_map/ppermute | solution.py:424
  5.7 7.1 %collective-permute-start.6 = (f32[200,128]{1,0:T(8,128)S(1)}, f32[200,128]{1,0:T(8,128)S(1)}, u32[]{:S(2)}, u32[]{:S(2)}) collective-permute-start(f32[200,128]{1,0:T(8,128)S(1)} %get-tuple-element.36.home_ref), channel_id=1, source_target_pairs={{0,4},{1,9},{2,6},{3,11},{4,0},{5,13},{6,2},{7,15},{8,12},{9,1},{1... | collective-permute-start | bytes 307208 | tf_op jit(solution)/shard_map/ppermute | solution.py:424
  5.8 4.4 %collective-permute-start.1 = (f32[16,1152]{1,0:T(8,128)S(1)}, f32[16,1152]{1,0:T(8,128)S(1)}, u32[]{:S(2)}, u32[]{:S(2)}) collective-permute-start(f32[16,1152]{1,0:T(8,128)S(1)} %get-tuple-element.29), channel_id=1, source_target_pairs={{0,2},{1,3},{2,0},{3,1},{4,6},{5,7},{6,4},{7,5},{8,10},{9,11},{10,... | collective-permute-start | bytes 221192 | tf_op jit(solution)/shard_map/ppermute | solution.py:403
  7.7 6.4 %collective-permute-start.4 = (f32[2,90,128]{2,1,0:T(8,128)S(1)}, f32[2,90,128]{2,1,0:T(8,128)S(1)}, u32[]{:S(2)}, u32[]{:S(2)}) collective-permute-start(f32[2,90,128]{2,1,0:T(8,128)S(1)} %get-tuple-element.33), channel_id=1, source_target_pairs={{0,4},{4,0},{8,12},{12,8},{1,5},{5,1},{9,13},{13,9},{2,6},{6,2},{1... | collective-permute-start | bytes 276488 | tf_op jit(solution)/shard_map/ppermute | solution.py:403
  9.3 4.9 %collective-permute-start.5 = (f32[2,90,128]{2,1,0:T(8,128)S(1)}, f32[2,90,128]{2,1,0:T(8,128)S(1)}, u32[]{:S(2)}, u32[]{:S(2)}) collective-permute-start(f32[2,90,128]{2,1,0:T(8,128)S(1)} %get-tuple-element.34), channel_id=1, source_target_pairs={{0,1},{1,0},{2,3},{3,2},{4,8},{5,9},{6,10},{7,11},{8,4},{9,5},{10,... | collective-permute-start | bytes 276488 | tf_op jit(solution)/shard_map/ppermute | solution.py:414
  10.2 5.2 %collective-permute-start.2 = (f32[90,128]{1,0:T(8,128)S(1)}, f32[90,128]{1,0:T(8,128)S(1)}, u32[]{:S(2)}, u32[]{:S(2)}) collective-permute-start(f32[90,128]{1,0:T(8,128)S(1)} %get-tuple-element.31), channel_id=1, source_target_pairs={{0,4},{4,0},{8,12},{12,8},{1,5},{5,1},{9,13},{13,9},{2,6},{6,2},{1... | collective-permute-start | bytes 138248 | tf_op jit(solution)/shard_map/ppermute | solution.py:403
  12.8 2.7 %collective-permute-start.3 = (f32[90,128]{1,0:T(8,128)S(1)}, f32[90,128]{1,0:T(8,128)S(1)}, u32[]{:S(2)}, u32[]{:S(2)}) collective-permute-start(f32[90,128]{1,0:T(8,128)S(1)} %get-tuple-element.32), channel_id=1, source_target_pairs={{0,1},{1,0},{2,3},{3,2},{4,8},{5,9},{6,10},{7,11},{8,4},{9,5},{10,... | collective-permute-start | bytes 138248 | tf_op jit(solution)/shard_map/ppermute | solution.py:414
  15.6 1.4 %collective-permute-start.8 = (f32[2,16,1152]{2,1,0:T(8,128)S(1)}, f32[2,16,1152]{2,1,0:T(8,128)S(1)}, u32[]{:S(2)}, u32[]{:S(2)}) collective-permute-start(f32[2,16,1152]{2,1,0:T(8,128)S(1)} %get-tuple-element.41), channel_id=1, source_target_pairs={{0,1},{1,0},{2,3},{3,2},{4,5},{5,4},{6,7},{7,6},{8,9},{9,8},{10,11... | collective-permute-start | bytes 442376 | tf_op jit(solution)/shard_map/ppermute | solution.py:403
  15.8 1.3 %copy-start.1 = (s32[16,2048]{1,0:T(8,128)S(1)}, s32[16,2048]{1,0:T(8,128)}, u32[]{:S(2)}) copy-start(s32[16,2048]{1,0:T(8,128)} %mask_ref.1) | copy-start | bytes 393220
  17.1 5.1 %collective-permute-start.9 = (f32[90,128]{1,0:T(8,128)S(1)}, f32[90,128]{1,0:T(8,128)S(1)}, u32[]{:S(2)}, u32[]{:S(2)}) collective-permute-start(f32[90,128]{1,0:T(8,128)S(1)} %get-tuple-element.43), channel_id=1, source_target_pairs={{0,4},{4,0},{8,12},{12,8},{1,5},{5,1},{9,13},{13,9},{2,6},{6,2},{1... | collective-permute-start | bytes 138248 | tf_op jit(solution)/shard_map/ppermute | solution.py:403
  20.0 2.3 %collective-permute-start.10 = (f32[90,128]{1,0:T(8,128)S(1)}, f32[90,128]{1,0:T(8,128)S(1)}, u32[]{:S(2)}, u32[]{:S(2)}) collective-permute-start(f32[90,128]{1,0:T(8,128)S(1)} %get-tuple-element.44), channel_id=1, source_target_pairs={{0,1},{1,0},{2,3},{3,2},{4,8},{5,9},{6,10},{7,11},{8,4},{9,5},{10,... | collective-permute-start | bytes 138248 | tf_op jit(solution)/shard_map/ppermute | solution.py:414
  22.3 7.1 %copy-start = (f32[2,16,2048]{2,1,0:T(8,128)S(1)}, f32[2,16,2048]{2,1,0:T(8,128)}, u32[]{:S(2)}) copy-start(f32[2,16,2048]{2,1,0:T(8,128)} %control_ref.1) | copy-start | bytes 786436
  23.5 4.4 %collective-permute-start.13 = (f32[16,1024]{1,0:T(8,128)S(1)}, f32[16,1024]{1,0:T(8,128)S(1)}, u32[]{:S(2)}, u32[]{:S(2)}) collective-permute-start(f32[16,1024]{1,0:T(8,128)S(1)} %shard_map.116.refs_0_), channel_id=1, source_target_pairs={{0,3},{1,2},{2,1},{3,0},{4,7},{5,6},{6,5},{7,4},{8,11},{9,10},{10,... | collective-permute-start | bytes 196616 | tf_op jit(solution)/shard_map/ppermute | solution.py:403
  24.5 4.9 %collective-permute-start.12 = (f32[16,1024]{1,0:T(8,128)S(1)}, f32[16,1024]{1,0:T(8,128)S(1)}, u32[]{:S(2)}, u32[]{:S(2)}) collective-permute-start(f32[16,1024]{1,0:T(8,128)S(1)} %shard_map.116.refs_0_), channel_id=1, source_target_pairs={{0,2},{1,3},{2,0},{3,1},{4,6},{5,7},{6,4},{7,5},{8,10},{9,11},{10,... | collective-permute-start | bytes 196616 | tf_op jit(solution)/shard_map/ppermute | solution.py:403
  25.2 4.2 %collective-permute-start.11 = (f32[16,1024]{1,0:T(8,128)S(1)}, f32[16,1024]{1,0:T(8,128)S(1)}, u32[]{:S(2)}, u32[]{:S(2)}) collective-permute-start(f32[16,1024]{1,0:T(8,128)S(1)} %shard_map.116.refs_0_), channel_id=1, source_target_pairs={{0,1},{1,0},{2,3},{3,2},{4,5},{5,4},{6,7},{7,6},{8,9},{9,8},{10,11... | collective-permute-start | bytes 196616 | tf_op jit(solution)/shard_map/ppermute | solution.py:403

commit v2 on v1

--- a/solution.py
+++ b/solution.py
@@ -352,7 +352,7 @@
     return [f[:rows] for f in fields]
 
 
-def faces_kernel(margin, even_ref, odd_ref, kappa_ref, sums_ref, *refs):
+def faces_kernel(margin, odd_ref, even_ref, kappa_ref, sums_ref, *refs):
     coef_ref, sums_out, one_ref, two_ref = refs[-4:]
     sums_out[...] = sums_ref[...]
     rows = kappa_ref.shape[1]
@@ -361,7 +361,7 @@
     face_weights(coef_ref, one_ref, two_ref, rows, margin)
 
 
-def smooth_kernel(margin, own_ref, even_ref, odd_ref, coef_ref, out_ref, ring_ref):
+def smooth_kernel(margin, own_ref, odd_ref, even_ref, coef_ref, out_ref, ring_ref):
     rows = own_ref.shape[0]
     lay_ring(ring_ref, own_ref[...], even_ref, odd_ref, margin)
     for j, field in enumerate(diffuse(ring_ref, coef_ref, rows, margin)):
@@ -411,7 +411,8 @@
         for q in range(members):
             to = other * members + q if 0 <= other < tiles else t * members + (q ^ 1)
             pairs.append((t * members + q, to))
-    return swap(even, "tile", 1), lax.ppermute(odd, ("tile", "var"), pairs)
+    odd = lax.ppermute(odd, ("tile", "var"), pairs)
+    return swap(even, "tile", 1), odd
 
 
 def deliver(chunk, turn):
@@ -496,7 +497,7 @@
         [VMEM] * 4 + [AFTER] * 2,
         [ring, ring],
         cost=cost(1000),
-    )(kappa_even, kappa_odd, kappa, sums_other, even, odd)
+    )(kappa_odd, kappa_even, kappa, sums_other, odd, even)
     more_sums = swap(sums_other, "var", 1)
     (smooth,) = call(
         functools.partial(smooth_kernel, margin),
@@ -504,7 +505,7 @@
         [VMEM] * 4,
         [ring],
         cost=cost(4000),
-    )(smooth_in, even, odd, coef)
+    )(smooth_in, odd, even, coef)
     adjoint, even, odd = call(
         functools.partial(adjoint_kernel, margin), [view, edge, edge], [VMEM] * 4, cost=cost(500)
     )(smooth, land_mask, sums, more_sums)

time: 30.4 us -> 30.3 us (level)
  waiting for transfers between devices: 8.22 us -> 7.01 us
  starting transfers between devices: 14.5 us -> 15.2 us
  Pallas kernels: 7.34 us -> 7.85 us
    ppermute x3, starting transfers between devices: 0.31 us -> 2.61 us  [swap_edges(): odd = lax.ppermute(odd, ('tile', 'var'), pairs)]
    ppermute x9, starting transfers between devices: 11.5 us -> 9.84 us  [swap(): return lax.ppermute(values, axis, [(i, i ^ bit) for i in range(count)])]
    ppermute x9, waiting for transfers between devices: 8.21 us -> 7 us  [swap(): return lax.ppermute(values, axis, [(i, i ^ bit) for i in range(count)])]
    pallas_call x1, Pallas kernels: 1.29 us -> 1.8 us  [local(): call(functools.partial(scatter_kernel, slots, blocks), [view2, view2], [A...]
  transfers between devices with their start and end apart: 14 -> 14, of which waited for: 6 -> 5; matrix products, arithmetic and copies ran while one was open for 0% -> 0% of each run, Pallas kernels for 9% -> 10%
where the time goes in v2:
time: 30.3 us; the launch traced here: 30.1 us
  starting transfers between devices  15.2 us (50%)
  Pallas kernels  7.85 us (26%)
  waiting for transfers between devices  7.01 us (23%)
    ppermute x9, starting transfers between devices, swap(): return lax.ppermute(values, axis, [(i, i ^ bit) for i in range(count)])  9.84 us
    ppermute x9, waiting for transfers between devices, swap(): return lax.ppermute(values, axis, [(i, i ^ bit) for i in range(count)])  7 us
    ppermute x2, starting transfers between devices, deliver(): return lax.ppermute(chunk, ('tile', 'var'), pairs)  2.73 us
    ppermute x3, starting transfers between devices, swap_edges(): odd = lax.ppermute(odd, ('tile', 'var'), pairs)  2.61 us
    pallas_call x1, Pallas kernels, local(): call(functools.partial(first_kernel, slots, margin), [field, field, jax.S...  2.48 us
    pallas_call x1, Pallas kernels, local(): call(functools.partial(scatter_kernel, slots, blocks), [view2, view2], [A...  1.8 us
    pallas_call x1, Pallas kernels, local(): call(functools.partial(smooth_kernel, margin), [view], [VMEM] * 4, [ring]...  1.25 us
    pallas_call x1, Pallas kernels, local(): call(functools.partial(spread_kernel, margin), [share], [VMEM] * 4, [ring...  1.25 us
  transfers between devices with their start and end apart: 14, of which 5 were waited for; matrix products, arithmetic and copies ran while one was open for 0% of the time, Pallas kernels for 10%

profile of v2, /device:TPU:0, one launch (start us, length us, event | category | flops | bytes accessed | tf_op | source)
XLA Modules:
  0.0 30.1 jit_solution(14669501574200751696)
XLA Ops:
  0.0 2.5 %shard_map.109 = (f32[16,2048]{1,0:T(8,128)S(1)}, f32[16,2048]{1,0:T(8,128)S(1)}, f32[2,2,8,128]{3,2,1,0:T(8,128)S(1)}, f32[2,16,1152]{2,1,0:T(8,128)S(1)}, f32[...) custom-call(f32[2,8]{1,0:T(2,128)} %sens_hbm.1, ...), custom_call_target="tpu_custom_call" | custom-call | flops 12288000 | bytes 3072000 | tf_op jit(solution)/shard_map/pallas_call | solution.py:450
  2.5 0.5 %collective-permute-start = (f32[16,2048]{1,0:T(8,128)S(1)}, f32[16,2048]{1,0:T(8,128)S(1)}, u32[]{:S(2)}, u32[]{:S(2)}) collective-permute-start(f32[16,2048]{1,0:T(8,128)S(1)} %get-tuple-element.27), channel_id=1, source_target_pairs={{0,1},{1,0},{2,3},{3,2},{4,5},{5,4},{6,7},{7,6},{8,9},{9,8},{10,11... | collective-permute-start | bytes 393224 | tf_op jit(solution)/shard_map/ppermute | solution.py:403
  3.0 2.6 %collective-permute-start.7 = (f32[200,128]{1,0:T(8,128)S(1)}, f32[200,128]{1,0:T(8,128)S(1)}, u32[]{:S(2)}, u32[]{:S(2)}) collective-permute-start(f32[200,128]{1,0:T(8,128)S(1)} %get-tuple-element.37), channel_id=1, source_target_pairs={{0,4},{1,13},{2,6},{3,15},{4,0},{5,9},{6,2},{7,11},{8,12},{9,5},{1... | collective-permute-start | bytes 307208 | tf_op jit(solution)/shard_map/ppermute | solution.py:425
  5.7 0.1 collective-permute-start.6
  5.8 1.9 %collective-permute-start.1 = (f32[16,1152]{1,0:T(8,128)S(1)}, f32[16,1152]{1,0:T(8,128)S(1)}, u32[]{:S(2)}, u32[]{:S(2)}) collective-permute-start(f32[16,1152]{1,0:T(8,128)S(1)} %get-tuple-element.29), channel_id=1, source_target_pairs={{0,2},{1,3},{2,0},{3,1},{4,6},{5,7},{6,4},{7,5},{8,10},{9,11},{10,... | collective-permute-start | bytes 221192 | tf_op jit(solution)/shard_map/ppermute | solution.py:403
  7.7 1.5 %collective-permute-start.4 = (f32[2,90,128]{2,1,0:T(8,128)S(1)}, f32[2,90,128]{2,1,0:T(8,128)S(1)}, u32[]{:S(2)}, u32[]{:S(2)}) collective-permute-start(f32[2,90,128]{2,1,0:T(8,128)S(1)} %get-tuple-element.33), channel_id=1, source_target_pairs={{0,1},{1,0},{2,3},{3,2},{4,8},{5,9},{6,10},{7,11},{8,4},{9,5},{10,... | collective-permute-start | bytes 276488 | tf_op jit(solution)/shard_map/ppermute | solution.py:414
  9.1 1.7 %collective-permute-start.5 = (f32[2,90,128]{2,1,0:T(8,128)S(1)}, f32[2,90,128]{2,1,0:T(8,128)S(1)}, u32[]{:S(2)}, u32[]{:S(2)}) collective-permute-start(f32[2,90,128]{2,1,0:T(8,128)S(1)} %get-tuple-element.34), channel_id=1, source_target_pairs={{0,4},{4,0},{8,12},{12,8},{1,5},{5,1},{9,13},{13,9},{2,6},{6,2},{1... | collective-permute-start | bytes 276488 | tf_op jit(solution)/shard_map/ppermute | solution.py:403
  10.8 0.0 collective-permute-done.1.refs_1_
  10.9 1.0 %collective-permute-start.2 = (f32[90,128]{1,0:T(8,128)S(1)}, f32[90,128]{1,0:T(8,128)S(1)}, u32[]{:S(2)}, u32[]{:S(2)}) collective-permute-start(f32[90,128]{1,0:T(8,128)S(1)} %get-tuple-element.31), channel_id=1, source_target_pairs={{0,1},{1,0},{2,3},{3,2},{4,8},{5,9},{6,10},{7,11},{8,4},{9,5},{10,... | collective-permute-start | bytes 138248 | tf_op jit(solution)/shard_map/ppermute | solution.py:414
  11.9 1.9 %collective-permute-start.3 = (f32[90,128]{1,0:T(8,128)S(1)}, f32[90,128]{1,0:T(8,128)S(1)}, u32[]{:S(2)}, u32[]{:S(2)}) collective-permute-start(f32[90,128]{1,0:T(8,128)S(1)} %get-tuple-element.32), channel_id=1, source_target_pairs={{0,4},{4,0},{8,12},{12,8},{1,5},{5,1},{9,13},{13,9},{2,6},{6,2},{1... | collective-permute-start | bytes 138248 | tf_op jit(solution)/shard_map/ppermute | solution.py:403
  13.8 0.0 collective-permute-done.6.refs_0_
  13.8 1.8 %shard_map.112 = (f32[2,16,1152]{2,1,0:T(8,128)S(1)}, f32[2,16,1152]{2,1,0:T(8,128)S(1)}) custom-call(f32[16,1152]{1,0:T(8,128)S(1)} %get-tuple-element.30.after_ref.own_ref, f32[200,128]{1,0:T(8,128)S(1)} %get-tuple-element.36.home_ref, f32[200,128]{1,0:T(8,128)S(1)} %collective-permute-done.6.refs_0_, f32[200,128]{1,0:T(8,128)S(1)} %collective-permute-done.7.refs_1_), custom_call_target="tpu_custom_call" | custom-call | flops 409600000 | bytes 102400000 | tf_op jit(solution)/shard_map/pallas_call | solution.py:481
  15.6 0.0 collective-permute-done.4.odd_ref
  15.6 0.0 collective-permute-done.5.even_ref
  15.6 0.7 %collective-permute-done.3.refs_1_.even_ref = f32[90,128]{1,0:T(8,128)S(1)} collective-permute-done((f32[90,128]{1,0:T(8,128)S(1)}, f32[90,128]{1,0:T(8,128)S(1)}, u32[]{:S(2)}, u32[]{:S(2)}) %collective-permute-start.3) | collective-permute-done | bytes 46112 | tf_op jit(solution)/shard_map/ppermute | solution.py:403
  16.4 0.2 shard_map.113
  16.6 0.1 collective-permute-start.8
  16.7 0.0 copy-start.1
  16.7 1.3 %shard_map.114.smooth_ref = f32[16,1152]{1,0:T(8,128)S(1)} custom-call(f32[16,1152]{1,0:T(8,128)S(1)} %get-tuple-element.30.after_ref.own_ref, f32[90,128]{1,0:T(8,128)S(1)} %collective-permute-done.2.refs_0_.odd_ref, f32[90,128]{1,0:T(8,128)S(1)} %collective-permute-done.3.refs_1_.even_ref, f32[5,40,1152]{2,1,0:T(8,128)S(1)} %get-tuple-element.39.coef_ref), custom_call_target="tpu_custom_call" | custom-call | flops 16384000 | bytes 4096000 | tf_op jit(solution)/shard_map/pallas_call | solution.py:502
  17.9 0.1 collective-permute-done.8.more_ref
  18.1 1.8 %collective-permute-start.9 = (f32[90,128]{1,0:T(8,128)S(1)}, f32[90,128]{1,0:T(8,128)S(1)}, u32[]{:S(2)}, u32[]{:S(2)}) collective-permute-start(f32[90,128]{1,0:T(8,128)S(1)} %get-tuple-element.43), channel_id=1, source_target_pairs={{0,4},{4,0},{8,12},{12,8},{1,5},{5,1},{9,13},{13,9},{2,6},{6,2},{1... | collective-permute-start | bytes 138248 | tf_op jit(solution)/shard_map/ppermute | solution.py:403
  19.9 0.1 collective-permute-start.10
  20.0 2.2 %collective-permute-done.9.even_ref = f32[90,128]{1,0:T(8,128)S(1)} collective-permute-done((f32[90,128]{1,0:T(8,128)S(1)}, f32[90,128]{1,0:T(8,128)S(1)}, u32[]{:S(2)}, u32[]{:S(2)}) %collective-permute-start.9) | collective-permute-done | bytes 46112 | tf_op jit(solution)/shard_map/ppermute | solution.py:403
  22.2 0.0 collective-permute-done.10.odd_ref
  22.2 1.2 %shard_map.116.refs_0_ = f32[16,1024]{1,0:T(8,128)S(1)} custom-call(f32[16,1152]{1,0:T(8,128)S(1)} %get-tuple-element.42.own_ref, f32[90,128]{1,0:T(8,128)S(1)} %collective-permute-done.9.even_ref, f32[90,128]{1,0:T(8,128)S(1)} %collective-permute-done.10.odd_ref, f32[5,40,1152]{2,1,0:T(8,128)S(1)} %get-tuple-element.39.coef_ref), custom_call_target="tpu_custom_call" | custom-call | flops 16384000 | bytes 4096000 | tf_op jit(solution)/shard_map/pallas_call | solution.py:513
  23.5 0.4 %collective-permute-start.13 = (f32[16,1024]{1,0:T(8,128)S(1)}, f32[16,1024]{1,0:T(8,128)S(1)}, u32[]{:S(2)}, u32[]{:S(2)}) collective-permute-start(f32[16,1024]{1,0:T(8,128)S(1)} %shard_map.116.refs_0_), channel_id=1, source_target_pairs={{0,3},{1,2},{2,1},{3,0},{4,7},{5,6},{6,5},{7,4},{8,11},{9,10},{10,... | collective-permute-start | bytes 196616 | tf_op jit(solution)/shard_map/ppermute | solution.py:403
  23.9 1.2 %collective-permute-start.12 = (f32[16,1024]{1,0:T(8,128)S(1)}, f32[16,1024]{1,0:T(8,128)S(1)}, u32[]{:S(2)}, u32[]{:S(2)}) collective-permute-start(f32[16,1024]{1,0:T(8,128)S(1)} %shard_map.116.refs_0_), channel_id=1, source_target_pairs={{0,2},{1,3},{2,0},{3,1},{4,6},{5,7},{6,4},{7,5},{8,10},{9,11},{10,... | collective-permute-start | bytes 196616 | tf_op jit(solution)/shard_map/ppermute | solution.py:403
  25.1 0.3 %collective-permute-start.11 = (f32[16,1024]{1,0:T(8,128)S(1)}, f32[16,1024]{1,0:T(8,128)S(1)}, u32[]{:S(2)}, u32[]{:S(2)}) collective-permute-start(f32[16,1024]{1,0:T(8,128)S(1)} %shard_map.116.refs_0_), channel_id=1, source_target_pairs={{0,1},{1,0},{2,3},{3,2},{4,5},{5,4},{6,7},{7,6},{8,9},{9,8},{10,11... | collective-permute-start | bytes 196616 | tf_op jit(solution)/shard_map/ppermute | solution.py:403
  25.4 2.5 %collective-permute-done.13.refs_3_ = f32[16,1024]{1,0:T(8,128)S(1)} collective-permute-done((f32[16,1024]{1,0:T(8,128)S(1)}, f32[16,1024]{1,0:T(8,128)S(1)}, u32[]{:S(2)}, u32[]{:S(2)}) %collective-permute-start.13) | collective-permute-done | bytes 65568 | tf_op jit(solution)/shard_map/ppermute | solution.py:403
  27.9 1.4 %collective-permute-done.12.refs_2_ = f32[16,1024]{1,0:T(8,128)S(1)} collective-permute-done((f32[16,1024]{1,0:T(8,128)S(1)}, f32[16,1024]{1,0:T(8,128)S(1)}, u32[]{:S(2)}, u32[]{:S(2)}) %collective-permute-start.12) | collective-permute-done | bytes 65568 | tf_op jit(solution)/shard_map/ppermute | solution.py:403
  29.4 0.0 collective-permute-done.11.refs_1_
  29.4 0.8 %shard_map.117 = f32[2,16,2048]{2,1,0:T(8,128)} custom-call(f32[2,2,8,128]{3,2,1,0:T(8,128)S(1)} %get-tuple-element.25.response_ref, f32[2,16,2048]{2,1,0:T(8,128)S(1)} %copy-done, f32[16,1024]{1,0:T(8,128)S(1)} %shard_map.116.refs_0_, f32[16,1024]{1,0:T(8,128)S(1)} %collective-permute-done.11.refs_1_, f32[16,1024]{1,0:T(8,128)S(1)} %collective-permute-done.12.refs_2_, ...), custom_call_target="tpu_custom_call" | custom-call | flops 4096000 | bytes 1024000 | tf_op jit(solution)/shard_map/pallas_call | solution.py:521
  (9 shorter events, 0.1 us)
Async XLA Ops:
  2.5 3.2 %collective-permute-start = (f32[16,2048]{1,0:T(8,128)S(1)}, f32[16,2048]{1,0:T(8,128)S(1)}, u32[]{:S(2)}, u32[]{:S(2)}) collective-permute-start(f32[16,2048]{1,0:T(8,128)S(1)} %get-tuple-element.27), channel_id=1, source_target_pairs={{0,1},{1,0},{2,3},{3,2},{4,5},{5,4},{6,7},{7,6},{8,9},{9,8},{10,11... | collective-permute-start | bytes 393224 | tf_op jit(solution)/shard_map/ppermute | solution.py:403
  3.0 8.9 %collective-permute-start.7 = (f32[200,128]{1,0:T(8,128)S(1)}, f32[200,128]{1,0:T(8,128)S(1)}, u32[]{:S(2)}, u32[]{:S(2)}) collective-permute-start(f32[200,128]{1,0:T(8,128)S(1)} %get-tuple-element.37), channel_id=1, source_target_pairs={{0,4},{1,13},{2,6},{3,15},{4,0},{5,9},{6,2},{7,11},{8,12},{9,5},{1... | collective-permute-start | bytes 307208 | tf_op jit(solution)/shard_map/ppermute | solution.py:425
  5.7 8.1 %collective-permute-start.6 = (f32[200,128]{1,0:T(8,128)S(1)}, f32[200,128]{1,0:T(8,128)S(1)}, u32[]{:S(2)}, u32[]{:S(2)}) collective-permute-start(f32[200,128]{1,0:T(8,128)S(1)} %get-tuple-element.36.home_ref), channel_id=1, source_target_pairs={{0,4},{1,9},{2,6},{3,11},{4,0},{5,13},{6,2},{7,15},{8,12},{9,1},{1... | collective-permute-start | bytes 307208 | tf_op jit(solution)/shard_map/ppermute | solution.py:425
  5.8 5.1 %collective-permute-start.1 = (f32[16,1152]{1,0:T(8,128)S(1)}, f32[16,1152]{1,0:T(8,128)S(1)}, u32[]{:S(2)}, u32[]{:S(2)}) collective-permute-start(f32[16,1152]{1,0:T(8,128)S(1)} %get-tuple-element.29), channel_id=1, source_target_pairs={{0,2},{1,3},{2,0},{3,1},{4,6},{5,7},{6,4},{7,5},{8,10},{9,11},{10,... | collective-permute-start | bytes 221192 | tf_op jit(solution)/shard_map/ppermute | solution.py:403
  7.7 7.9 %collective-permute-start.4 = (f32[2,90,128]{2,1,0:T(8,128)S(1)}, f32[2,90,128]{2,1,0:T(8,128)S(1)}, u32[]{:S(2)}, u32[]{:S(2)}) collective-permute-start(f32[2,90,128]{2,1,0:T(8,128)S(1)} %get-tuple-element.33), channel_id=1, source_target_pairs={{0,1},{1,0},{2,3},{3,2},{4,8},{5,9},{6,10},{7,11},{8,4},{9,5},{10,... | collective-permute-start | bytes 276488 | tf_op jit(solution)/shard_map/ppermute | solution.py:414
  9.1 6.5 %collective-permute-start.5 = (f32[2,90,128]{2,1,0:T(8,128)S(1)}, f32[2,90,128]{2,1,0:T(8,128)S(1)}, u32[]{:S(2)}, u32[]{:S(2)}) collective-permute-start(f32[2,90,128]{2,1,0:T(8,128)S(1)} %get-tuple-element.34), channel_id=1, source_target_pairs={{0,4},{4,0},{8,12},{12,8},{1,5},{5,1},{9,13},{13,9},{2,6},{6,2},{1... | collective-permute-start | bytes 276488 | tf_op jit(solution)/shard_map/ppermute | solution.py:403
  10.9 4.8 %collective-permute-start.2 = (f32[90,128]{1,0:T(8,128)S(1)}, f32[90,128]{1,0:T(8,128)S(1)}, u32[]{:S(2)}, u32[]{:S(2)}) collective-permute-start(f32[90,128]{1,0:T(8,128)S(1)} %get-tuple-element.31), channel_id=1, source_target_pairs={{0,1},{1,0},{2,3},{3,2},{4,8},{5,9},{6,10},{7,11},{8,4},{9,5},{10,... | collective-permute-start | bytes 138248 | tf_op jit(solution)/shard_map/ppermute | solution.py:414
  11.9 4.5 %collective-permute-start.3 = (f32[90,128]{1,0:T(8,128)S(1)}, f32[90,128]{1,0:T(8,128)S(1)}, u32[]{:S(2)}, u32[]{:S(2)}) collective-permute-start(f32[90,128]{1,0:T(8,128)S(1)} %get-tuple-element.32), channel_id=1, source_target_pairs={{0,4},{4,0},{8,12},{12,8},{1,5},{5,1},{9,13},{13,9},{2,6},{6,2},{1... | collective-permute-start | bytes 138248 | tf_op jit(solution)/shard_map/ppermute | solution.py:403
  16.6 1.4 %collective-permute-start.8 = (f32[2,16,1152]{2,1,0:T(8,128)S(1)}, f32[2,16,1152]{2,1,0:T(8,128)S(1)}, u32[]{:S(2)}, u32[]{:S(2)}) collective-permute-start(f32[2,16,1152]{2,1,0:T(8,128)S(1)} %get-tuple-element.41), channel_id=1, source_target_pairs={{0,1},{1,0},{2,3},{3,2},{4,5},{5,4},{6,7},{7,6},{8,9},{9,8},{10,11... | collective-permute-start | bytes 442376 | tf_op jit(solution)/shard_map/ppermute | solution.py:403
  16.7 1.4 %copy-start.1 = (s32[16,2048]{1,0:T(8,128)S(1)}, s32[16,2048]{1,0:T(8,128)}, u32[]{:S(2)}) copy-start(s32[16,2048]{1,0:T(8,128)} %mask_ref.1) | copy-start | bytes 393220
  18.1 4.2 %collective-permute-start.9 = (f32[90,128]{1,0:T(8,128)S(1)}, f32[90,128]{1,0:T(8,128)S(1)}, u32[]{:S(2)}, u32[]{:S(2)}) collective-permute-start(f32[90,128]{1,0:T(8,128)S(1)} %get-tuple-element.43), channel_id=1, source_target_pairs={{0,4},{4,0},{8,12},{12,8},{1,5},{5,1},{9,13},{13,9},{2,6},{6,2},{1... | collective-permute-start | bytes 138248 | tf_op jit(solution)/shard_map/ppermute | solution.py:403
  19.9 2.4 %collective-permute-start.10 = (f32[90,128]{1,0:T(8,128)S(1)}, f32[90,128]{1,0:T(8,128)S(1)}, u32[]{:S(2)}, u32[]{:S(2)}) collective-permute-start(f32[90,128]{1,0:T(8,128)S(1)} %get-tuple-element.44), channel_id=1, source_target_pairs={{0,1},{1,0},{2,3},{3,2},{4,8},{5,9},{6,10},{7,11},{8,4},{9,5},{10,... | collective-permute-start | bytes 138248 | tf_op jit(solution)/shard_map/ppermute | solution.py:414
  22.2 7.1 %copy-start = (f32[2,16,2048]{2,1,0:T(8,128)S(1)}, f32[2,16,2048]{2,1,0:T(8,128)}, u32[]{:S(2)}) copy-start(f32[2,16,2048]{2,1,0:T(8,128)} %control_ref.1) | copy-start | bytes 786436
  23.5 4.4 %collective-permute-start.13 = (f32[16,1024]{1,0:T(8,128)S(1)}, f32[16,1024]{1,0:T(8,128)S(1)}, u32[]{:S(2)}, u32[]{:S(2)}) collective-permute-start(f32[16,1024]{1,0:T(8,128)S(1)} %shard_map.116.refs_0_), channel_id=1, source_target_pairs={{0,3},{1,2},{2,1},{3,0},{4,7},{5,6},{6,5},{7,4},{8,11},{9,10},{10,... | collective-permute-start | bytes 196616 | tf_op jit(solution)/shard_map/ppermute | solution.py:403
  23.9 5.4 %collective-permute-start.12 = (f32[16,1024]{1,0:T(8,128)S(1)}, f32[16,1024]{1,0:T(8,128)S(1)}, u32[]{:S(2)}, u32[]{:S(2)}) collective-permute-start(f32[16,1024]{1,0:T(8,128)S(1)} %shard_map.116.refs_0_), channel_id=1, source_target_pairs={{0,2},{1,3},{2,0},{3,1},{4,6},{5,7},{6,4},{7,5},{8,10},{9,11},{10,... | collective-permute-start | bytes 196616 | tf_op jit(solution)/shard_map/ppermute | solution.py:403
  25.1 4.3 %collective-permute-start.11 = (f32[16,1024]{1,0:T(8,128)S(1)}, f32[16,1024]{1,0:T(8,128)S(1)}, u32[]{:S(2)}, u32[]{:S(2)}) collective-permute-start(f32[16,1024]{1,0:T(8,128)S(1)} %shard_map.116.refs_0_), channel_id=1, source_target_pairs={{0,1},{1,0},{2,3},{3,2},{4,5},{5,4},{6,7},{7,6},{8,9},{9,8},{10,11... | collective-permute-start | bytes 196616 | tf_op jit(solution)/shard_map/ppermute | solution.py:403

commit v3 on v2

--- a/solution.py
+++ b/solution.py
@@ -416,13 +416,17 @@
 
 
 def deliver(chunk, turn):
-    tiles, members = lax.axis_size("tile"), lax.axis_size("var")
+    groups, tiles, members = (lax.axis_size(name) for name in ("grp", "tile", "var"))
     pairs = []
-    for t in range(tiles):
-        for q in range(members):
-            offset = (q % 2) * (tiles // 2) + turn
-            pairs.append((t * members + q, (t ^ max(offset, 1)) * members + q))
-    return lax.ppermute(chunk, ("tile", "var"), pairs)
+    for g in range(groups):
+        for t in range(tiles):
+            for q in range(members):
+                offset = (q % 2) * (tiles // 2) + turn
+                to_group = g if offset else g ^ 1
+                pairs.append((
+                    (g * tiles + t) * members + q, (to_group * tiles + (t ^ offset)) * members + q
+                ))
+    return lax.ppermute(chunk, ("grp", "tile", "var"), pairs)
 
 
 def local(control, diffusivity, land_mask, panel_tile, panel_row, panel_cols, obs_values,

time: 30.3 us -> 31.6 us (1.043)
  starting transfers between devices: 15.2 us -> 16.9 us
  waiting for transfers between devices: 7.01 us -> 6.62 us
    ppermute x9, starting transfers between devices: 9.84 us -> 12.1 us  [swap(): return lax.ppermute(values, axis, [(i, i ^ bit) for i in range(count)])]
    ppermute x3, starting transfers between devices: 2.61 us -> 0.6 us  [swap_edges(): odd = lax.ppermute(odd, ('tile', 'var'), pairs)]
    ppermute x2, starting transfers between devices: 2.73 us -> 4.17 us  [deliver(): return lax.ppermute(chunk, ('grp', 'tile', 'var'), pairs)]
    ppermute x9, waiting for transfers between devices: 7 us -> 6.61 us  [swap(): return lax.ppermute(values, axis, [(i, i ^ bit) for i in range(count)])]
  transfers between devices with their start and end apart: 14 -> 14, of which waited for: 5 -> 6; matrix products, arithmetic and copies ran while one was open for 0% -> 0% of each run, Pallas kernels for 10% -> 10%
where the time goes in v3:
time: 31.6 us; the launch traced here: 31.5 us
  starting transfers between devices  16.9 us (53%)
  Pallas kernels  7.86 us (25%)
  waiting for transfers between devices  6.62 us (21%)
    ppermute x9, starting transfers between devices, swap(): return lax.ppermute(values, axis, [(i, i ^ bit) for i in range(count)])  12.1 us
    ppermute x9, waiting for transfers between devices, swap(): return lax.ppermute(values, axis, [(i, i ^ bit) for i in range(count)])  6.61 us
    ppermute x2, starting transfers between devices, deliver(): return lax.ppermute(chunk, ('grp', 'tile', 'var'), pairs)  4.17 us
    pallas_call x1, Pallas kernels, local(): call(functools.partial(first_kernel, slots, margin), [field, field, jax.S...  2.48 us
    pallas_call x1, Pallas kernels, local(): call(functools.partial(scatter_kernel, slots, blocks), [view2, view2], [A...  1.81 us
    pallas_call x1, Pallas kernels, local(): call(functools.partial(smooth_kernel, margin), [view], [VMEM] * 4, [ring]...  1.25 us
    pallas_call x1, Pallas kernels, local(): call(functools.partial(spread_kernel, margin), [share], [VMEM] * 4, [ring...  1.25 us
    pallas_call x1, Pallas kernels, local(): call(result_kernel, [jax.ShapeDtypeStruct(control.shape, F32)], [VMEM] *...  0.78 us
  transfers between devices with their start and end apart: 14, of which 6 were waited for; matrix products, arithmetic and copies ran while one was open for 0% of the time, Pallas kernels for 10%

profile of v3, /device:TPU:0, one launch (start us, length us, event | category | flops | bytes accessed | tf_op | source)
XLA Modules:
  0.0 31.5 jit_solution(14207467315485469507)
XLA Ops:
  0.0 2.5 %shard_map.109 = (f32[16,2048]{1,0:T(8,128)S(1)}, f32[16,2048]{1,0:T(8,128)S(1)}, f32[2,2,8,128]{3,2,1,0:T(8,128)S(1)}, f32[2,16,1152]{2,1,0:T(8,128)S(1)}, f32[...) custom-call(f32[2,8]{1,0:T(2,128)} %sens_hbm.1, ...), custom_call_target="tpu_custom_call" | custom-call | flops 12288000 | bytes 3072000 | tf_op jit(solution)/shard_map/pallas_call | solution.py:454
  2.5 0.5 %collective-permute-start = (f32[16,2048]{1,0:T(8,128)S(1)}, f32[16,2048]{1,0:T(8,128)S(1)}, u32[]{:S(2)}, u32[]{:S(2)}) collective-permute-start(f32[16,2048]{1,0:T(8,128)S(1)} %get-tuple-element.27), channel_id=1, source_target_pairs={{0,1},{1,0},{2,3},{3,2},{4,5},{5,4},{6,7},{7,6},{8,9},{9,8},{10,11... | collective-permute-start | bytes 393224 | tf_op jit(solution)/shard_map/ppermute | solution.py:403
  3.0 2.6 %collective-permute-start.7 = (f32[200,128]{1,0:T(8,128)S(1)}, f32[200,128]{1,0:T(8,128)S(1)}, u32[]{:S(2)}, u32[]{:S(2)}) collective-permute-start(f32[200,128]{1,0:T(8,128)S(1)} %get-tuple-element.37), channel_id=1, source_target_pairs={{0,4},{1,13},{2,6},{3,15},{4,0},{5,9},{6,2},{7,11},{8,12},{9,5},{1... | collective-permute-start | bytes 307208 | tf_op jit(solution)/shard_map/ppermute | solution.py:429
  5.7 1.5 %collective-permute-start.6 = (f32[200,128]{1,0:T(8,128)S(1)}, f32[200,128]{1,0:T(8,128)S(1)}, u32[]{:S(2)}, u32[]{:S(2)}) collective-permute-start(f32[200,128]{1,0:T(8,128)S(1)} %get-tuple-element.36.home_ref), channel_id=1, source_target_pairs={{0,16},{1,9},{2,18},{3,11},{4,20},{5,13},{6,22},{7,15},{8,24},{9,1... | collective-permute-start | bytes 307208 | tf_op jit(solution)/shard_map/ppermute | solution.py:429
  7.2 0.0 collective-permute-done.second_ref
  7.2 1.6 %collective-permute-start.1 = (f32[16,1152]{1,0:T(8,128)S(1)}, f32[16,1152]{1,0:T(8,128)S(1)}, u32[]{:S(2)}, u32[]{:S(2)}) collective-permute-start(f32[16,1152]{1,0:T(8,128)S(1)} %get-tuple-element.29), channel_id=1, source_target_pairs={{0,2},{1,3},{2,0},{3,1},{4,6},{5,7},{6,4},{7,5},{8,10},{9,11},{10,... | collective-permute-start | bytes 221192 | tf_op jit(solution)/shard_map/ppermute | solution.py:403
  8.8 0.4 %collective-permute-start.4 = (f32[2,90,128]{2,1,0:T(8,128)S(1)}, f32[2,90,128]{2,1,0:T(8,128)S(1)}, u32[]{:S(2)}, u32[]{:S(2)}) collective-permute-start(f32[2,90,128]{2,1,0:T(8,128)S(1)} %get-tuple-element.33), channel_id=1, source_target_pairs={{0,1},{1,0},{2,3},{3,2},{4,8},{5,9},{6,10},{7,11},{8,4},{9,5},{10,... | collective-permute-start | bytes 276488 | tf_op jit(solution)/shard_map/ppermute | solution.py:414
  9.1 2.8 %collective-permute-start.5 = (f32[2,90,128]{2,1,0:T(8,128)S(1)}, f32[2,90,128]{2,1,0:T(8,128)S(1)}, u32[]{:S(2)}, u32[]{:S(2)}) collective-permute-start(f32[2,90,128]{2,1,0:T(8,128)S(1)} %get-tuple-element.34), channel_id=1, source_target_pairs={{0,4},{4,0},{8,12},{12,8},{1,5},{5,1},{9,13},{13,9},{2,6},{6,2},{1... | collective-permute-start | bytes 276488 | tf_op jit(solution)/shard_map/ppermute | solution.py:403
  11.9 0.2 collective-permute-done.1.refs_1_
  12.1 0.1 collective-permute-start.2
  12.2 0.0 collective-permute-done.7.refs_1_
  12.2 3.2 %collective-permute-start.3 = (f32[90,128]{1,0:T(8,128)S(1)}, f32[90,128]{1,0:T(8,128)S(1)}, u32[]{:S(2)}, u32[]{:S(2)}) collective-permute-start(f32[90,128]{1,0:T(8,128)S(1)} %get-tuple-element.32), channel_id=1, source_target_pairs={{0,4},{4,0},{8,12},{12,8},{1,5},{5,1},{9,13},{13,9},{2,6},{6,2},{1... | collective-permute-start | bytes 138248 | tf_op jit(solution)/shard_map/ppermute | solution.py:403
  15.4 0.0 collective-permute-done.6.refs_0_
  15.4 1.8 %shard_map.112 = (f32[2,16,1152]{2,1,0:T(8,128)S(1)}, f32[2,16,1152]{2,1,0:T(8,128)S(1)}) custom-call(f32[16,1152]{1,0:T(8,128)S(1)} %get-tuple-element.30.after_ref.own_ref, f32[200,128]{1,0:T(8,128)S(1)} %get-tuple-element.36.home_ref, f32[200,128]{1,0:T(8,128)S(1)} %collective-permute-done.6.refs_0_, f32[200,128]{1,0:T(8,128)S(1)} %collective-permute-done.7.refs_1_), custom_call_target="tpu_custom_call" | custom-call | flops 409600000 | bytes 102400000 | tf_op jit(solution)/shard_map/pallas_call | solution.py:485
  17.2 0.0 collective-permute-done.5.even_ref
  17.2 0.0 collective-permute-done.2.refs_0_.odd_ref
  17.3 0.2 collective-permute-done.3.refs_1_.even_ref
  17.5 0.2 shard_map.113
  17.7 0.1 collective-permute-start.8
  17.8 0.0 copy-start.1
  17.8 1.3 %shard_map.114.smooth_ref = f32[16,1152]{1,0:T(8,128)S(1)} custom-call(f32[16,1152]{1,0:T(8,128)S(1)} %get-tuple-element.30.after_ref.own_ref, f32[90,128]{1,0:T(8,128)S(1)} %collective-permute-done.2.refs_0_.odd_ref, f32[90,128]{1,0:T(8,128)S(1)} %collective-permute-done.3.refs_1_.even_ref, f32[5,40,1152]{2,1,0:T(8,128)S(1)} %get-tuple-element.39.coef_ref), custom_call_target="tpu_custom_call" | custom-call | flops 16384000 | bytes 4096000 | tf_op jit(solution)/shard_map/pallas_call | solution.py:506
  19.0 0.1 collective-permute-done.8.more_ref
  19.2 2.1 %collective-permute-start.9 = (f32[90,128]{1,0:T(8,128)S(1)}, f32[90,128]{1,0:T(8,128)S(1)}, u32[]{:S(2)}, u32[]{:S(2)}) collective-permute-start(f32[90,128]{1,0:T(8,128)S(1)} %get-tuple-element.43), channel_id=1, source_target_pairs={{0,4},{4,0},{8,12},{12,8},{1,5},{5,1},{9,13},{13,9},{2,6},{6,2},{1... | collective-permute-start | bytes 138248 | tf_op jit(solution)/shard_map/ppermute | solution.py:403
  21.3 0.1 collective-permute-start.10
  21.4 2.2 %collective-permute-done.9.even_ref = f32[90,128]{1,0:T(8,128)S(1)} collective-permute-done((f32[90,128]{1,0:T(8,128)S(1)}, f32[90,128]{1,0:T(8,128)S(1)}, u32[]{:S(2)}, u32[]{:S(2)}) %collective-permute-start.9) | collective-permute-done | bytes 46112 | tf_op jit(solution)/shard_map/ppermute | solution.py:403
  23.6 1.2 %shard_map.116.refs_0_ = f32[16,1024]{1,0:T(8,128)S(1)} custom-call(f32[16,1152]{1,0:T(8,128)S(1)} %get-tuple-element.42.own_ref, f32[90,128]{1,0:T(8,128)S(1)} %collective-permute-done.9.even_ref, f32[90,128]{1,0:T(8,128)S(1)} %collective-permute-done.10.odd_ref, f32[5,40,1152]{2,1,0:T(8,128)S(1)} %get-tuple-element.39.coef_ref), custom_call_target="tpu_custom_call" | custom-call | flops 16384000 | bytes 4096000 | tf_op jit(solution)/shard_map/pallas_call | solution.py:517
  24.8 1.0 %collective-permute-start.13 = (f32[16,1024]{1,0:T(8,128)S(1)}, f32[16,1024]{1,0:T(8,128)S(1)}, u32[]{:S(2)}, u32[]{:S(2)}) collective-permute-start(f32[16,1024]{1,0:T(8,128)S(1)} %shard_map.116.refs_0_), channel_id=1, source_target_pairs={{0,3},{1,2},{2,1},{3,0},{4,7},{5,6},{6,5},{7,4},{8,11},{9,10},{10,... | collective-permute-start | bytes 196616 | tf_op jit(solution)/shard_map/ppermute | solution.py:403
  25.8 0.6 %collective-permute-start.12 = (f32[16,1024]{1,0:T(8,128)S(1)}, f32[16,1024]{1,0:T(8,128)S(1)}, u32[]{:S(2)}, u32[]{:S(2)}) collective-permute-start(f32[16,1024]{1,0:T(8,128)S(1)} %shard_map.116.refs_0_), channel_id=1, source_target_pairs={{0,2},{1,3},{2,0},{3,1},{4,6},{5,7},{6,4},{7,5},{8,10},{9,11},{10,... | collective-permute-start | bytes 196616 | tf_op jit(solution)/shard_map/ppermute | solution.py:403
  26.5 0.3 collective-permute-start.11
  26.8 2.5 %collective-permute-done.13.refs_3_ = f32[16,1024]{1,0:T(8,128)S(1)} collective-permute-done((f32[16,1024]{1,0:T(8,128)S(1)}, f32[16,1024]{1,0:T(8,128)S(1)}, u32[]{:S(2)}, u32[]{:S(2)}) %collective-permute-start.13) | collective-permute-done | bytes 65568 | tf_op jit(solution)/shard_map/ppermute | solution.py:403
  29.2 1.5 %collective-permute-done.12.refs_2_ = f32[16,1024]{1,0:T(8,128)S(1)} collective-permute-done((f32[16,1024]{1,0:T(8,128)S(1)}, f32[16,1024]{1,0:T(8,128)S(1)}, u32[]{:S(2)}, u32[]{:S(2)}) %collective-permute-start.12) | collective-permute-done | bytes 65568 | tf_op jit(solution)/shard_map/ppermute | solution.py:403
  30.7 0.8 %shard_map.117 = f32[2,16,2048]{2,1,0:T(8,128)} custom-call(f32[2,2,8,128]{3,2,1,0:T(8,128)S(1)} %get-tuple-element.25.response_ref, f32[2,16,2048]{2,1,0:T(8,128)S(1)} %copy-done, f32[16,1024]{1,0:T(8,128)S(1)} %shard_map.116.refs_0_, f32[16,1024]{1,0:T(8,128)S(1)} %collective-permute-done.11.refs_1_, f32[16,1024]{1,0:T(8,128)S(1)} %collective-permute-done.12.refs_2_, ...), custom_call_target="tpu_custom_call" | custom-call | flops 4096000 | bytes 1024000 | tf_op jit(solution)/shard_map/pallas_call | solution.py:525
  (9 shorter events, 0.1 us)
Async XLA Ops:
  2.5 4.7 %collective-permute-start = (f32[16,2048]{1,0:T(8,128)S(1)}, f32[16,2048]{1,0:T(8,128)S(1)}, u32[]{:S(2)}, u32[]{:S(2)}) collective-permute-start(f32[16,2048]{1,0:T(8,128)S(1)} %get-tuple-element.27), channel_id=1, source_target_pairs={{0,1},{1,0},{2,3},{3,2},{4,5},{5,4},{6,7},{7,6},{8,9},{9,8},{10,11... | collective-permute-start | bytes 393224 | tf_op jit(solution)/shard_map/ppermute | solution.py:403
  3.0 9.2 %collective-permute-start.7 = (f32[200,128]{1,0:T(8,128)S(1)}, f32[200,128]{1,0:T(8,128)S(1)}, u32[]{:S(2)}, u32[]{:S(2)}) collective-permute-start(f32[200,128]{1,0:T(8,128)S(1)} %get-tuple-element.37), channel_id=1, source_target_pairs={{0,4},{1,13},{2,6},{3,15},{4,0},{5,9},{6,2},{7,11},{8,12},{9,5},{1... | collective-permute-start | bytes 307208 | tf_op jit(solution)/shard_map/ppermute | solution.py:429
  5.7 9.8 %collective-permute-start.6 = (f32[200,128]{1,0:T(8,128)S(1)}, f32[200,128]{1,0:T(8,128)S(1)}, u32[]{:S(2)}, u32[]{:S(2)}) collective-permute-start(f32[200,128]{1,0:T(8,128)S(1)} %get-tuple-element.36.home_ref), channel_id=1, source_target_pairs={{0,16},{1,9},{2,18},{3,11},{4,20},{5,13},{6,22},{7,15},{8,24},{9,1... | collective-permute-start | bytes 307208 | tf_op jit(solution)/shard_map/ppermute | solution.py:429
  7.2 4.9 %collective-permute-start.1 = (f32[16,1152]{1,0:T(8,128)S(1)}, f32[16,1152]{1,0:T(8,128)S(1)}, u32[]{:S(2)}, u32[]{:S(2)}) collective-permute-start(f32[16,1152]{1,0:T(8,128)S(1)} %get-tuple-element.29), channel_id=1, source_target_pairs={{0,2},{1,3},{2,0},{3,1},{4,6},{5,7},{6,4},{7,5},{8,10},{9,11},{10,... | collective-permute-start | bytes 221192 | tf_op jit(solution)/shard_map/ppermute | solution.py:403
  8.8 8.5 %collective-permute-start.4 = (f32[2,90,128]{2,1,0:T(8,128)S(1)}, f32[2,90,128]{2,1,0:T(8,128)S(1)}, u32[]{:S(2)}, u32[]{:S(2)}) collective-permute-start(f32[2,90,128]{2,1,0:T(8,128)S(1)} %get-tuple-element.33), channel_id=1, source_target_pairs={{0,1},{1,0},{2,3},{3,2},{4,8},{5,9},{6,10},{7,11},{8,4},{9,5},{10,... | collective-permute-start | bytes 276488 | tf_op jit(solution)/shard_map/ppermute | solution.py:414
  9.1 8.1 %collective-permute-start.5 = (f32[2,90,128]{2,1,0:T(8,128)S(1)}, f32[2,90,128]{2,1,0:T(8,128)S(1)}, u32[]{:S(2)}, u32[]{:S(2)}) collective-permute-start(f32[2,90,128]{2,1,0:T(8,128)S(1)} %get-tuple-element.34), channel_id=1, source_target_pairs={{0,4},{4,0},{8,12},{12,8},{1,5},{5,1},{9,13},{13,9},{2,6},{6,2},{1... | collective-permute-start | bytes 276488 | tf_op jit(solution)/shard_map/ppermute | solution.py:403
  12.1 5.1 %collective-permute-start.2 = (f32[90,128]{1,0:T(8,128)S(1)}, f32[90,128]{1,0:T(8,128)S(1)}, u32[]{:S(2)}, u32[]{:S(2)}) collective-permute-start(f32[90,128]{1,0:T(8,128)S(1)} %get-tuple-element.31), channel_id=1, source_target_pairs={{0,1},{1,0},{2,3},{3,2},{4,8},{5,9},{6,10},{7,11},{8,4},{9,5},{10,... | collective-permute-start | bytes 138248 | tf_op jit(solution)/shard_map/ppermute | solution.py:414
  12.2 5.3 %collective-permute-start.3 = (f32[90,128]{1,0:T(8,128)S(1)}, f32[90,128]{1,0:T(8,128)S(1)}, u32[]{:S(2)}, u32[]{:S(2)}) collective-permute-start(f32[90,128]{1,0:T(8,128)S(1)} %get-tuple-element.32), channel_id=1, source_target_pairs={{0,4},{4,0},{8,12},{12,8},{1,5},{5,1},{9,13},{13,9},{2,6},{6,2},{1... | collective-permute-start | bytes 138248 | tf_op jit(solution)/shard_map/ppermute | solution.py:403
  17.7 1.4 %collective-permute-start.8 = (f32[2,16,1152]{2,1,0:T(8,128)S(1)}, f32[2,16,1152]{2,1,0:T(8,128)S(1)}, u32[]{:S(2)}, u32[]{:S(2)}) collective-permute-start(f32[2,16,1152]{2,1,0:T(8,128)S(1)} %get-tuple-element.41), channel_id=1, source_target_pairs={{0,1},{1,0},{2,3},{3,2},{4,5},{5,4},{6,7},{7,6},{8,9},{9,8},{10,11... | collective-permute-start | bytes 442376 | tf_op jit(solution)/shard_map/ppermute | solution.py:403
  17.8 1.4 %copy-start.1 = (s32[16,2048]{1,0:T(8,128)S(1)}, s32[16,2048]{1,0:T(8,128)}, u32[]{:S(2)}) copy-start(s32[16,2048]{1,0:T(8,128)} %mask_ref.1) | copy-start | bytes 393220
  19.2 4.4 %collective-permute-start.9 = (f32[90,128]{1,0:T(8,128)S(1)}, f32[90,128]{1,0:T(8,128)S(1)}, u32[]{:S(2)}, u32[]{:S(2)}) collective-permute-start(f32[90,128]{1,0:T(8,128)S(1)} %get-tuple-element.43), channel_id=1, source_target_pairs={{0,4},{4,0},{8,12},{12,8},{1,5},{5,1},{9,13},{13,9},{2,6},{6,2},{1... | collective-permute-start | bytes 138248 | tf_op jit(solution)/shard_map/ppermute | solution.py:403
  21.3 2.3 %collective-permute-start.10 = (f32[90,128]{1,0:T(8,128)S(1)}, f32[90,128]{1,0:T(8,128)S(1)}, u32[]{:S(2)}, u32[]{:S(2)}) collective-permute-start(f32[90,128]{1,0:T(8,128)S(1)} %get-tuple-element.44), channel_id=1, source_target_pairs={{0,1},{1,0},{2,3},{3,2},{4,8},{5,9},{6,10},{7,11},{8,4},{9,5},{10,... | collective-permute-start | bytes 138248 | tf_op jit(solution)/shard_map/ppermute | solution.py:414
  23.6 7.1 %copy-start = (f32[2,16,2048]{2,1,0:T(8,128)S(1)}, f32[2,16,2048]{2,1,0:T(8,128)}, u32[]{:S(2)}) copy-start(f32[2,16,2048]{2,1,0:T(8,128)} %control_ref.1) | copy-start | bytes 786436
  24.8 4.4 %collective-permute-start.13 = (f32[16,1024]{1,0:T(8,128)S(1)}, f32[16,1024]{1,0:T(8,128)S(1)}, u32[]{:S(2)}, u32[]{:S(2)}) collective-permute-start(f32[16,1024]{1,0:T(8,128)S(1)} %shard_map.116.refs_0_), channel_id=1, source_target_pairs={{0,3},{1,2},{2,1},{3,0},{4,7},{5,6},{6,5},{7,4},{8,11},{9,10},{10,... | collective-permute-start | bytes 196616 | tf_op jit(solution)/shard_map/ppermute | solution.py:403
  25.8 4.9 %collective-permute-start.12 = (f32[16,1024]{1,0:T(8,128)S(1)}, f32[16,1024]{1,0:T(8,128)S(1)}, u32[]{:S(2)}, u32[]{:S(2)}) collective-permute-start(f32[16,1024]{1,0:T(8,128)S(1)} %shard_map.116.refs_0_), channel_id=1, source_target_pairs={{0,2},{1,3},{2,0},{3,1},{4,6},{5,7},{6,4},{7,5},{8,10},{9,11},{10,... | collective-permute-start | bytes 196616 | tf_op jit(solution)/shard_map/ppermute | solution.py:403
  26.5 4.2 %collective-permute-start.11 = (f32[16,1024]{1,0:T(8,128)S(1)}, f32[16,1024]{1,0:T(8,128)S(1)}, u32[]{:S(2)}, u32[]{:S(2)}) collective-permute-start(f32[16,1024]{1,0:T(8,128)S(1)} %shard_map.116.refs_0_), channel_id=1, source_target_pairs={{0,1},{1,0},{2,3},{3,2},{4,5},{5,4},{6,7},{7,6},{8,9},{9,8},{10,11... | collective-permute-start | bytes 196616 | tf_op jit(solution)/shard_map/ppermute | solution.py:403

commit v4 on v1

--- a/solution.py
+++ b/solution.py
@@ -85,9 +85,8 @@
     for copy in copies:
         copy.start()
     send_ref[...] = jnp.zeros(send_ref.shape, F32)
-    turns = len(chunk_refs)
-    for turn in range(turns):
-        count_ref[turn] = 0
+    for source in range(lax.axis_size("tile")):
+        count_ref[source] = 0
     for copy in copies:
         copy.wait()
 
@@ -106,29 +105,41 @@
     for i in range(2):
         pack_edges(even_ref.at[i], odd_ref.at[i], kappa_ref[i], margin)
 
+    tiles = lax.axis_size("tile")
+    full = tiles // 2 - 1
+    first = jnp.where(core == 0, 1, tiles // 2)
     panels = value_ref.shape[0]
-    sub = lax.broadcasted_iota(jnp.int32, (8 * turns, LANES), 0)
-    lane = lax.broadcasted_iota(jnp.int32, (8 * turns, LANES), 1)
+    sub = lax.broadcasted_iota(jnp.int32, (8, LANES), 0)
+    lane = lax.broadcasted_iota(jnp.int32, (8, LANES), 1)
     trash = 3 * slots + 7
 
     def place(p, meta):
-        turn = (tile_ref[p] ^ mine) - core * turns
-        keep = (turn >= 0) & (turn < turns)
-        turn = jnp.where(keep, turn, 0)
-        slot = count_ref[turn]
-        count_ref[turn] = slot + keep.astype(jnp.int32)
+        source = tile_ref[p] ^ mine
+        count = count_ref[source]
+        count_ref[source] = count + 1
+        parity, slot = count % 2, count // 2
+        whole = (source >= first) & (source < first + full)
+        shared = ((source == 0) | (source == tiles - 1)) & (parity == core)
+        keep = whole | shared
+        half = jnp.where(whole, 2 * (source - first) + parity, jnp.where(source == 0, tiles - 1, tiles - 2))
+        half = jnp.where(keep, half, 0)
         rows = (value_ref[pl.ds(p, 1), :], weight_ref[pl.ds(p, 1), :], cols_ref[pl.ds(p, 1), :].astype(F32))
         for part, row in enumerate(rows):
-            send_ref[turn, pl.ds(jnp.where(keep, part * slots + slot, trash), 1), :] = row
-        facts = jnp.where(sub == 8 * turn, row_ref[p], sensor_ref[p]).astype(F32)
-        here = (lane == jnp.where(keep, slot, LANES)) & (sub // 8 == turn)
-        return jnp.where(here, facts, meta)
-
-    meta = lax.fori_loop(0, panels, place, jnp.zeros((8 * turns, LANES), F32), unroll=8)
-    for turn, chunk_ref in enumerate(chunk_refs):
-        chunk_ref[: 3 * slots] = send_ref[turn, : 3 * slots]
-        facts = meta[8 * turn : 8 * turn + 8]
-        chunk_ref[3 * slots :] = jnp.where(lane[:8] == slots, count_ref[turn].astype(F32), facts)
+            send_ref[half, pl.ds(jnp.where(keep, part * slots + slot, trash), 1), :] = row
+        facts = jnp.where(sub == 0, row_ref[p], sensor_ref[p]).astype(F32)
+        return jnp.where(lane == jnp.where(keep, half * slots + slot, LANES), facts, meta)
+
+    meta = lax.fori_loop(0, panels, place, jnp.zeros((8, LANES), F32), unroll=8)
+    for half in range(tiles):
+        if half < 2 * full:
+            held = (count_ref[first + half // 2] + 1 - half % 2) // 2
+        else:
+            held = (count_ref[0 if half == tiles - 1 else tiles - 1] + 1 - core) // 2
+        meta = jnp.where((sub == 2) & (lane == half), held.astype(F32), meta)
+    for half in range(tiles):
+        out_ref = chunk_refs[half // 2].at[half % 2] if half < 2 * full else chunk_refs[half - full]
+        out_ref[: 3 * slots] = send_ref[half, : 3 * slots]
+        out_ref[3 * slots :] = meta
 
 
 def pieces(values):
@@ -136,11 +147,11 @@
     return top, values - top
 
 
-def scatter_kernel(slots, blocks_all, after_ref, home_ref, *refs):
-    got_refs, (own_ref, other_ref, first_ref, acc_ref, meta_ref, sems) = refs[:-6], refs[-6:]
+def scatter_kernel(slots, blocks_all, after_ref, *refs):
+    got_refs, (own_ref, other_ref, acc_ref, meta_ref, sems) = refs[:-5], refs[-5:]
     core = lax.axis_index("var") % 2
-    first_ref[...] = jnp.where(core == 0, home_ref[...], got_refs[0][...])
-    got_refs = (first_ref, *got_refs[1:])
+    got_refs = [r.at[i] for r in got_refs[:-2] for i in (0, 1)] + list(got_refs[-2:])
+    size_of_group = min(GROUP, slots)
     copies = [
         pltpu.make_async_copy(ref.at[pl.ds(3 * slots, 8)], meta_ref.at[pl.ds(8 * s, 8)], sems.at[s])
         for s, ref in enumerate(got_refs)
@@ -157,17 +168,17 @@
     place = jnp.where(is_weight, place, place - per_kind) + start
     lane_ids = lax.broadcasted_iota(jnp.int32, (LANES, LANES), 0).astype(F32).astype(jnp.bfloat16)
     one, zero = jnp.bfloat16(1), jnp.bfloat16(0)
-    sub = lax.broadcasted_iota(jnp.int32, (GROUP, LANES), 0)
+    sub = lax.broadcasted_iota(jnp.int32, (size_of_group, LANES), 0)
     blank = jnp.zeros((2 * tall, LANES), jnp.bfloat16)
     for copy in copies:
         copy.wait()
 
     def load(s, base):
         got_ref = got_refs[s]
-        count = meta_ref[8 * s, slots].astype(jnp.int32)
-        value = got_ref[pl.ds(base, GROUP), :]
-        weight = got_ref[pl.ds(slots + base, GROUP), :]
-        cell = got_ref[pl.ds(2 * slots + base, GROUP), :].astype(jnp.int32)
+        count = meta_ref[8 * s + 2, s].astype(jnp.int32)
+        value = got_ref[pl.ds(base, size_of_group), :]
+        weight = got_ref[pl.ds(slots + base, size_of_group), :]
+        cell = got_ref[pl.ds(2 * slots + base, size_of_group), :].astype(jnp.int32)
         weight = jnp.where(sub + base < count, weight, 0.0)
         return pieces(weight), pieces(weight * value), (cell % LANES).astype(F32), cell // LANES
 
@@ -184,9 +195,9 @@
         return left, jnp.where(lane_ids == column, one, zero)
 
     def pair(s, g, carry):
-        base = pl.multiple_of(g * GROUP, GROUP)
+        base = pl.multiple_of(g * size_of_group, size_of_group)
         loaded = [load(s + i, base) for i in (0, 1)]
-        for k in range(GROUP):
+        for k in range(size_of_group):
             hots = [one_hots(loaded[i], k) for i in (0, 1)]
             left = jnp.concatenate(
                 [
@@ -200,16 +211,16 @@
                 preferred_element_type=F32,
             )
             for i in (0, 1):
-                row = meta_ref[8 * (s + i), base + k].astype(jnp.int32)
-                sensor = meta_ref[8 * (s + i) + 1, base + k].astype(jnp.int32)
+                row = meta_ref[8 * (s + i), (s + i) * slots + base + k].astype(jnp.int32)
+                sensor = meta_ref[8 * (s + i) + 1, (s + i) * slots + base + k].astype(jnp.int32)
                 at = pl.multiple_of((sensor * rows + row) * tall, 8)
                 mine = both[2 * i * tall : 2 * (i + 1) * tall]
                 acc_ref[pl.ds(at, tall), :] += mine[:tall] + mine[tall:]
         return carry
 
     for s in range(0, len(got_refs), 2):
-        most = jnp.maximum(meta_ref[8 * s, slots], meta_ref[8 * s + 8, slots]).astype(jnp.int32)
-        lax.fori_loop(0, (most + GROUP - 1) // GROUP, functools.partial(pair, s), 0)
+        most = jnp.maximum(meta_ref[8 * s + 2, s], meta_ref[8 * s + 10, s + 1]).astype(jnp.int32)
+        lax.fori_loop(0, (most + size_of_group - 1) // size_of_group, functools.partial(pair, s), 0)
     for sensor, out_ref in ((core, own_ref), (1 - core, other_ref)):
         begin = sensor * rows * tall
         for kind in range(2):
@@ -414,14 +425,17 @@
     return swap(even, "tile", 1), lax.ppermute(odd, ("tile", "var"), pairs)
 
 
-def deliver(chunk, turn):
+def deliver(chunks):
     tiles, members = lax.axis_size("tile"), lax.axis_size("var")
-    pairs = []
-    for t in range(tiles):
-        for q in range(members):
-            offset = (q % 2) * (tiles // 2) + turn
-            pairs.append((t * members + q, (t ^ max(offset, 1)) * members + q))
-    return lax.ppermute(chunk, ("tile", "var"), pairs)
+    got = []
+    for turn, chunk in enumerate(chunks[:-1]):
+        pairs = []
+        for t in range(tiles):
+            for q in range(members):
+                offset = tiles - 1 if turn == len(chunks) - 2 else 1 + turn + (q % 2) * (tiles // 2 - 1)
+                pairs.append((t * members + q, (t ^ offset) * members + q))
+        got.append(lax.ppermute(chunk, ("tile", "var"), pairs))
+    return got + [chunks[-1]]
 
 
 def local(control, diffusivity, land_mask, panel_tile, panel_row, panel_cols, obs_values,
@@ -430,8 +444,7 @@
     var_dev = control.shape[0]
     tiles, members = lax.axis_size("tile"), lax.axis_size("var")
     panels, panel_width = panel_cols.shape
-    slots = 2 * panels // tiles
-    turns = tiles // 2
+    slots = panels // tiles
     blocks = width // LANES
     margin = PASSES
     total = ring_rows(rows, margin)
@@ -443,13 +456,14 @@
     view2 = jax.ShapeDtypeStruct((2, *view.shape), F32)
     edge = jax.ShapeDtypeStruct((margin * size, LANES), F32)
     edge2 = jax.ShapeDtypeStruct((2, *edge.shape), F32)
-    chunk = jax.ShapeDtypeStruct((3 * slots + 8, panel_width), F32)
+    half = jax.ShapeDtypeStruct((3 * slots + 8, panel_width), F32)
+    chunks = [jax.ShapeDtypeStruct((2, *half.shape), F32)] * (tiles // 2 - 1) + [half] * 2
     ints = pltpu.SMEM((panels,), jnp.int32)
 
     own, other, responses, kappa, kappa_even, kappa_odd, *chunks = call(
         functools.partial(first_kernel, slots, margin),
         [field, field, jax.ShapeDtypeStruct((2, var_dev, 8, LANES), F32), view2, edge2, edge2]
-        + [chunk] * turns,
+        + chunks,
         [HBM] * 10,
         [
             pltpu.SMEM(sensitivity.shape, F32),
@@ -459,15 +473,15 @@
             pltpu.VMEM(obs_values.shape, F32),
             pltpu.VMEM(obs_weights.shape, F32),
             pltpu.VMEM(panel_cols.shape, jnp.int32),
-            pltpu.VMEM((turns, *chunk.shape), F32),
-            pltpu.SMEM((turns,), jnp.int32),
+            pltpu.VMEM((tiles, *half.shape), F32),
+            pltpu.SMEM((tiles,), jnp.int32),
             pltpu.SemaphoreType.DMA((10,)),
         ],
         cost=cost(3000),
     )(*(in_hbm(x) for x in (sensitivity, cross_factor, control, diffusivity, panel_tile.reshape(-1),
                             panel_row, panel_sensor, obs_values, obs_weights, panel_cols)))
 
-    got = [deliver(c, turn) for turn, c in enumerate(chunks)]
+    got = deliver(chunks)
     part, *parts = call(cut_kernel, [view] * chips, [VMEM] * 2, cost=cost(200))(
         own, swap(other, "var", 1)
     )
@@ -480,15 +494,14 @@
     sums, sums_other = call(
         functools.partial(scatter_kernel, slots, blocks),
         [view2, view2],
-        [AFTER] + [VMEM] * (turns + 1),
+        [AFTER] + [VMEM] * len(got),
         [
-            pltpu.VMEM(chunk.shape, F32),
             pltpu.VMEM((2 * rows * 2 * padded_blocks(size), LANES), F32),
-            pltpu.SMEM((8 * turns, LANES), F32),
-            pltpu.SemaphoreType.DMA((turns,)),
+            pltpu.SMEM((8 * tiles, LANES), F32),
+            pltpu.SemaphoreType.DMA((tiles,)),
         ],
         cost=cost(100000),
-    )(smooth_in, chunks[0], *got)
+    )(smooth_in, *got)
     ring = pltpu.VMEM((total, size * LANES), F32)
     coef, sums_other = call(
         functools.partial(faces_kernel, margin),

time: 30.4 us -> 31.4 us (1.033)
  Pallas kernels: 7.34 us -> 9.71 us
  starting transfers between devices: 14.5 us -> 13.5 us
  waiting for transfers between devices: 8.22 us -> 7.82 us
    ppermute x9, starting transfers between devices: 11.5 us -> 7.37 us  [swap(): return lax.ppermute(values, axis, [(i, i ^ bit) for i in range(count)])]
    ppermute x2, starting transfers between devices: 2.73 us -> 5.94 us  [deliver(): got.append(lax.ppermute(chunk, ('tile', 'var'), pairs))]
    ppermute x9, waiting for transfers between devices: 8.21 us -> 6.61 us  [swap(): return lax.ppermute(values, axis, [(i, i ^ bit) for i in range(count)])]
    pallas_call x1, Pallas kernels: 2.48 us -> 3.71 us  [local(): call(functools.partial(first_kernel, slots, margin), [field, field, jax.S...]
    ppermute x2, waiting for transfers between devices: 0.01 us -> 1.21 us  [deliver(): got.append(lax.ppermute(chunk, ('tile', 'var'), pairs))]
    pallas_call x1, Pallas kernels: 1.29 us -> 2.43 us  [local(): call(functools.partial(scatter_kernel, slots, blocks), [view2, view2], [A...]
  transfers between devices with their start and end apart: 14 -> 14, of which waited for: 6 -> 7; matrix products, arithmetic and copies ran while one was open for 0% -> 0% of each run, Pallas kernels for 9% -> 12%
where the time goes in v4:
time: 31.4 us; the launch traced here: 31.1 us
  starting transfers between devices  13.5 us (43%)
  Pallas kernels  9.71 us (31%)
  waiting for transfers between devices  7.82 us (25%)
    ppermute x9, starting transfers between devices, swap(): return lax.ppermute(values, axis, [(i, i ^ bit) for i in range(count)])  7.37 us
    ppermute x9, waiting for transfers between devices, swap(): return lax.ppermute(values, axis, [(i, i ^ bit) for i in range(count)])  6.61 us
    ppermute x2, starting transfers between devices, deliver(): got.append(lax.ppermute(chunk, ('tile', 'var'), pairs))  5.94 us
    pallas_call x1, Pallas kernels, local(): call(functools.partial(first_kernel, slots, margin), [field, field, jax.S...  3.71 us
    pallas_call x1, Pallas kernels, local(): call(functools.partial(scatter_kernel, slots, blocks), [view2, view2], [A...  2.43 us
    pallas_call x1, Pallas kernels, local(): call(functools.partial(smooth_kernel, margin), [view], [VMEM] * 4, [ring]...  1.25 us
    pallas_call x1, Pallas kernels, local(): call(functools.partial(spread_kernel, margin), [share], [VMEM] * 4, [ring...  1.25 us
    ppermute x2, waiting for transfers between devices, deliver(): got.append(lax.ppermute(chunk, ('tile', 'var'), pairs))  1.21 us
  transfers between devices with their start and end apart: 14, of which 7 were waited for; matrix products, arithmetic and copies ran while one was open for 0% of the time, Pallas kernels for 12%

profile of v4, /device:TPU:0, one launch (start us, length us, event | category | flops | bytes accessed | tf_op | source)
XLA Modules:
  0.0 31.1 jit_solution(452103693612169586)
XLA Ops:
  0.0 3.7 %shard_map.109 = (f32[16,2048]{1,0:T(8,128)S(1)}, f32[16,2048]{1,0:T(8,128)S(1)}, f32[2,2,8,128]{3,2,1,0:T(8,128)S(1)}, f32[2,16,1152]{2,1,0:T(8,128)S(1)}, f32[...) custom-call(f32[2,8]{1,0:T(2,128)} %sens_hbm.1, ...), custom_call_target="tpu_custom_call" | custom-call | flops 12288000 | bytes 3072000 | tf_op jit(solution)/shard_map/pallas_call | solution.py:463
  3.7 0.5 %collective-permute-start = (f32[16,2048]{1,0:T(8,128)S(1)}, f32[16,2048]{1,0:T(8,128)S(1)}, u32[]{:S(2)}, u32[]{:S(2)}) collective-permute-start(f32[16,2048]{1,0:T(8,128)S(1)} %get-tuple-element.28), channel_id=1, source_target_pairs={{0,1},{1,0},{2,3},{3,2},{4,5},{5,4},{6,7},{7,6},{8,9},{9,8},{10,11... | collective-permute-start | bytes 393224 | tf_op jit(solution)/shard_map/ppermute | solution.py:414
  4.2 2.6 %collective-permute-start.6 = (f32[2,104,128]{2,1,0:T(8,128)S(1)}, f32[2,104,128]{2,1,0:T(8,128)S(1)}, u32[]{:S(2)}, u32[]{:S(2)}) collective-permute-start(f32[2,104,128]{2,1,0:T(8,128)S(1)} %get-tuple-element.37), channel_id=1, source_target_pairs={{0,4},{1,9},{2,6},{3,11},{4,0},{5,13},{6,2},{7,15},{8,12},{9,1},{1... | collective-permute-start | bytes 319496 | tf_op jit(solution)/shard_map/ppermute | solution.py:437
  6.9 0.0 collective-permute-done.second_ref
  6.9 1.6 %collective-permute-start.1 = (f32[16,1152]{1,0:T(8,128)S(1)}, f32[16,1152]{1,0:T(8,128)S(1)}, u32[]{:S(2)}, u32[]{:S(2)}) collective-permute-start(f32[16,1152]{1,0:T(8,128)S(1)} %get-tuple-element.30), channel_id=1, source_target_pairs={{0,2},{1,3},{2,0},{3,1},{4,6},{5,7},{6,4},{7,5},{8,10},{9,11},{10,... | collective-permute-start | bytes 221192 | tf_op jit(solution)/shard_map/ppermute | solution.py:414
  8.5 3.3 %collective-permute-start.7 = (f32[104,128]{1,0:T(8,128)S(1)}, f32[104,128]{1,0:T(8,128)S(1)}, u32[]{:S(2)}, u32[]{:S(2)}) collective-permute-start(f32[104,128]{1,0:T(8,128)S(1)} %get-tuple-element.38), channel_id=1, source_target_pairs={{0,12},{1,13},{2,14},{3,15},{4,8},{5,9},{6,10},{7,11},{8,4},{9,5},... | collective-permute-start | bytes 159752 | tf_op jit(solution)/shard_map/ppermute | solution.py:437
  11.8 0.2 collective-permute-done.1.refs_1_
  12.0 1.9 %collective-permute-start.2 = (f32[90,128]{1,0:T(8,128)S(1)}, f32[90,128]{1,0:T(8,128)S(1)}, u32[]{:S(2)}, u32[]{:S(2)}) collective-permute-start(f32[90,128]{1,0:T(8,128)S(1)} %get-tuple-element.32), channel_id=1, source_target_pairs={{0,4},{4,0},{8,12},{12,8},{1,5},{5,1},{9,13},{13,9},{2,6},{6,2},{1... | collective-permute-start | bytes 138248 | tf_op jit(solution)/shard_map/ppermute | solution.py:414
  13.9 1.2 %collective-permute-done.7.refs_1_ = f32[104,128]{1,0:T(8,128)S(1)} collective-permute-done((f32[104,128]{1,0:T(8,128)S(1)}, f32[104,128]{1,0:T(8,128)S(1)}, u32[]{:S(2)}, u32[]{:S(2)}) %collective-permute-start.7) | collective-permute-done | bytes 53280 | tf_op jit(solution)/shard_map/ppermute | solution.py:437
  15.1 0.0 collective-permute-start.3
  15.1 0.0 collective-permute-done.6.refs_0_
  15.1 2.4 %shard_map.112 = (f32[2,16,1152]{2,1,0:T(8,128)S(1)}, f32[2,16,1152]{2,1,0:T(8,128)S(1)}) custom-call(f32[16,1152]{1,0:T(8,128)S(1)} %get-tuple-element.31.after_ref.own_ref, f32[2,104,128]{2,1,0:T(8,128)S(1)} %collective-permute-done.6.refs_0_, f32[104,128]{1,0:T(8,128)S(1)} %collective-permute-done.7.refs_1_, f32[104,128]{1,0:T(8,128)S(1)} %get-tuple-element.39.refs_2_), custom_call_target="tpu_custom_call" | custom-call | flops 409600000 | bytes 102400000 | tf_op jit(solution)/shard_map/pallas_call | solution.py:494
  17.6 0.0 collective-permute-done.5.odd_ref
  17.6 0.6 %collective-permute-done.2.refs_0_.even_ref = f32[90,128]{1,0:T(8,128)S(1)} collective-permute-done((f32[90,128]{1,0:T(8,128)S(1)}, f32[90,128]{1,0:T(8,128)S(1)}, u32[]{:S(2)}, u32[]{:S(2)}) %collective-permute-start.2) | collective-permute-done | bytes 46112 | tf_op jit(solution)/shard_map/ppermute | solution.py:414
  18.1 0.0 collective-permute-done.3.refs_1_.odd_ref
  18.2 0.2 shard_map.113
  18.4 0.1 collective-permute-start.8
  18.4 0.0 copy-start.1
  18.4 1.3 %shard_map.114.smooth_ref = f32[16,1152]{1,0:T(8,128)S(1)} custom-call(f32[16,1152]{1,0:T(8,128)S(1)} %get-tuple-element.31.after_ref.own_ref, f32[90,128]{1,0:T(8,128)S(1)} %collective-permute-done.2.refs_0_.even_ref, f32[90,128]{1,0:T(8,128)S(1)} %collective-permute-done.3.refs_1_.odd_ref, f32[5,40,1152]{2,1,0:T(8,128)S(1)} %get-tuple-element.41.coef_ref), custom_call_target="tpu_custom_call" | custom-call | flops 16384000 | bytes 4096000 | tf_op jit(solution)/shard_map/pallas_call | solution.py:514
  19.7 0.1 collective-permute-done.8.more_ref
  19.9 1.4 %collective-permute-start.9 = (f32[90,128]{1,0:T(8,128)S(1)}, f32[90,128]{1,0:T(8,128)S(1)}, u32[]{:S(2)}, u32[]{:S(2)}) collective-permute-start(f32[90,128]{1,0:T(8,128)S(1)} %get-tuple-element.45), channel_id=1, source_target_pairs={{0,4},{4,0},{8,12},{12,8},{1,5},{5,1},{9,13},{13,9},{2,6},{6,2},{1... | collective-permute-start | bytes 138248 | tf_op jit(solution)/shard_map/ppermute | solution.py:414
  21.2 0.1 collective-permute-start.10
  21.4 2.6 %collective-permute-done.9.even_ref = f32[90,128]{1,0:T(8,128)S(1)} collective-permute-done((f32[90,128]{1,0:T(8,128)S(1)}, f32[90,128]{1,0:T(8,128)S(1)}, u32[]{:S(2)}, u32[]{:S(2)}) %collective-permute-start.9) | collective-permute-done | bytes 46112 | tf_op jit(solution)/shard_map/ppermute | solution.py:414
  24.0 0.0 collective-permute-done.10.odd_ref
  24.0 1.2 %shard_map.116.refs_0_ = f32[16,1024]{1,0:T(8,128)S(1)} custom-call(f32[16,1152]{1,0:T(8,128)S(1)} %get-tuple-element.44.own_ref, f32[90,128]{1,0:T(8,128)S(1)} %collective-permute-done.9.even_ref, f32[90,128]{1,0:T(8,128)S(1)} %collective-permute-done.10.odd_ref, f32[5,40,1152]{2,1,0:T(8,128)S(1)} %get-tuple-element.41.coef_ref), custom_call_target="tpu_custom_call" | custom-call | flops 16384000 | bytes 4096000 | tf_op jit(solution)/shard_map/pallas_call | solution.py:525
  25.3 0.1 collective-permute-start.13
  25.3 0.9 %collective-permute-start.12 = (f32[16,1024]{1,0:T(8,128)S(1)}, f32[16,1024]{1,0:T(8,128)S(1)}, u32[]{:S(2)}, u32[]{:S(2)}) collective-permute-start(f32[16,1024]{1,0:T(8,128)S(1)} %shard_map.116.refs_0_), channel_id=1, source_target_pairs={{0,2},{1,3},{2,0},{3,1},{4,6},{5,7},{6,4},{7,5},{8,10},{9,11},{10,... | collective-permute-start | bytes 196616 | tf_op jit(solution)/shard_map/ppermute | solution.py:414
  26.2 1.0 %collective-permute-start.11 = (f32[16,1024]{1,0:T(8,128)S(1)}, f32[16,1024]{1,0:T(8,128)S(1)}, u32[]{:S(2)}, u32[]{:S(2)}) collective-permute-start(f32[16,1024]{1,0:T(8,128)S(1)} %shard_map.116.refs_0_), channel_id=1, source_target_pairs={{0,1},{1,0},{2,3},{3,2},{4,5},{5,4},{6,7},{7,6},{8,9},{9,8},{10,11... | collective-permute-start | bytes 196616 | tf_op jit(solution)/shard_map/ppermute | solution.py:414
  27.2 2.2 %collective-permute-done.13.refs_3_ = f32[16,1024]{1,0:T(8,128)S(1)} collective-permute-done((f32[16,1024]{1,0:T(8,128)S(1)}, f32[16,1024]{1,0:T(8,128)S(1)}, u32[]{:S(2)}, u32[]{:S(2)}) %collective-permute-start.13) | collective-permute-done | bytes 65568 | tf_op jit(solution)/shard_map/ppermute | solution.py:414
  29.4 0.9 %collective-permute-done.12.refs_2_ = f32[16,1024]{1,0:T(8,128)S(1)} collective-permute-done((f32[16,1024]{1,0:T(8,128)S(1)}, f32[16,1024]{1,0:T(8,128)S(1)}, u32[]{:S(2)}, u32[]{:S(2)}) %collective-permute-start.12) | collective-permute-done | bytes 65568 | tf_op jit(solution)/shard_map/ppermute | solution.py:414
  30.3 0.0 collective-permute-done.11.refs_1_
  30.3 0.8 %shard_map.117 = f32[2,16,2048]{2,1,0:T(8,128)} custom-call(f32[2,2,8,128]{3,2,1,0:T(8,128)S(1)} %get-tuple-element.26.response_ref, f32[2,16,2048]{2,1,0:T(8,128)S(1)} %copy-done, f32[16,1024]{1,0:T(8,128)S(1)} %shard_map.116.refs_0_, f32[16,1024]{1,0:T(8,128)S(1)} %collective-permute-done.11.refs_1_, f32[16,1024]{1,0:T(8,128)S(1)} %collective-permute-done.12.refs_2_, ...), custom_call_target="tpu_custom_call" | custom-call | flops 4096000 | bytes 1024000 | tf_op jit(solution)/shard_map/pallas_call | solution.py:533
  (9 shorter events, 0.1 us)
Async XLA Ops:
  3.7 3.2 %collective-permute-start = (f32[16,2048]{1,0:T(8,128)S(1)}, f32[16,2048]{1,0:T(8,128)S(1)}, u32[]{:S(2)}, u32[]{:S(2)}) collective-permute-start(f32[16,2048]{1,0:T(8,128)S(1)} %get-tuple-element.28), channel_id=1, source_target_pairs={{0,1},{1,0},{2,3},{3,2},{4,5},{5,4},{6,7},{7,6},{8,9},{9,8},{10,11... | collective-permute-start | bytes 393224 | tf_op jit(solution)/shard_map/ppermute | solution.py:414
  4.2 10.9 %collective-permute-start.6 = (f32[2,104,128]{2,1,0:T(8,128)S(1)}, f32[2,104,128]{2,1,0:T(8,128)S(1)}, u32[]{:S(2)}, u32[]{:S(2)}) collective-permute-start(f32[2,104,128]{2,1,0:T(8,128)S(1)} %get-tuple-element.37), channel_id=1, source_target_pairs={{0,4},{1,9},{2,6},{3,11},{4,0},{5,13},{6,2},{7,15},{8,12},{9,1},{1... | collective-permute-start | bytes 319496 | tf_op jit(solution)/shard_map/ppermute | solution.py:437
  6.9 5.0 %collective-permute-start.1 = (f32[16,1152]{1,0:T(8,128)S(1)}, f32[16,1152]{1,0:T(8,128)S(1)}, u32[]{:S(2)}, u32[]{:S(2)}) collective-permute-start(f32[16,1152]{1,0:T(8,128)S(1)} %get-tuple-element.30), channel_id=1, source_target_pairs={{0,2},{1,3},{2,0},{3,1},{4,6},{5,7},{6,4},{7,5},{8,10},{9,11},{10,... | collective-permute-start | bytes 221192 | tf_op jit(solution)/shard_map/ppermute | solution.py:414
  8.5 6.6 %collective-permute-start.7 = (f32[104,128]{1,0:T(8,128)S(1)}, f32[104,128]{1,0:T(8,128)S(1)}, u32[]{:S(2)}, u32[]{:S(2)}) collective-permute-start(f32[104,128]{1,0:T(8,128)S(1)} %get-tuple-element.38), channel_id=1, source_target_pairs={{0,12},{1,13},{2,14},{3,15},{4,8},{5,9},{6,10},{7,11},{8,4},{9,5},... | collective-permute-start | bytes 159752 | tf_op jit(solution)/shard_map/ppermute | solution.py:437
  11.8 5.8 %collective-permute-start.4 = (f32[2,90,128]{2,1,0:T(8,128)S(1)}, f32[2,90,128]{2,1,0:T(8,128)S(1)}, u32[]{:S(2)}, u32[]{:S(2)}) collective-permute-start(f32[2,90,128]{2,1,0:T(8,128)S(1)} %get-tuple-element.34), channel_id=1, source_target_pairs={{0,4},{4,0},{8,12},{12,8},{1,5},{5,1},{9,13},{13,9},{2,6},{6,2},{1... | collective-permute-start | bytes 276488 | tf_op jit(solution)/shard_map/ppermute | solution.py:414
  11.8 5.8 %collective-permute-start.5 = (f32[2,90,128]{2,1,0:T(8,128)S(1)}, f32[2,90,128]{2,1,0:T(8,128)S(1)}, u32[]{:S(2)}, u32[]{:S(2)}) collective-permute-start(f32[2,90,128]{2,1,0:T(8,128)S(1)} %get-tuple-element.35), channel_id=1, source_target_pairs={{0,1},{1,0},{2,3},{3,2},{4,8},{5,9},{6,10},{7,11},{8,4},{9,5},{10,... | collective-permute-start | bytes 276488 | tf_op jit(solution)/shard_map/ppermute | solution.py:425
  12.0 6.2 %collective-permute-start.2 = (f32[90,128]{1,0:T(8,128)S(1)}, f32[90,128]{1,0:T(8,128)S(1)}, u32[]{:S(2)}, u32[]{:S(2)}) collective-permute-start(f32[90,128]{1,0:T(8,128)S(1)} %get-tuple-element.32), channel_id=1, source_target_pairs={{0,4},{4,0},{8,12},{12,8},{1,5},{5,1},{9,13},{13,9},{2,6},{6,2},{1... | collective-permute-start | bytes 138248 | tf_op jit(solution)/shard_map/ppermute | solution.py:414
  15.1 3.1 %collective-permute-start.3 = (f32[90,128]{1,0:T(8,128)S(1)}, f32[90,128]{1,0:T(8,128)S(1)}, u32[]{:S(2)}, u32[]{:S(2)}) collective-permute-start(f32[90,128]{1,0:T(8,128)S(1)} %get-tuple-element.33), channel_id=1, source_target_pairs={{0,1},{1,0},{2,3},{3,2},{4,8},{5,9},{6,10},{7,11},{8,4},{9,5},{10,... | collective-permute-start | bytes 138248 | tf_op jit(solution)/shard_map/ppermute | solution.py:425
  18.4 1.4 %collective-permute-start.8 = (f32[2,16,1152]{2,1,0:T(8,128)S(1)}, f32[2,16,1152]{2,1,0:T(8,128)S(1)}, u32[]{:S(2)}, u32[]{:S(2)}) collective-permute-start(f32[2,16,1152]{2,1,0:T(8,128)S(1)} %get-tuple-element.43), channel_id=1, source_target_pairs={{0,1},{1,0},{2,3},{3,2},{4,5},{5,4},{6,7},{7,6},{8,9},{9,8},{10,11... | collective-permute-start | bytes 442376 | tf_op jit(solution)/shard_map/ppermute | solution.py:414
  18.4 1.4 %copy-start.1 = (s32[16,2048]{1,0:T(8,128)S(1)}, s32[16,2048]{1,0:T(8,128)}, u32[]{:S(2)}) copy-start(s32[16,2048]{1,0:T(8,128)} %mask_ref.1) | copy-start | bytes 393220
  19.9 4.2 %collective-permute-start.9 = (f32[90,128]{1,0:T(8,128)S(1)}, f32[90,128]{1,0:T(8,128)S(1)}, u32[]{:S(2)}, u32[]{:S(2)}) collective-permute-start(f32[90,128]{1,0:T(8,128)S(1)} %get-tuple-element.45), channel_id=1, source_target_pairs={{0,4},{4,0},{8,12},{12,8},{1,5},{5,1},{9,13},{13,9},{2,6},{6,2},{1... | collective-permute-start | bytes 138248 | tf_op jit(solution)/shard_map/ppermute | solution.py:414
  21.2 2.8 %collective-permute-start.10 = (f32[90,128]{1,0:T(8,128)S(1)}, f32[90,128]{1,0:T(8,128)S(1)}, u32[]{:S(2)}, u32[]{:S(2)}) collective-permute-start(f32[90,128]{1,0:T(8,128)S(1)} %get-tuple-element.46), channel_id=1, source_target_pairs={{0,1},{1,0},{2,3},{3,2},{4,8},{5,9},{6,10},{7,11},{8,4},{9,5},{10,... | collective-permute-start | bytes 138248 | tf_op jit(solution)/shard_map/ppermute | solution.py:425
  24.0 6.3 %copy-start = (f32[2,16,2048]{2,1,0:T(8,128)S(1)}, f32[2,16,2048]{2,1,0:T(8,128)}, u32[]{:S(2)}) copy-start(f32[2,16,2048]{2,1,0:T(8,128)} %control_ref.1) | copy-start | bytes 786436
  25.3 4.2 %collective-permute-start.13 = (f32[16,1024]{1,0:T(8,128)S(1)}, f32[16,1024]{1,0:T(8,128)S(1)}, u32[]{:S(2)}, u32[]{:S(2)}) collective-permute-start(f32[16,1024]{1,0:T(8,128)S(1)} %shard_map.116.refs_0_), channel_id=1, source_target_pairs={{0,3},{1,2},{2,1},{3,0},{4,7},{5,6},{6,5},{7,4},{8,11},{9,10},{10,... | collective-permute-start | bytes 196616 | tf_op jit(solution)/shard_map/ppermute | solution.py:414
  25.3 5.0 %collective-permute-start.12 = (f32[16,1024]{1,0:T(8,128)S(1)}, f32[16,1024]{1,0:T(8,128)S(1)}, u32[]{:S(2)}, u32[]{:S(2)}) collective-permute-start(f32[16,1024]{1,0:T(8,128)S(1)} %shard_map.116.refs_0_), channel_id=1, source_target_pairs={{0,2},{1,3},{2,0},{3,1},{4,6},{5,7},{6,4},{7,5},{8,10},{9,11},{10,... | collective-permute-start | bytes 196616 | tf_op jit(solution)/shard_map/ppermute | solution.py:414
  26.2 4.1 %collective-permute-start.11 = (f32[16,1024]{1,0:T(8,128)S(1)}, f32[16,1024]{1,0:T(8,128)S(1)}, u32[]{:S(2)}, u32[]{:S(2)}) collective-permute-start(f32[16,1024]{1,0:T(8,128)S(1)} %shard_map.116.refs_0_), channel_id=1, source_target_pairs={{0,1},{1,0},{2,3},{3,2},{4,5},{5,4},{6,7},{7,6},{8,9},{9,8},{10,11... | collective-permute-start | bytes 196616 | tf_op jit(solution)/shard_map/ppermute | solution.py:414

commit v5 on v4

--- a/solution.py
+++ b/solution.py
@@ -72,9 +72,9 @@
 def first_kernel(slots, margin, sens_hbm, factor_hbm, control_hbm, kappa_hbm, tile_hbm, row_hbm, sensor_hbm,
                  value_hbm, weight_hbm, cols_hbm, own_ref, other_ref, response_ref, kappa_ref, even_ref,
                  odd_ref, *refs):
-    chunk_refs = refs[:-12]
+    chunk_refs = refs[:-11]
     (sens_ref, factor_ref, control_ref, tile_ref, row_ref, sensor_ref, value_ref, weight_ref, cols_ref,
-     send_ref, count_ref, sems) = refs[-12:]
+     before_ref, sems) = refs[-11:]
     window = lanes(*window_of(my_chip(), chip_count(), own_ref.shape[1] // LANES))
     pairs = (
         (sens_hbm, sens_ref), (factor_hbm, factor_ref), (control_hbm, control_ref),
@@ -84,9 +84,9 @@
     copies = [pltpu.make_async_copy(src, dst, sems.at[i]) for i, (src, dst) in enumerate(pairs)]
     for copy in copies:
         copy.start()
-    send_ref[...] = jnp.zeros(send_ref.shape, F32)
-    for source in range(lax.axis_size("tile")):
-        count_ref[source] = 0
+    from_panel = lax.broadcasted_iota(jnp.int32, before_ref.shape, 0)
+    to_panel = lax.broadcasted_iota(jnp.int32, before_ref.shape, 1)
+    before_ref[...] = jnp.where(from_panel < to_panel, 1.0, 0.0).astype(jnp.bfloat16)
     for copy in copies:
         copy.wait()
 
@@ -109,37 +109,54 @@
     full = tiles // 2 - 1
     first = jnp.where(core == 0, 1, tiles // 2)
     panels = value_ref.shape[0]
-    sub = lax.broadcasted_iota(jnp.int32, (8, LANES), 0)
-    lane = lax.broadcasted_iota(jnp.int32, (8, LANES), 1)
-    trash = 3 * slots + 7
-
-    def place(p, meta):
-        source = tile_ref[p] ^ mine
-        count = count_ref[source]
-        count_ref[source] = count + 1
-        parity, slot = count % 2, count // 2
-        whole = (source >= first) & (source < first + full)
-        shared = ((source == 0) | (source == tiles - 1)) & (parity == core)
-        keep = whole | shared
-        half = jnp.where(whole, 2 * (source - first) + parity, jnp.where(source == 0, tiles - 1, tiles - 2))
-        half = jnp.where(keep, half, 0)
-        rows = (value_ref[pl.ds(p, 1), :], weight_ref[pl.ds(p, 1), :], cols_ref[pl.ds(p, 1), :].astype(F32))
-        for part, row in enumerate(rows):
-            send_ref[half, pl.ds(jnp.where(keep, part * slots + slot, trash), 1), :] = row
-        facts = jnp.where(sub == 0, row_ref[p], sensor_ref[p]).astype(F32)
-        return jnp.where(lane == jnp.where(keep, half * slots + slot, LANES), facts, meta)
-
-    meta = lax.fori_loop(0, panels, place, jnp.zeros((8, LANES), F32), unroll=8)
-    for half in range(tiles):
-        if half < 2 * full:
-            held = (count_ref[first + half // 2] + 1 - half % 2) // 2
-        else:
-            held = (count_ref[0 if half == tiles - 1 else tiles - 1] + 1 - core) // 2
-        meta = jnp.where((sub == 2) & (lane == half), held.astype(F32), meta)
-    for half in range(tiles):
-        out_ref = chunk_refs[half // 2].at[half % 2] if half < 2 * full else chunk_refs[half - full]
-        out_ref[: 3 * slots] = send_ref[half, : 3 * slots]
+    source = tile_ref[...] ^ mine
+    names = lax.broadcasted_iota(jnp.int32, (-(-tiles // 8) * 8, panels), 0)
+    hits = jnp.where(names == source, 1.0, 0.0)
+    ranks = jnp.dot(hits.astype(jnp.bfloat16), before_ref[...], preferred_element_type=F32)
+    rank = jnp.sum(hits * ranks, axis=0, keepdims=True).astype(jnp.int32)
+    parity, slot = rank % 2, rank // 2
+    whole = (source >= first) & (source < first + full)
+    home = source == 0
+    keep = whole | ((home | (source == tiles - 1)) & (parity == core))
+    half = jnp.where(whole, 2 * (source - first) + parity, jnp.where(home, tiles - 1, tiles - 2))
+    place = jnp.where(keep, half * slots + slot, -1)
+    spots = lax.broadcasted_iota(jnp.int32, (tiles * slots, panels), 0)
+    pick = jnp.where(spots == place, 1.0, 0.0).astype(jnp.bfloat16)
+
+    def picked(parts):
+        total = None
+        for part in parts:
+            term = jnp.dot(pick, part.astype(jnp.bfloat16), preferred_element_type=F32)
+            total = term if total is None else total + term
+        return total
+
+    cols = cols_ref[...]
+    sent = (
+        picked(thirds(value_ref[...])),
+        picked(thirds(weight_ref[...])),
+        picked(((cols // LANES * LANES).astype(F32), (cols % LANES).astype(F32))),
+    )
+    sub = lax.broadcasted_iota(jnp.int32, (8, panels), 0)
+    lane = lax.broadcasted_iota(jnp.int32, (8, panels), 1)
+    facts = jnp.where(sub == 0, row_ref[...], jnp.where(sub == 1, sensor_ref[...], 0)).astype(F32)
+    meta = lax.dot_general(
+        facts.astype(jnp.bfloat16), pick, (((1,), (1,)), ((), ())), preferred_element_type=F32
+    )
+    for i in range(tiles):
+        held = jnp.sum(jnp.where(keep & (half == i), 1.0, 0.0), axis=1, keepdims=True)
+        meta = jnp.where((sub == 2) & (lane == i), held, meta)
+    for i in range(tiles):
+        out_ref = chunk_refs[i // 2].at[i % 2] if i < 2 * full else chunk_refs[i - full]
+        for part, rows in enumerate(sent):
+            out_ref[part * slots : (part + 1) * slots] = rows[i * slots : (i + 1) * slots]
         out_ref[3 * slots :] = meta
+
+
+def thirds(values):
+    top = values.astype(jnp.bfloat16).astype(F32)
+    rest = values - top
+    middle = rest.astype(jnp.bfloat16).astype(F32)
+    return top, middle, rest - middle
 
 
 def pieces(values):
@@ -458,7 +475,7 @@
     edge2 = jax.ShapeDtypeStruct((2, *edge.shape), F32)
     half = jax.ShapeDtypeStruct((3 * slots + 8, panel_width), F32)
     chunks = [jax.ShapeDtypeStruct((2, *half.shape), F32)] * (tiles // 2 - 1) + [half] * 2
-    ints = pltpu.SMEM((panels,), jnp.int32)
+    line = pltpu.VMEM((1, panels), jnp.int32)
 
     own, other, responses, kappa, kappa_even, kappa_odd, *chunks = call(
         functools.partial(first_kernel, slots, margin),
@@ -469,17 +486,17 @@
             pltpu.SMEM(sensitivity.shape, F32),
             pltpu.SMEM(cross_factor.shape, F32),
             pltpu.VMEM(control.shape, F32),
-            ints, ints, ints,
+            line, line, line,
             pltpu.VMEM(obs_values.shape, F32),
             pltpu.VMEM(obs_weights.shape, F32),
             pltpu.VMEM(panel_cols.shape, jnp.int32),
-            pltpu.VMEM((tiles, *half.shape), F32),
-            pltpu.SMEM((tiles,), jnp.int32),
+            pltpu.VMEM((panels, panels), jnp.bfloat16),
             pltpu.SemaphoreType.DMA((10,)),
         ],
         cost=cost(3000),
-    )(*(in_hbm(x) for x in (sensitivity, cross_factor, control, diffusivity, panel_tile.reshape(-1),
-                            panel_row, panel_sensor, obs_values, obs_weights, panel_cols)))
+    )(*(in_hbm(x) for x in (sensitivity, cross_factor, control, diffusivity, panel_tile.reshape(1, -1),
+                            panel_row.reshape(1, -1), panel_sensor.reshape(1, -1), obs_values,
+                            obs_weights, panel_cols)))
 
     got = deliver(chunks)
     part, *parts = call(cut_kernel, [view] * chips, [VMEM] * 2, cost=cost(200))(

time: 31.4 us -> 29.4 us (0.936)
  Pallas kernels: 9.71 us -> 7.07 us
  waiting for transfers between devices: 7.82 us -> 8.35 us
    pallas_call x1, Pallas kernels: 3.71 us -> 1.58 us  [local(): call(functools.partial(first_kernel, slots, margin), [field, field, jax.S...]
    ppermute x9, waiting for transfers between devices: 6.61 us -> 7.13 us  [swap(): return lax.ppermute(values, axis, [(i, i ^ bit) for i in range(count)])]
    pallas_call x1, Pallas kernels: 2.43 us -> 1.92 us  [local(): call(functools.partial(scatter_kernel, slots, blocks), [view2, view2], [A...]
  transfers between devices with their start and end apart: 14 -> 14, of which waited for: 7 -> 8; matrix products, arithmetic and copies ran while one was open for 0% -> 0% of each run, Pallas kernels for 12% -> 11%
where the time goes in v5:
time: 29.4 us; the launch traced here: 29 us
  starting transfers between devices  13.5 us (46%)
  waiting for transfers between devices  8.35 us (28%)
  Pallas kernels  7.07 us (24%)
    ppermute x9, starting transfers between devices, swap(): return lax.ppermute(values, axis, [(i, i ^ bit) for i in range(count)])  7.38 us
    ppermute x9, waiting for transfers between devices, swap(): return lax.ppermute(values, axis, [(i, i ^ bit) for i in range(count)])  7.13 us
    ppermute x2, starting transfers between devices, deliver(): got.append(lax.ppermute(chunk, ('tile', 'var'), pairs))  5.93 us
    pallas_call x1, Pallas kernels, local(): call(functools.partial(scatter_kernel, slots, blocks), [view2, view2], [A...  1.92 us
    pallas_call x1, Pallas kernels, local(): call(functools.partial(first_kernel, slots, margin), [field, field, jax.S...  1.58 us
    pallas_call x1, Pallas kernels, local(): call(functools.partial(smooth_kernel, margin), [view], [VMEM] * 4, [ring]...  1.25 us
    pallas_call x1, Pallas kernels, local(): call(functools.partial(spread_kernel, margin), [share], [VMEM] * 4, [ring...  1.25 us
    ppermute x2, waiting for transfers between devices, deliver(): got.append(lax.ppermute(chunk, ('tile', 'var'), pairs))  1.21 us
  transfers between devices with their start and end apart: 14, of which 8 were waited for; matrix products, arithmetic and copies ran while one was open for 0% of the time, Pallas kernels for 11%

profile of v5, /device:TPU:0, one launch (start us, length us, event | category | flops | bytes accessed | tf_op | source)
XLA Modules:
  0.0 29.0 jit_solution(9514284557346298826)
XLA Ops:
  0.0 1.6 %shard_map.109 = (f32[16,2048]{1,0:T(8,128)S(1)}, f32[16,2048]{1,0:T(8,128)S(1)}, f32[2,2,8,128]{3,2,1,0:T(8,128)S(1)}, f32[2,16,1152]{2,1,0:T(8,128)S(1)}, f32[...) custom-call(f32[2,8]{1,0:T(2,128)} %sens_hbm.1, ...), custom_call_target="tpu_custom_call" | custom-call | flops 12288000 | bytes 3072000 | tf_op jit(solution)/shard_map/pallas_call | solution.py:480
  1.6 0.5 %collective-permute-start = (f32[16,2048]{1,0:T(8,128)S(1)}, f32[16,2048]{1,0:T(8,128)S(1)}, u32[]{:S(2)}, u32[]{:S(2)}) collective-permute-start(f32[16,2048]{1,0:T(8,128)S(1)} %get-tuple-element.28), channel_id=1, source_target_pairs={{0,1},{1,0},{2,3},{3,2},{4,5},{5,4},{6,7},{7,6},{8,9},{9,8},{10,11... | collective-permute-start | bytes 393224 | tf_op jit(solution)/shard_map/ppermute | solution.py:431
  2.1 2.6 %collective-permute-start.6 = (f32[2,104,128]{2,1,0:T(8,128)S(1)}, f32[2,104,128]{2,1,0:T(8,128)S(1)}, u32[]{:S(2)}, u32[]{:S(2)}) collective-permute-start(f32[2,104,128]{2,1,0:T(8,128)S(1)} %get-tuple-element.37), channel_id=1, source_target_pairs={{0,4},{1,9},{2,6},{3,11},{4,0},{5,13},{6,2},{7,15},{8,12},{9,1},{1... | collective-permute-start | bytes 319496 | tf_op jit(solution)/shard_map/ppermute | solution.py:454
  4.8 0.0 collective-permute-done.second_ref
  4.8 1.6 %collective-permute-start.1 = (f32[16,1152]{1,0:T(8,128)S(1)}, f32[16,1152]{1,0:T(8,128)S(1)}, u32[]{:S(2)}, u32[]{:S(2)}) collective-permute-start(f32[16,1152]{1,0:T(8,128)S(1)} %get-tuple-element.30), channel_id=1, source_target_pairs={{0,2},{1,3},{2,0},{3,1},{4,6},{5,7},{6,4},{7,5},{8,10},{9,11},{10,... | collective-permute-start | bytes 221192 | tf_op jit(solution)/shard_map/ppermute | solution.py:431
  6.3 3.3 %collective-permute-start.7 = (f32[104,128]{1,0:T(8,128)S(1)}, f32[104,128]{1,0:T(8,128)S(1)}, u32[]{:S(2)}, u32[]{:S(2)}) collective-permute-start(f32[104,128]{1,0:T(8,128)S(1)} %get-tuple-element.38), channel_id=1, source_target_pairs={{0,12},{1,13},{2,14},{3,15},{4,8},{5,9},{6,10},{7,11},{8,4},{9,5},... | collective-permute-start | bytes 159752 | tf_op jit(solution)/shard_map/ppermute | solution.py:454
  9.6 0.0 collective-permute-start.4
  9.6 0.2 collective-permute-done.1.refs_1_
  9.8 1.9 %collective-permute-start.2 = (f32[90,128]{1,0:T(8,128)S(1)}, f32[90,128]{1,0:T(8,128)S(1)}, u32[]{:S(2)}, u32[]{:S(2)}) collective-permute-start(f32[90,128]{1,0:T(8,128)S(1)} %get-tuple-element.32), channel_id=1, source_target_pairs={{0,4},{4,0},{8,12},{12,8},{1,5},{5,1},{9,13},{13,9},{2,6},{6,2},{1... | collective-permute-start | bytes 138248 | tf_op jit(solution)/shard_map/ppermute | solution.py:431
  11.8 1.2 %collective-permute-done.7.refs_1_ = f32[104,128]{1,0:T(8,128)S(1)} collective-permute-done((f32[104,128]{1,0:T(8,128)S(1)}, f32[104,128]{1,0:T(8,128)S(1)}, u32[]{:S(2)}, u32[]{:S(2)}) %collective-permute-start.7) | collective-permute-done | bytes 53280 | tf_op jit(solution)/shard_map/ppermute | solution.py:454
  13.0 0.0 collective-permute-start.3
  13.0 1.9 %shard_map.112 = (f32[2,16,1152]{2,1,0:T(8,128)S(1)}, f32[2,16,1152]{2,1,0:T(8,128)S(1)}) custom-call(f32[16,1152]{1,0:T(8,128)S(1)} %get-tuple-element.31.after_ref.own_ref, f32[2,104,128]{2,1,0:T(8,128)S(1)} %collective-permute-done.6.refs_0_, f32[104,128]{1,0:T(8,128)S(1)} %collective-permute-done.7.refs_1_, f32[104,128]{1,0:T(8,128)S(1)} %get-tuple-element.39.refs_2_), custom_call_target="tpu_custom_call" | custom-call | flops 409600000 | bytes 102400000 | tf_op jit(solution)/shard_map/pallas_call | solution.py:511
  14.9 0.4 %collective-permute-done.4.even_ref = f32[2,90,128]{2,1,0:T(8,128)S(1)} collective-permute-done((f32[2,90,128]{2,1,0:T(8,128)S(1)}, f32[2,90,128]{2,1,0:T(8,128)S(1)}, u32[]{:S(2)}, u32[]{:S(2)}) %collective-permute-start.4) | collective-permute-done | bytes 92192 | tf_op jit(solution)/shard_map/ppermute | solution.py:431
  15.3 0.0 collective-permute-done.5.odd_ref
  15.3 0.7 %collective-permute-done.2.refs_0_.even_ref = f32[90,128]{1,0:T(8,128)S(1)} collective-permute-done((f32[90,128]{1,0:T(8,128)S(1)}, f32[90,128]{1,0:T(8,128)S(1)}, u32[]{:S(2)}, u32[]{:S(2)}) %collective-permute-start.2) | collective-permute-done | bytes 46112 | tf_op jit(solution)/shard_map/ppermute | solution.py:431
  16.0 0.0 collective-permute-done.3.refs_1_.odd_ref
  16.0 0.2 shard_map.113
  16.2 0.1 collective-permute-start.8
  16.3 0.0 copy-start.1
  16.3 1.3 %shard_map.114.smooth_ref = f32[16,1152]{1,0:T(8,128)S(1)} custom-call(f32[16,1152]{1,0:T(8,128)S(1)} %get-tuple-element.31.after_ref.own_ref, f32[90,128]{1,0:T(8,128)S(1)} %collective-permute-done.2.refs_0_.even_ref, f32[90,128]{1,0:T(8,128)S(1)} %collective-permute-done.3.refs_1_.odd_ref, f32[5,40,1152]{2,1,0:T(8,128)S(1)} %get-tuple-element.41.coef_ref), custom_call_target="tpu_custom_call" | custom-call | flops 16384000 | bytes 4096000 | tf_op jit(solution)/shard_map/pallas_call | solution.py:531
  17.6 0.1 collective-permute-done.8.more_ref
  17.7 1.4 %collective-permute-start.9 = (f32[90,128]{1,0:T(8,128)S(1)}, f32[90,128]{1,0:T(8,128)S(1)}, u32[]{:S(2)}, u32[]{:S(2)}) collective-permute-start(f32[90,128]{1,0:T(8,128)S(1)} %get-tuple-element.45), channel_id=1, source_target_pairs={{0,4},{4,0},{8,12},{12,8},{1,5},{5,1},{9,13},{13,9},{2,6},{6,2},{1... | collective-permute-start | bytes 138248 | tf_op jit(solution)/shard_map/ppermute | solution.py:431
  19.1 0.1 collective-permute-start.10
  19.2 2.6 %collective-permute-done.9.even_ref = f32[90,128]{1,0:T(8,128)S(1)} collective-permute-done((f32[90,128]{1,0:T(8,128)S(1)}, f32[90,128]{1,0:T(8,128)S(1)}, u32[]{:S(2)}, u32[]{:S(2)}) %collective-permute-start.9) | collective-permute-done | bytes 46112 | tf_op jit(solution)/shard_map/ppermute | solution.py:431
  21.9 0.0 collective-permute-done.10.odd_ref
  21.9 1.2 %shard_map.116.refs_0_ = f32[16,1024]{1,0:T(8,128)S(1)} custom-call(f32[16,1152]{1,0:T(8,128)S(1)} %get-tuple-element.44.own_ref, f32[90,128]{1,0:T(8,128)S(1)} %collective-permute-done.9.even_ref, f32[90,128]{1,0:T(8,128)S(1)} %collective-permute-done.10.odd_ref, f32[5,40,1152]{2,1,0:T(8,128)S(1)} %get-tuple-element.41.coef_ref), custom_call_target="tpu_custom_call" | custom-call | flops 16384000 | bytes 4096000 | tf_op jit(solution)/shard_map/pallas_call | solution.py:542
  23.1 0.1 collective-permute-start.13
  23.2 0.9 %collective-permute-start.12 = (f32[16,1024]{1,0:T(8,128)S(1)}, f32[16,1024]{1,0:T(8,128)S(1)}, u32[]{:S(2)}, u32[]{:S(2)}) collective-permute-start(f32[16,1024]{1,0:T(8,128)S(1)} %shard_map.116.refs_0_), channel_id=1, source_target_pairs={{0,2},{1,3},{2,0},{3,1},{4,6},{5,7},{6,4},{7,5},{8,10},{9,11},{10,... | collective-permute-start | bytes 196616 | tf_op jit(solution)/shard_map/ppermute | solution.py:431
  24.1 1.0 %collective-permute-start.11 = (f32[16,1024]{1,0:T(8,128)S(1)}, f32[16,1024]{1,0:T(8,128)S(1)}, u32[]{:S(2)}, u32[]{:S(2)}) collective-permute-start(f32[16,1024]{1,0:T(8,128)S(1)} %shard_map.116.refs_0_), channel_id=1, source_target_pairs={{0,1},{1,0},{2,3},{3,2},{4,5},{5,4},{6,7},{7,6},{8,9},{9,8},{10,11... | collective-permute-start | bytes 196616 | tf_op jit(solution)/shard_map/ppermute | solution.py:431
  25.1 2.2 %collective-permute-done.13.refs_3_ = f32[16,1024]{1,0:T(8,128)S(1)} collective-permute-done((f32[16,1024]{1,0:T(8,128)S(1)}, f32[16,1024]{1,0:T(8,128)S(1)}, u32[]{:S(2)}, u32[]{:S(2)}) %collective-permute-start.13) | collective-permute-done | bytes 65568 | tf_op jit(solution)/shard_map/ppermute | solution.py:431
  27.3 0.9 %collective-permute-done.12.refs_2_ = f32[16,1024]{1,0:T(8,128)S(1)} collective-permute-done((f32[16,1024]{1,0:T(8,128)S(1)}, f32[16,1024]{1,0:T(8,128)S(1)}, u32[]{:S(2)}, u32[]{:S(2)}) %collective-permute-start.12) | collective-permute-done | bytes 65568 | tf_op jit(solution)/shard_map/ppermute | solution.py:431
  28.2 0.8 %shard_map.117 = f32[2,16,2048]{2,1,0:T(8,128)} custom-call(f32[2,2,8,128]{3,2,1,0:T(8,128)S(1)} %get-tuple-element.26.response_ref, f32[2,16,2048]{2,1,0:T(8,128)S(1)} %copy-done, f32[16,1024]{1,0:T(8,128)S(1)} %shard_map.116.refs_0_, f32[16,1024]{1,0:T(8,128)S(1)} %collective-permute-done.11.refs_1_, f32[16,1024]{1,0:T(8,128)S(1)} %collective-permute-done.12.refs_2_, ...), custom_call_target="tpu_custom_call" | custom-call | flops 4096000 | bytes 1024000 | tf_op jit(solution)/shard_map/pallas_call | solution.py:550
  (9 shorter events, 0.1 us)
Async XLA Ops:
  1.6 3.2 %collective-permute-start = (f32[16,2048]{1,0:T(8,128)S(1)}, f32[16,2048]{1,0:T(8,128)S(1)}, u32[]{:S(2)}, u32[]{:S(2)}) collective-permute-start(f32[16,2048]{1,0:T(8,128)S(1)} %get-tuple-element.28), channel_id=1, source_target_pairs={{0,1},{1,0},{2,3},{3,2},{4,5},{5,4},{6,7},{7,6},{8,9},{9,8},{10,11... | collective-permute-start | bytes 393224 | tf_op jit(solution)/shard_map/ppermute | solution.py:431
  2.1 10.9 %collective-permute-start.6 = (f32[2,104,128]{2,1,0:T(8,128)S(1)}, f32[2,104,128]{2,1,0:T(8,128)S(1)}, u32[]{:S(2)}, u32[]{:S(2)}) collective-permute-start(f32[2,104,128]{2,1,0:T(8,128)S(1)} %get-tuple-element.37), channel_id=1, source_target_pairs={{0,4},{1,9},{2,6},{3,11},{4,0},{5,13},{6,2},{7,15},{8,12},{9,1},{1... | collective-permute-start | bytes 319496 | tf_op jit(solution)/shard_map/ppermute | solution.py:454
  4.8 5.0 %collective-permute-start.1 = (f32[16,1152]{1,0:T(8,128)S(1)}, f32[16,1152]{1,0:T(8,128)S(1)}, u32[]{:S(2)}, u32[]{:S(2)}) collective-permute-start(f32[16,1152]{1,0:T(8,128)S(1)} %get-tuple-element.30), channel_id=1, source_target_pairs={{0,2},{1,3},{2,0},{3,1},{4,6},{5,7},{6,4},{7,5},{8,10},{9,11},{10,... | collective-permute-start | bytes 221192 | tf_op jit(solution)/shard_map/ppermute | solution.py:431
  6.3 6.6 %collective-permute-start.7 = (f32[104,128]{1,0:T(8,128)S(1)}, f32[104,128]{1,0:T(8,128)S(1)}, u32[]{:S(2)}, u32[]{:S(2)}) collective-permute-start(f32[104,128]{1,0:T(8,128)S(1)} %get-tuple-element.38), channel_id=1, source_target_pairs={{0,12},{1,13},{2,14},{3,15},{4,8},{5,9},{6,10},{7,11},{8,4},{9,5},... | collective-permute-start | bytes 159752 | tf_op jit(solution)/shard_map/ppermute | solution.py:454
  9.6 5.7 %collective-permute-start.4 = (f32[2,90,128]{2,1,0:T(8,128)S(1)}, f32[2,90,128]{2,1,0:T(8,128)S(1)}, u32[]{:S(2)}, u32[]{:S(2)}) collective-permute-start(f32[2,90,128]{2,1,0:T(8,128)S(1)} %get-tuple-element.34), channel_id=1, source_target_pairs={{0,4},{4,0},{8,12},{12,8},{1,5},{5,1},{9,13},{13,9},{2,6},{6,2},{1... | collective-permute-start | bytes 276488 | tf_op jit(solution)/shard_map/ppermute | solution.py:431
  9.6 5.7 %collective-permute-start.5 = (f32[2,90,128]{2,1,0:T(8,128)S(1)}, f32[2,90,128]{2,1,0:T(8,128)S(1)}, u32[]{:S(2)}, u32[]{:S(2)}) collective-permute-start(f32[2,90,128]{2,1,0:T(8,128)S(1)} %get-tuple-element.35), channel_id=1, source_target_pairs={{0,1},{1,0},{2,3},{3,2},{4,8},{5,9},{6,10},{7,11},{8,4},{9,5},{10,... | collective-permute-start | bytes 276488 | tf_op jit(solution)/shard_map/ppermute | solution.py:442
  9.8 6.2 %collective-permute-start.2 = (f32[90,128]{1,0:T(8,128)S(1)}, f32[90,128]{1,0:T(8,128)S(1)}, u32[]{:S(2)}, u32[]{:S(2)}) collective-permute-start(f32[90,128]{1,0:T(8,128)S(1)} %get-tuple-element.32), channel_id=1, source_target_pairs={{0,4},{4,0},{8,12},{12,8},{1,5},{5,1},{9,13},{13,9},{2,6},{6,2},{1... | collective-permute-start | bytes 138248 | tf_op jit(solution)/shard_map/ppermute | solution.py:431
  13.0 3.1 %collective-permute-start.3 = (f32[90,128]{1,0:T(8,128)S(1)}, f32[90,128]{1,0:T(8,128)S(1)}, u32[]{:S(2)}, u32[]{:S(2)}) collective-permute-start(f32[90,128]{1,0:T(8,128)S(1)} %get-tuple-element.33), channel_id=1, source_target_pairs={{0,1},{1,0},{2,3},{3,2},{4,8},{5,9},{6,10},{7,11},{8,4},{9,5},{10,... | collective-permute-start | bytes 138248 | tf_op jit(solution)/shard_map/ppermute | solution.py:442
  16.2 1.4 %collective-permute-start.8 = (f32[2,16,1152]{2,1,0:T(8,128)S(1)}, f32[2,16,1152]{2,1,0:T(8,128)S(1)}, u32[]{:S(2)}, u32[]{:S(2)}) collective-permute-start(f32[2,16,1152]{2,1,0:T(8,128)S(1)} %get-tuple-element.43), channel_id=1, source_target_pairs={{0,1},{1,0},{2,3},{3,2},{4,5},{5,4},{6,7},{7,6},{8,9},{9,8},{10,11... | collective-permute-start | bytes 442376 | tf_op jit(solution)/shard_map/ppermute | solution.py:431
  16.3 1.4 %copy-start.1 = (s32[16,2048]{1,0:T(8,128)S(1)}, s32[16,2048]{1,0:T(8,128)}, u32[]{:S(2)}) copy-start(s32[16,2048]{1,0:T(8,128)} %mask_ref.1) | copy-start | bytes 393220
  17.7 4.2 %collective-permute-start.9 = (f32[90,128]{1,0:T(8,128)S(1)}, f32[90,128]{1,0:T(8,128)S(1)}, u32[]{:S(2)}, u32[]{:S(2)}) collective-permute-start(f32[90,128]{1,0:T(8,128)S(1)} %get-tuple-element.45), channel_id=1, source_target_pairs={{0,4},{4,0},{8,12},{12,8},{1,5},{5,1},{9,13},{13,9},{2,6},{6,2},{1... | collective-permute-start | bytes 138248 | tf_op jit(solution)/shard_map/ppermute | solution.py:431
  19.1 2.8 %collective-permute-start.10 = (f32[90,128]{1,0:T(8,128)S(1)}, f32[90,128]{1,0:T(8,128)S(1)}, u32[]{:S(2)}, u32[]{:S(2)}) collective-permute-start(f32[90,128]{1,0:T(8,128)S(1)} %get-tuple-element.46), channel_id=1, source_target_pairs={{0,1},{1,0},{2,3},{3,2},{4,8},{5,9},{6,10},{7,11},{8,4},{9,5},{10,... | collective-permute-start | bytes 138248 | tf_op jit(solution)/shard_map/ppermute | solution.py:442
  21.9 6.3 %copy-start = (f32[2,16,2048]{2,1,0:T(8,128)S(1)}, f32[2,16,2048]{2,1,0:T(8,128)}, u32[]{:S(2)}) copy-start(f32[2,16,2048]{2,1,0:T(8,128)} %control_ref.1) | copy-start | bytes 786436
  23.1 4.2 %collective-permute-start.13 = (f32[16,1024]{1,0:T(8,128)S(1)}, f32[16,1024]{1,0:T(8,128)S(1)}, u32[]{:S(2)}, u32[]{:S(2)}) collective-permute-start(f32[16,1024]{1,0:T(8,128)S(1)} %shard_map.116.refs_0_), channel_id=1, source_target_pairs={{0,3},{1,2},{2,1},{3,0},{4,7},{5,6},{6,5},{7,4},{8,11},{9,10},{10,... | collective-permute-start | bytes 196616 | tf_op jit(solution)/shard_map/ppermute | solution.py:431
  23.2 5.0 %collective-permute-start.12 = (f32[16,1024]{1,0:T(8,128)S(1)}, f32[16,1024]{1,0:T(8,128)S(1)}, u32[]{:S(2)}, u32[]{:S(2)}) collective-permute-start(f32[16,1024]{1,0:T(8,128)S(1)} %shard_map.116.refs_0_), channel_id=1, source_target_pairs={{0,2},{1,3},{2,0},{3,1},{4,6},{5,7},{6,4},{7,5},{8,10},{9,11},{10,... | collective-permute-start | bytes 196616 | tf_op jit(solution)/shard_map/ppermute | solution.py:431
  24.1 4.1 %collective-permute-start.11 = (f32[16,1024]{1,0:T(8,128)S(1)}, f32[16,1024]{1,0:T(8,128)S(1)}, u32[]{:S(2)}, u32[]{:S(2)}) collective-permute-start(f32[16,1024]{1,0:T(8,128)S(1)} %shard_map.116.refs_0_), channel_id=1, source_target_pairs={{0,1},{1,0},{2,3},{3,2},{4,5},{5,4},{6,7},{7,6},{8,9},{9,8},{10,11... | collective-permute-start | bytes 196616 | tf_op jit(solution)/shard_map/ppermute | solution.py:431

commit v6 on v5

--- a/solution.py
+++ b/solution.py
@@ -107,7 +107,7 @@
 
     tiles = lax.axis_size("tile")
     full = tiles // 2 - 1
-    first = jnp.where(core == 0, 1, tiles // 2)
+    first = jnp.where(core == 0, 1, tiles // 2 + 1)
     panels = value_ref.shape[0]
     source = tile_ref[...] ^ mine
     names = lax.broadcasted_iota(jnp.int32, (-(-tiles // 8) * 8, panels), 0)
@@ -117,7 +117,7 @@
     parity, slot = rank % 2, rank // 2
     whole = (source >= first) & (source < first + full)
     home = source == 0
-    keep = whole | ((home | (source == tiles - 1)) & (parity == core))
+    keep = whole | ((home | (source == tiles // 2)) & (parity == core))
     half = jnp.where(whole, 2 * (source - first) + parity, jnp.where(home, tiles - 1, tiles - 2))
     place = jnp.where(keep, half * slots + slot, -1)
     spots = lax.broadcasted_iota(jnp.int32, (tiles * slots, panels), 0)
@@ -415,8 +415,13 @@
     out_ref[...] = ring_ref[:rows, lanes(my_chip() * own - start, own)]
 
 
+def sent_last(members):
+    return [0, 1] + sorted(range(2, members), key=lambda d: -(d % 2))
+
+
 def result_kernel(response_ref, control_ref, *refs):
     own, out_ref = refs[0].shape[1] // LANES, refs[-1]
+    refs = [refs[sent_last(len(refs) - 1).index(d)] for d in range(len(refs) - 1)]
     for d in range(len(refs) // 2):
         window = lanes((my_chip() ^ d) * own, own)
         for v in range(control_ref.shape[0]):
@@ -449,7 +454,7 @@
         pairs = []
         for t in range(tiles):
             for q in range(members):
-                offset = tiles - 1 if turn == len(chunks) - 2 else 1 + turn + (q % 2) * (tiles // 2 - 1)
+                offset = tiles // 2 if turn == len(chunks) - 2 else 1 + turn + (q % 2) * (tiles // 2)
                 pairs.append((t * members + q, (t ^ offset) * members + q))
         got.append(lax.ppermute(chunk, ("tile", "var"), pairs))
     return got + [chunks[-1]]
@@ -546,7 +551,7 @@
         [ring],
         cost=cost(4000),
     )(adjoint, even, odd, coef)
-    shares = [mine] + [swap(mine, "var", d) for d in range(1, members)]
+    shares = [mine] + [swap(mine, "var", d) for d in sent_last(members)[1:]]
     (out,) = call(
         result_kernel,
         [jax.ShapeDtypeStruct(control.shape, F32)],

time: 29.4 us -> 29.1 us (0.990)
  waiting for transfers between devices: 8.35 us -> 7.17 us
  Pallas kernels: 7.07 us -> 8.06 us
    ppermute x9, waiting for transfers between devices: 7.13 us -> 5.52 us  [swap(): return lax.ppermute(values, axis, [(i, i ^ bit) for i in range(count)])]
    pallas_call x1, Pallas kernels: 1.92 us -> 2.9 us  [local(): call(functools.partial(scatter_kernel, slots, blocks), [view2, view2], [A...]
    ppermute x2, starting transfers between devices: 5.93 us -> 5.23 us  [deliver(): got.append(lax.ppermute(chunk, ('tile', 'var'), pairs))]
    ppermute x9, starting transfers between devices: 7.38 us -> 8.05 us  [swap(): return lax.ppermute(values, axis, [(i, i ^ bit) for i in range(count)])]
    ppermute x2, waiting for transfers between devices: 1.21 us -> 1.65 us  [deliver(): got.append(lax.ppermute(chunk, ('tile', 'var'), pairs))]
  transfers between devices with their start and end apart: 14 -> 14, of which waited for: 8 -> 3; matrix products, arithmetic and copies ran while one was open for 0% -> 0% of each run, Pallas kernels for 11% -> 15%
where the time goes in v6:
time: 29.1 us; the launch traced here: 28.8 us
  starting transfers between devices  13.5 us (46%)
  Pallas kernels  8.06 us (28%)
  waiting for transfers between devices  7.17 us (25%)
    ppermute x9, starting transfers between devices, swap(): return lax.ppermute(values, axis, [(i, i ^ bit) for i in range(count)])  8.05 us
    ppermute x9, waiting for transfers between devices, swap(): return lax.ppermute(values, axis, [(i, i ^ bit) for i in range(count)])  5.52 us
    ppermute x2, starting transfers between devices, deliver(): got.append(lax.ppermute(chunk, ('tile', 'var'), pairs))  5.23 us
    pallas_call x1, Pallas kernels, local(): call(functools.partial(scatter_kernel, slots, blocks), [view2, view2], [A...  2.9 us
    ppermute x2, waiting for transfers between devices, deliver(): got.append(lax.ppermute(chunk, ('tile', 'var'), pairs))  1.65 us
    pallas_call x1, Pallas kernels, local(): call(functools.partial(first_kernel, slots, margin), [field, field, jax.S...  1.58 us
    pallas_call x1, Pallas kernels, local(): call(functools.partial(spread_kernel, margin), [share], [VMEM] * 4, [ring...  1.25 us
    pallas_call x1, Pallas kernels, local(): call(functools.partial(smooth_kernel, margin), [view], [VMEM] * 4, [ring]...  1.25 us
  transfers between devices with their start and end apart: 14, of which 3 were waited for; matrix products, arithmetic and copies ran while one was open for 0% of the time, Pallas kernels for 15%

profile of v6, /device:TPU:0, one launch (start us, length us, event | category | flops | bytes accessed | tf_op | source)
XLA Modules:
  0.0 28.8 jit_solution(13118705944004994896)
XLA Ops:
  0.0 1.6 %shard_map.109 = (f32[16,2048]{1,0:T(8,128)S(1)}, f32[16,2048]{1,0:T(8,128)S(1)}, f32[2,2,8,128]{3,2,1,0:T(8,128)S(1)}, f32[2,16,1152]{2,1,0:T(8,128)S(1)}, f32[...) custom-call(f32[2,8]{1,0:T(2,128)} %sens_hbm.1, ...), custom_call_target="tpu_custom_call" | custom-call | flops 12288000 | bytes 3072000 | tf_op jit(solution)/shard_map/pallas_call | solution.py:485
  1.6 0.5 %collective-permute-start = (f32[16,2048]{1,0:T(8,128)S(1)}, f32[16,2048]{1,0:T(8,128)S(1)}, u32[]{:S(2)}, u32[]{:S(2)}) collective-permute-start(f32[16,2048]{1,0:T(8,128)S(1)} %get-tuple-element.28), channel_id=1, source_target_pairs={{0,1},{1,0},{2,3},{3,2},{4,5},{5,4},{6,7},{7,6},{8,9},{9,8},{10,11... | collective-permute-start | bytes 393224 | tf_op jit(solution)/shard_map/ppermute | solution.py:436
  2.1 2.6 %collective-permute-start.6 = (f32[2,104,128]{2,1,0:T(8,128)S(1)}, f32[2,104,128]{2,1,0:T(8,128)S(1)}, u32[]{:S(2)}, u32[]{:S(2)}) collective-permute-start(f32[2,104,128]{2,1,0:T(8,128)S(1)} %get-tuple-element.37), channel_id=1, source_target_pairs={{0,4},{1,13},{2,6},{3,15},{4,0},{5,9},{6,2},{7,11},{8,12},{9,5},{1... | collective-permute-start | bytes 319496 | tf_op jit(solution)/shard_map/ppermute | solution.py:459
  4.8 0.0 collective-permute-done.second_ref
  4.8 1.6 %collective-permute-start.1 = (f32[16,1152]{1,0:T(8,128)S(1)}, f32[16,1152]{1,0:T(8,128)S(1)}, u32[]{:S(2)}, u32[]{:S(2)}) collective-permute-start(f32[16,1152]{1,0:T(8,128)S(1)} %get-tuple-element.30), channel_id=1, source_target_pairs={{0,2},{1,3},{2,0},{3,1},{4,6},{5,7},{6,4},{7,5},{8,10},{9,11},{10,... | collective-permute-start | bytes 221192 | tf_op jit(solution)/shard_map/ppermute | solution.py:436
  6.3 2.6 %collective-permute-start.7 = (f32[104,128]{1,0:T(8,128)S(1)}, f32[104,128]{1,0:T(8,128)S(1)}, u32[]{:S(2)}, u32[]{:S(2)}) collective-permute-start(f32[104,128]{1,0:T(8,128)S(1)} %get-tuple-element.38), channel_id=1, source_target_pairs={{0,8},{1,9},{2,10},{3,11},{4,12},{5,13},{6,14},{7,15},{8,0},{9,1},... | collective-permute-start | bytes 159752 | tf_op jit(solution)/shard_map/ppermute | solution.py:459
  8.9 1.3 %collective-permute-start.4 = (f32[2,90,128]{2,1,0:T(8,128)S(1)}, f32[2,90,128]{2,1,0:T(8,128)S(1)}, u32[]{:S(2)}, u32[]{:S(2)}) collective-permute-start(f32[2,90,128]{2,1,0:T(8,128)S(1)} %get-tuple-element.34), channel_id=1, source_target_pairs={{0,4},{4,0},{8,12},{12,8},{1,5},{5,1},{9,13},{13,9},{2,6},{6,2},{1... | collective-permute-start | bytes 276488 | tf_op jit(solution)/shard_map/ppermute | solution.py:436
  10.2 0.0 collective-permute-start.5
  10.2 0.0 collective-permute-done.1.refs_1_
  10.2 1.0 %collective-permute-start.2 = (f32[90,128]{1,0:T(8,128)S(1)}, f32[90,128]{1,0:T(8,128)S(1)}, u32[]{:S(2)}, u32[]{:S(2)}) collective-permute-start(f32[90,128]{1,0:T(8,128)S(1)} %get-tuple-element.32), channel_id=1, source_target_pairs={{0,4},{4,0},{8,12},{12,8},{1,5},{5,1},{9,13},{13,9},{2,6},{6,2},{1... | collective-permute-start | bytes 138248 | tf_op jit(solution)/shard_map/ppermute | solution.py:436
  11.2 1.6 %collective-permute-done.7.refs_1_ = f32[104,128]{1,0:T(8,128)S(1)} collective-permute-done((f32[104,128]{1,0:T(8,128)S(1)}, f32[104,128]{1,0:T(8,128)S(1)}, u32[]{:S(2)}, u32[]{:S(2)}) %collective-permute-start.7) | collective-permute-done | bytes 53280 | tf_op jit(solution)/shard_map/ppermute | solution.py:459
  12.8 0.1 collective-permute-start.3
  12.9 2.9 %shard_map.112 = (f32[2,16,1152]{2,1,0:T(8,128)S(1)}, f32[2,16,1152]{2,1,0:T(8,128)S(1)}) custom-call(f32[16,1152]{1,0:T(8,128)S(1)} %get-tuple-element.31.after_ref.own_ref, f32[2,104,128]{2,1,0:T(8,128)S(1)} %collective-permute-done.6.refs_0_, f32[104,128]{1,0:T(8,128)S(1)} %collective-permute-done.7.refs_1_, f32[104,128]{1,0:T(8,128)S(1)} %get-tuple-element.39.refs_2_), custom_call_target="tpu_custom_call" | custom-call | flops 409600000 | bytes 102400000 | tf_op jit(solution)/shard_map/pallas_call | solution.py:516
  15.8 0.0 collective-permute-done.4.even_ref
  15.8 0.0 collective-permute-done.2.refs_0_.even_ref
  15.9 0.0 collective-permute-done.3.refs_1_.odd_ref
  15.9 0.2 shard_map.113
  16.1 0.5 %collective-permute-start.8 = (f32[2,16,1152]{2,1,0:T(8,128)S(1)}, f32[2,16,1152]{2,1,0:T(8,128)S(1)}, u32[]{:S(2)}, u32[]{:S(2)}) collective-permute-start(f32[2,16,1152]{2,1,0:T(8,128)S(1)} %get-tuple-element.43), channel_id=1, source_target_pairs={{0,1},{1,0},{2,3},{3,2},{4,5},{5,4},{6,7},{7,6},{8,9},{9,8},{10,11... | collective-permute-start | bytes 442376 | tf_op jit(solution)/shard_map/ppermute | solution.py:436
  16.6 1.2 %shard_map.114.smooth_ref = f32[16,1152]{1,0:T(8,128)S(1)} custom-call(f32[16,1152]{1,0:T(8,128)S(1)} %get-tuple-element.31.after_ref.own_ref, f32[90,128]{1,0:T(8,128)S(1)} %collective-permute-done.2.refs_0_.even_ref, f32[90,128]{1,0:T(8,128)S(1)} %collective-permute-done.3.refs_1_.odd_ref, f32[5,40,1152]{2,1,0:T(8,128)S(1)} %get-tuple-element.41.coef_ref), custom_call_target="tpu_custom_call" | custom-call | flops 16384000 | bytes 4096000 | tf_op jit(solution)/shard_map/pallas_call | solution.py:536
  17.8 0.0 collective-permute-done.8.more_ref
  17.9 1.0 %collective-permute-start.9 = (f32[90,128]{1,0:T(8,128)S(1)}, f32[90,128]{1,0:T(8,128)S(1)}, u32[]{:S(2)}, u32[]{:S(2)}) collective-permute-start(f32[90,128]{1,0:T(8,128)S(1)} %get-tuple-element.45), channel_id=1, source_target_pairs={{0,4},{4,0},{8,12},{12,8},{1,5},{5,1},{9,13},{13,9},{2,6},{6,2},{1... | collective-permute-start | bytes 138248 | tf_op jit(solution)/shard_map/ppermute | solution.py:436
  18.9 0.1 collective-permute-start.10
  19.1 3.0 %collective-permute-done.9.even_ref = f32[90,128]{1,0:T(8,128)S(1)} collective-permute-done((f32[90,128]{1,0:T(8,128)S(1)}, f32[90,128]{1,0:T(8,128)S(1)}, u32[]{:S(2)}, u32[]{:S(2)}) %collective-permute-start.9) | collective-permute-done | bytes 46112 | tf_op jit(solution)/shard_map/ppermute | solution.py:436
  22.1 0.0 collective-permute-done.10.odd_ref
  22.1 1.2 %shard_map.116.refs_0_ = f32[16,1024]{1,0:T(8,128)S(1)} custom-call(f32[16,1152]{1,0:T(8,128)S(1)} %get-tuple-element.44.own_ref, f32[90,128]{1,0:T(8,128)S(1)} %collective-permute-done.9.even_ref, f32[90,128]{1,0:T(8,128)S(1)} %collective-permute-done.10.odd_ref, f32[5,40,1152]{2,1,0:T(8,128)S(1)} %get-tuple-element.41.coef_ref), custom_call_target="tpu_custom_call" | custom-call | flops 16384000 | bytes 4096000 | tf_op jit(solution)/shard_map/pallas_call | solution.py:547
  23.3 0.3 %collective-permute-start.13 = (f32[16,1024]{1,0:T(8,128)S(1)}, f32[16,1024]{1,0:T(8,128)S(1)}, u32[]{:S(2)}, u32[]{:S(2)}) collective-permute-start(f32[16,1024]{1,0:T(8,128)S(1)} %shard_map.116.refs_0_), channel_id=1, source_target_pairs={{0,2},{1,3},{2,0},{3,1},{4,6},{5,7},{6,4},{7,5},{8,10},{9,11},{10,... | collective-permute-start | bytes 196616 | tf_op jit(solution)/shard_map/ppermute | solution.py:436
  23.7 0.0 collective-permute-start.12
  23.7 1.8 %collective-permute-start.11 = (f32[16,1024]{1,0:T(8,128)S(1)}, f32[16,1024]{1,0:T(8,128)S(1)}, u32[]{:S(2)}, u32[]{:S(2)}) collective-permute-start(f32[16,1024]{1,0:T(8,128)S(1)} %shard_map.116.refs_0_), channel_id=1, source_target_pairs={{0,1},{1,0},{2,3},{3,2},{4,5},{5,4},{6,7},{7,6},{8,9},{9,8},{10,11... | collective-permute-start | bytes 196616 | tf_op jit(solution)/shard_map/ppermute | solution.py:436
  25.5 2.5 %collective-permute-done.13.refs_3_ = f32[16,1024]{1,0:T(8,128)S(1)} collective-permute-done((f32[16,1024]{1,0:T(8,128)S(1)}, f32[16,1024]{1,0:T(8,128)S(1)}, u32[]{:S(2)}, u32[]{:S(2)}) %collective-permute-start.13) | collective-permute-done | bytes 65568 | tf_op jit(solution)/shard_map/ppermute | solution.py:436
  28.0 0.0 collective-permute-done.12.refs_2_
  28.1 0.0 collective-permute-done.11.refs_1_
  28.1 0.8 %shard_map.117 = f32[2,16,2048]{2,1,0:T(8,128)} custom-call(f32[2,2,8,128]{3,2,1,0:T(8,128)S(1)} %get-tuple-element.26.response_ref, f32[2,16,2048]{2,1,0:T(8,128)S(1)} %copy-done, f32[16,1024]{1,0:T(8,128)S(1)} %shard_map.116.refs_0_, f32[16,1024]{1,0:T(8,128)S(1)} %collective-permute-done.11.refs_1_, f32[16,1024]{1,0:T(8,128)S(1)} %collective-permute-done.12.refs_2_, ...), custom_call_target="tpu_custom_call" | custom-call | flops 4096000 | bytes 1024000 | tf_op jit(solution)/shard_map/pallas_call | solution.py:555
  (9 shorter events, 0.1 us)
Async XLA Ops:
  1.6 3.2 %collective-permute-start = (f32[16,2048]{1,0:T(8,128)S(1)}, f32[16,2048]{1,0:T(8,128)S(1)}, u32[]{:S(2)}, u32[]{:S(2)}) collective-permute-start(f32[16,2048]{1,0:T(8,128)S(1)} %get-tuple-element.28), channel_id=1, source_target_pairs={{0,1},{1,0},{2,3},{3,2},{4,5},{5,4},{6,7},{7,6},{8,9},{9,8},{10,11... | collective-permute-start | bytes 393224 | tf_op jit(solution)/shard_map/ppermute | solution.py:436
  2.1 10.8 %collective-permute-start.6 = (f32[2,104,128]{2,1,0:T(8,128)S(1)}, f32[2,104,128]{2,1,0:T(8,128)S(1)}, u32[]{:S(2)}, u32[]{:S(2)}) collective-permute-start(f32[2,104,128]{2,1,0:T(8,128)S(1)} %get-tuple-element.37), channel_id=1, source_target_pairs={{0,4},{1,13},{2,6},{3,15},{4,0},{5,9},{6,2},{7,11},{8,12},{9,5},{1... | collective-permute-start | bytes 319496 | tf_op jit(solution)/shard_map/ppermute | solution.py:459
  4.8 5.4 %collective-permute-start.1 = (f32[16,1152]{1,0:T(8,128)S(1)}, f32[16,1152]{1,0:T(8,128)S(1)}, u32[]{:S(2)}, u32[]{:S(2)}) collective-permute-start(f32[16,1152]{1,0:T(8,128)S(1)} %get-tuple-element.30), channel_id=1, source_target_pairs={{0,2},{1,3},{2,0},{3,1},{4,6},{5,7},{6,4},{7,5},{8,10},{9,11},{10,... | collective-permute-start | bytes 221192 | tf_op jit(solution)/shard_map/ppermute | solution.py:436
  6.3 6.5 %collective-permute-start.7 = (f32[104,128]{1,0:T(8,128)S(1)}, f32[104,128]{1,0:T(8,128)S(1)}, u32[]{:S(2)}, u32[]{:S(2)}) collective-permute-start(f32[104,128]{1,0:T(8,128)S(1)} %get-tuple-element.38), channel_id=1, source_target_pairs={{0,8},{1,9},{2,10},{3,11},{4,12},{5,13},{6,14},{7,15},{8,0},{9,1},... | collective-permute-start | bytes 159752 | tf_op jit(solution)/shard_map/ppermute | solution.py:459
  8.9 6.9 %collective-permute-start.4 = (f32[2,90,128]{2,1,0:T(8,128)S(1)}, f32[2,90,128]{2,1,0:T(8,128)S(1)}, u32[]{:S(2)}, u32[]{:S(2)}) collective-permute-start(f32[2,90,128]{2,1,0:T(8,128)S(1)} %get-tuple-element.34), channel_id=1, source_target_pairs={{0,4},{4,0},{8,12},{12,8},{1,5},{5,1},{9,13},{13,9},{2,6},{6,2},{1... | collective-permute-start | bytes 276488 | tf_op jit(solution)/shard_map/ppermute | solution.py:436
  10.2 5.6 %collective-permute-start.5 = (f32[2,90,128]{2,1,0:T(8,128)S(1)}, f32[2,90,128]{2,1,0:T(8,128)S(1)}, u32[]{:S(2)}, u32[]{:S(2)}) collective-permute-start(f32[2,90,128]{2,1,0:T(8,128)S(1)} %get-tuple-element.35), channel_id=1, source_target_pairs={{0,1},{1,0},{2,3},{3,2},{4,8},{5,9},{6,10},{7,11},{8,4},{9,5},{10,... | collective-permute-start | bytes 276488 | tf_op jit(solution)/shard_map/ppermute | solution.py:447
  10.2 5.6 %collective-permute-start.2 = (f32[90,128]{1,0:T(8,128)S(1)}, f32[90,128]{1,0:T(8,128)S(1)}, u32[]{:S(2)}, u32[]{:S(2)}) collective-permute-start(f32[90,128]{1,0:T(8,128)S(1)} %get-tuple-element.32), channel_id=1, source_target_pairs={{0,4},{4,0},{8,12},{12,8},{1,5},{5,1},{9,13},{13,9},{2,6},{6,2},{1... | collective-permute-start | bytes 138248 | tf_op jit(solution)/shard_map/ppermute | solution.py:436
  12.8 3.0 %collective-permute-start.3 = (f32[90,128]{1,0:T(8,128)S(1)}, f32[90,128]{1,0:T(8,128)S(1)}, u32[]{:S(2)}, u32[]{:S(2)}) collective-permute-start(f32[90,128]{1,0:T(8,128)S(1)} %get-tuple-element.33), channel_id=1, source_target_pairs={{0,1},{1,0},{2,3},{3,2},{4,8},{5,9},{6,10},{7,11},{8,4},{9,5},{10,... | collective-permute-start | bytes 138248 | tf_op jit(solution)/shard_map/ppermute | solution.py:447
  16.1 1.8 %collective-permute-start.8 = (f32[2,16,1152]{2,1,0:T(8,128)S(1)}, f32[2,16,1152]{2,1,0:T(8,128)S(1)}, u32[]{:S(2)}, u32[]{:S(2)}) collective-permute-start(f32[2,16,1152]{2,1,0:T(8,128)S(1)} %get-tuple-element.43), channel_id=1, source_target_pairs={{0,1},{1,0},{2,3},{3,2},{4,5},{5,4},{6,7},{7,6},{8,9},{9,8},{10,11... | collective-permute-start | bytes 442376 | tf_op jit(solution)/shard_map/ppermute | solution.py:436
  16.6 1.3 %copy-start.1 = (s32[16,2048]{1,0:T(8,128)S(1)}, s32[16,2048]{1,0:T(8,128)}, u32[]{:S(2)}) copy-start(s32[16,2048]{1,0:T(8,128)} %mask_ref.1) | copy-start | bytes 393220
  17.9 4.2 %collective-permute-start.9 = (f32[90,128]{1,0:T(8,128)S(1)}, f32[90,128]{1,0:T(8,128)S(1)}, u32[]{:S(2)}, u32[]{:S(2)}) collective-permute-start(f32[90,128]{1,0:T(8,128)S(1)} %get-tuple-element.45), channel_id=1, source_target_pairs={{0,4},{4,0},{8,12},{12,8},{1,5},{5,1},{9,13},{13,9},{2,6},{6,2},{1... | collective-permute-start | bytes 138248 | tf_op jit(solution)/shard_map/ppermute | solution.py:436
  18.9 3.1 %collective-permute-start.10 = (f32[90,128]{1,0:T(8,128)S(1)}, f32[90,128]{1,0:T(8,128)S(1)}, u32[]{:S(2)}, u32[]{:S(2)}) collective-permute-start(f32[90,128]{1,0:T(8,128)S(1)} %get-tuple-element.46), channel_id=1, source_target_pairs={{0,1},{1,0},{2,3},{3,2},{4,8},{5,9},{6,10},{7,11},{8,4},{9,5},{10,... | collective-permute-start | bytes 138248 | tf_op jit(solution)/shard_map/ppermute | solution.py:447
  22.1 6.0 %copy-start = (f32[2,16,2048]{2,1,0:T(8,128)S(1)}, f32[2,16,2048]{2,1,0:T(8,128)}, u32[]{:S(2)}) copy-start(f32[2,16,2048]{2,1,0:T(8,128)} %control_ref.1) | copy-start | bytes 786436
  23.3 4.7 %collective-permute-start.13 = (f32[16,1024]{1,0:T(8,128)S(1)}, f32[16,1024]{1,0:T(8,128)S(1)}, u32[]{:S(2)}, u32[]{:S(2)}) collective-permute-start(f32[16,1024]{1,0:T(8,128)S(1)} %shard_map.116.refs_0_), channel_id=1, source_target_pairs={{0,2},{1,3},{2,0},{3,1},{4,6},{5,7},{6,4},{7,5},{8,10},{9,11},{10,... | collective-permute-start | bytes 196616 | tf_op jit(solution)/shard_map/ppermute | solution.py:436
  23.7 4.4 %collective-permute-start.12 = (f32[16,1024]{1,0:T(8,128)S(1)}, f32[16,1024]{1,0:T(8,128)S(1)}, u32[]{:S(2)}, u32[]{:S(2)}) collective-permute-start(f32[16,1024]{1,0:T(8,128)S(1)} %shard_map.116.refs_0_), channel_id=1, source_target_pairs={{0,3},{1,2},{2,1},{3,0},{4,7},{5,6},{6,5},{7,4},{8,11},{9,10},{10,... | collective-permute-start | bytes 196616 | tf_op jit(solution)/shard_map/ppermute | solution.py:436
  23.7 4.4 %collective-permute-start.11 = (f32[16,1024]{1,0:T(8,128)S(1)}, f32[16,1024]{1,0:T(8,128)S(1)}, u32[]{:S(2)}, u32[]{:S(2)}) collective-permute-start(f32[16,1024]{1,0:T(8,128)S(1)} %shard_map.116.refs_0_), channel_id=1, source_target_pairs={{0,1},{1,0},{2,3},{3,2},{4,5},{5,4},{6,7},{7,6},{8,9},{9,8},{10,11... | collective-permute-start | bytes 196616 | tf_op jit(solution)/shard_map/ppermute | solution.py:436

commit v7 on v6

--- a/solution.py
+++ b/solution.py
@@ -167,7 +167,7 @@
 def scatter_kernel(slots, blocks_all, after_ref, *refs):
     got_refs, (own_ref, other_ref, acc_ref, meta_ref, sems) = refs[:-5], refs[-5:]
     core = lax.axis_index("var") % 2
-    got_refs = [r.at[i] for r in got_refs[:-2] for i in (0, 1)] + list(got_refs[-2:])
+    got_refs = [r.at[i] for r in got_refs[1:-1] for i in (0, 1)] + [got_refs[0], got_refs[-1]]
     size_of_group = min(GROUP, slots)
     copies = [
         pltpu.make_async_copy(ref.at[pl.ds(3 * slots, 8)], meta_ref.at[pl.ds(8 * s, 8)], sems.at[s])
@@ -523,7 +523,7 @@
             pltpu.SemaphoreType.DMA((tiles,)),
         ],
         cost=cost(100000),
-    )(smooth_in, *got)
+    )(smooth_in, got[-2], *got[:-2], got[-1])
     ring = pltpu.VMEM((total, size * LANES), F32)
     coef, sums_other = call(
         functools.partial(faces_kernel, margin),

time: 29.1 us -> 29.1 us (level)
  waiting for transfers between devices: 7.17 us -> 6.75 us
  starting transfers between devices: 13.5 us -> 13.9 us
    ppermute x9, starting transfers between devices: 8.05 us -> 8.48 us  [swap(): return lax.ppermute(values, axis, [(i, i ^ bit) for i in range(count)])]
    ppermute x9, waiting for transfers between devices: 5.52 us -> 5.1 us  [swap(): return lax.ppermute(values, axis, [(i, i ^ bit) for i in range(count)])]
  transfers between devices with their start and end apart: 14 -> 14, of which waited for: 3 -> 3; matrix products, arithmetic and copies ran while one was open for 0% -> 0% of each run, Pallas kernels for 15% -> 14%
where the time goes in v7:
time: 29.1 us; the launch traced here: 28.9 us
  starting transfers between devices  13.9 us (48%)
  Pallas kernels  8.05 us (28%)
  waiting for transfers between devices  6.75 us (23%)
    ppermute x9, starting transfers between devices, swap(): return lax.ppermute(values, axis, [(i, i ^ bit) for i in range(count)])  8.48 us
    ppermute x2, starting transfers between devices, deliver(): got.append(lax.ppermute(chunk, ('tile', 'var'), pairs))  5.23 us
    ppermute x9, waiting for transfers between devices, swap(): return lax.ppermute(values, axis, [(i, i ^ bit) for i in range(count)])  5.1 us
    pallas_call x1, Pallas kernels, local(): call(functools.partial(scatter_kernel, slots, blocks), [view2, view2], [A...  2.89 us
    ppermute x2, waiting for transfers between devices, deliver(): got.append(lax.ppermute(chunk, ('tile', 'var'), pairs))  1.65 us
    pallas_call x1, Pallas kernels, local(): call(functools.partial(first_kernel, slots, margin), [field, field, jax.S...  1.58 us
    pallas_call x1, Pallas kernels, local(): call(functools.partial(spread_kernel, margin), [share], [VMEM] * 4, [ring...  1.25 us
    pallas_call x1, Pallas kernels, local(): call(functools.partial(smooth_kernel, margin), [view], [VMEM] * 4, [ring]...  1.25 us
  transfers between devices with their start and end apart: 14, of which 3 were waited for; matrix products, arithmetic and copies ran while one was open for 0% of the time, Pallas kernels for 14%

profile of v7, /device:TPU:0, one launch (start us, length us, event | category | flops | bytes accessed | tf_op | source)
XLA Modules:
  0.0 28.9 jit_solution(12014638626873041590)
XLA Ops:
  0.0 1.6 %shard_map.109 = (f32[16,2048]{1,0:T(8,128)S(1)}, f32[16,2048]{1,0:T(8,128)S(1)}, f32[2,2,8,128]{3,2,1,0:T(8,128)S(1)}, f32[2,16,1152]{2,1,0:T(8,128)S(1)}, f32[...) custom-call(f32[2,8]{1,0:T(2,128)} %sens_hbm.1, ...), custom_call_target="tpu_custom_call" | custom-call | flops 12288000 | bytes 3072000 | tf_op jit(solution)/shard_map/pallas_call | solution.py:485
  1.6 0.5 %collective-permute-start = (f32[16,2048]{1,0:T(8,128)S(1)}, f32[16,2048]{1,0:T(8,128)S(1)}, u32[]{:S(2)}, u32[]{:S(2)}) collective-permute-start(f32[16,2048]{1,0:T(8,128)S(1)} %get-tuple-element.28), channel_id=1, source_target_pairs={{0,1},{1,0},{2,3},{3,2},{4,5},{5,4},{6,7},{7,6},{8,9},{9,8},{10,11... | collective-permute-start | bytes 393224 | tf_op jit(solution)/shard_map/ppermute | solution.py:436
  2.1 2.6 %collective-permute-start.7 = (f32[2,104,128]{2,1,0:T(8,128)S(1)}, f32[2,104,128]{2,1,0:T(8,128)S(1)}, u32[]{:S(2)}, u32[]{:S(2)}) collective-permute-start(f32[2,104,128]{2,1,0:T(8,128)S(1)} %get-tuple-element.38), channel_id=1, source_target_pairs={{0,4},{1,13},{2,6},{3,15},{4,0},{5,9},{6,2},{7,11},{8,12},{9,5},{1... | collective-permute-start | bytes 319496 | tf_op jit(solution)/shard_map/ppermute | solution.py:459
  4.8 0.0 collective-permute-done.second_ref
  4.8 1.6 %collective-permute-start.1 = (f32[16,1152]{1,0:T(8,128)S(1)}, f32[16,1152]{1,0:T(8,128)S(1)}, u32[]{:S(2)}, u32[]{:S(2)}) collective-permute-start(f32[16,1152]{1,0:T(8,128)S(1)} %get-tuple-element.30), channel_id=1, source_target_pairs={{0,2},{1,3},{2,0},{3,1},{4,6},{5,7},{6,4},{7,5},{8,10},{9,11},{10,... | collective-permute-start | bytes 221192 | tf_op jit(solution)/shard_map/ppermute | solution.py:436
  6.3 2.6 %collective-permute-start.6 = (f32[104,128]{1,0:T(8,128)S(1)}, f32[104,128]{1,0:T(8,128)S(1)}, u32[]{:S(2)}, u32[]{:S(2)}) collective-permute-start(f32[104,128]{1,0:T(8,128)S(1)} %get-tuple-element.37), channel_id=1, source_target_pairs={{0,8},{1,9},{2,10},{3,11},{4,12},{5,13},{6,14},{7,15},{8,0},{9,1},... | collective-permute-start | bytes 159752 | tf_op jit(solution)/shard_map/ppermute | solution.py:459
  8.9 1.3 %collective-permute-start.4 = (f32[2,90,128]{2,1,0:T(8,128)S(1)}, f32[2,90,128]{2,1,0:T(8,128)S(1)}, u32[]{:S(2)}, u32[]{:S(2)}) collective-permute-start(f32[2,90,128]{2,1,0:T(8,128)S(1)} %get-tuple-element.34), channel_id=1, source_target_pairs={{0,4},{4,0},{8,12},{12,8},{1,5},{5,1},{9,13},{13,9},{2,6},{6,2},{1... | collective-permute-start | bytes 276488 | tf_op jit(solution)/shard_map/ppermute | solution.py:436
  10.2 0.0 collective-permute-start.5
  10.2 0.0 collective-permute-done.1.refs_1_
  10.2 1.0 %collective-permute-start.2 = (f32[90,128]{1,0:T(8,128)S(1)}, f32[90,128]{1,0:T(8,128)S(1)}, u32[]{:S(2)}, u32[]{:S(2)}) collective-permute-start(f32[90,128]{1,0:T(8,128)S(1)} %get-tuple-element.32), channel_id=1, source_target_pairs={{0,4},{4,0},{8,12},{12,8},{1,5},{5,1},{9,13},{13,9},{2,6},{6,2},{1... | collective-permute-start | bytes 138248 | tf_op jit(solution)/shard_map/ppermute | solution.py:436
  11.2 1.6 %collective-permute-done.6.refs_0_ = f32[104,128]{1,0:T(8,128)S(1)} collective-permute-done((f32[104,128]{1,0:T(8,128)S(1)}, f32[104,128]{1,0:T(8,128)S(1)}, u32[]{:S(2)}, u32[]{:S(2)}) %collective-permute-start.6) | collective-permute-done | bytes 53280 | tf_op jit(solution)/shard_map/ppermute | solution.py:459
  12.8 0.1 collective-permute-start.3
  12.9 0.0 collective-permute-done.7.refs_1_
  12.9 2.9 %shard_map.112 = (f32[2,16,1152]{2,1,0:T(8,128)S(1)}, f32[2,16,1152]{2,1,0:T(8,128)S(1)}) custom-call(f32[16,1152]{1,0:T(8,128)S(1)} %get-tuple-element.31.after_ref.own_ref, f32[104,128]{1,0:T(8,128)S(1)} %collective-permute-done.6.refs_0_, f32[2,104,128]{2,1,0:T(8,128)S(1)} %collective-permute-done.7.refs_1_, f32[104,128]{1,0:T(8,128)S(1)} %get-tuple-element.39.refs_2_), custom_call_target="tpu_custom_call" | custom-call | flops 409600000 | bytes 102400000 | tf_op jit(solution)/shard_map/pallas_call | solution.py:516
  15.8 0.0 collective-permute-done.4.even_ref
  15.8 0.0 collective-permute-done.5.odd_ref
  15.8 0.0 collective-permute-done.2.refs_0_.even_ref
  15.9 0.2 shard_map.113
  16.1 0.5 %collective-permute-start.8 = (f32[2,16,1152]{2,1,0:T(8,128)S(1)}, f32[2,16,1152]{2,1,0:T(8,128)S(1)}, u32[]{:S(2)}, u32[]{:S(2)}) collective-permute-start(f32[2,16,1152]{2,1,0:T(8,128)S(1)} %get-tuple-element.43), channel_id=1, source_target_pairs={{0,1},{1,0},{2,3},{3,2},{4,5},{5,4},{6,7},{7,6},{8,9},{9,8},{10,11... | collective-permute-start | bytes 442376 | tf_op jit(solution)/shard_map/ppermute | solution.py:436
  16.6 1.2 %shard_map.114.smooth_ref = f32[16,1152]{1,0:T(8,128)S(1)} custom-call(f32[16,1152]{1,0:T(8,128)S(1)} %get-tuple-element.31.after_ref.own_ref, f32[90,128]{1,0:T(8,128)S(1)} %collective-permute-done.2.refs_0_.even_ref, f32[90,128]{1,0:T(8,128)S(1)} %collective-permute-done.3.refs_1_.odd_ref, f32[5,40,1152]{2,1,0:T(8,128)S(1)} %get-tuple-element.41.coef_ref), custom_call_target="tpu_custom_call" | custom-call | flops 16384000 | bytes 4096000 | tf_op jit(solution)/shard_map/pallas_call | solution.py:536
  17.8 0.0 collective-permute-done.8.more_ref
  17.9 1.4 %collective-permute-start.9 = (f32[90,128]{1,0:T(8,128)S(1)}, f32[90,128]{1,0:T(8,128)S(1)}, u32[]{:S(2)}, u32[]{:S(2)}) collective-permute-start(f32[90,128]{1,0:T(8,128)S(1)} %get-tuple-element.45), channel_id=1, source_target_pairs={{0,4},{4,0},{8,12},{12,8},{1,5},{5,1},{9,13},{13,9},{2,6},{6,2},{1... | collective-permute-start | bytes 138248 | tf_op jit(solution)/shard_map/ppermute | solution.py:436
  19.4 0.1 collective-permute-start.10
  19.5 2.6 %collective-permute-done.9.even_ref = f32[90,128]{1,0:T(8,128)S(1)} collective-permute-done((f32[90,128]{1,0:T(8,128)S(1)}, f32[90,128]{1,0:T(8,128)S(1)}, u32[]{:S(2)}, u32[]{:S(2)}) %collective-permute-start.9) | collective-permute-done | bytes 46112 | tf_op jit(solution)/shard_map/ppermute | solution.py:436
  22.1 1.2 %shard_map.116.refs_0_ = f32[16,1024]{1,0:T(8,128)S(1)} custom-call(f32[16,1152]{1,0:T(8,128)S(1)} %get-tuple-element.44.own_ref, f32[90,128]{1,0:T(8,128)S(1)} %collective-permute-done.9.even_ref, f32[90,128]{1,0:T(8,128)S(1)} %collective-permute-done.10.odd_ref, f32[5,40,1152]{2,1,0:T(8,128)S(1)} %get-tuple-element.41.coef_ref), custom_call_target="tpu_custom_call" | custom-call | flops 16384000 | bytes 4096000 | tf_op jit(solution)/shard_map/pallas_call | solution.py:547
  23.3 0.3 %collective-permute-start.13 = (f32[16,1024]{1,0:T(8,128)S(1)}, f32[16,1024]{1,0:T(8,128)S(1)}, u32[]{:S(2)}, u32[]{:S(2)}) collective-permute-start(f32[16,1024]{1,0:T(8,128)S(1)} %shard_map.116.refs_0_), channel_id=1, source_target_pairs={{0,2},{1,3},{2,0},{3,1},{4,6},{5,7},{6,4},{7,5},{8,10},{9,11},{10,... | collective-permute-start | bytes 196616 | tf_op jit(solution)/shard_map/ppermute | solution.py:436
  23.7 0.0 collective-permute-start.12
  23.7 1.8 %collective-permute-start.11 = (f32[16,1024]{1,0:T(8,128)S(1)}, f32[16,1024]{1,0:T(8,128)S(1)}, u32[]{:S(2)}, u32[]{:S(2)}) collective-permute-start(f32[16,1024]{1,0:T(8,128)S(1)} %shard_map.116.refs_0_), channel_id=1, source_target_pairs={{0,1},{1,0},{2,3},{3,2},{4,5},{5,4},{6,7},{7,6},{8,9},{9,8},{10,11... | collective-permute-start | bytes 196616 | tf_op jit(solution)/shard_map/ppermute | solution.py:436
  25.5 2.5 %collective-permute-done.13.refs_3_ = f32[16,1024]{1,0:T(8,128)S(1)} collective-permute-done((f32[16,1024]{1,0:T(8,128)S(1)}, f32[16,1024]{1,0:T(8,128)S(1)}, u32[]{:S(2)}, u32[]{:S(2)}) %collective-permute-start.13) | collective-permute-done | bytes 65568 | tf_op jit(solution)/shard_map/ppermute | solution.py:436
  28.1 0.0 collective-permute-done.12.refs_2_
  28.1 0.0 collective-permute-done.11.refs_1_
  28.1 0.8 %shard_map.117 = f32[2,16,2048]{2,1,0:T(8,128)} custom-call(f32[2,2,8,128]{3,2,1,0:T(8,128)S(1)} %get-tuple-element.26.response_ref, f32[2,16,2048]{2,1,0:T(8,128)S(1)} %copy-done, f32[16,1024]{1,0:T(8,128)S(1)} %shard_map.116.refs_0_, f32[16,1024]{1,0:T(8,128)S(1)} %collective-permute-done.11.refs_1_, f32[16,1024]{1,0:T(8,128)S(1)} %collective-permute-done.12.refs_2_, ...), custom_call_target="tpu_custom_call" | custom-call | flops 4096000 | bytes 1024000 | tf_op jit(solution)/shard_map/pallas_call | solution.py:555
  (9 shorter events, 0.1 us)
Async XLA Ops:
  1.6 3.2 %collective-permute-start = (f32[16,2048]{1,0:T(8,128)S(1)}, f32[16,2048]{1,0:T(8,128)S(1)}, u32[]{:S(2)}, u32[]{:S(2)}) collective-permute-start(f32[16,2048]{1,0:T(8,128)S(1)} %get-tuple-element.28), channel_id=1, source_target_pairs={{0,1},{1,0},{2,3},{3,2},{4,5},{5,4},{6,7},{7,6},{8,9},{9,8},{10,11... | collective-permute-start | bytes 393224 | tf_op jit(solution)/shard_map/ppermute | solution.py:436
  2.1 10.8 %collective-permute-start.7 = (f32[2,104,128]{2,1,0:T(8,128)S(1)}, f32[2,104,128]{2,1,0:T(8,128)S(1)}, u32[]{:S(2)}, u32[]{:S(2)}) collective-permute-start(f32[2,104,128]{2,1,0:T(8,128)S(1)} %get-tuple-element.38), channel_id=1, source_target_pairs={{0,4},{1,13},{2,6},{3,15},{4,0},{5,9},{6,2},{7,11},{8,12},{9,5},{1... | collective-permute-start | bytes 319496 | tf_op jit(solution)/shard_map/ppermute | solution.py:459
  4.8 5.4 %collective-permute-start.1 = (f32[16,1152]{1,0:T(8,128)S(1)}, f32[16,1152]{1,0:T(8,128)S(1)}, u32[]{:S(2)}, u32[]{:S(2)}) collective-permute-start(f32[16,1152]{1,0:T(8,128)S(1)} %get-tuple-element.30), channel_id=1, source_target_pairs={{0,2},{1,3},{2,0},{3,1},{4,6},{5,7},{6,4},{7,5},{8,10},{9,11},{10,... | collective-permute-start | bytes 221192 | tf_op jit(solution)/shard_map/ppermute | solution.py:436
  6.3 6.5 %collective-permute-start.6 = (f32[104,128]{1,0:T(8,128)S(1)}, f32[104,128]{1,0:T(8,128)S(1)}, u32[]{:S(2)}, u32[]{:S(2)}) collective-permute-start(f32[104,128]{1,0:T(8,128)S(1)} %get-tuple-element.37), channel_id=1, source_target_pairs={{0,8},{1,9},{2,10},{3,11},{4,12},{5,13},{6,14},{7,15},{8,0},{9,1},... | collective-permute-start | bytes 159752 | tf_op jit(solution)/shard_map/ppermute | solution.py:459
  8.9 6.9 %collective-permute-start.4 = (f32[2,90,128]{2,1,0:T(8,128)S(1)}, f32[2,90,128]{2,1,0:T(8,128)S(1)}, u32[]{:S(2)}, u32[]{:S(2)}) collective-permute-start(f32[2,90,128]{2,1,0:T(8,128)S(1)} %get-tuple-element.34), channel_id=1, source_target_pairs={{0,4},{4,0},{8,12},{12,8},{1,5},{5,1},{9,13},{13,9},{2,6},{6,2},{1... | collective-permute-start | bytes 276488 | tf_op jit(solution)/shard_map/ppermute | solution.py:436
  10.2 5.6 %collective-permute-start.5 = (f32[2,90,128]{2,1,0:T(8,128)S(1)}, f32[2,90,128]{2,1,0:T(8,128)S(1)}, u32[]{:S(2)}, u32[]{:S(2)}) collective-permute-start(f32[2,90,128]{2,1,0:T(8,128)S(1)} %get-tuple-element.35), channel_id=1, source_target_pairs={{0,1},{1,0},{2,3},{3,2},{4,8},{5,9},{6,10},{7,11},{8,4},{9,5},{10,... | collective-permute-start | bytes 276488 | tf_op jit(solution)/shard_map/ppermute | solution.py:447
  10.2 5.6 %collective-permute-start.2 = (f32[90,128]{1,0:T(8,128)S(1)}, f32[90,128]{1,0:T(8,128)S(1)}, u32[]{:S(2)}, u32[]{:S(2)}) collective-permute-start(f32[90,128]{1,0:T(8,128)S(1)} %get-tuple-element.32), channel_id=1, source_target_pairs={{0,4},{4,0},{8,12},{12,8},{1,5},{5,1},{9,13},{13,9},{2,6},{6,2},{1... | collective-permute-start | bytes 138248 | tf_op jit(solution)/shard_map/ppermute | solution.py:436
  12.8 3.0 %collective-permute-start.3 = (f32[90,128]{1,0:T(8,128)S(1)}, f32[90,128]{1,0:T(8,128)S(1)}, u32[]{:S(2)}, u32[]{:S(2)}) collective-permute-start(f32[90,128]{1,0:T(8,128)S(1)} %get-tuple-element.33), channel_id=1, source_target_pairs={{0,1},{1,0},{2,3},{3,2},{4,8},{5,9},{6,10},{7,11},{8,4},{9,5},{10,... | collective-permute-start | bytes 138248 | tf_op jit(solution)/shard_map/ppermute | solution.py:447
  16.1 1.8 %collective-permute-start.8 = (f32[2,16,1152]{2,1,0:T(8,128)S(1)}, f32[2,16,1152]{2,1,0:T(8,128)S(1)}, u32[]{:S(2)}, u32[]{:S(2)}) collective-permute-start(f32[2,16,1152]{2,1,0:T(8,128)S(1)} %get-tuple-element.43), channel_id=1, source_target_pairs={{0,1},{1,0},{2,3},{3,2},{4,5},{5,4},{6,7},{7,6},{8,9},{9,8},{10,11... | collective-permute-start | bytes 442376 | tf_op jit(solution)/shard_map/ppermute | solution.py:436
  16.6 1.3 %copy-start.1 = (s32[16,2048]{1,0:T(8,128)S(1)}, s32[16,2048]{1,0:T(8,128)}, u32[]{:S(2)}) copy-start(s32[16,2048]{1,0:T(8,128)} %mask_ref.1) | copy-start | bytes 393220
  17.9 4.2 %collective-permute-start.9 = (f32[90,128]{1,0:T(8,128)S(1)}, f32[90,128]{1,0:T(8,128)S(1)}, u32[]{:S(2)}, u32[]{:S(2)}) collective-permute-start(f32[90,128]{1,0:T(8,128)S(1)} %get-tuple-element.45), channel_id=1, source_target_pairs={{0,4},{4,0},{8,12},{12,8},{1,5},{5,1},{9,13},{13,9},{2,6},{6,2},{1... | collective-permute-start | bytes 138248 | tf_op jit(solution)/shard_map/ppermute | solution.py:436
  19.4 2.7 %collective-permute-start.10 = (f32[90,128]{1,0:T(8,128)S(1)}, f32[90,128]{1,0:T(8,128)S(1)}, u32[]{:S(2)}, u32[]{:S(2)}) collective-permute-start(f32[90,128]{1,0:T(8,128)S(1)} %get-tuple-element.46), channel_id=1, source_target_pairs={{0,1},{1,0},{2,3},{3,2},{4,8},{5,9},{6,10},{7,11},{8,4},{9,5},{10,... | collective-permute-start | bytes 138248 | tf_op jit(solution)/shard_map/ppermute | solution.py:447
  22.1 6.0 %copy-start = (f32[2,16,2048]{2,1,0:T(8,128)S(1)}, f32[2,16,2048]{2,1,0:T(8,128)}, u32[]{:S(2)}) copy-start(f32[2,16,2048]{2,1,0:T(8,128)} %control_ref.1) | copy-start | bytes 786436
  23.3 4.7 %collective-permute-start.13 = (f32[16,1024]{1,0:T(8,128)S(1)}, f32[16,1024]{1,0:T(8,128)S(1)}, u32[]{:S(2)}, u32[]{:S(2)}) collective-permute-start(f32[16,1024]{1,0:T(8,128)S(1)} %shard_map.116.refs_0_), channel_id=1, source_target_pairs={{0,2},{1,3},{2,0},{3,1},{4,6},{5,7},{6,4},{7,5},{8,10},{9,11},{10,... | collective-permute-start | bytes 196616 | tf_op jit(solution)/shard_map/ppermute | solution.py:436
  23.7 4.4 %collective-permute-start.12 = (f32[16,1024]{1,0:T(8,128)S(1)}, f32[16,1024]{1,0:T(8,128)S(1)}, u32[]{:S(2)}, u32[]{:S(2)}) collective-permute-start(f32[16,1024]{1,0:T(8,128)S(1)} %shard_map.116.refs_0_), channel_id=1, source_target_pairs={{0,3},{1,2},{2,1},{3,0},{4,7},{5,6},{6,5},{7,4},{8,11},{9,10},{10,... | collective-permute-start | bytes 196616 | tf_op jit(solution)/shard_map/ppermute | solution.py:436
  23.7 4.4 %collective-permute-start.11 = (f32[16,1024]{1,0:T(8,128)S(1)}, f32[16,1024]{1,0:T(8,128)S(1)}, u32[]{:S(2)}, u32[]{:S(2)}) collective-permute-start(f32[16,1024]{1,0:T(8,128)S(1)} %shard_map.116.refs_0_), channel_id=1, source_target_pairs={{0,1},{1,0},{2,3},{3,2},{4,5},{5,4},{6,7},{7,6},{8,9},{9,8},{10,11... | collective-permute-start | bytes 196616 | tf_op jit(solution)/shard_map/ppermute | solution.py:436

commit v8 on v7

--- a/solution.py
+++ b/solution.py
@@ -280,8 +280,8 @@
         out_ref[...] = first_ref[:, window] + second_ref[:, window]
 
 
-def edges_kernel(margin, *refs):
-    terms, (total_ref, even_ref, odd_ref) = refs[:-3], refs[-3:]
+def edges_kernel(margin, chips, *refs):
+    terms, (total_ref, even_ref, odd_ref) = refs[:chips], refs[-3:]
     total = terms[0][...]
     for term in terms[1:]:
         total = total + term[...]
@@ -510,8 +510,11 @@
     parts = [swap(p, "var", 2 * (d + 1)) for d, p in enumerate(parts)]
     kappa_even, kappa_odd = swap_edges(kappa_even, kappa_odd)
     smooth_in, even, odd = call(
-        functools.partial(edges_kernel, margin), [view, edge, edge], [VMEM] * chips, cost=cost(500)
-    )(part, *parts)
+        functools.partial(edges_kernel, margin, chips),
+        [view, edge, edge],
+        [VMEM] * chips + [AFTER] * len(got[:-2]),
+        cost=cost(500),
+    )(part, *parts, *got[:-2])
     even, odd = swap_edges(even, odd)
     sums, sums_other = call(
         functools.partial(scatter_kernel, slots, blocks),

time: 29.1 us -> 32 us (1.100)
  the two profiles are of different devices: /device:TPU:0 before, /device:TPU:13 now
where the time goes in v8:
time: 32 us; the launch traced here: 31.7 us
  starting transfers between devices  16.2 us (51%)
  waiting for transfers between devices  8.3 us (26%)
  Pallas kernels  7.08 us (22%)
    ppermute x9, starting transfers between devices, swap(): return lax.ppermute(values, axis, [(i, i ^ bit) for i in range(count)])  12.8 us
    ppermute x9, waiting for transfers between devices, swap(): return lax.ppermute(values, axis, [(i, i ^ bit) for i in range(count)])  4.62 us
    ppermute x3, waiting for transfers between devices, swap_edges(): return (swap(even, 'tile', 1), lax.ppermute(odd, ('tile', 'var'), pairs))  2.93 us
    ppermute x2, starting transfers between devices, deliver(): got.append(lax.ppermute(chunk, ('tile', 'var'), pairs))  2.41 us
    pallas_call x1, Pallas kernels, local(): call(functools.partial(scatter_kernel, slots, blocks), [view2, view2], [A...  1.93 us
    pallas_call x1, Pallas kernels, local(): call(functools.partial(first_kernel, slots, margin), [field, field, jax.S...  1.58 us
    pallas_call x1, Pallas kernels, local(): call(functools.partial(smooth_kernel, margin), [view], [VMEM] * 4, [ring]...  1.25 us
    pallas_call x1, Pallas kernels, local(): call(functools.partial(spread_kernel, margin), [share], [VMEM] * 4, [ring...  1.25 us
  transfers between devices with their start and end apart: 14, of which 6 were waited for; matrix products, arithmetic and copies ran while one was open for 0% of the time, Pallas kernels for 10%

profile of v8, /device:TPU:13, one launch (start us, length us, event | category | flops | bytes accessed | tf_op | source)
XLA Modules:
  0.0 31.7 jit_solution(7508685802933733759)
XLA Ops:
  0.0 1.6 %shard_map.109 = (f32[16,2048]{1,0:T(8,128)S(1)}, f32[16,2048]{1,0:T(8,128)S(1)}, f32[2,2,8,128]{3,2,1,0:T(8,128)S(1)}, f32[2,16,1152]{2,1,0:T(8,128)S(1)}, f32[...) custom-call(f32[2,8]{1,0:T(2,128)} %sens_hbm.1, ...), custom_call_target="tpu_custom_call" | custom-call | flops 12288000 | bytes 3072000 | tf_op jit(solution)/shard_map/pallas_call | solution.py:485
  1.6 0.7 %collective-permute-start = (f32[16,2048]{1,0:T(8,128)S(1)}, f32[16,2048]{1,0:T(8,128)S(1)}, u32[]{:S(2)}, u32[]{:S(2)}) collective-permute-start(f32[16,2048]{1,0:T(8,128)S(1)} %get-tuple-element.28), channel_id=1, source_target_pairs={{0,1},{1,0},{2,3},{3,2},{4,5},{5,4},{6,7},{7,6},{8,9},{9,8},{10,11... | collective-permute-start | bytes 393224 | tf_op jit(solution)/shard_map/ppermute | solution.py:436
  2.3 1.3 %collective-permute-start.2 = (f32[2,104,128]{2,1,0:T(8,128)S(1)}, f32[2,104,128]{2,1,0:T(8,128)S(1)}, u32[]{:S(2)}, u32[]{:S(2)}) collective-permute-start(f32[2,104,128]{2,1,0:T(8,128)S(1)} %get-tuple-element.31), channel_id=1, source_target_pairs={{0,4},{1,13},{2,6},{3,15},{4,0},{5,9},{6,2},{7,11},{8,12},{9,5},{1... | collective-permute-start | bytes 319496 | tf_op jit(solution)/shard_map/ppermute | solution.py:459
  3.6 0.0 collective-permute-done.second_ref
  3.7 1.3 %collective-permute-start.1 = (f32[16,1152]{1,0:T(8,128)S(1)}, f32[16,1152]{1,0:T(8,128)S(1)}, u32[]{:S(2)}, u32[]{:S(2)}) collective-permute-start(f32[16,1152]{1,0:T(8,128)S(1)} %get-tuple-element.30), channel_id=1, source_target_pairs={{0,2},{1,3},{2,0},{3,1},{4,6},{5,7},{6,4},{7,5},{8,10},{9,11},{10,... | collective-permute-start | bytes 221192 | tf_op jit(solution)/shard_map/ppermute | solution.py:436
  4.9 2.2 %collective-permute-start.5 = (f32[2,90,128]{2,1,0:T(8,128)S(1)}, f32[2,90,128]{2,1,0:T(8,128)S(1)}, u32[]{:S(2)}, u32[]{:S(2)}) collective-permute-start(f32[2,90,128]{2,1,0:T(8,128)S(1)} %get-tuple-element.35), channel_id=1, source_target_pairs={{0,4},{4,0},{8,12},{12,8},{1,5},{5,1},{9,13},{13,9},{2,6},{6,2},{1... | collective-permute-start | bytes 276488 | tf_op jit(solution)/shard_map/ppermute | solution.py:436
  7.1 0.1 collective-permute-start.6
  7.2 1.1 %collective-permute-start.7 = (f32[104,128]{1,0:T(8,128)S(1)}, f32[104,128]{1,0:T(8,128)S(1)}, u32[]{:S(2)}, u32[]{:S(2)}) collective-permute-start(f32[104,128]{1,0:T(8,128)S(1)} %get-tuple-element.38), channel_id=1, source_target_pairs={{0,8},{1,9},{2,10},{3,11},{4,12},{5,13},{6,14},{7,15},{8,0},{9,1},... | collective-permute-start | bytes 159752 | tf_op jit(solution)/shard_map/ppermute | solution.py:459
  8.3 0.0 collective-permute-done.2.refs_2_.refs_1_
  8.4 1.5 %collective-permute-start.3 = (f32[90,128]{1,0:T(8,128)S(1)}, f32[90,128]{1,0:T(8,128)S(1)}, u32[]{:S(2)}, u32[]{:S(2)}) collective-permute-start(f32[90,128]{1,0:T(8,128)S(1)} %get-tuple-element.33), channel_id=1, source_target_pairs={{0,4},{4,0},{8,12},{12,8},{1,5},{5,1},{9,13},{13,9},{2,6},{6,2},{1... | collective-permute-start | bytes 138248 | tf_op jit(solution)/shard_map/ppermute | solution.py:436
  9.9 0.6 %collective-permute-start.4 = (f32[90,128]{1,0:T(8,128)S(1)}, f32[90,128]{1,0:T(8,128)S(1)}, u32[]{:S(2)}, u32[]{:S(2)}) collective-permute-start(f32[90,128]{1,0:T(8,128)S(1)} %get-tuple-element.34), channel_id=1, source_target_pairs={{0,1},{1,0},{2,3},{3,2},{4,8},{5,9},{6,10},{7,11},{8,4},{9,5},{10,... | collective-permute-start | bytes 138248 | tf_op jit(solution)/shard_map/ppermute | solution.py:447
  10.5 0.7 %collective-permute-done.7.refs_0_ = f32[104,128]{1,0:T(8,128)S(1)} collective-permute-done((f32[104,128]{1,0:T(8,128)S(1)}, f32[104,128]{1,0:T(8,128)S(1)}, u32[]{:S(2)}, u32[]{:S(2)}) %collective-permute-start.7) | collective-permute-done | bytes 53280 | tf_op jit(solution)/shard_map/ppermute | solution.py:459
  11.2 1.9 %shard_map.112 = (f32[2,16,1152]{2,1,0:T(8,128)S(1)}, f32[2,16,1152]{2,1,0:T(8,128)S(1)}) custom-call(f32[16,1152]{1,0:T(8,128)S(1)} %get-tuple-element.32.after_ref.own_ref, f32[104,128]{1,0:T(8,128)S(1)} %collective-permute-done.7.refs_0_, f32[2,104,128]{2,1,0:T(8,128)S(1)} %collective-permute-done.2.refs_2_.refs_1_, f32[104,128]{1,0:T(8,128)S(1)} %get-tuple-element.39.refs_2_), custom_call_target="tpu_custom_call" | custom-call | flops 409600000 | bytes 102400000 | tf_op jit(solution)/shard_map/pallas_call | solution.py:519
  13.2 0.0 collective-permute-done.6.odd_ref
  13.2 0.1 collective-permute-done.3.refs_0_.even_ref
  13.3 1.5 %collective-permute-done.4.refs_1_.odd_ref = f32[90,128]{1,0:T(8,128)S(1)} collective-permute-done((f32[90,128]{1,0:T(8,128)S(1)}, f32[90,128]{1,0:T(8,128)S(1)}, u32[]{:S(2)}, u32[]{:S(2)}) %collective-permute-start.4) | collective-permute-done | bytes 46112 | tf_op jit(solution)/shard_map/ppermute | solution.py:447
  14.7 0.2 shard_map.113
  14.9 0.9 %collective-permute-start.8 = (f32[2,16,1152]{2,1,0:T(8,128)S(1)}, f32[2,16,1152]{2,1,0:T(8,128)S(1)}, u32[]{:S(2)}, u32[]{:S(2)}) collective-permute-start(f32[2,16,1152]{2,1,0:T(8,128)S(1)} %get-tuple-element.43), channel_id=1, source_target_pairs={{0,1},{1,0},{2,3},{3,2},{4,5},{5,4},{6,7},{7,6},{8,9},{9,8},{10,11... | collective-permute-start | bytes 442376 | tf_op jit(solution)/shard_map/ppermute | solution.py:436
  15.8 1.2 %shard_map.114.smooth_ref = f32[16,1152]{1,0:T(8,128)S(1)} custom-call(f32[16,1152]{1,0:T(8,128)S(1)} %get-tuple-element.32.after_ref.own_ref, f32[90,128]{1,0:T(8,128)S(1)} %collective-permute-done.3.refs_0_.even_ref, f32[90,128]{1,0:T(8,128)S(1)} %collective-permute-done.4.refs_1_.odd_ref, f32[5,40,1152]{2,1,0:T(8,128)S(1)} %get-tuple-element.41.coef_ref), custom_call_target="tpu_custom_call" | custom-call | flops 16384000 | bytes 4096000 | tf_op jit(solution)/shard_map/pallas_call | solution.py:539
  17.1 0.0 collective-permute-done.8.more_ref
  17.1 2.7 %collective-permute-start.9 = (f32[90,128]{1,0:T(8,128)S(1)}, f32[90,128]{1,0:T(8,128)S(1)}, u32[]{:S(2)}, u32[]{:S(2)}) collective-permute-start(f32[90,128]{1,0:T(8,128)S(1)} %get-tuple-element.45), channel_id=1, source_target_pairs={{0,4},{4,0},{8,12},{12,8},{1,5},{5,1},{9,13},{13,9},{2,6},{6,2},{1... | collective-permute-start | bytes 138248 | tf_op jit(solution)/shard_map/ppermute | solution.py:436
  19.9 0.3 collective-permute-start.10
  20.1 1.2 %collective-permute-done.9.even_ref = f32[90,128]{1,0:T(8,128)S(1)} collective-permute-done((f32[90,128]{1,0:T(8,128)S(1)}, f32[90,128]{1,0:T(8,128)S(1)}, u32[]{:S(2)}, u32[]{:S(2)}) %collective-permute-start.9) | collective-permute-done | bytes 46112 | tf_op jit(solution)/shard_map/ppermute | solution.py:436
  21.3 1.5 %collective-permute-done.10.odd_ref = f32[90,128]{1,0:T(8,128)S(1)} collective-permute-done((f32[90,128]{1,0:T(8,128)S(1)}, f32[90,128]{1,0:T(8,128)S(1)}, u32[]{:S(2)}, u32[]{:S(2)}) %collective-permute-start.10) | collective-permute-done | bytes 46112 | tf_op jit(solution)/shard_map/ppermute | solution.py:447
  22.8 1.2 %shard_map.116.refs_0_ = f32[16,1024]{1,0:T(8,128)S(1)} custom-call(f32[16,1152]{1,0:T(8,128)S(1)} %get-tuple-element.44.own_ref, f32[90,128]{1,0:T(8,128)S(1)} %collective-permute-done.9.even_ref, f32[90,128]{1,0:T(8,128)S(1)} %collective-permute-done.10.odd_ref, f32[5,40,1152]{2,1,0:T(8,128)S(1)} %get-tuple-element.41.coef_ref), custom_call_target="tpu_custom_call" | custom-call | flops 16384000 | bytes 4096000 | tf_op jit(solution)/shard_map/pallas_call | solution.py:550
  24.1 0.3 %collective-permute-start.13 = (f32[16,1024]{1,0:T(8,128)S(1)}, f32[16,1024]{1,0:T(8,128)S(1)}, u32[]{:S(2)}, u32[]{:S(2)}) collective-permute-start(f32[16,1024]{1,0:T(8,128)S(1)} %shard_map.116.refs_0_), channel_id=1, source_target_pairs={{0,2},{1,3},{2,0},{3,1},{4,6},{5,7},{6,4},{7,5},{8,10},{9,11},{10,... | collective-permute-start | bytes 196616 | tf_op jit(solution)/shard_map/ppermute | solution.py:436
  24.4 3.2 %collective-permute-start.12 = (f32[16,1024]{1,0:T(8,128)S(1)}, f32[16,1024]{1,0:T(8,128)S(1)}, u32[]{:S(2)}, u32[]{:S(2)}) collective-permute-start(f32[16,1024]{1,0:T(8,128)S(1)} %shard_map.116.refs_0_), channel_id=1, source_target_pairs={{0,3},{1,2},{2,1},{3,0},{4,7},{5,6},{6,5},{7,4},{8,11},{9,10},{10,... | collective-permute-start | bytes 196616 | tf_op jit(solution)/shard_map/ppermute | solution.py:436
  27.6 0.0 collective-permute-start.11
  27.6 0.0 collective-permute-done.13.refs_3_
  27.6 3.3 %collective-permute-done.12.refs_2_ = f32[16,1024]{1,0:T(8,128)S(1)} collective-permute-done((f32[16,1024]{1,0:T(8,128)S(1)}, f32[16,1024]{1,0:T(8,128)S(1)}, u32[]{:S(2)}, u32[]{:S(2)}) %collective-permute-start.12) | collective-permute-done | bytes 65568 | tf_op jit(solution)/shard_map/ppermute | solution.py:436
  30.9 0.0 collective-permute-done.11.refs_1_
  30.9 0.8 %shard_map.117 = f32[2,16,2048]{2,1,0:T(8,128)} custom-call(f32[2,2,8,128]{3,2,1,0:T(8,128)S(1)} %get-tuple-element.26.response_ref, f32[2,16,2048]{2,1,0:T(8,128)S(1)} %copy-done, f32[16,1024]{1,0:T(8,128)S(1)} %shard_map.116.refs_0_, f32[16,1024]{1,0:T(8,128)S(1)} %collective-permute-done.11.refs_1_, f32[16,1024]{1,0:T(8,128)S(1)} %collective-permute-done.12.refs_2_, ...), custom_call_target="tpu_custom_call" | custom-call | flops 4096000 | bytes 1024000 | tf_op jit(solution)/shard_map/pallas_call | solution.py:558
  (9 shorter events, 0.1 us)
Async XLA Ops:
  1.6 2.0 %collective-permute-start = (f32[16,2048]{1,0:T(8,128)S(1)}, f32[16,2048]{1,0:T(8,128)S(1)}, u32[]{:S(2)}, u32[]{:S(2)}) collective-permute-start(f32[16,2048]{1,0:T(8,128)S(1)} %get-tuple-element.28), channel_id=1, source_target_pairs={{0,1},{1,0},{2,3},{3,2},{4,5},{5,4},{6,7},{7,6},{8,9},{9,8},{10,11... | collective-permute-start | bytes 393224 | tf_op jit(solution)/shard_map/ppermute | solution.py:436
  2.3 6.0 %collective-permute-start.2 = (f32[2,104,128]{2,1,0:T(8,128)S(1)}, f32[2,104,128]{2,1,0:T(8,128)S(1)}, u32[]{:S(2)}, u32[]{:S(2)}) collective-permute-start(f32[2,104,128]{2,1,0:T(8,128)S(1)} %get-tuple-element.31), channel_id=1, source_target_pairs={{0,4},{1,13},{2,6},{3,15},{4,0},{5,9},{6,2},{7,11},{8,12},{9,5},{1... | collective-permute-start | bytes 319496 | tf_op jit(solution)/shard_map/ppermute | solution.py:459
  3.7 4.7 %collective-permute-start.1 = (f32[16,1152]{1,0:T(8,128)S(1)}, f32[16,1152]{1,0:T(8,128)S(1)}, u32[]{:S(2)}, u32[]{:S(2)}) collective-permute-start(f32[16,1152]{1,0:T(8,128)S(1)} %get-tuple-element.30), channel_id=1, source_target_pairs={{0,2},{1,3},{2,0},{3,1},{4,6},{5,7},{6,4},{7,5},{8,10},{9,11},{10,... | collective-permute-start | bytes 221192 | tf_op jit(solution)/shard_map/ppermute | solution.py:436
  4.9 8.2 %collective-permute-start.5 = (f32[2,90,128]{2,1,0:T(8,128)S(1)}, f32[2,90,128]{2,1,0:T(8,128)S(1)}, u32[]{:S(2)}, u32[]{:S(2)}) collective-permute-start(f32[2,90,128]{2,1,0:T(8,128)S(1)} %get-tuple-element.35), channel_id=1, source_target_pairs={{0,4},{4,0},{8,12},{12,8},{1,5},{5,1},{9,13},{13,9},{2,6},{6,2},{1... | collective-permute-start | bytes 276488 | tf_op jit(solution)/shard_map/ppermute | solution.py:436
  7.1 6.0 %collective-permute-start.6 = (f32[2,90,128]{2,1,0:T(8,128)S(1)}, f32[2,90,128]{2,1,0:T(8,128)S(1)}, u32[]{:S(2)}, u32[]{:S(2)}) collective-permute-start(f32[2,90,128]{2,1,0:T(8,128)S(1)} %get-tuple-element.36), channel_id=1, source_target_pairs={{0,1},{1,0},{2,3},{3,2},{4,8},{5,9},{6,10},{7,11},{8,4},{9,5},{10,... | collective-permute-start | bytes 276488 | tf_op jit(solution)/shard_map/ppermute | solution.py:447
  7.2 4.0 %collective-permute-start.7 = (f32[104,128]{1,0:T(8,128)S(1)}, f32[104,128]{1,0:T(8,128)S(1)}, u32[]{:S(2)}, u32[]{:S(2)}) collective-permute-start(f32[104,128]{1,0:T(8,128)S(1)} %get-tuple-element.38), channel_id=1, source_target_pairs={{0,8},{1,9},{2,10},{3,11},{4,12},{5,13},{6,14},{7,15},{8,0},{9,1},... | collective-permute-start | bytes 159752 | tf_op jit(solution)/shard_map/ppermute | solution.py:459
  8.4 4.9 %collective-permute-start.3 = (f32[90,128]{1,0:T(8,128)S(1)}, f32[90,128]{1,0:T(8,128)S(1)}, u32[]{:S(2)}, u32[]{:S(2)}) collective-permute-start(f32[90,128]{1,0:T(8,128)S(1)} %get-tuple-element.33), channel_id=1, source_target_pairs={{0,4},{4,0},{8,12},{12,8},{1,5},{5,1},{9,13},{13,9},{2,6},{6,2},{1... | collective-permute-start | bytes 138248 | tf_op jit(solution)/shard_map/ppermute | solution.py:436
  9.9 4.8 %collective-permute-start.4 = (f32[90,128]{1,0:T(8,128)S(1)}, f32[90,128]{1,0:T(8,128)S(1)}, u32[]{:S(2)}, u32[]{:S(2)}) collective-permute-start(f32[90,128]{1,0:T(8,128)S(1)} %get-tuple-element.34), channel_id=1, source_target_pairs={{0,1},{1,0},{2,3},{3,2},{4,8},{5,9},{6,10},{7,11},{8,4},{9,5},{10,... | collective-permute-start | bytes 138248 | tf_op jit(solution)/shard_map/ppermute | solution.py:447
  14.9 2.1 %collective-permute-start.8 = (f32[2,16,1152]{2,1,0:T(8,128)S(1)}, f32[2,16,1152]{2,1,0:T(8,128)S(1)}, u32[]{:S(2)}, u32[]{:S(2)}) collective-permute-start(f32[2,16,1152]{2,1,0:T(8,128)S(1)} %get-tuple-element.43), channel_id=1, source_target_pairs={{0,1},{1,0},{2,3},{3,2},{4,5},{5,4},{6,7},{7,6},{8,9},{9,8},{10,11... | collective-permute-start | bytes 442376 | tf_op jit(solution)/shard_map/ppermute | solution.py:436
  15.8 1.3 %copy-start.1 = (s32[16,2048]{1,0:T(8,128)S(1)}, s32[16,2048]{1,0:T(8,128)}, u32[]{:S(2)}) copy-start(s32[16,2048]{1,0:T(8,128)} %mask_ref.1) | copy-start | bytes 393220
  17.1 4.2 %collective-permute-start.9 = (f32[90,128]{1,0:T(8,128)S(1)}, f32[90,128]{1,0:T(8,128)S(1)}, u32[]{:S(2)}, u32[]{:S(2)}) collective-permute-start(f32[90,128]{1,0:T(8,128)S(1)} %get-tuple-element.45), channel_id=1, source_target_pairs={{0,4},{4,0},{8,12},{12,8},{1,5},{5,1},{9,13},{13,9},{2,6},{6,2},{1... | collective-permute-start | bytes 138248 | tf_op jit(solution)/shard_map/ppermute | solution.py:436
  19.9 2.9 %collective-permute-start.10 = (f32[90,128]{1,0:T(8,128)S(1)}, f32[90,128]{1,0:T(8,128)S(1)}, u32[]{:S(2)}, u32[]{:S(2)}) collective-permute-start(f32[90,128]{1,0:T(8,128)S(1)} %get-tuple-element.46), channel_id=1, source_target_pairs={{0,1},{1,0},{2,3},{3,2},{4,8},{5,9},{6,10},{7,11},{8,4},{9,5},{10,... | collective-permute-start | bytes 138248 | tf_op jit(solution)/shard_map/ppermute | solution.py:447
  22.8 8.1 %copy-start = (f32[2,16,2048]{2,1,0:T(8,128)S(1)}, f32[2,16,2048]{2,1,0:T(8,128)}, u32[]{:S(2)}) copy-start(f32[2,16,2048]{2,1,0:T(8,128)} %control_ref.1) | copy-start | bytes 786436
  24.1 3.5 %collective-permute-start.13 = (f32[16,1024]{1,0:T(8,128)S(1)}, f32[16,1024]{1,0:T(8,128)S(1)}, u32[]{:S(2)}, u32[]{:S(2)}) collective-permute-start(f32[16,1024]{1,0:T(8,128)S(1)} %shard_map.116.refs_0_), channel_id=1, source_target_pairs={{0,2},{1,3},{2,0},{3,1},{4,6},{5,7},{6,4},{7,5},{8,10},{9,11},{10,... | collective-permute-start | bytes 196616 | tf_op jit(solution)/shard_map/ppermute | solution.py:436
  24.4 6.5 %collective-permute-start.12 = (f32[16,1024]{1,0:T(8,128)S(1)}, f32[16,1024]{1,0:T(8,128)S(1)}, u32[]{:S(2)}, u32[]{:S(2)}) collective-permute-start(f32[16,1024]{1,0:T(8,128)S(1)} %shard_map.116.refs_0_), channel_id=1, source_target_pairs={{0,3},{1,2},{2,1},{3,0},{4,7},{5,6},{6,5},{7,4},{8,11},{9,10},{10,... | collective-permute-start | bytes 196616 | tf_op jit(solution)/shard_map/ppermute | solution.py:436
  27.6 3.3 %collective-permute-start.11 = (f32[16,1024]{1,0:T(8,128)S(1)}, f32[16,1024]{1,0:T(8,128)S(1)}, u32[]{:S(2)}, u32[]{:S(2)}) collective-permute-start(f32[16,1024]{1,0:T(8,128)S(1)} %shard_map.116.refs_0_), channel_id=1, source_target_pairs={{0,1},{1,0},{2,3},{3,2},{4,5},{5,4},{6,7},{7,6},{8,9},{9,8},{10,11... | collective-permute-start | bytes 196616 | tf_op jit(solution)/shard_map/ppermute | solution.py:436

commit v9 on v7

--- a/solution.py
+++ b/solution.py
@@ -107,7 +107,7 @@
 
     tiles = lax.axis_size("tile")
     full = tiles // 2 - 1
-    first = jnp.where(core == 0, 1, tiles // 2 + 1)
+    first = jnp.where(core == 0, 2, tiles // 2 + 1)
     panels = value_ref.shape[0]
     source = tile_ref[...] ^ mine
     names = lax.broadcasted_iota(jnp.int32, (-(-tiles // 8) * 8, panels), 0)
@@ -117,7 +117,7 @@
     parity, slot = rank % 2, rank // 2
     whole = (source >= first) & (source < first + full)
     home = source == 0
-    keep = whole | ((home | (source == tiles // 2)) & (parity == core))
+    keep = whole | ((home | (source == 1)) & (parity == core))
     half = jnp.where(whole, 2 * (source - first) + parity, jnp.where(home, tiles - 1, tiles - 2))
     place = jnp.where(keep, half * slots + slot, -1)
     spots = lax.broadcasted_iota(jnp.int32, (tiles * slots, panels), 0)
@@ -211,33 +211,38 @@
         column = jnp.concatenate([column] * (LANES // 16), axis=0)
         return left, jnp.where(lane_ids == column, one, zero)
 
-    def pair(s, g, carry):
+    def step(chosen, g, carry):
         base = pl.multiple_of(g * size_of_group, size_of_group)
-        loaded = [load(s + i, base) for i in (0, 1)]
+        loaded = {s: load(s, base) for s in chosen}
         for k in range(size_of_group):
-            hots = [one_hots(loaded[i], k) for i in (0, 1)]
-            left = jnp.concatenate(
-                [
-                    jnp.concatenate([hots[0][0], blank], axis=1),
-                    jnp.concatenate([blank, hots[1][0]], axis=1),
-                ],
-                axis=0,
-            )
-            both = lax.dot_general(
-                left, jnp.concatenate([hots[0][1], hots[1][1]], axis=1), (((1,), (1,)), ((), ())),
-                preferred_element_type=F32,
-            )
-            for i in (0, 1):
-                row = meta_ref[8 * (s + i), (s + i) * slots + base + k].astype(jnp.int32)
-                sensor = meta_ref[8 * (s + i) + 1, (s + i) * slots + base + k].astype(jnp.int32)
-                at = pl.multiple_of((sensor * rows + row) * tall, 8)
-                mine = both[2 * i * tall : 2 * (i + 1) * tall]
-                acc_ref[pl.ds(at, tall), :] += mine[:tall] + mine[tall:]
+            for pair in zip(chosen[::2], chosen[1::2]):
+                hots = [one_hots(loaded[s], k) for s in pair]
+                left = jnp.concatenate(
+                    [
+                        jnp.concatenate([hots[0][0], blank], axis=1),
+                        jnp.concatenate([blank, hots[1][0]], axis=1),
+                    ],
+                    axis=0,
+                )
+                both = lax.dot_general(
+                    left, jnp.concatenate([hots[0][1], hots[1][1]], axis=1), (((1,), (1,)), ((), ())),
+                    preferred_element_type=F32,
+                )
+                for i, s in enumerate(pair):
+                    row = meta_ref[8 * s, s * slots + base + k].astype(jnp.int32)
+                    sensor = meta_ref[8 * s + 1, s * slots + base + k].astype(jnp.int32)
+                    at = pl.multiple_of((sensor * rows + row) * tall, 8)
+                    mine = both[2 * i * tall : 2 * (i + 1) * tall]
+                    acc_ref[pl.ds(at, tall), :] += mine[:tall] + mine[tall:]
         return carry
 
-    for s in range(0, len(got_refs), 2):
-        most = jnp.maximum(meta_ref[8 * s + 2, s], meta_ref[8 * s + 10, s + 1]).astype(jnp.int32)
-        lax.fori_loop(0, (most + size_of_group - 1) // size_of_group, functools.partial(pair, s), 0)
+    for s in range(0, len(got_refs), 4):
+        chosen = list(range(s, s + 4))
+        most = meta_ref[8 * s + 2, s]
+        for other in chosen[1:]:
+            most = jnp.maximum(most, meta_ref[8 * other + 2, other])
+        turns = (most.astype(jnp.int32) + size_of_group - 1) // size_of_group
+        lax.fori_loop(0, turns, functools.partial(step, chosen), 0)
     for sensor, out_ref in ((core, own_ref), (1 - core, other_ref)):
         begin = sensor * rows * tall
         for kind in range(2):
@@ -454,7 +459,7 @@
         pairs = []
         for t in range(tiles):
             for q in range(members):
-                offset = tiles // 2 if turn == len(chunks) - 2 else 1 + turn + (q % 2) * (tiles // 2)
+                offset = 1 if turn == len(chunks) - 2 else 2 + turn + (q % 2) * (tiles // 2 - 1)
                 pairs.append((t * members + q, (t ^ offset) * members + q))
         got.append(lax.ppermute(chunk, ("tile", "var"), pairs))
     return got + [chunks[-1]]

time: 29.1 us -> 29.3 us (level)
  waiting for transfers between devices: 6.75 us -> 7.57 us
  Pallas kernels: 8.05 us -> 7.7 us
    ppermute x9, waiting for transfers between devices: 5.1 us -> 6.92 us  [swap(): return lax.ppermute(values, axis, [(i, i ^ bit) for i in range(count)])]
    ppermute x2, waiting for transfers between devices: 1.65 us -> 0.64 us  [deliver(): got.append(lax.ppermute(chunk, ('tile', 'var'), pairs))]
    ppermute x9, starting transfers between devices: 8.48 us -> 8 us  [swap(): return lax.ppermute(values, axis, [(i, i ^ bit) for i in range(count)])]
    pallas_call x1, Pallas kernels: 2.89 us -> 2.55 us  [local(): call(functools.partial(scatter_kernel, slots, blocks), [view2, view2], [A...]
  transfers between devices with their start and end apart: 14 -> 14, of which waited for: 3 -> 6; matrix products, arithmetic and copies ran while one was open for 0% -> 0% of each run, Pallas kernels for 14% -> 13%
where the time goes in v9:
time: 29.3 us; the launch traced here: 29.1 us
  starting transfers between devices  13.7 us (47%)
  Pallas kernels  7.7 us (26%)
  waiting for transfers between devices  7.57 us (26%)
    ppermute x9, starting transfers between devices, swap(): return lax.ppermute(values, axis, [(i, i ^ bit) for i in range(count)])  8 us
    ppermute x9, waiting for transfers between devices, swap(): return lax.ppermute(values, axis, [(i, i ^ bit) for i in range(count)])  6.92 us
    ppermute x2, starting transfers between devices, deliver(): got.append(lax.ppermute(chunk, ('tile', 'var'), pairs))  5.23 us
    pallas_call x1, Pallas kernels, local(): call(functools.partial(scatter_kernel, slots, blocks), [view2, view2], [A...  2.55 us
    pallas_call x1, Pallas kernels, local(): call(functools.partial(first_kernel, slots, margin), [field, field, jax.S...  1.58 us
    pallas_call x1, Pallas kernels, local(): call(functools.partial(spread_kernel, margin), [share], [VMEM] * 4, [ring...  1.25 us
    pallas_call x1, Pallas kernels, local(): call(functools.partial(smooth_kernel, margin), [view], [VMEM] * 4, [ring]...  1.25 us
    pallas_call x1, Pallas kernels, local(): call(result_kernel, [jax.ShapeDtypeStruct(control.shape, F32)], [VMEM] *...  0.78 us
  transfers between devices with their start and end apart: 14, of which 6 were waited for; matrix products, arithmetic and copies ran while one was open for 0% of the time, Pallas kernels for 13%

profile of v9, /device:TPU:0, one launch (start us, length us, event | category | flops | bytes accessed | tf_op | source)
XLA Modules:
  0.0 29.1 jit_solution(12243500954485964344)
XLA Ops:
  0.0 1.6 %shard_map.109 = (f32[16,2048]{1,0:T(8,128)S(1)}, f32[16,2048]{1,0:T(8,128)S(1)}, f32[2,2,8,128]{3,2,1,0:T(8,128)S(1)}, f32[2,16,1152]{2,1,0:T(8,128)S(1)}, f32[...) custom-call(f32[2,8]{1,0:T(2,128)} %sens_hbm.1, ...), custom_call_target="tpu_custom_call" | custom-call | flops 12288000 | bytes 3072000 | tf_op jit(solution)/shard_map/pallas_call | solution.py:490
  1.6 0.5 %collective-permute-start = (f32[16,2048]{1,0:T(8,128)S(1)}, f32[16,2048]{1,0:T(8,128)S(1)}, u32[]{:S(2)}, u32[]{:S(2)}) collective-permute-start(f32[16,2048]{1,0:T(8,128)S(1)} %get-tuple-element.28), channel_id=1, source_target_pairs={{0,1},{1,0},{2,3},{3,2},{4,5},{5,4},{6,7},{7,6},{8,9},{9,8},{10,11... | collective-permute-start | bytes 393224 | tf_op jit(solution)/shard_map/ppermute | solution.py:441
  2.1 3.7 %collective-permute-start.7 = (f32[2,104,128]{2,1,0:T(8,128)S(1)}, f32[2,104,128]{2,1,0:T(8,128)S(1)}, u32[]{:S(2)}, u32[]{:S(2)}) collective-permute-start(f32[2,104,128]{2,1,0:T(8,128)S(1)} %get-tuple-element.38), channel_id=1, source_target_pairs={{0,8},{1,13},{2,10},{3,15},{4,12},{5,9},{6,14},{7,11},{8,0},{9,5},... | collective-permute-start | bytes 319496 | tf_op jit(solution)/shard_map/ppermute | solution.py:464
  5.8 0.0 collective-permute-done.second_ref
  5.8 1.6 %collective-permute-start.1 = (f32[16,1152]{1,0:T(8,128)S(1)}, f32[16,1152]{1,0:T(8,128)S(1)}, u32[]{:S(2)}, u32[]{:S(2)}) collective-permute-start(f32[16,1152]{1,0:T(8,128)S(1)} %get-tuple-element.30), channel_id=1, source_target_pairs={{0,2},{1,3},{2,0},{3,1},{4,6},{5,7},{6,4},{7,5},{8,10},{9,11},{10,... | collective-permute-start | bytes 221192 | tf_op jit(solution)/shard_map/ppermute | solution.py:441
  7.4 1.6 %collective-permute-start.6 = (f32[104,128]{1,0:T(8,128)S(1)}, f32[104,128]{1,0:T(8,128)S(1)}, u32[]{:S(2)}, u32[]{:S(2)}) collective-permute-start(f32[104,128]{1,0:T(8,128)S(1)} %get-tuple-element.37), channel_id=1, source_target_pairs={{0,4},{1,5},{2,6},{3,7},{4,0},{5,1},{6,2},{7,3},{8,12},{9,13},{10,... | collective-permute-start | bytes 159752 | tf_op jit(solution)/shard_map/ppermute | solution.py:464
  8.9 0.4 %collective-permute-start.4 = (f32[2,90,128]{2,1,0:T(8,128)S(1)}, f32[2,90,128]{2,1,0:T(8,128)S(1)}, u32[]{:S(2)}, u32[]{:S(2)}) collective-permute-start(f32[2,90,128]{2,1,0:T(8,128)S(1)} %get-tuple-element.34), channel_id=1, source_target_pairs={{0,4},{4,0},{8,12},{12,8},{1,5},{5,1},{9,13},{13,9},{2,6},{6,2},{1... | collective-permute-start | bytes 276488 | tf_op jit(solution)/shard_map/ppermute | solution.py:441
  9.4 0.3 %collective-permute-start.5 = (f32[2,90,128]{2,1,0:T(8,128)S(1)}, f32[2,90,128]{2,1,0:T(8,128)S(1)}, u32[]{:S(2)}, u32[]{:S(2)}) collective-permute-start(f32[2,90,128]{2,1,0:T(8,128)S(1)} %get-tuple-element.35), channel_id=1, source_target_pairs={{0,1},{1,0},{2,3},{3,2},{4,8},{5,9},{6,10},{7,11},{8,4},{9,5},{10,... | collective-permute-start | bytes 276488 | tf_op jit(solution)/shard_map/ppermute | solution.py:452
  9.7 1.1 %collective-permute-done.1.refs_1_ = f32[16,1152]{1,0:T(8,128)S(1)} collective-permute-done((f32[16,1152]{1,0:T(8,128)S(1)}, f32[16,1152]{1,0:T(8,128)S(1)}, u32[]{:S(2)}, u32[]{:S(2)}) %collective-permute-start.1) | collective-permute-done | bytes 73760 | tf_op jit(solution)/shard_map/ppermute | solution.py:441
  10.8 1.1 %collective-permute-start.2 = (f32[90,128]{1,0:T(8,128)S(1)}, f32[90,128]{1,0:T(8,128)S(1)}, u32[]{:S(2)}, u32[]{:S(2)}) collective-permute-start(f32[90,128]{1,0:T(8,128)S(1)} %get-tuple-element.32), channel_id=1, source_target_pairs={{0,4},{4,0},{8,12},{12,8},{1,5},{5,1},{9,13},{13,9},{2,6},{6,2},{1... | collective-permute-start | bytes 138248 | tf_op jit(solution)/shard_map/ppermute | solution.py:441
  11.9 0.6 %collective-permute-done.6.refs_0_ = f32[104,128]{1,0:T(8,128)S(1)} collective-permute-done((f32[104,128]{1,0:T(8,128)S(1)}, f32[104,128]{1,0:T(8,128)S(1)}, u32[]{:S(2)}, u32[]{:S(2)}) %collective-permute-start.6) | collective-permute-done | bytes 53280 | tf_op jit(solution)/shard_map/ppermute | solution.py:464
  12.5 0.0 collective-permute-start.3
  12.6 0.0 collective-permute-done.7.refs_1_
  12.6 2.6 %shard_map.112 = (f32[2,16,1152]{2,1,0:T(8,128)S(1)}, f32[2,16,1152]{2,1,0:T(8,128)S(1)}) custom-call(f32[16,1152]{1,0:T(8,128)S(1)} %get-tuple-element.31.after_ref.own_ref, f32[104,128]{1,0:T(8,128)S(1)} %collective-permute-done.6.refs_0_, f32[2,104,128]{2,1,0:T(8,128)S(1)} %collective-permute-done.7.refs_1_, f32[104,128]{1,0:T(8,128)S(1)} %get-tuple-element.39.refs_2_), custom_call_target="tpu_custom_call" | custom-call | flops 409600000 | bytes 102400000 | tf_op jit(solution)/shard_map/pallas_call | solution.py:521
  15.1 0.0 collective-permute-done.4.even_ref
  15.1 0.0 collective-permute-done.5.odd_ref
  15.2 0.5 %collective-permute-done.2.refs_0_.even_ref = f32[90,128]{1,0:T(8,128)S(1)} collective-permute-done((f32[90,128]{1,0:T(8,128)S(1)}, f32[90,128]{1,0:T(8,128)S(1)}, u32[]{:S(2)}, u32[]{:S(2)}) %collective-permute-start.2) | collective-permute-done | bytes 46112 | tf_op jit(solution)/shard_map/ppermute | solution.py:441
  15.7 0.2 shard_map.113
  15.9 0.1 collective-permute-start.8
  16.0 1.2 %shard_map.114.smooth_ref = f32[16,1152]{1,0:T(8,128)S(1)} custom-call(f32[16,1152]{1,0:T(8,128)S(1)} %get-tuple-element.31.after_ref.own_ref, f32[90,128]{1,0:T(8,128)S(1)} %collective-permute-done.2.refs_0_.even_ref, f32[90,128]{1,0:T(8,128)S(1)} %collective-permute-done.3.refs_1_.odd_ref, f32[5,40,1152]{2,1,0:T(8,128)S(1)} %get-tuple-element.41.coef_ref), custom_call_target="tpu_custom_call" | custom-call | flops 16384000 | bytes 4096000 | tf_op jit(solution)/shard_map/pallas_call | solution.py:541
  17.3 0.0 collective-permute-done.8.more_ref
  17.4 2.0 %collective-permute-start.9 = (f32[90,128]{1,0:T(8,128)S(1)}, f32[90,128]{1,0:T(8,128)S(1)}, u32[]{:S(2)}, u32[]{:S(2)}) collective-permute-start(f32[90,128]{1,0:T(8,128)S(1)} %get-tuple-element.45), channel_id=1, source_target_pairs={{0,4},{4,0},{8,12},{12,8},{1,5},{5,1},{9,13},{13,9},{2,6},{6,2},{1... | collective-permute-start | bytes 138248 | tf_op jit(solution)/shard_map/ppermute | solution.py:441
  19.4 0.1 collective-permute-start.10
  19.6 2.2 %collective-permute-done.9.even_ref = f32[90,128]{1,0:T(8,128)S(1)} collective-permute-done((f32[90,128]{1,0:T(8,128)S(1)}, f32[90,128]{1,0:T(8,128)S(1)}, u32[]{:S(2)}, u32[]{:S(2)}) %collective-permute-start.9) | collective-permute-done | bytes 46112 | tf_op jit(solution)/shard_map/ppermute | solution.py:441
  21.7 0.0 collective-permute-done.10.odd_ref
  21.7 1.2 %shard_map.116.refs_0_ = f32[16,1024]{1,0:T(8,128)S(1)} custom-call(f32[16,1152]{1,0:T(8,128)S(1)} %get-tuple-element.44.own_ref, f32[90,128]{1,0:T(8,128)S(1)} %collective-permute-done.9.even_ref, f32[90,128]{1,0:T(8,128)S(1)} %collective-permute-done.10.odd_ref, f32[5,40,1152]{2,1,0:T(8,128)S(1)} %get-tuple-element.41.coef_ref), custom_call_target="tpu_custom_call" | custom-call | flops 16384000 | bytes 4096000 | tf_op jit(solution)/shard_map/pallas_call | solution.py:552
  23.0 0.9 %collective-permute-start.13 = (f32[16,1024]{1,0:T(8,128)S(1)}, f32[16,1024]{1,0:T(8,128)S(1)}, u32[]{:S(2)}, u32[]{:S(2)}) collective-permute-start(f32[16,1024]{1,0:T(8,128)S(1)} %shard_map.116.refs_0_), channel_id=1, source_target_pairs={{0,2},{1,3},{2,0},{3,1},{4,6},{5,7},{6,4},{7,5},{8,10},{9,11},{10,... | collective-permute-start | bytes 196616 | tf_op jit(solution)/shard_map/ppermute | solution.py:441
  23.9 0.3 collective-permute-start.12
  24.2 1.0 %collective-permute-start.11 = (f32[16,1024]{1,0:T(8,128)S(1)}, f32[16,1024]{1,0:T(8,128)S(1)}, u32[]{:S(2)}, u32[]{:S(2)}) collective-permute-start(f32[16,1024]{1,0:T(8,128)S(1)} %shard_map.116.refs_0_), channel_id=1, source_target_pairs={{0,1},{1,0},{2,3},{3,2},{4,5},{5,4},{6,7},{7,6},{8,9},{9,8},{10,11... | collective-permute-start | bytes 196616 | tf_op jit(solution)/shard_map/ppermute | solution.py:441
  25.2 2.5 %collective-permute-done.13.refs_3_ = f32[16,1024]{1,0:T(8,128)S(1)} collective-permute-done((f32[16,1024]{1,0:T(8,128)S(1)}, f32[16,1024]{1,0:T(8,128)S(1)}, u32[]{:S(2)}, u32[]{:S(2)}) %collective-permute-start.13) | collective-permute-done | bytes 65568 | tf_op jit(solution)/shard_map/ppermute | solution.py:441
  27.8 0.6 %collective-permute-done.12.refs_2_ = f32[16,1024]{1,0:T(8,128)S(1)} collective-permute-done((f32[16,1024]{1,0:T(8,128)S(1)}, f32[16,1024]{1,0:T(8,128)S(1)}, u32[]{:S(2)}, u32[]{:S(2)}) %collective-permute-start.12) | collective-permute-done | bytes 65568 | tf_op jit(solution)/shard_map/ppermute | solution.py:441
  28.3 0.8 %shard_map.117 = f32[2,16,2048]{2,1,0:T(8,128)} custom-call(f32[2,2,8,128]{3,2,1,0:T(8,128)S(1)} %get-tuple-element.26.response_ref, f32[2,16,2048]{2,1,0:T(8,128)S(1)} %copy-done, f32[16,1024]{1,0:T(8,128)S(1)} %shard_map.116.refs_0_, f32[16,1024]{1,0:T(8,128)S(1)} %collective-permute-done.11.refs_1_, f32[16,1024]{1,0:T(8,128)S(1)} %collective-permute-done.12.refs_2_, ...), custom_call_target="tpu_custom_call" | custom-call | flops 4096000 | bytes 1024000 | tf_op jit(solution)/shard_map/pallas_call | solution.py:560
  (9 shorter events, 0.1 us)
Async XLA Ops:
  1.6 4.2 %collective-permute-start = (f32[16,2048]{1,0:T(8,128)S(1)}, f32[16,2048]{1,0:T(8,128)S(1)}, u32[]{:S(2)}, u32[]{:S(2)}) collective-permute-start(f32[16,2048]{1,0:T(8,128)S(1)} %get-tuple-element.28), channel_id=1, source_target_pairs={{0,1},{1,0},{2,3},{3,2},{4,5},{5,4},{6,7},{7,6},{8,9},{9,8},{10,11... | collective-permute-start | bytes 393224 | tf_op jit(solution)/shard_map/ppermute | solution.py:441
  2.1 10.5 %collective-permute-start.7 = (f32[2,104,128]{2,1,0:T(8,128)S(1)}, f32[2,104,128]{2,1,0:T(8,128)S(1)}, u32[]{:S(2)}, u32[]{:S(2)}) collective-permute-start(f32[2,104,128]{2,1,0:T(8,128)S(1)} %get-tuple-element.38), channel_id=1, source_target_pairs={{0,8},{1,13},{2,10},{3,15},{4,12},{5,9},{6,14},{7,11},{8,0},{9,5},... | collective-permute-start | bytes 319496 | tf_op jit(solution)/shard_map/ppermute | solution.py:464
  5.8 5.0 %collective-permute-start.1 = (f32[16,1152]{1,0:T(8,128)S(1)}, f32[16,1152]{1,0:T(8,128)S(1)}, u32[]{:S(2)}, u32[]{:S(2)}) collective-permute-start(f32[16,1152]{1,0:T(8,128)S(1)} %get-tuple-element.30), channel_id=1, source_target_pairs={{0,2},{1,3},{2,0},{3,1},{4,6},{5,7},{6,4},{7,5},{8,10},{9,11},{10,... | collective-permute-start | bytes 221192 | tf_op jit(solution)/shard_map/ppermute | solution.py:441
  7.4 5.2 %collective-permute-start.6 = (f32[104,128]{1,0:T(8,128)S(1)}, f32[104,128]{1,0:T(8,128)S(1)}, u32[]{:S(2)}, u32[]{:S(2)}) collective-permute-start(f32[104,128]{1,0:T(8,128)S(1)} %get-tuple-element.37), channel_id=1, source_target_pairs={{0,4},{1,5},{2,6},{3,7},{4,0},{5,1},{6,2},{7,3},{8,12},{9,13},{10,... | collective-permute-start | bytes 159752 | tf_op jit(solution)/shard_map/ppermute | solution.py:464
  8.9 6.2 %collective-permute-start.4 = (f32[2,90,128]{2,1,0:T(8,128)S(1)}, f32[2,90,128]{2,1,0:T(8,128)S(1)}, u32[]{:S(2)}, u32[]{:S(2)}) collective-permute-start(f32[2,90,128]{2,1,0:T(8,128)S(1)} %get-tuple-element.34), channel_id=1, source_target_pairs={{0,4},{4,0},{8,12},{12,8},{1,5},{5,1},{9,13},{13,9},{2,6},{6,2},{1... | collective-permute-start | bytes 276488 | tf_op jit(solution)/shard_map/ppermute | solution.py:441
  9.4 5.8 %collective-permute-start.5 = (f32[2,90,128]{2,1,0:T(8,128)S(1)}, f32[2,90,128]{2,1,0:T(8,128)S(1)}, u32[]{:S(2)}, u32[]{:S(2)}) collective-permute-start(f32[2,90,128]{2,1,0:T(8,128)S(1)} %get-tuple-element.35), channel_id=1, source_target_pairs={{0,1},{1,0},{2,3},{3,2},{4,8},{5,9},{6,10},{7,11},{8,4},{9,5},{10,... | collective-permute-start | bytes 276488 | tf_op jit(solution)/shard_map/ppermute | solution.py:452
  10.8 4.8 %collective-permute-start.2 = (f32[90,128]{1,0:T(8,128)S(1)}, f32[90,128]{1,0:T(8,128)S(1)}, u32[]{:S(2)}, u32[]{:S(2)}) collective-permute-start(f32[90,128]{1,0:T(8,128)S(1)} %get-tuple-element.32), channel_id=1, source_target_pairs={{0,4},{4,0},{8,12},{12,8},{1,5},{5,1},{9,13},{13,9},{2,6},{6,2},{1... | collective-permute-start | bytes 138248 | tf_op jit(solution)/shard_map/ppermute | solution.py:441
  12.5 3.1 %collective-permute-start.3 = (f32[90,128]{1,0:T(8,128)S(1)}, f32[90,128]{1,0:T(8,128)S(1)}, u32[]{:S(2)}, u32[]{:S(2)}) collective-permute-start(f32[90,128]{1,0:T(8,128)S(1)} %get-tuple-element.33), channel_id=1, source_target_pairs={{0,1},{1,0},{2,3},{3,2},{4,8},{5,9},{6,10},{7,11},{8,4},{9,5},{10,... | collective-permute-start | bytes 138248 | tf_op jit(solution)/shard_map/ppermute | solution.py:452
  15.9 1.4 %collective-permute-start.8 = (f32[2,16,1152]{2,1,0:T(8,128)S(1)}, f32[2,16,1152]{2,1,0:T(8,128)S(1)}, u32[]{:S(2)}, u32[]{:S(2)}) collective-permute-start(f32[2,16,1152]{2,1,0:T(8,128)S(1)} %get-tuple-element.43), channel_id=1, source_target_pairs={{0,1},{1,0},{2,3},{3,2},{4,5},{5,4},{6,7},{7,6},{8,9},{9,8},{10,11... | collective-permute-start | bytes 442376 | tf_op jit(solution)/shard_map/ppermute | solution.py:441
  16.0 1.3 %copy-start.1 = (s32[16,2048]{1,0:T(8,128)S(1)}, s32[16,2048]{1,0:T(8,128)}, u32[]{:S(2)}) copy-start(s32[16,2048]{1,0:T(8,128)} %mask_ref.1) | copy-start | bytes 393220
  17.4 4.4 %collective-permute-start.9 = (f32[90,128]{1,0:T(8,128)S(1)}, f32[90,128]{1,0:T(8,128)S(1)}, u32[]{:S(2)}, u32[]{:S(2)}) collective-permute-start(f32[90,128]{1,0:T(8,128)S(1)} %get-tuple-element.45), channel_id=1, source_target_pairs={{0,4},{4,0},{8,12},{12,8},{1,5},{5,1},{9,13},{13,9},{2,6},{6,2},{1... | collective-permute-start | bytes 138248 | tf_op jit(solution)/shard_map/ppermute | solution.py:441
  19.4 2.3 %collective-permute-start.10 = (f32[90,128]{1,0:T(8,128)S(1)}, f32[90,128]{1,0:T(8,128)S(1)}, u32[]{:S(2)}, u32[]{:S(2)}) collective-permute-start(f32[90,128]{1,0:T(8,128)S(1)} %get-tuple-element.46), channel_id=1, source_target_pairs={{0,1},{1,0},{2,3},{3,2},{4,8},{5,9},{6,10},{7,11},{8,4},{9,5},{10,... | collective-permute-start | bytes 138248 | tf_op jit(solution)/shard_map/ppermute | solution.py:452
  21.7 6.6 %copy-start = (f32[2,16,2048]{2,1,0:T(8,128)S(1)}, f32[2,16,2048]{2,1,0:T(8,128)}, u32[]{:S(2)}) copy-start(f32[2,16,2048]{2,1,0:T(8,128)} %control_ref.1) | copy-start | bytes 786436
  23.0 4.8 %collective-permute-start.13 = (f32[16,1024]{1,0:T(8,128)S(1)}, f32[16,1024]{1,0:T(8,128)S(1)}, u32[]{:S(2)}, u32[]{:S(2)}) collective-permute-start(f32[16,1024]{1,0:T(8,128)S(1)} %shard_map.116.refs_0_), channel_id=1, source_target_pairs={{0,2},{1,3},{2,0},{3,1},{4,6},{5,7},{6,4},{7,5},{8,10},{9,11},{10,... | collective-permute-start | bytes 196616 | tf_op jit(solution)/shard_map/ppermute | solution.py:441
  23.9 4.4 %collective-permute-start.12 = (f32[16,1024]{1,0:T(8,128)S(1)}, f32[16,1024]{1,0:T(8,128)S(1)}, u32[]{:S(2)}, u32[]{:S(2)}) collective-permute-start(f32[16,1024]{1,0:T(8,128)S(1)} %shard_map.116.refs_0_), channel_id=1, source_target_pairs={{0,3},{1,2},{2,1},{3,0},{4,7},{5,6},{6,5},{7,4},{8,11},{9,10},{10,... | collective-permute-start | bytes 196616 | tf_op jit(solution)/shard_map/ppermute | solution.py:441
  24.2 4.1 %collective-permute-start.11 = (f32[16,1024]{1,0:T(8,128)S(1)}, f32[16,1024]{1,0:T(8,128)S(1)}, u32[]{:S(2)}, u32[]{:S(2)}) collective-permute-start(f32[16,1024]{1,0:T(8,128)S(1)} %shard_map.116.refs_0_), channel_id=1, source_target_pairs={{0,1},{1,0},{2,3},{3,2},{4,5},{5,4},{6,7},{7,6},{8,9},{9,8},{10,11... | collective-permute-start | bytes 196616 | tf_op jit(solution)/shard_map/ppermute | solution.py:441

commit v10 on v9

--- a/solution.py
+++ b/solution.py
@@ -515,7 +515,10 @@
     parts = [swap(p, "var", 2 * (d + 1)) for d, p in enumerate(parts)]
     kappa_even, kappa_odd = swap_edges(kappa_even, kappa_odd)
     smooth_in, even, odd = call(
-        functools.partial(edges_kernel, margin), [view, edge, edge], [VMEM] * chips, cost=cost(500)
+        functools.partial(edges_kernel, margin),
+        [view, edge, edge],
+        [VMEM] * chips,
+        cost=cost(150000),
     )(part, *parts)
     even, odd = swap_edges(even, odd)
     sums, sums_other = call(

time: 29.3 us -> 31.3 us (1.068)
  waiting for transfers between devices: 7.57 us -> 9.17 us
  starting transfers between devices: 13.7 us -> 14.7 us
  Pallas kernels: 7.7 us -> 6.9 us
    ppermute x9, starting transfers between devices: 8 us -> 10.4 us  [swap(): return lax.ppermute(values, axis, [(i, i ^ bit) for i in range(count)])]
    ppermute x2, waiting for transfers between devices: 0.64 us -> 2.32 us  [deliver(): got.append(lax.ppermute(chunk, ('tile', 'var'), pairs))]
    ppermute x2, starting transfers between devices: 5.23 us -> 4.16 us  [deliver(): got.append(lax.ppermute(chunk, ('tile', 'var'), pairs))]
    pallas_call x1, Pallas kernels: 2.55 us -> 1.75 us  [local(): call(functools.partial(scatter_kernel, slots, blocks), [view2, view2], [A...]
    ppermute x3, starting transfers between devices: 0.51 us -> 0.19 us  [swap_edges(): return (swap(even, 'tile', 1), lax.ppermute(odd, ('tile', 'var'), pairs))]
  transfers between devices with their start and end apart: 14 -> 14, of which waited for: 6 -> 7; matrix products, arithmetic and copies ran while one was open for 0% -> 0% of each run, Pallas kernels for 13% -> 10%
where the time goes in v10:
time: 31.3 us; the launch traced here: 30.9 us
  starting transfers between devices  14.7 us (47%)
  waiting for transfers between devices  9.17 us (29%)
  Pallas kernels  6.9 us (22%)
    ppermute x9, starting transfers between devices, swap(): return lax.ppermute(values, axis, [(i, i ^ bit) for i in range(count)])  10.4 us
    ppermute x9, waiting for transfers between devices, swap(): return lax.ppermute(values, axis, [(i, i ^ bit) for i in range(count)])  6.84 us
    ppermute x2, starting transfers between devices, deliver(): got.append(lax.ppermute(chunk, ('tile', 'var'), pairs))  4.16 us
    ppermute x2, waiting for transfers between devices, deliver(): got.append(lax.ppermute(chunk, ('tile', 'var'), pairs))  2.32 us
    pallas_call x1, Pallas kernels, local(): call(functools.partial(scatter_kernel, slots, blocks), [view2, view2], [A...  1.75 us
    pallas_call x1, Pallas kernels, local(): call(functools.partial(first_kernel, slots, margin), [field, field, jax.S...  1.58 us
    pallas_call x1, Pallas kernels, local(): call(functools.partial(smooth_kernel, margin), [view], [VMEM] * 4, [ring]...  1.25 us
    pallas_call x1, Pallas kernels, local(): call(functools.partial(spread_kernel, margin), [share], [VMEM] * 4, [ring...  1.25 us
  transfers between devices with their start and end apart: 14, of which 7 were waited for; matrix products, arithmetic and copies ran while one was open for 0% of the time, Pallas kernels for 10%

profile of v10, /device:TPU:0, one launch (start us, length us, event | category | flops | bytes accessed | tf_op | source)
XLA Modules:
  0.0 30.9 jit_solution(3003212829117383785)
XLA Ops:
  0.0 1.6 %shard_map.109 = (f32[16,2048]{1,0:T(8,128)S(1)}, f32[16,2048]{1,0:T(8,128)S(1)}, f32[2,2,8,128]{3,2,1,0:T(8,128)S(1)}, f32[2,16,1152]{2,1,0:T(8,128)S(1)}, f32[...) custom-call(f32[2,8]{1,0:T(2,128)} %sens_hbm.1, ...), custom_call_target="tpu_custom_call" | custom-call | flops 12288000 | bytes 3072000 | tf_op jit(solution)/shard_map/pallas_call | solution.py:490
  1.6 0.5 %collective-permute-start = (f32[16,2048]{1,0:T(8,128)S(1)}, f32[16,2048]{1,0:T(8,128)S(1)}, u32[]{:S(2)}, u32[]{:S(2)}) collective-permute-start(f32[16,2048]{1,0:T(8,128)S(1)} %get-tuple-element.28), channel_id=1, source_target_pairs={{0,1},{1,0},{2,3},{3,2},{4,5},{5,4},{6,7},{7,6},{8,9},{9,8},{10,11... | collective-permute-start | bytes 393224 | tf_op jit(solution)/shard_map/ppermute | solution.py:441
  2.1 1.0 %collective-permute-done.second_ref = f32[16,2048]{1,0:T(8,128)S(1)} collective-permute-done((f32[16,2048]{1,0:T(8,128)S(1)}, f32[16,2048]{1,0:T(8,128)S(1)}, u32[]{:S(2)}, u32[]{:S(2)}) %collective-permute-start) | collective-permute-done | bytes 131104 | tf_op jit(solution)/shard_map/ppermute | solution.py:441
  3.1 2.9 %collective-permute-start.1 = (f32[16,1152]{1,0:T(8,128)S(1)}, f32[16,1152]{1,0:T(8,128)S(1)}, u32[]{:S(2)}, u32[]{:S(2)}) collective-permute-start(f32[16,1152]{1,0:T(8,128)S(1)} %get-tuple-element.30), channel_id=1, source_target_pairs={{0,2},{1,3},{2,0},{3,1},{4,6},{5,7},{6,4},{7,5},{8,10},{9,11},{10,... | collective-permute-start | bytes 221192 | tf_op jit(solution)/shard_map/ppermute | solution.py:441
  6.0 2.6 %collective-permute-start.7 = (f32[2,104,128]{2,1,0:T(8,128)S(1)}, f32[2,104,128]{2,1,0:T(8,128)S(1)}, u32[]{:S(2)}, u32[]{:S(2)}) collective-permute-start(f32[2,104,128]{2,1,0:T(8,128)S(1)} %get-tuple-element.38), channel_id=1, source_target_pairs={{0,8},{1,13},{2,10},{3,15},{4,12},{5,9},{6,14},{7,11},{8,0},{9,5},... | collective-permute-start | bytes 319496 | tf_op jit(solution)/shard_map/ppermute | solution.py:464
  8.6 1.6 %collective-permute-start.6 = (f32[104,128]{1,0:T(8,128)S(1)}, f32[104,128]{1,0:T(8,128)S(1)}, u32[]{:S(2)}, u32[]{:S(2)}) collective-permute-start(f32[104,128]{1,0:T(8,128)S(1)} %get-tuple-element.37), channel_id=1, source_target_pairs={{0,4},{1,5},{2,6},{3,7},{4,0},{5,1},{6,2},{7,3},{8,12},{9,13},{10,... | collective-permute-start | bytes 159752 | tf_op jit(solution)/shard_map/ppermute | solution.py:464
  10.2 0.4 %collective-permute-start.4 = (f32[2,90,128]{2,1,0:T(8,128)S(1)}, f32[2,90,128]{2,1,0:T(8,128)S(1)}, u32[]{:S(2)}, u32[]{:S(2)}) collective-permute-start(f32[2,90,128]{2,1,0:T(8,128)S(1)} %get-tuple-element.34), channel_id=1, source_target_pairs={{0,4},{4,0},{8,12},{12,8},{1,5},{5,1},{9,13},{13,9},{2,6},{6,2},{1... | collective-permute-start | bytes 276488 | tf_op jit(solution)/shard_map/ppermute | solution.py:441
  10.6 0.0 collective-permute-start.5
  10.7 1.6 %collective-permute-start.2 = (f32[90,128]{1,0:T(8,128)S(1)}, f32[90,128]{1,0:T(8,128)S(1)}, u32[]{:S(2)}, u32[]{:S(2)}) collective-permute-start(f32[90,128]{1,0:T(8,128)S(1)} %get-tuple-element.32), channel_id=1, source_target_pairs={{0,4},{4,0},{8,12},{12,8},{1,5},{5,1},{9,13},{13,9},{2,6},{6,2},{1... | collective-permute-start | bytes 138248 | tf_op jit(solution)/shard_map/ppermute | solution.py:441
  12.3 1.7 %collective-permute-done.6.refs_0_ = f32[104,128]{1,0:T(8,128)S(1)} collective-permute-done((f32[104,128]{1,0:T(8,128)S(1)}, f32[104,128]{1,0:T(8,128)S(1)}, u32[]{:S(2)}, u32[]{:S(2)}) %collective-permute-start.6) | collective-permute-done | bytes 53280 | tf_op jit(solution)/shard_map/ppermute | solution.py:464
  14.0 0.6 %collective-permute-done.7.refs_1_ = f32[2,104,128]{2,1,0:T(8,128)S(1)} collective-permute-done((f32[2,104,128]{2,1,0:T(8,128)S(1)}, f32[2,104,128]{2,1,0:T(8,128)S(1)}, u32[]{:S(2)}, u32[]{:S(2)}) %collective-permute-start.7) | collective-permute-done | bytes 106528 | tf_op jit(solution)/shard_map/ppermute | solution.py:464
  14.7 1.8 %shard_map.112 = (f32[2,16,1152]{2,1,0:T(8,128)S(1)}, f32[2,16,1152]{2,1,0:T(8,128)S(1)}) custom-call(f32[16,1152]{1,0:T(8,128)S(1)} %get-tuple-element.31.after_ref.own_ref, f32[104,128]{1,0:T(8,128)S(1)} %collective-permute-done.6.refs_0_, f32[2,104,128]{2,1,0:T(8,128)S(1)} %collective-permute-done.7.refs_1_, f32[104,128]{1,0:T(8,128)S(1)} %get-tuple-element.39.refs_2_), custom_call_target="tpu_custom_call" | custom-call | flops 409600000 | bytes 102400000 | tf_op jit(solution)/shard_map/pallas_call | solution.py:524
  16.4 0.0 collective-permute-done.4.even_ref
  16.4 0.0 collective-permute-done.5.odd_ref
  16.4 0.8 %collective-permute-done.2.refs_0_.even_ref = f32[90,128]{1,0:T(8,128)S(1)} collective-permute-done((f32[90,128]{1,0:T(8,128)S(1)}, f32[90,128]{1,0:T(8,128)S(1)}, u32[]{:S(2)}, u32[]{:S(2)}) %collective-permute-start.2) | collective-permute-done | bytes 46112 | tf_op jit(solution)/shard_map/ppermute | solution.py:441
  17.2 0.2 shard_map.113
  17.4 0.1 collective-permute-start.8
  17.5 0.0 copy-start.1
  17.5 1.3 %shard_map.114.smooth_ref = f32[16,1152]{1,0:T(8,128)S(1)} custom-call(f32[16,1152]{1,0:T(8,128)S(1)} %get-tuple-element.31.after_ref.own_ref, f32[90,128]{1,0:T(8,128)S(1)} %collective-permute-done.2.refs_0_.even_ref, f32[90,128]{1,0:T(8,128)S(1)} %collective-permute-done.3.refs_1_.odd_ref, f32[5,40,1152]{2,1,0:T(8,128)S(1)} %get-tuple-element.41.coef_ref), custom_call_target="tpu_custom_call" | custom-call | flops 16384000 | bytes 4096000 | tf_op jit(solution)/shard_map/pallas_call | solution.py:544
  18.8 0.1 collective-permute-done.8.more_ref
  18.9 2.6 %collective-permute-start.9 = (f32[90,128]{1,0:T(8,128)S(1)}, f32[90,128]{1,0:T(8,128)S(1)}, u32[]{:S(2)}, u32[]{:S(2)}) collective-permute-start(f32[90,128]{1,0:T(8,128)S(1)} %get-tuple-element.45), channel_id=1, source_target_pairs={{0,4},{4,0},{8,12},{12,8},{1,5},{5,1},{9,13},{13,9},{2,6},{6,2},{1... | collective-permute-start | bytes 138248 | tf_op jit(solution)/shard_map/ppermute | solution.py:441
  21.5 0.1 collective-permute-start.10
  21.7 2.2 %collective-permute-done.9.even_ref = f32[90,128]{1,0:T(8,128)S(1)} collective-permute-done((f32[90,128]{1,0:T(8,128)S(1)}, f32[90,128]{1,0:T(8,128)S(1)}, u32[]{:S(2)}, u32[]{:S(2)}) %collective-permute-start.9) | collective-permute-done | bytes 46112 | tf_op jit(solution)/shard_map/ppermute | solution.py:441
  23.8 0.0 collective-permute-done.10.odd_ref
  23.8 1.2 %shard_map.116.refs_0_ = f32[16,1024]{1,0:T(8,128)S(1)} custom-call(f32[16,1152]{1,0:T(8,128)S(1)} %get-tuple-element.44.own_ref, f32[90,128]{1,0:T(8,128)S(1)} %collective-permute-done.9.even_ref, f32[90,128]{1,0:T(8,128)S(1)} %collective-permute-done.10.odd_ref, f32[5,40,1152]{2,1,0:T(8,128)S(1)} %get-tuple-element.41.coef_ref), custom_call_target="tpu_custom_call" | custom-call | flops 16384000 | bytes 4096000 | tf_op jit(solution)/shard_map/pallas_call | solution.py:555
  25.1 0.6 %collective-permute-start.13 = (f32[16,1024]{1,0:T(8,128)S(1)}, f32[16,1024]{1,0:T(8,128)S(1)}, u32[]{:S(2)}, u32[]{:S(2)}) collective-permute-start(f32[16,1024]{1,0:T(8,128)S(1)} %shard_map.116.refs_0_), channel_id=1, source_target_pairs={{0,2},{1,3},{2,0},{3,1},{4,6},{5,7},{6,4},{7,5},{8,10},{9,11},{10,... | collective-permute-start | bytes 196616 | tf_op jit(solution)/shard_map/ppermute | solution.py:441
  25.7 0.7 %collective-permute-start.12 = (f32[16,1024]{1,0:T(8,128)S(1)}, f32[16,1024]{1,0:T(8,128)S(1)}, u32[]{:S(2)}, u32[]{:S(2)}) collective-permute-start(f32[16,1024]{1,0:T(8,128)S(1)} %shard_map.116.refs_0_), channel_id=1, source_target_pairs={{0,3},{1,2},{2,1},{3,0},{4,7},{5,6},{6,5},{7,4},{8,11},{9,10},{10,... | collective-permute-start | bytes 196616 | tf_op jit(solution)/shard_map/ppermute | solution.py:441
  26.3 1.0 %collective-permute-start.11 = (f32[16,1024]{1,0:T(8,128)S(1)}, f32[16,1024]{1,0:T(8,128)S(1)}, u32[]{:S(2)}, u32[]{:S(2)}) collective-permute-start(f32[16,1024]{1,0:T(8,128)S(1)} %shard_map.116.refs_0_), channel_id=1, source_target_pairs={{0,1},{1,0},{2,3},{3,2},{4,5},{5,4},{6,7},{7,6},{8,9},{9,8},{10,11... | collective-permute-start | bytes 196616 | tf_op jit(solution)/shard_map/ppermute | solution.py:441
  27.3 2.8 %collective-permute-done.13.refs_3_ = f32[16,1024]{1,0:T(8,128)S(1)} collective-permute-done((f32[16,1024]{1,0:T(8,128)S(1)}, f32[16,1024]{1,0:T(8,128)S(1)}, u32[]{:S(2)}, u32[]{:S(2)}) %collective-permute-start.13) | collective-permute-done | bytes 65568 | tf_op jit(solution)/shard_map/ppermute | solution.py:441
  30.1 0.0 collective-permute-done.12.refs_2_
  30.1 0.0 collective-permute-done.11.refs_1_
  30.1 0.8 %shard_map.117 = f32[2,16,2048]{2,1,0:T(8,128)} custom-call(f32[2,2,8,128]{3,2,1,0:T(8,128)S(1)} %get-tuple-element.26.response_ref, f32[2,16,2048]{2,1,0:T(8,128)S(1)} %copy-done, f32[16,1024]{1,0:T(8,128)S(1)} %shard_map.116.refs_0_, f32[16,1024]{1,0:T(8,128)S(1)} %collective-permute-done.11.refs_1_, f32[16,1024]{1,0:T(8,128)S(1)} %collective-permute-done.12.refs_2_, ...), custom_call_target="tpu_custom_call" | custom-call | flops 4096000 | bytes 1024000 | tf_op jit(solution)/shard_map/pallas_call | solution.py:563
  (9 shorter events, 0.1 us)
Async XLA Ops:
  1.6 1.5 %collective-permute-start = (f32[16,2048]{1,0:T(8,128)S(1)}, f32[16,2048]{1,0:T(8,128)S(1)}, u32[]{:S(2)}, u32[]{:S(2)}) collective-permute-start(f32[16,2048]{1,0:T(8,128)S(1)} %get-tuple-element.28), channel_id=1, source_target_pairs={{0,1},{1,0},{2,3},{3,2},{4,5},{5,4},{6,7},{7,6},{8,9},{9,8},{10,11... | collective-permute-start | bytes 393224 | tf_op jit(solution)/shard_map/ppermute | solution.py:441
  3.1 7.6 %collective-permute-start.1 = (f32[16,1152]{1,0:T(8,128)S(1)}, f32[16,1152]{1,0:T(8,128)S(1)}, u32[]{:S(2)}, u32[]{:S(2)}) collective-permute-start(f32[16,1152]{1,0:T(8,128)S(1)} %get-tuple-element.30), channel_id=1, source_target_pairs={{0,2},{1,3},{2,0},{3,1},{4,6},{5,7},{6,4},{7,5},{8,10},{9,11},{10,... | collective-permute-start | bytes 221192 | tf_op jit(solution)/shard_map/ppermute | solution.py:441
  6.0 8.6 %collective-permute-start.7 = (f32[2,104,128]{2,1,0:T(8,128)S(1)}, f32[2,104,128]{2,1,0:T(8,128)S(1)}, u32[]{:S(2)}, u32[]{:S(2)}) collective-permute-start(f32[2,104,128]{2,1,0:T(8,128)S(1)} %get-tuple-element.38), channel_id=1, source_target_pairs={{0,8},{1,13},{2,10},{3,15},{4,12},{5,9},{6,14},{7,11},{8,0},{9,5},... | collective-permute-start | bytes 319496 | tf_op jit(solution)/shard_map/ppermute | solution.py:464
  8.6 5.4 %collective-permute-start.6 = (f32[104,128]{1,0:T(8,128)S(1)}, f32[104,128]{1,0:T(8,128)S(1)}, u32[]{:S(2)}, u32[]{:S(2)}) collective-permute-start(f32[104,128]{1,0:T(8,128)S(1)} %get-tuple-element.37), channel_id=1, source_target_pairs={{0,4},{1,5},{2,6},{3,7},{4,0},{5,1},{6,2},{7,3},{8,12},{9,13},{10,... | collective-permute-start | bytes 159752 | tf_op jit(solution)/shard_map/ppermute | solution.py:464
  10.2 6.2 %collective-permute-start.4 = (f32[2,90,128]{2,1,0:T(8,128)S(1)}, f32[2,90,128]{2,1,0:T(8,128)S(1)}, u32[]{:S(2)}, u32[]{:S(2)}) collective-permute-start(f32[2,90,128]{2,1,0:T(8,128)S(1)} %get-tuple-element.34), channel_id=1, source_target_pairs={{0,4},{4,0},{8,12},{12,8},{1,5},{5,1},{9,13},{13,9},{2,6},{6,2},{1... | collective-permute-start | bytes 276488 | tf_op jit(solution)/shard_map/ppermute | solution.py:441
  10.6 5.8 %collective-permute-start.5 = (f32[2,90,128]{2,1,0:T(8,128)S(1)}, f32[2,90,128]{2,1,0:T(8,128)S(1)}, u32[]{:S(2)}, u32[]{:S(2)}) collective-permute-start(f32[2,90,128]{2,1,0:T(8,128)S(1)} %get-tuple-element.35), channel_id=1, source_target_pairs={{0,1},{1,0},{2,3},{3,2},{4,8},{5,9},{6,10},{7,11},{8,4},{9,5},{10,... | collective-permute-start | bytes 276488 | tf_op jit(solution)/shard_map/ppermute | solution.py:452
  10.7 6.5 %collective-permute-start.2 = (f32[90,128]{1,0:T(8,128)S(1)}, f32[90,128]{1,0:T(8,128)S(1)}, u32[]{:S(2)}, u32[]{:S(2)}) collective-permute-start(f32[90,128]{1,0:T(8,128)S(1)} %get-tuple-element.32), channel_id=1, source_target_pairs={{0,4},{4,0},{8,12},{12,8},{1,5},{5,1},{9,13},{13,9},{2,6},{6,2},{1... | collective-permute-start | bytes 138248 | tf_op jit(solution)/shard_map/ppermute | solution.py:441
  14.0 3.2 %collective-permute-start.3 = (f32[90,128]{1,0:T(8,128)S(1)}, f32[90,128]{1,0:T(8,128)S(1)}, u32[]{:S(2)}, u32[]{:S(2)}) collective-permute-start(f32[90,128]{1,0:T(8,128)S(1)} %get-tuple-element.33), channel_id=1, source_target_pairs={{0,1},{1,0},{2,3},{3,2},{4,8},{5,9},{6,10},{7,11},{8,4},{9,5},{10,... | collective-permute-start | bytes 138248 | tf_op jit(solution)/shard_map/ppermute | solution.py:452
  17.4 1.4 %collective-permute-start.8 = (f32[2,16,1152]{2,1,0:T(8,128)S(1)}, f32[2,16,1152]{2,1,0:T(8,128)S(1)}, u32[]{:S(2)}, u32[]{:S(2)}) collective-permute-start(f32[2,16,1152]{2,1,0:T(8,128)S(1)} %get-tuple-element.43), channel_id=1, source_target_pairs={{0,1},{1,0},{2,3},{3,2},{4,5},{5,4},{6,7},{7,6},{8,9},{9,8},{10,11... | collective-permute-start | bytes 442376 | tf_op jit(solution)/shard_map/ppermute | solution.py:441
  17.5 1.4 %copy-start.1 = (s32[16,2048]{1,0:T(8,128)S(1)}, s32[16,2048]{1,0:T(8,128)}, u32[]{:S(2)}) copy-start(s32[16,2048]{1,0:T(8,128)} %mask_ref.1) | copy-start | bytes 393220
  18.9 4.9 %collective-permute-start.9 = (f32[90,128]{1,0:T(8,128)S(1)}, f32[90,128]{1,0:T(8,128)S(1)}, u32[]{:S(2)}, u32[]{:S(2)}) collective-permute-start(f32[90,128]{1,0:T(8,128)S(1)} %get-tuple-element.45), channel_id=1, source_target_pairs={{0,4},{4,0},{8,12},{12,8},{1,5},{5,1},{9,13},{13,9},{2,6},{6,2},{1... | collective-permute-start | bytes 138248 | tf_op jit(solution)/shard_map/ppermute | solution.py:441
  21.5 2.3 %collective-permute-start.10 = (f32[90,128]{1,0:T(8,128)S(1)}, f32[90,128]{1,0:T(8,128)S(1)}, u32[]{:S(2)}, u32[]{:S(2)}) collective-permute-start(f32[90,128]{1,0:T(8,128)S(1)} %get-tuple-element.46), channel_id=1, source_target_pairs={{0,1},{1,0},{2,3},{3,2},{4,8},{5,9},{6,10},{7,11},{8,4},{9,5},{10,... | collective-permute-start | bytes 138248 | tf_op jit(solution)/shard_map/ppermute | solution.py:452
  23.8 6.3 %copy-start = (f32[2,16,2048]{2,1,0:T(8,128)S(1)}, f32[2,16,2048]{2,1,0:T(8,128)}, u32[]{:S(2)}) copy-start(f32[2,16,2048]{2,1,0:T(8,128)} %control_ref.1) | copy-start | bytes 786436
  25.1 5.0 %collective-permute-start.13 = (f32[16,1024]{1,0:T(8,128)S(1)}, f32[16,1024]{1,0:T(8,128)S(1)}, u32[]{:S(2)}, u32[]{:S(2)}) collective-permute-start(f32[16,1024]{1,0:T(8,128)S(1)} %shard_map.116.refs_0_), channel_id=1, source_target_pairs={{0,2},{1,3},{2,0},{3,1},{4,6},{5,7},{6,4},{7,5},{8,10},{9,11},{10,... | collective-permute-start | bytes 196616 | tf_op jit(solution)/shard_map/ppermute | solution.py:441
  25.7 4.4 %collective-permute-start.12 = (f32[16,1024]{1,0:T(8,128)S(1)}, f32[16,1024]{1,0:T(8,128)S(1)}, u32[]{:S(2)}, u32[]{:S(2)}) collective-permute-start(f32[16,1024]{1,0:T(8,128)S(1)} %shard_map.116.refs_0_), channel_id=1, source_target_pairs={{0,3},{1,2},{2,1},{3,0},{4,7},{5,6},{6,5},{7,4},{8,11},{9,10},{10,... | collective-permute-start | bytes 196616 | tf_op jit(solution)/shard_map/ppermute | solution.py:441
  26.3 3.7 %collective-permute-start.11 = (f32[16,1024]{1,0:T(8,128)S(1)}, f32[16,1024]{1,0:T(8,128)S(1)}, u32[]{:S(2)}, u32[]{:S(2)}) collective-permute-start(f32[16,1024]{1,0:T(8,128)S(1)} %shard_map.116.refs_0_), channel_id=1, source_target_pairs={{0,1},{1,0},{2,3},{3,2},{4,5},{5,4},{6,7},{7,6},{8,9},{9,8},{10,11... | collective-permute-start | bytes 196616 | tf_op jit(solution)/shard_map/ppermute | solution.py:441

commit v11 on v9

--- a/solution.py
+++ b/solution.py
@@ -70,8 +70,8 @@
 
 
 def first_kernel(slots, margin, sens_hbm, factor_hbm, control_hbm, kappa_hbm, tile_hbm, row_hbm, sensor_hbm,
-                 value_hbm, weight_hbm, cols_hbm, own_ref, other_ref, response_ref, kappa_ref, even_ref,
-                 odd_ref, *refs):
+                 value_hbm, weight_hbm, cols_hbm, own_ref, other_ref, response_ref, kappa_ref, odd_ref,
+                 *refs):
     chunk_refs = refs[:-11]
     (sens_ref, factor_ref, control_ref, tile_ref, row_ref, sensor_ref, value_ref, weight_ref, cols_ref,
      before_ref, sems) = refs[-11:]
@@ -103,7 +103,8 @@
         out_ref[...] = total
 
     for i in range(2):
-        pack_edges(even_ref.at[i], odd_ref.at[i], kappa_ref[i], margin)
+        even_ref = even_kappa(chunk_refs[-2], slots, odd_ref.shape[1], i)
+        pack_edges(even_ref, odd_ref.at[i], kappa_ref[i], margin)
 
     tiles = lax.axis_size("tile")
     full = tiles // 2 - 1
@@ -149,7 +150,7 @@
         out_ref = chunk_refs[i // 2].at[i % 2] if i < 2 * full else chunk_refs[i - full]
         for part, rows in enumerate(sent):
             out_ref[part * slots : (part + 1) * slots] = rows[i * slots : (i + 1) * slots]
-        out_ref[3 * slots :] = meta
+        out_ref[3 * slots : 3 * slots + 8] = meta
 
 
 def thirds(values):
@@ -278,6 +279,10 @@
         odd_ref[b * margin : (b + 1) * margin] = jnp.where(even, head, tail)
 
 
+def even_kappa(ref, slots, edge_rows, i):
+    return ref.at[pl.ds(3 * slots + 8 + i * (-(-edge_rows // 8) * 8), edge_rows)]
+
+
 def cut_kernel(first_ref, second_ref, mine_ref, *out_refs):
     chip, chips, blocks = my_chip(), chip_count(), first_ref.shape[1] // LANES
     for d, out_ref in enumerate((mine_ref, *out_refs)):
@@ -385,12 +390,13 @@
     return [f[:rows] for f in fields]
 
 
-def faces_kernel(margin, even_ref, odd_ref, kappa_ref, sums_ref, *refs):
+def faces_kernel(margin, slots, shared_ref, odd_ref, kappa_ref, sums_ref, *refs):
     coef_ref, sums_out, one_ref, two_ref = refs[-4:]
     sums_out[...] = sums_ref[...]
     rows = kappa_ref.shape[1]
-    lay_ring(one_ref, kappa_ref[0], even_ref.at[0], odd_ref.at[0], margin)
-    lay_ring(two_ref, kappa_ref[1], even_ref.at[1], odd_ref.at[1], margin)
+    for i, ring_ref in enumerate((one_ref, two_ref)):
+        even_ref = even_kappa(shared_ref, slots, odd_ref.shape[1], i)
+        lay_ring(ring_ref, kappa_ref[i], even_ref, odd_ref.at[i], margin)
     face_weights(coef_ref, one_ref, two_ref, rows, margin)
 
 
@@ -441,7 +447,7 @@
     return lax.ppermute(values, axis, [(i, i ^ bit) for i in range(count)])
 
 
-def swap_edges(even, odd):
+def swap_odd(edges):
     tiles, members = lax.axis_size("tile"), lax.axis_size("var")
     pairs = []
     for t in range(tiles):
@@ -449,7 +455,11 @@
         for q in range(members):
             to = other * members + q if 0 <= other < tiles else t * members + (q ^ 1)
             pairs.append((t * members + q, to))
-    return swap(even, "tile", 1), lax.ppermute(odd, ("tile", "var"), pairs)
+    return lax.ppermute(edges, ("tile", "var"), pairs)
+
+
+def swap_edges(even, odd):
+    return swap(even, "tile", 1), swap_odd(odd)
 
 
 def deliver(chunks):
@@ -484,12 +494,13 @@
     edge = jax.ShapeDtypeStruct((margin * size, LANES), F32)
     edge2 = jax.ShapeDtypeStruct((2, *edge.shape), F32)
     half = jax.ShapeDtypeStruct((3 * slots + 8, panel_width), F32)
-    chunks = [jax.ShapeDtypeStruct((2, *half.shape), F32)] * (tiles // 2 - 1) + [half] * 2
+    shared = jax.ShapeDtypeStruct((half.shape[0] + 2 * (-(-edge.shape[0] // 8) * 8), panel_width), F32)
+    chunks = [jax.ShapeDtypeStruct((2, *half.shape), F32)] * (tiles // 2 - 1) + [shared, half]
     line = pltpu.VMEM((1, panels), jnp.int32)
 
-    own, other, responses, kappa, kappa_even, kappa_odd, *chunks = call(
+    own, other, responses, kappa, kappa_odd, *chunks = call(
         functools.partial(first_kernel, slots, margin),
-        [field, field, jax.ShapeDtypeStruct((2, var_dev, 8, LANES), F32), view2, edge2, edge2]
+        [field, field, jax.ShapeDtypeStruct((2, var_dev, 8, LANES), F32), view2, edge2]
         + chunks,
         [HBM] * 10,
         [
@@ -513,7 +524,7 @@
         own, swap(other, "var", 1)
     )
     parts = [swap(p, "var", 2 * (d + 1)) for d, p in enumerate(parts)]
-    kappa_even, kappa_odd = swap_edges(kappa_even, kappa_odd)
+    kappa_odd = swap_odd(kappa_odd)
     smooth_in, even, odd = call(
         functools.partial(edges_kernel, margin), [view, edge, edge], [VMEM] * chips, cost=cost(500)
     )(part, *parts)
@@ -531,12 +542,12 @@
     )(smooth_in, got[-2], *got[:-2], got[-1])
     ring = pltpu.VMEM((total, size * LANES), F32)
     coef, sums_other = call(
-        functools.partial(faces_kernel, margin),
+        functools.partial(faces_kernel, margin, slots),
         [jax.ShapeDtypeStruct((5, total, size * LANES), F32), view2],
         [VMEM] * 4 + [AFTER] * 2,
         [ring, ring],
         cost=cost(1000),
-    )(kappa_even, kappa_odd, kappa, sums_other, even, odd)
+    )(got[-2], kappa_odd, kappa, sums_other, even, odd)
     more_sums = swap(sums_other, "var", 1)
     (smooth,) = call(
         functools.partial(smooth_kernel, margin),

time: 29.3 us -> 30 us (1.024)
  waiting for transfers between devices: 7.57 us -> 10.5 us
  starting transfers between devices: 13.7 us -> 12.3 us
  Pallas kernels: 7.7 us -> 6.88 us
    ppermute x9 -> x8, waiting for transfers between devices: 6.92 us -> 10.5 us  [swap(): return lax.ppermute(values, axis, [(i, i ^ bit) for i in range(count)])]
    ppermute x9 -> x8, starting transfers between devices: 8 us -> 6.95 us  [swap(): return lax.ppermute(values, axis, [(i, i ^ bit) for i in range(count)])]
    pallas_call x1, Pallas kernels: 2.55 us -> 1.74 us  [local(): call(functools.partial(scatter_kernel, slots, blocks), [view2, view2], [A...]
    ppermute x2, waiting for transfers between devices: 0.64 us -> 0.01 us  [deliver(): got.append(lax.ppermute(chunk, ('tile', 'var'), pairs))]
    ppermute x3, starting transfers between devices: 0.51 us -> 0.15 us  [swap_odd(): return lax.ppermute(edges, ('tile', 'var'), pairs)]
  transfers between devices with their start and end apart: 14 -> 13, of which waited for: 6 -> 6; matrix products, arithmetic and copies ran while one was open for 0% -> 0% of each run, Pallas kernels for 13% -> 10%
where the time goes in v11:
time: 30 us; the launch traced here: 29.9 us
  starting transfers between devices  12.3 us (41%)
  waiting for transfers between devices  10.5 us (35%)
  Pallas kernels  6.88 us (23%)
    ppermute x8, waiting for transfers between devices, swap(): return lax.ppermute(values, axis, [(i, i ^ bit) for i in range(count)])  10.5 us
    ppermute x8, starting transfers between devices, swap(): return lax.ppermute(values, axis, [(i, i ^ bit) for i in range(count)])  6.95 us
    ppermute x2, starting transfers between devices, deliver(): got.append(lax.ppermute(chunk, ('tile', 'var'), pairs))  5.23 us
    pallas_call x1, Pallas kernels, local(): call(functools.partial(scatter_kernel, slots, blocks), [view2, view2], [A...  1.74 us
    pallas_call x1, Pallas kernels, local(): call(functools.partial(first_kernel, slots, margin), [field, field, jax.S...  1.59 us
    pallas_call x1, Pallas kernels, local(): call(functools.partial(smooth_kernel, margin), [view], [VMEM] * 4, [ring]...  1.24 us
    pallas_call x1, Pallas kernels, local(): call(functools.partial(spread_kernel, margin), [share], [VMEM] * 4, [ring...  1.23 us
    pallas_call x1, Pallas kernels, local(): call(result_kernel, [jax.ShapeDtypeStruct(control.shape, F32)], [VMEM] *...  0.78 us
  transfers between devices with their start and end apart: 13, of which 6 were waited for; matrix products, arithmetic and copies ran while one was open for 0% of the time, Pallas kernels for 10%

profile of v11, /device:TPU:0, one launch (start us, length us, event | category | flops | bytes accessed | tf_op | source)
XLA Modules:
  0.0 29.9 jit_solution(17783531539252593405)
XLA Ops:
  0.0 1.6 %shard_map.109 = (f32[16,2048]{1,0:T(8,128)S(1)}, f32[16,2048]{1,0:T(8,128)S(1)}, f32[2,2,8,128]{3,2,1,0:T(8,128)S(1)}, f32[2,16,1152]{2,1,0:T(8,128)S(1)}, f32[...) custom-call(f32[2,8]{1,0:T(2,128)} %sens_hbm.1, ...), custom_call_target="tpu_custom_call" | custom-call | flops 12288000 | bytes 3072000 | tf_op jit(solution)/shard_map/pallas_call | solution.py:501
  1.6 0.5 %collective-permute-start = (f32[16,2048]{1,0:T(8,128)S(1)}, f32[16,2048]{1,0:T(8,128)S(1)}, u32[]{:S(2)}, u32[]{:S(2)}) collective-permute-start(f32[16,2048]{1,0:T(8,128)S(1)} %get-tuple-element.27), channel_id=1, source_target_pairs={{0,1},{1,0},{2,3},{3,2},{4,5},{5,4},{6,7},{7,6},{8,9},{9,8},{10,11... | collective-permute-start | bytes 393224 | tf_op jit(solution)/shard_map/ppermute | solution.py:447
  2.1 2.6 %collective-permute-start.4 = (f32[296,128]{1,0:T(8,128)S(1)}, f32[296,128]{1,0:T(8,128)S(1)}, u32[]{:S(2)}, u32[]{:S(2)}) collective-permute-start(f32[296,128]{1,0:T(8,128)S(1)} %get-tuple-element.33), channel_id=1, source_target_pairs={{0,4},{1,5},{2,6},{3,7},{4,0},{5,1},{6,2},{7,3},{8,12},{9,13},{10,... | collective-permute-start | bytes 454664 | tf_op jit(solution)/shard_map/ppermute | solution.py:474
  4.8 2.6 %collective-permute-start.6 = (f32[2,104,128]{2,1,0:T(8,128)S(1)}, f32[2,104,128]{2,1,0:T(8,128)S(1)}, u32[]{:S(2)}, u32[]{:S(2)}) collective-permute-start(f32[2,104,128]{2,1,0:T(8,128)S(1)} %get-tuple-element.36), channel_id=1, source_target_pairs={{0,8},{1,13},{2,10},{3,15},{4,12},{5,9},{6,14},{7,11},{8,0},{9,5},... | collective-permute-start | bytes 319496 | tf_op jit(solution)/shard_map/ppermute | solution.py:474
  7.4 0.0 collective-permute-done.second_ref
  7.4 1.6 %collective-permute-start.1 = (f32[16,1152]{1,0:T(8,128)S(1)}, f32[16,1152]{1,0:T(8,128)S(1)}, u32[]{:S(2)}, u32[]{:S(2)}) collective-permute-start(f32[16,1152]{1,0:T(8,128)S(1)} %get-tuple-element.29), channel_id=1, source_target_pairs={{0,2},{1,3},{2,0},{3,1},{4,6},{5,7},{6,4},{7,5},{8,10},{9,11},{10,... | collective-permute-start | bytes 221192 | tf_op jit(solution)/shard_map/ppermute | solution.py:447
  8.9 0.0 collective-permute-start.5
  8.9 2.9 %collective-permute-done.1.refs_1_ = f32[16,1152]{1,0:T(8,128)S(1)} collective-permute-done((f32[16,1152]{1,0:T(8,128)S(1)}, f32[16,1152]{1,0:T(8,128)S(1)}, u32[]{:S(2)}, u32[]{:S(2)}) %collective-permute-start.1) | collective-permute-done | bytes 73760 | tf_op jit(solution)/shard_map/ppermute | solution.py:447
  11.8 0.5 %collective-permute-start.2 = (f32[90,128]{1,0:T(8,128)S(1)}, f32[90,128]{1,0:T(8,128)S(1)}, u32[]{:S(2)}, u32[]{:S(2)}) collective-permute-start(f32[90,128]{1,0:T(8,128)S(1)} %get-tuple-element.31), channel_id=1, source_target_pairs={{0,4},{4,0},{8,12},{12,8},{1,5},{5,1},{9,13},{13,9},{2,6},{6,2},{1... | collective-permute-start | bytes 138248 | tf_op jit(solution)/shard_map/ppermute | solution.py:447
  12.3 0.0 collective-permute-start.3
  12.3 0.0 collective-permute-done.6.refs_1_
  12.3 0.0 collective-permute-done.4.refs_0_.shared_ref
  12.4 1.7 %shard_map.112 = (f32[2,16,1152]{2,1,0:T(8,128)S(1)}, f32[2,16,1152]{2,1,0:T(8,128)S(1)}) custom-call(f32[16,1152]{1,0:T(8,128)S(1)} %get-tuple-element.30.after_ref.own_ref, f32[296,128]{1,0:T(8,128)S(1)} %collective-permute-done.4.refs_0_.shared_ref, f32[2,104,128]{2,1,0:T(8,128)S(1)} %collective-permute-done.6.refs_1_, ...), custom_call_target="tpu_custom_call" | custom-call | flops 409600000 | bytes 102400000 | tf_op jit(solution)/shard_map/pallas_call | solution.py:532
  14.1 0.0 collective-permute-done.5.odd_ref
  14.1 1.9 %collective-permute-done.2.refs_0_.even_ref = f32[90,128]{1,0:T(8,128)S(1)} collective-permute-done((f32[90,128]{1,0:T(8,128)S(1)}, f32[90,128]{1,0:T(8,128)S(1)}, u32[]{:S(2)}, u32[]{:S(2)}) %collective-permute-start.2) | collective-permute-done | bytes 46112 | tf_op jit(solution)/shard_map/ppermute | solution.py:447
  16.0 0.0 collective-permute-done.3.refs_1_.odd_ref
  16.0 0.2 shard_map.113
  16.2 0.1 collective-permute-start.7
  16.3 0.0 copy-start.1
  16.3 1.2 %shard_map.114.smooth_ref = f32[16,1152]{1,0:T(8,128)S(1)} custom-call(f32[16,1152]{1,0:T(8,128)S(1)} %get-tuple-element.30.after_ref.own_ref, f32[90,128]{1,0:T(8,128)S(1)} %collective-permute-done.2.refs_0_.even_ref, f32[90,128]{1,0:T(8,128)S(1)} %collective-permute-done.3.refs_1_.odd_ref, f32[5,40,1152]{2,1,0:T(8,128)S(1)} %get-tuple-element.39.coef_ref), custom_call_target="tpu_custom_call" | custom-call | flops 16384000 | bytes 4096000 | tf_op jit(solution)/shard_map/pallas_call | solution.py:552
  17.5 0.1 collective-permute-done.7.more_ref
  17.7 2.1 %collective-permute-start.8 = (f32[90,128]{1,0:T(8,128)S(1)}, f32[90,128]{1,0:T(8,128)S(1)}, u32[]{:S(2)}, u32[]{:S(2)}) collective-permute-start(f32[90,128]{1,0:T(8,128)S(1)} %get-tuple-element.43), channel_id=1, source_target_pairs={{0,4},{4,0},{8,12},{12,8},{1,5},{5,1},{9,13},{13,9},{2,6},{6,2},{1... | collective-permute-start | bytes 138248 | tf_op jit(solution)/shard_map/ppermute | solution.py:447
  19.8 0.1 collective-permute-start.9
  19.9 2.2 %collective-permute-done.8.even_ref = f32[90,128]{1,0:T(8,128)S(1)} collective-permute-done((f32[90,128]{1,0:T(8,128)S(1)}, f32[90,128]{1,0:T(8,128)S(1)}, u32[]{:S(2)}, u32[]{:S(2)}) %collective-permute-start.8) | collective-permute-done | bytes 46112 | tf_op jit(solution)/shard_map/ppermute | solution.py:447
  22.1 1.2 %shard_map.116.refs_0_ = f32[16,1024]{1,0:T(8,128)S(1)} custom-call(f32[16,1152]{1,0:T(8,128)S(1)} %get-tuple-element.42.own_ref, f32[90,128]{1,0:T(8,128)S(1)} %collective-permute-done.8.even_ref, f32[90,128]{1,0:T(8,128)S(1)} %collective-permute-done.9.odd_ref, f32[5,40,1152]{2,1,0:T(8,128)S(1)} %get-tuple-element.39.coef_ref), custom_call_target="tpu_custom_call" | custom-call | flops 16384000 | bytes 4096000 | tf_op jit(solution)/shard_map/pallas_call | solution.py:563
  23.3 1.6 %collective-permute-start.12 = (f32[16,1024]{1,0:T(8,128)S(1)}, f32[16,1024]{1,0:T(8,128)S(1)}, u32[]{:S(2)}, u32[]{:S(2)}) collective-permute-start(f32[16,1024]{1,0:T(8,128)S(1)} %shard_map.116.refs_0_), channel_id=1, source_target_pairs={{0,2},{1,3},{2,0},{3,1},{4,6},{5,7},{6,4},{7,5},{8,10},{9,11},{10,... | collective-permute-start | bytes 196616 | tf_op jit(solution)/shard_map/ppermute | solution.py:447
  24.9 0.0 collective-permute-start.11
  24.9 0.6 %collective-permute-start.10 = (f32[16,1024]{1,0:T(8,128)S(1)}, f32[16,1024]{1,0:T(8,128)S(1)}, u32[]{:S(2)}, u32[]{:S(2)}) collective-permute-start(f32[16,1024]{1,0:T(8,128)S(1)} %shard_map.116.refs_0_), channel_id=1, source_target_pairs={{0,1},{1,0},{2,3},{3,2},{4,5},{5,4},{6,7},{7,6},{8,9},{9,8},{10,11... | collective-permute-start | bytes 196616 | tf_op jit(solution)/shard_map/ppermute | solution.py:447
  25.5 2.1 %collective-permute-done.12.refs_3_ = f32[16,1024]{1,0:T(8,128)S(1)} collective-permute-done((f32[16,1024]{1,0:T(8,128)S(1)}, f32[16,1024]{1,0:T(8,128)S(1)}, u32[]{:S(2)}, u32[]{:S(2)}) %collective-permute-start.12) | collective-permute-done | bytes 65568 | tf_op jit(solution)/shard_map/ppermute | solution.py:447
  27.7 1.4 %collective-permute-done.11.refs_2_ = f32[16,1024]{1,0:T(8,128)S(1)} collective-permute-done((f32[16,1024]{1,0:T(8,128)S(1)}, f32[16,1024]{1,0:T(8,128)S(1)}, u32[]{:S(2)}, u32[]{:S(2)}) %collective-permute-start.11) | collective-permute-done | bytes 65568 | tf_op jit(solution)/shard_map/ppermute | solution.py:447
  29.1 0.0 collective-permute-done.10.refs_1_
  29.1 0.8 %shard_map.117 = f32[2,16,2048]{2,1,0:T(8,128)} custom-call(f32[2,2,8,128]{3,2,1,0:T(8,128)S(1)} %get-tuple-element.25.response_ref, f32[2,16,2048]{2,1,0:T(8,128)S(1)} %copy-done, f32[16,1024]{1,0:T(8,128)S(1)} %shard_map.116.refs_0_, f32[16,1024]{1,0:T(8,128)S(1)} %collective-permute-done.10.refs_1_, f32[16,1024]{1,0:T(8,128)S(1)} %collective-permute-done.11.refs_2_, ...), custom_call_target="tpu_custom_call" | custom-call | flops 4096000 | bytes 1024000 | tf_op jit(solution)/shard_map/pallas_call | solution.py:571
  (7 shorter events, 0.1 us)
Async XLA Ops:
  1.6 5.8 %collective-permute-start = (f32[16,2048]{1,0:T(8,128)S(1)}, f32[16,2048]{1,0:T(8,128)S(1)}, u32[]{:S(2)}, u32[]{:S(2)}) collective-permute-start(f32[16,2048]{1,0:T(8,128)S(1)} %get-tuple-element.27), channel_id=1, source_target_pairs={{0,1},{1,0},{2,3},{3,2},{4,5},{5,4},{6,7},{7,6},{8,9},{9,8},{10,11... | collective-permute-start | bytes 393224 | tf_op jit(solution)/shard_map/ppermute | solution.py:447
  2.1 10.2 %collective-permute-start.4 = (f32[296,128]{1,0:T(8,128)S(1)}, f32[296,128]{1,0:T(8,128)S(1)}, u32[]{:S(2)}, u32[]{:S(2)}) collective-permute-start(f32[296,128]{1,0:T(8,128)S(1)} %get-tuple-element.33), channel_id=1, source_target_pairs={{0,4},{1,5},{2,6},{3,7},{4,0},{5,1},{6,2},{7,3},{8,12},{9,13},{10,... | collective-permute-start | bytes 454664 | tf_op jit(solution)/shard_map/ppermute | solution.py:474
  4.8 7.6 %collective-permute-start.6 = (f32[2,104,128]{2,1,0:T(8,128)S(1)}, f32[2,104,128]{2,1,0:T(8,128)S(1)}, u32[]{:S(2)}, u32[]{:S(2)}) collective-permute-start(f32[2,104,128]{2,1,0:T(8,128)S(1)} %get-tuple-element.36), channel_id=1, source_target_pairs={{0,8},{1,13},{2,10},{3,15},{4,12},{5,9},{6,14},{7,11},{8,0},{9,5},... | collective-permute-start | bytes 319496 | tf_op jit(solution)/shard_map/ppermute | solution.py:474
  7.4 4.4 %collective-permute-start.1 = (f32[16,1152]{1,0:T(8,128)S(1)}, f32[16,1152]{1,0:T(8,128)S(1)}, u32[]{:S(2)}, u32[]{:S(2)}) collective-permute-start(f32[16,1152]{1,0:T(8,128)S(1)} %get-tuple-element.29), channel_id=1, source_target_pairs={{0,2},{1,3},{2,0},{3,1},{4,6},{5,7},{6,4},{7,5},{8,10},{9,11},{10,... | collective-permute-start | bytes 221192 | tf_op jit(solution)/shard_map/ppermute | solution.py:447
  8.9 5.2 %collective-permute-start.5 = (f32[2,90,128]{2,1,0:T(8,128)S(1)}, f32[2,90,128]{2,1,0:T(8,128)S(1)}, u32[]{:S(2)}, u32[]{:S(2)}) collective-permute-start(f32[2,90,128]{2,1,0:T(8,128)S(1)} %get-tuple-element.34), channel_id=1, source_target_pairs={{0,1},{1,0},{2,3},{3,2},{4,8},{5,9},{6,10},{7,11},{8,4},{9,5},{10,... | collective-permute-start | bytes 276488 | tf_op jit(solution)/shard_map/ppermute | solution.py:458
  11.8 4.2 %collective-permute-start.2 = (f32[90,128]{1,0:T(8,128)S(1)}, f32[90,128]{1,0:T(8,128)S(1)}, u32[]{:S(2)}, u32[]{:S(2)}) collective-permute-start(f32[90,128]{1,0:T(8,128)S(1)} %get-tuple-element.31), channel_id=1, source_target_pairs={{0,4},{4,0},{8,12},{12,8},{1,5},{5,1},{9,13},{13,9},{2,6},{6,2},{1... | collective-permute-start | bytes 138248 | tf_op jit(solution)/shard_map/ppermute | solution.py:447
  12.3 3.6 %collective-permute-start.3 = (f32[90,128]{1,0:T(8,128)S(1)}, f32[90,128]{1,0:T(8,128)S(1)}, u32[]{:S(2)}, u32[]{:S(2)}) collective-permute-start(f32[90,128]{1,0:T(8,128)S(1)} %get-tuple-element.32), channel_id=1, source_target_pairs={{0,1},{1,0},{2,3},{3,2},{4,8},{5,9},{6,10},{7,11},{8,4},{9,5},{10,... | collective-permute-start | bytes 138248 | tf_op jit(solution)/shard_map/ppermute | solution.py:458
  16.2 1.4 %collective-permute-start.7 = (f32[2,16,1152]{2,1,0:T(8,128)S(1)}, f32[2,16,1152]{2,1,0:T(8,128)S(1)}, u32[]{:S(2)}, u32[]{:S(2)}) collective-permute-start(f32[2,16,1152]{2,1,0:T(8,128)S(1)} %get-tuple-element.41), channel_id=1, source_target_pairs={{0,1},{1,0},{2,3},{3,2},{4,5},{5,4},{6,7},{7,6},{8,9},{9,8},{10,11... | collective-permute-start | bytes 442376 | tf_op jit(solution)/shard_map/ppermute | solution.py:447
  16.3 1.4 %copy-start.1 = (s32[16,2048]{1,0:T(8,128)S(1)}, s32[16,2048]{1,0:T(8,128)}, u32[]{:S(2)}) copy-start(s32[16,2048]{1,0:T(8,128)} %mask_ref.1) | copy-start | bytes 393220
  17.7 4.4 %collective-permute-start.8 = (f32[90,128]{1,0:T(8,128)S(1)}, f32[90,128]{1,0:T(8,128)S(1)}, u32[]{:S(2)}, u32[]{:S(2)}) collective-permute-start(f32[90,128]{1,0:T(8,128)S(1)} %get-tuple-element.43), channel_id=1, source_target_pairs={{0,4},{4,0},{8,12},{12,8},{1,5},{5,1},{9,13},{13,9},{2,6},{6,2},{1... | collective-permute-start | bytes 138248 | tf_op jit(solution)/shard_map/ppermute | solution.py:447
  19.8 2.3 %collective-permute-start.9 = (f32[90,128]{1,0:T(8,128)S(1)}, f32[90,128]{1,0:T(8,128)S(1)}, u32[]{:S(2)}, u32[]{:S(2)}) collective-permute-start(f32[90,128]{1,0:T(8,128)S(1)} %get-tuple-element.44), channel_id=1, source_target_pairs={{0,1},{1,0},{2,3},{3,2},{4,8},{5,9},{6,10},{7,11},{8,4},{9,5},{10,... | collective-permute-start | bytes 138248 | tf_op jit(solution)/shard_map/ppermute | solution.py:458
  22.1 7.0 %copy-start = (f32[2,16,2048]{2,1,0:T(8,128)S(1)}, f32[2,16,2048]{2,1,0:T(8,128)}, u32[]{:S(2)}) copy-start(f32[2,16,2048]{2,1,0:T(8,128)} %control_ref.1) | copy-start | bytes 786436
  23.3 4.3 %collective-permute-start.12 = (f32[16,1024]{1,0:T(8,128)S(1)}, f32[16,1024]{1,0:T(8,128)S(1)}, u32[]{:S(2)}, u32[]{:S(2)}) collective-permute-start(f32[16,1024]{1,0:T(8,128)S(1)} %shard_map.116.refs_0_), channel_id=1, source_target_pairs={{0,2},{1,3},{2,0},{3,1},{4,6},{5,7},{6,4},{7,5},{8,10},{9,11},{10,... | collective-permute-start | bytes 196616 | tf_op jit(solution)/shard_map/ppermute | solution.py:447
  24.9 4.2 %collective-permute-start.11 = (f32[16,1024]{1,0:T(8,128)S(1)}, f32[16,1024]{1,0:T(8,128)S(1)}, u32[]{:S(2)}, u32[]{:S(2)}) collective-permute-start(f32[16,1024]{1,0:T(8,128)S(1)} %shard_map.116.refs_0_), channel_id=1, source_target_pairs={{0,3},{1,2},{2,1},{3,0},{4,7},{5,6},{6,5},{7,4},{8,11},{9,10},{10,... | collective-permute-start | bytes 196616 | tf_op jit(solution)/shard_map/ppermute | solution.py:447
  24.9 4.2 %collective-permute-start.10 = (f32[16,1024]{1,0:T(8,128)S(1)}, f32[16,1024]{1,0:T(8,128)S(1)}, u32[]{:S(2)}, u32[]{:S(2)}) collective-permute-start(f32[16,1024]{1,0:T(8,128)S(1)} %shard_map.116.refs_0_), channel_id=1, source_target_pairs={{0,1},{1,0},{2,3},{3,2},{4,5},{5,4},{6,7},{7,6},{8,9},{9,8},{10,11... | collective-permute-start | bytes 196616 | tf_op jit(solution)/shard_map/ppermute | solution.py:447

commit v12 on v11

--- a/solution.py
+++ b/solution.py
@@ -526,7 +526,10 @@
     parts = [swap(p, "var", 2 * (d + 1)) for d, p in enumerate(parts)]
     kappa_odd = swap_odd(kappa_odd)
     smooth_in, even, odd = call(
-        functools.partial(edges_kernel, margin), [view, edge, edge], [VMEM] * chips, cost=cost(500)
+        functools.partial(edges_kernel, margin),
+        [view, edge, edge],
+        [VMEM] * chips,
+        cost=cost(130000),
     )(part, *parts)
     even, odd = swap_edges(even, odd)
     sums, sums_other = call(

time: 30 us -> 31.3 us (1.043)
  the two profiles are of different devices: /device:TPU:0 before, /device:TPU:21 now
where the time goes in v12:
time: 31.3 us; the launch traced here: 31.1 us
  starting transfers between devices  14.1 us (45%)
  waiting for transfers between devices  10 us (32%)
  Pallas kernels  6.89 us (22%)
    ppermute x8, starting transfers between devices, swap(): return lax.ppermute(values, axis, [(i, i ^ bit) for i in range(count)])  11.1 us
    ppermute x8, waiting for transfers between devices, swap(): return lax.ppermute(values, axis, [(i, i ^ bit) for i in range(count)])  6.12 us
    ppermute x3, waiting for transfers between devices, swap_odd(): return lax.ppermute(edges, ('tile', 'var'), pairs)  3.76 us
    ppermute x3, starting transfers between devices, swap_odd(): return lax.ppermute(edges, ('tile', 'var'), pairs)  1.77 us
    pallas_call x1, Pallas kernels, local(): call(functools.partial(scatter_kernel, slots, blocks), [view2, view2], [A...  1.75 us
    pallas_call x1, Pallas kernels, local(): call(functools.partial(first_kernel, slots, margin), [field, field, jax.S...  1.59 us
    ppermute x2, starting transfers between devices, deliver(): got.append(lax.ppermute(chunk, ('tile', 'var'), pairs))  1.31 us
    pallas_call x1, Pallas kernels, local(): call(functools.partial(smooth_kernel, margin), [view], [VMEM] * 4, [ring]...  1.24 us
  transfers between devices with their start and end apart: 13, of which 7 were waited for; matrix products, arithmetic and copies ran while one was open for 0% of the time, Pallas kernels for 10%

profile of v12, /device:TPU:21, one launch (start us, length us, event | category | flops | bytes accessed | tf_op | source)
XLA Modules:
  0.0 31.1 jit_solution(12743450514136885026)
XLA Ops:
  0.0 1.6 %shard_map.109 = (f32[16,2048]{1,0:T(8,128)S(1)}, f32[16,2048]{1,0:T(8,128)S(1)}, f32[2,2,8,128]{3,2,1,0:T(8,128)S(1)}, f32[2,16,1152]{2,1,0:T(8,128)S(1)}, f32[...) custom-call(f32[2,8]{1,0:T(2,128)} %sens_hbm.1, ...), custom_call_target="tpu_custom_call" | custom-call | flops 12288000 | bytes 3072000 | tf_op jit(solution)/shard_map/pallas_call | solution.py:501
  1.6 0.7 %collective-permute-start = (f32[16,2048]{1,0:T(8,128)S(1)}, f32[16,2048]{1,0:T(8,128)S(1)}, u32[]{:S(2)}, u32[]{:S(2)}) collective-permute-start(f32[16,2048]{1,0:T(8,128)S(1)} %get-tuple-element.27), channel_id=1, source_target_pairs={{0,1},{1,0},{2,3},{3,2},{4,5},{5,4},{6,7},{7,6},{8,9},{9,8},{10,11... | collective-permute-start | bytes 393224 | tf_op jit(solution)/shard_map/ppermute | solution.py:447
  2.3 1.3 %collective-permute-start.4 = (f32[296,128]{1,0:T(8,128)S(1)}, f32[296,128]{1,0:T(8,128)S(1)}, u32[]{:S(2)}, u32[]{:S(2)}) collective-permute-start(f32[296,128]{1,0:T(8,128)S(1)} %get-tuple-element.33), channel_id=1, source_target_pairs={{0,4},{1,5},{2,6},{3,7},{4,0},{5,1},{6,2},{7,3},{8,12},{9,13},{10,... | collective-permute-start | bytes 454664 | tf_op jit(solution)/shard_map/ppermute | solution.py:474
  3.6 0.0 collective-permute-done.second_ref
  3.7 1.3 %collective-permute-start.1 = (f32[16,1152]{1,0:T(8,128)S(1)}, f32[16,1152]{1,0:T(8,128)S(1)}, u32[]{:S(2)}, u32[]{:S(2)}) collective-permute-start(f32[16,1152]{1,0:T(8,128)S(1)} %get-tuple-element.29), channel_id=1, source_target_pairs={{0,2},{1,3},{2,0},{3,1},{4,6},{5,7},{6,4},{7,5},{8,10},{9,11},{10,... | collective-permute-start | bytes 221192 | tf_op jit(solution)/shard_map/ppermute | solution.py:447
  4.9 0.0 collective-permute-start.6
  5.0 1.5 %collective-permute-start.5 = (f32[2,90,128]{2,1,0:T(8,128)S(1)}, f32[2,90,128]{2,1,0:T(8,128)S(1)}, u32[]{:S(2)}, u32[]{:S(2)}) collective-permute-start(f32[2,90,128]{2,1,0:T(8,128)S(1)} %get-tuple-element.34), channel_id=1, source_target_pairs={{0,1},{1,0},{2,3},{3,2},{4,8},{5,9},{6,10},{7,11},{8,4},{9,5},{10,... | collective-permute-start | bytes 276488 | tf_op jit(solution)/shard_map/ppermute | solution.py:458
  6.4 0.8 %collective-permute-done.1.refs_1_ = f32[16,1152]{1,0:T(8,128)S(1)} collective-permute-done((f32[16,1152]{1,0:T(8,128)S(1)}, f32[16,1152]{1,0:T(8,128)S(1)}, u32[]{:S(2)}, u32[]{:S(2)}) %collective-permute-start.1) | collective-permute-done | bytes 73760 | tf_op jit(solution)/shard_map/ppermute | solution.py:447
  7.3 1.0 %collective-permute-start.2 = (f32[90,128]{1,0:T(8,128)S(1)}, f32[90,128]{1,0:T(8,128)S(1)}, u32[]{:S(2)}, u32[]{:S(2)}) collective-permute-start(f32[90,128]{1,0:T(8,128)S(1)} %get-tuple-element.31), channel_id=1, source_target_pairs={{0,4},{4,0},{8,12},{12,8},{1,5},{5,1},{9,13},{13,9},{2,6},{6,2},{1... | collective-permute-start | bytes 138248 | tf_op jit(solution)/shard_map/ppermute | solution.py:447
  8.3 0.3 collective-permute-start.3
  8.6 0.2 collective-permute-done.6.refs_1_
  8.8 0.0 collective-permute-done.4.refs_0_.shared_ref
  8.8 1.8 %shard_map.112 = (f32[2,16,1152]{2,1,0:T(8,128)S(1)}, f32[2,16,1152]{2,1,0:T(8,128)S(1)}) custom-call(f32[16,1152]{1,0:T(8,128)S(1)} %get-tuple-element.30.after_ref.own_ref, f32[296,128]{1,0:T(8,128)S(1)} %collective-permute-done.4.refs_0_.shared_ref, f32[2,104,128]{2,1,0:T(8,128)S(1)} %collective-permute-done.6.refs_1_, ...), custom_call_target="tpu_custom_call" | custom-call | flops 409600000 | bytes 102400000 | tf_op jit(solution)/shard_map/pallas_call | solution.py:535
  10.5 1.8 %collective-permute-done.5.odd_ref = f32[2,90,128]{2,1,0:T(8,128)S(1)} collective-permute-done((f32[2,90,128]{2,1,0:T(8,128)S(1)}, f32[2,90,128]{2,1,0:T(8,128)S(1)}, u32[]{:S(2)}, u32[]{:S(2)}) %collective-permute-start.5) | collective-permute-done | bytes 92192 | tf_op jit(solution)/shard_map/ppermute | solution.py:458
  12.3 0.0 collective-permute-done.2.refs_0_.even_ref
  12.3 1.1 %collective-permute-done.3.refs_1_.odd_ref = f32[90,128]{1,0:T(8,128)S(1)} collective-permute-done((f32[90,128]{1,0:T(8,128)S(1)}, f32[90,128]{1,0:T(8,128)S(1)}, u32[]{:S(2)}, u32[]{:S(2)}) %collective-permute-start.3) | collective-permute-done | bytes 46112 | tf_op jit(solution)/shard_map/ppermute | solution.py:458
  13.3 0.2 shard_map.113
  13.5 2.5 %collective-permute-start.7 = (f32[2,16,1152]{2,1,0:T(8,128)S(1)}, f32[2,16,1152]{2,1,0:T(8,128)S(1)}, u32[]{:S(2)}, u32[]{:S(2)}) collective-permute-start(f32[2,16,1152]{2,1,0:T(8,128)S(1)} %get-tuple-element.41), channel_id=1, source_target_pairs={{0,1},{1,0},{2,3},{3,2},{4,5},{5,4},{6,7},{7,6},{8,9},{9,8},{10,11... | collective-permute-start | bytes 442376 | tf_op jit(solution)/shard_map/ppermute | solution.py:447
  16.1 1.2 %shard_map.114.smooth_ref = f32[16,1152]{1,0:T(8,128)S(1)} custom-call(f32[16,1152]{1,0:T(8,128)S(1)} %get-tuple-element.30.after_ref.own_ref, f32[90,128]{1,0:T(8,128)S(1)} %collective-permute-done.2.refs_0_.even_ref, f32[90,128]{1,0:T(8,128)S(1)} %collective-permute-done.3.refs_1_.odd_ref, f32[5,40,1152]{2,1,0:T(8,128)S(1)} %get-tuple-element.39.coef_ref), custom_call_target="tpu_custom_call" | custom-call | flops 16384000 | bytes 4096000 | tf_op jit(solution)/shard_map/pallas_call | solution.py:555
  17.3 0.0 collective-permute-done.7.more_ref
  17.3 0.1 shard_map.115
  17.4 2.3 %collective-permute-start.8 = (f32[90,128]{1,0:T(8,128)S(1)}, f32[90,128]{1,0:T(8,128)S(1)}, u32[]{:S(2)}, u32[]{:S(2)}) collective-permute-start(f32[90,128]{1,0:T(8,128)S(1)} %get-tuple-element.43), channel_id=1, source_target_pairs={{0,4},{4,0},{8,12},{12,8},{1,5},{5,1},{9,13},{13,9},{2,6},{6,2},{1... | collective-permute-start | bytes 138248 | tf_op jit(solution)/shard_map/ppermute | solution.py:447
  19.7 0.0 collective-permute-start.9
  19.7 2.0 %collective-permute-done.8.even_ref = f32[90,128]{1,0:T(8,128)S(1)} collective-permute-done((f32[90,128]{1,0:T(8,128)S(1)}, f32[90,128]{1,0:T(8,128)S(1)}, u32[]{:S(2)}, u32[]{:S(2)}) %collective-permute-start.8) | collective-permute-done | bytes 46112 | tf_op jit(solution)/shard_map/ppermute | solution.py:447
  21.7 0.9 %collective-permute-done.9.odd_ref = f32[90,128]{1,0:T(8,128)S(1)} collective-permute-done((f32[90,128]{1,0:T(8,128)S(1)}, f32[90,128]{1,0:T(8,128)S(1)}, u32[]{:S(2)}, u32[]{:S(2)}) %collective-permute-start.9) | collective-permute-done | bytes 46112 | tf_op jit(solution)/shard_map/ppermute | solution.py:458
  22.6 1.2 %shard_map.116.refs_0_ = f32[16,1024]{1,0:T(8,128)S(1)} custom-call(f32[16,1152]{1,0:T(8,128)S(1)} %get-tuple-element.42.own_ref, f32[90,128]{1,0:T(8,128)S(1)} %collective-permute-done.8.even_ref, f32[90,128]{1,0:T(8,128)S(1)} %collective-permute-done.9.odd_ref, f32[5,40,1152]{2,1,0:T(8,128)S(1)} %get-tuple-element.39.coef_ref), custom_call_target="tpu_custom_call" | custom-call | flops 16384000 | bytes 4096000 | tf_op jit(solution)/shard_map/pallas_call | solution.py:566
  23.9 0.3 collective-permute-start.12
  24.2 2.9 %collective-permute-start.11 = (f32[16,1024]{1,0:T(8,128)S(1)}, f32[16,1024]{1,0:T(8,128)S(1)}, u32[]{:S(2)}, u32[]{:S(2)}) collective-permute-start(f32[16,1024]{1,0:T(8,128)S(1)} %shard_map.116.refs_0_), channel_id=1, source_target_pairs={{0,3},{1,2},{2,1},{3,0},{4,7},{5,6},{6,5},{7,4},{8,11},{9,10},{10,... | collective-permute-start | bytes 196616 | tf_op jit(solution)/shard_map/ppermute | solution.py:447
  27.1 0.0 collective-permute-start.10
  27.1 0.0 collective-permute-done.12.refs_3_
  27.1 3.3 %collective-permute-done.11.refs_2_ = f32[16,1024]{1,0:T(8,128)S(1)} collective-permute-done((f32[16,1024]{1,0:T(8,128)S(1)}, f32[16,1024]{1,0:T(8,128)S(1)}, u32[]{:S(2)}, u32[]{:S(2)}) %collective-permute-start.11) | collective-permute-done | bytes 65568 | tf_op jit(solution)/shard_map/ppermute | solution.py:447
  30.4 0.8 %shard_map.117 = f32[2,16,2048]{2,1,0:T(8,128)} custom-call(f32[2,2,8,128]{3,2,1,0:T(8,128)S(1)} %get-tuple-element.25.response_ref, f32[2,16,2048]{2,1,0:T(8,128)S(1)} %copy-done, f32[16,1024]{1,0:T(8,128)S(1)} %shard_map.116.refs_0_, f32[16,1024]{1,0:T(8,128)S(1)} %collective-permute-done.10.refs_1_, f32[16,1024]{1,0:T(8,128)S(1)} %collective-permute-done.11.refs_2_, ...), custom_call_target="tpu_custom_call" | custom-call | flops 4096000 | bytes 1024000 | tf_op jit(solution)/shard_map/pallas_call | solution.py:574
  (7 shorter events, 0.1 us)
Async XLA Ops:
  1.6 2.1 %collective-permute-start = (f32[16,2048]{1,0:T(8,128)S(1)}, f32[16,2048]{1,0:T(8,128)S(1)}, u32[]{:S(2)}, u32[]{:S(2)}) collective-permute-start(f32[16,2048]{1,0:T(8,128)S(1)} %get-tuple-element.27), channel_id=1, source_target_pairs={{0,1},{1,0},{2,3},{3,2},{4,5},{5,4},{6,7},{7,6},{8,9},{9,8},{10,11... | collective-permute-start | bytes 393224 | tf_op jit(solution)/shard_map/ppermute | solution.py:447
  2.3 6.4 %collective-permute-start.4 = (f32[296,128]{1,0:T(8,128)S(1)}, f32[296,128]{1,0:T(8,128)S(1)}, u32[]{:S(2)}, u32[]{:S(2)}) collective-permute-start(f32[296,128]{1,0:T(8,128)S(1)} %get-tuple-element.33), channel_id=1, source_target_pairs={{0,4},{1,5},{2,6},{3,7},{4,0},{5,1},{6,2},{7,3},{8,12},{9,13},{10,... | collective-permute-start | bytes 454664 | tf_op jit(solution)/shard_map/ppermute | solution.py:474
  3.7 3.6 %collective-permute-start.1 = (f32[16,1152]{1,0:T(8,128)S(1)}, f32[16,1152]{1,0:T(8,128)S(1)}, u32[]{:S(2)}, u32[]{:S(2)}) collective-permute-start(f32[16,1152]{1,0:T(8,128)S(1)} %get-tuple-element.29), channel_id=1, source_target_pairs={{0,2},{1,3},{2,0},{3,1},{4,6},{5,7},{6,4},{7,5},{8,10},{9,11},{10,... | collective-permute-start | bytes 221192 | tf_op jit(solution)/shard_map/ppermute | solution.py:447
  4.9 3.8 %collective-permute-start.6 = (f32[2,104,128]{2,1,0:T(8,128)S(1)}, f32[2,104,128]{2,1,0:T(8,128)S(1)}, u32[]{:S(2)}, u32[]{:S(2)}) collective-permute-start(f32[2,104,128]{2,1,0:T(8,128)S(1)} %get-tuple-element.36), channel_id=1, source_target_pairs={{0,8},{1,13},{2,10},{3,15},{4,12},{5,9},{6,14},{7,11},{8,0},{9,5},... | collective-permute-start | bytes 319496 | tf_op jit(solution)/shard_map/ppermute | solution.py:474
  5.0 7.3 %collective-permute-start.5 = (f32[2,90,128]{2,1,0:T(8,128)S(1)}, f32[2,90,128]{2,1,0:T(8,128)S(1)}, u32[]{:S(2)}, u32[]{:S(2)}) collective-permute-start(f32[2,90,128]{2,1,0:T(8,128)S(1)} %get-tuple-element.34), channel_id=1, source_target_pairs={{0,1},{1,0},{2,3},{3,2},{4,8},{5,9},{6,10},{7,11},{8,4},{9,5},{10,... | collective-permute-start | bytes 276488 | tf_op jit(solution)/shard_map/ppermute | solution.py:458
  7.3 5.0 %collective-permute-start.2 = (f32[90,128]{1,0:T(8,128)S(1)}, f32[90,128]{1,0:T(8,128)S(1)}, u32[]{:S(2)}, u32[]{:S(2)}) collective-permute-start(f32[90,128]{1,0:T(8,128)S(1)} %get-tuple-element.31), channel_id=1, source_target_pairs={{0,4},{4,0},{8,12},{12,8},{1,5},{5,1},{9,13},{13,9},{2,6},{6,2},{1... | collective-permute-start | bytes 138248 | tf_op jit(solution)/shard_map/ppermute | solution.py:447
  8.3 5.0 %collective-permute-start.3 = (f32[90,128]{1,0:T(8,128)S(1)}, f32[90,128]{1,0:T(8,128)S(1)}, u32[]{:S(2)}, u32[]{:S(2)}) collective-permute-start(f32[90,128]{1,0:T(8,128)S(1)} %get-tuple-element.32), channel_id=1, source_target_pairs={{0,1},{1,0},{2,3},{3,2},{4,8},{5,9},{6,10},{7,11},{8,4},{9,5},{10,... | collective-permute-start | bytes 138248 | tf_op jit(solution)/shard_map/ppermute | solution.py:458
  13.5 3.8 %collective-permute-start.7 = (f32[2,16,1152]{2,1,0:T(8,128)S(1)}, f32[2,16,1152]{2,1,0:T(8,128)S(1)}, u32[]{:S(2)}, u32[]{:S(2)}) collective-permute-start(f32[2,16,1152]{2,1,0:T(8,128)S(1)} %get-tuple-element.41), channel_id=1, source_target_pairs={{0,1},{1,0},{2,3},{3,2},{4,5},{5,4},{6,7},{7,6},{8,9},{9,8},{10,11... | collective-permute-start | bytes 442376 | tf_op jit(solution)/shard_map/ppermute | solution.py:447
  16.1 1.3 %copy-start.1 = (s32[16,2048]{1,0:T(8,128)S(1)}, s32[16,2048]{1,0:T(8,128)}, u32[]{:S(2)}) copy-start(s32[16,2048]{1,0:T(8,128)} %mask_ref.1) | copy-start | bytes 393220
  17.4 4.3 %collective-permute-start.8 = (f32[90,128]{1,0:T(8,128)S(1)}, f32[90,128]{1,0:T(8,128)S(1)}, u32[]{:S(2)}, u32[]{:S(2)}) collective-permute-start(f32[90,128]{1,0:T(8,128)S(1)} %get-tuple-element.43), channel_id=1, source_target_pairs={{0,4},{4,0},{8,12},{12,8},{1,5},{5,1},{9,13},{13,9},{2,6},{6,2},{1... | collective-permute-start | bytes 138248 | tf_op jit(solution)/shard_map/ppermute | solution.py:447
  19.7 2.9 %collective-permute-start.9 = (f32[90,128]{1,0:T(8,128)S(1)}, f32[90,128]{1,0:T(8,128)S(1)}, u32[]{:S(2)}, u32[]{:S(2)}) collective-permute-start(f32[90,128]{1,0:T(8,128)S(1)} %get-tuple-element.44), channel_id=1, source_target_pairs={{0,1},{1,0},{2,3},{3,2},{4,8},{5,9},{6,10},{7,11},{8,4},{9,5},{10,... | collective-permute-start | bytes 138248 | tf_op jit(solution)/shard_map/ppermute | solution.py:458
  22.6 7.8 %copy-start = (f32[2,16,2048]{2,1,0:T(8,128)S(1)}, f32[2,16,2048]{2,1,0:T(8,128)}, u32[]{:S(2)}) copy-start(f32[2,16,2048]{2,1,0:T(8,128)} %control_ref.1) | copy-start | bytes 786436
  23.9 3.2 %collective-permute-start.12 = (f32[16,1024]{1,0:T(8,128)S(1)}, f32[16,1024]{1,0:T(8,128)S(1)}, u32[]{:S(2)}, u32[]{:S(2)}) collective-permute-start(f32[16,1024]{1,0:T(8,128)S(1)} %shard_map.116.refs_0_), channel_id=1, source_target_pairs={{0,2},{1,3},{2,0},{3,1},{4,6},{5,7},{6,4},{7,5},{8,10},{9,11},{10,... | collective-permute-start | bytes 196616 | tf_op jit(solution)/shard_map/ppermute | solution.py:447
  24.2 6.2 %collective-permute-start.11 = (f32[16,1024]{1,0:T(8,128)S(1)}, f32[16,1024]{1,0:T(8,128)S(1)}, u32[]{:S(2)}, u32[]{:S(2)}) collective-permute-start(f32[16,1024]{1,0:T(8,128)S(1)} %shard_map.116.refs_0_), channel_id=1, source_target_pairs={{0,3},{1,2},{2,1},{3,0},{4,7},{5,6},{6,5},{7,4},{8,11},{9,10},{10,... | collective-permute-start | bytes 196616 | tf_op jit(solution)/shard_map/ppermute | solution.py:447
  27.1 3.3 %collective-permute-start.10 = (f32[16,1024]{1,0:T(8,128)S(1)}, f32[16,1024]{1,0:T(8,128)S(1)}, u32[]{:S(2)}, u32[]{:S(2)}) collective-permute-start(f32[16,1024]{1,0:T(8,128)S(1)} %shard_map.116.refs_0_), channel_id=1, source_target_pairs={{0,1},{1,0},{2,3},{3,2},{4,5},{5,4},{6,7},{7,6},{8,9},{9,8},{10,11... | collective-permute-start | bytes 196616 | tf_op jit(solution)/shard_map/ppermute | solution.py:447

commit v13 on v9

--- a/solution.py
+++ b/solution.py
@@ -21,12 +21,12 @@
     return pltpu.with_memory_space_constraint(values, pltpu.HBM)
 
 
-def call(body, outs, ins, scratch=(), limit=16, cost=None):
+def call(body, outs, ins, scratch=(), limit=16, cost=None, space=None):
     return pl.pallas_call(
         body,
         out_shape=outs,
         in_specs=ins,
-        out_specs=[VMEM] * len(outs),
+        out_specs=[space or VMEM] * len(outs),
         scratch_shapes=list(scratch),
         compiler_params=pltpu.CompilerParams(vmem_limit_bytes=limit << 20),
         cost_estimate=cost,
@@ -165,20 +165,20 @@
 
 
 def scatter_kernel(slots, blocks_all, after_ref, *refs):
-    got_refs, (own_ref, other_ref, acc_ref, meta_ref, sems) = refs[:-5], refs[-5:]
+    got_refs, (own_ref, other_ref, acc_ref, meta_ref, where_ref, sems) = refs[:-6], refs[-6:]
     core = lax.axis_index("var") % 2
     got_refs = [r.at[i] for r in got_refs[1:-1] for i in (0, 1)] + [got_refs[0], got_refs[-1]]
     size_of_group = min(GROUP, slots)
-    copies = [
-        pltpu.make_async_copy(ref.at[pl.ds(3 * slots, 8)], meta_ref.at[pl.ds(8 * s, 8)], sems.at[s])
-        for s, ref in enumerate(got_refs)
-    ]
-    for copy in copies:
-        copy.start()
     rows = own_ref.shape[1]
     start, size = window_of(my_chip(), chip_count(), blocks_all)
     per_kind = padded_blocks(size)
     tall = 2 * per_kind
+    line = lax.broadcasted_iota(jnp.int32, (8, LANES), 0)
+    for s, ref in enumerate(got_refs):
+        facts = ref[3 * slots : 3 * slots + 8].astype(jnp.int32)
+        where_ref[8 * s : 8 * s + 8] = jnp.where(line == 0, (facts[1:2] * rows + facts[0:1]) * tall, facts)
+    copy = pltpu.make_async_copy(where_ref, meta_ref, sems.at[0])
+    copy.start()
     acc_ref[...] = jnp.zeros(acc_ref.shape, F32)
     place = lax.broadcasted_iota(jnp.int32, (tall, LANES), 0)
     is_weight = place < per_kind
@@ -187,12 +187,11 @@
     one, zero = jnp.bfloat16(1), jnp.bfloat16(0)
     sub = lax.broadcasted_iota(jnp.int32, (size_of_group, LANES), 0)
     blank = jnp.zeros((2 * tall, LANES), jnp.bfloat16)
-    for copy in copies:
-        copy.wait()
+    copy.wait()
 
     def load(s, base):
         got_ref = got_refs[s]
-        count = meta_ref[8 * s + 2, s].astype(jnp.int32)
+        count = meta_ref[8 * s + 2, s]
         value = got_ref[pl.ds(base, size_of_group), :]
         weight = got_ref[pl.ds(slots + base, size_of_group), :]
         cell = got_ref[pl.ds(2 * slots + base, size_of_group), :].astype(jnp.int32)
@@ -229,9 +228,7 @@
                     preferred_element_type=F32,
                 )
                 for i, s in enumerate(pair):
-                    row = meta_ref[8 * s, s * slots + base + k].astype(jnp.int32)
-                    sensor = meta_ref[8 * s + 1, s * slots + base + k].astype(jnp.int32)
-                    at = pl.multiple_of((sensor * rows + row) * tall, 8)
+                    at = pl.multiple_of(meta_ref[8 * s, s * slots + base + k], 8)
                     mine = both[2 * i * tall : 2 * (i + 1) * tall]
                     acc_ref[pl.ds(at, tall), :] += mine[:tall] + mine[tall:]
         return carry
@@ -241,7 +238,7 @@
         most = meta_ref[8 * s + 2, s]
         for other in chosen[1:]:
             most = jnp.maximum(most, meta_ref[8 * other + 2, other])
-        turns = (most.astype(jnp.int32) + size_of_group - 1) // size_of_group
+        turns = (most + size_of_group - 1) // size_of_group
         lax.fori_loop(0, turns, functools.partial(step, chosen), 0)
     for sensor, out_ref in ((core, own_ref), (1 - core, other_ref)):
         begin = sensor * rows * tall
@@ -425,15 +422,21 @@
 
 
 def result_kernel(response_ref, control_ref, *refs):
-    own, out_ref = refs[0].shape[1] // LANES, refs[-1]
-    refs = [refs[sent_last(len(refs) - 1).index(d)] for d in range(len(refs) - 1)]
-    for d in range(len(refs) // 2):
-        window = lanes((my_chip() ^ d) * own, own)
-        for v in range(control_ref.shape[0]):
-            mine, theirs = (response_ref[i, v][:1, :1] for i in range(2))
-            out_ref[v, :, window] = (
+    refs, (out_ref, line_ref, sems) = refs[:-3], refs[-3:]
+    own = refs[0].shape[1] // LANES
+    refs = [refs[sent_last(len(refs)).index(d)] for d in range(len(refs))]
+    copies = []
+    for v in range(control_ref.shape[0]):
+        mine, theirs = (response_ref[i, v][:1, :1] for i in range(2))
+        for d in range(len(refs) // 2):
+            window = lanes((my_chip() ^ d) * own, own)
+            line_ref[v, :, window] = (
                 control_ref[v, :, window] + mine * refs[2 * d][...] + theirs * refs[2 * d + 1][...]
             )
+        copies.append(pltpu.make_async_copy(line_ref.at[v], out_ref.at[v], sems.at[v]))
+        copies[-1].start()
+    for copy in copies:
+        copy.wait()
 
 
 def swap(values, axis, bit):
@@ -524,8 +527,9 @@
         [AFTER] + [VMEM] * len(got),
         [
             pltpu.VMEM((2 * rows * 2 * padded_blocks(size), LANES), F32),
-            pltpu.SMEM((8 * tiles, LANES), F32),
-            pltpu.SemaphoreType.DMA((tiles,)),
+            pltpu.SMEM((8 * tiles, LANES), jnp.int32),
+            pltpu.VMEM((8 * tiles, LANES), jnp.int32),
+            pltpu.SemaphoreType.DMA((1,)),
         ],
         cost=cost(100000),
     )(smooth_in, got[-2], *got[:-2], got[-1])
@@ -561,7 +565,9 @@
         result_kernel,
         [jax.ShapeDtypeStruct(control.shape, F32)],
         [VMEM] * (2 + members),
+        [pltpu.VMEM(control.shape, F32), pltpu.SemaphoreType.DMA((var_dev,))],
         cost=cost(1000),
+        space=HBM,
     )(responses, control, *shares)
     return out
 

time: 29.3 us -> 29.3 us (level)
  no operation moved by 1% of the time
where the time goes in v13:
time: 29.3 us; the launch traced here: 29.1 us
  starting transfers between devices  13.7 us (47%)
  Pallas kernels  7.71 us (26%)
  waiting for transfers between devices  7.56 us (26%)
    ppermute x9, starting transfers between devices, swap(): return lax.ppermute(values, axis, [(i, i ^ bit) for i in range(count)])  8 us
    ppermute x9, waiting for transfers between devices, swap(): return lax.ppermute(values, axis, [(i, i ^ bit) for i in range(count)])  6.9 us
    ppermute x2, starting transfers between devices, deliver(): got.append(lax.ppermute(chunk, ('tile', 'var'), pairs))  5.23 us
    pallas_call x1, Pallas kernels, local(): call(functools.partial(scatter_kernel, slots, blocks), [view2, view2], [A...  2.57 us
    pallas_call x1, Pallas kernels, local(): call(functools.partial(first_kernel, slots, margin), [field, field, jax.S...  1.58 us
    pallas_call x1, Pallas kernels, local(): call(functools.partial(spread_kernel, margin), [share], [VMEM] * 4, [ring...  1.25 us
    pallas_call x1, Pallas kernels, local(): call(functools.partial(smooth_kernel, margin), [view], [VMEM] * 4, [ring]...  1.25 us
    pallas_call x1, Pallas kernels, local(): call(result_kernel, [jax.ShapeDtypeStruct(control.shape, F32)], [VMEM] *...  0.77 us
  transfers between devices with their start and end apart: 14, of which 6 were waited for; matrix products, arithmetic and copies ran while one was open for 0% of the time, Pallas kernels for 13%

profile of v13, /device:TPU:0, one launch (start us, length us, event | category | flops | bytes accessed | tf_op | source)
XLA Modules:
  0.0 29.1 jit_solution(17089159892741539927)
XLA Ops:
  0.0 1.6 %shard_map.109 = (f32[16,2048]{1,0:T(8,128)S(1)}, f32[16,2048]{1,0:T(8,128)S(1)}, f32[2,2,8,128]{3,2,1,0:T(8,128)S(1)}, f32[2,16,1152]{2,1,0:T(8,128)S(1)}, f32[...) custom-call(f32[2,8]{1,0:T(2,128)} %sens_hbm.1, ...), custom_call_target="tpu_custom_call" | custom-call | flops 12288000 | bytes 3072000 | tf_op jit(solution)/shard_map/pallas_call | solution.py:493
  1.6 0.5 %collective-permute-start = (f32[16,2048]{1,0:T(8,128)S(1)}, f32[16,2048]{1,0:T(8,128)S(1)}, u32[]{:S(2)}, u32[]{:S(2)}) collective-permute-start(f32[16,2048]{1,0:T(8,128)S(1)} %get-tuple-element.28), channel_id=1, source_target_pairs={{0,1},{1,0},{2,3},{3,2},{4,5},{5,4},{6,7},{7,6},{8,9},{9,8},{10,11... | collective-permute-start | bytes 393224 | tf_op jit(solution)/shard_map/ppermute | solution.py:444
  2.1 3.7 %collective-permute-start.7 = (f32[2,104,128]{2,1,0:T(8,128)S(1)}, f32[2,104,128]{2,1,0:T(8,128)S(1)}, u32[]{:S(2)}, u32[]{:S(2)}) collective-permute-start(f32[2,104,128]{2,1,0:T(8,128)S(1)} %get-tuple-element.38), channel_id=1, source_target_pairs={{0,8},{1,13},{2,10},{3,15},{4,12},{5,9},{6,14},{7,11},{8,0},{9,5},... | collective-permute-start | bytes 319496 | tf_op jit(solution)/shard_map/ppermute | solution.py:467
  5.8 1.6 %collective-permute-start.1 = (f32[16,1152]{1,0:T(8,128)S(1)}, f32[16,1152]{1,0:T(8,128)S(1)}, u32[]{:S(2)}, u32[]{:S(2)}) collective-permute-start(f32[16,1152]{1,0:T(8,128)S(1)} %get-tuple-element.30), channel_id=1, source_target_pairs={{0,2},{1,3},{2,0},{3,1},{4,6},{5,7},{6,4},{7,5},{8,10},{9,11},{10,... | collective-permute-start | bytes 221192 | tf_op jit(solution)/shard_map/ppermute | solution.py:444
  7.4 1.6 %collective-permute-start.6 = (f32[104,128]{1,0:T(8,128)S(1)}, f32[104,128]{1,0:T(8,128)S(1)}, u32[]{:S(2)}, u32[]{:S(2)}) collective-permute-start(f32[104,128]{1,0:T(8,128)S(1)} %get-tuple-element.37), channel_id=1, source_target_pairs={{0,4},{1,5},{2,6},{3,7},{4,0},{5,1},{6,2},{7,3},{8,12},{9,13},{10,... | collective-permute-start | bytes 159752 | tf_op jit(solution)/shard_map/ppermute | solution.py:467
  8.9 0.4 %collective-permute-start.4 = (f32[2,90,128]{2,1,0:T(8,128)S(1)}, f32[2,90,128]{2,1,0:T(8,128)S(1)}, u32[]{:S(2)}, u32[]{:S(2)}) collective-permute-start(f32[2,90,128]{2,1,0:T(8,128)S(1)} %get-tuple-element.34), channel_id=1, source_target_pairs={{0,4},{4,0},{8,12},{12,8},{1,5},{5,1},{9,13},{13,9},{2,6},{6,2},{1... | collective-permute-start | bytes 276488 | tf_op jit(solution)/shard_map/ppermute | solution.py:444
  9.4 0.3 %collective-permute-start.5 = (f32[2,90,128]{2,1,0:T(8,128)S(1)}, f32[2,90,128]{2,1,0:T(8,128)S(1)}, u32[]{:S(2)}, u32[]{:S(2)}) collective-permute-start(f32[2,90,128]{2,1,0:T(8,128)S(1)} %get-tuple-element.35), channel_id=1, source_target_pairs={{0,1},{1,0},{2,3},{3,2},{4,8},{5,9},{6,10},{7,11},{8,4},{9,5},{10,... | collective-permute-start | bytes 276488 | tf_op jit(solution)/shard_map/ppermute | solution.py:455
  9.7 1.1 %collective-permute-done.1.refs_1_ = f32[16,1152]{1,0:T(8,128)S(1)} collective-permute-done((f32[16,1152]{1,0:T(8,128)S(1)}, f32[16,1152]{1,0:T(8,128)S(1)}, u32[]{:S(2)}, u32[]{:S(2)}) %collective-permute-start.1) | collective-permute-done | bytes 73760 | tf_op jit(solution)/shard_map/ppermute | solution.py:444
  10.8 1.1 %collective-permute-start.2 = (f32[90,128]{1,0:T(8,128)S(1)}, f32[90,128]{1,0:T(8,128)S(1)}, u32[]{:S(2)}, u32[]{:S(2)}) collective-permute-start(f32[90,128]{1,0:T(8,128)S(1)} %get-tuple-element.32), channel_id=1, source_target_pairs={{0,4},{4,0},{8,12},{12,8},{1,5},{5,1},{9,13},{13,9},{2,6},{6,2},{1... | collective-permute-start | bytes 138248 | tf_op jit(solution)/shard_map/ppermute | solution.py:444
  11.9 0.6 %collective-permute-done.6.refs_0_ = f32[104,128]{1,0:T(8,128)S(1)} collective-permute-done((f32[104,128]{1,0:T(8,128)S(1)}, f32[104,128]{1,0:T(8,128)S(1)}, u32[]{:S(2)}, u32[]{:S(2)}) %collective-permute-start.6) | collective-permute-done | bytes 53280 | tf_op jit(solution)/shard_map/ppermute | solution.py:467
  12.5 0.0 collective-permute-start.3
  12.6 0.0 collective-permute-done.7.refs_1_
  12.6 2.6 %shard_map.112 = (f32[2,16,1152]{2,1,0:T(8,128)S(1)}, f32[2,16,1152]{2,1,0:T(8,128)S(1)}) custom-call(f32[16,1152]{1,0:T(8,128)S(1)} %get-tuple-element.31.after_ref.own_ref, f32[104,128]{1,0:T(8,128)S(1)} %collective-permute-done.6.refs_0_, f32[2,104,128]{2,1,0:T(8,128)S(1)} %collective-permute-done.7.refs_1_, f32[104,128]{1,0:T(8,128)S(1)} %get-tuple-element.39.refs_2_), custom_call_target="tpu_custom_call" | custom-call | flops 409600000 | bytes 102400000 | tf_op jit(solution)/shard_map/pallas_call | solution.py:524
  15.2 0.0 collective-permute-done.4.even_ref
  15.2 0.0 collective-permute-done.5.odd_ref
  15.2 0.5 %collective-permute-done.2.refs_0_.even_ref = f32[90,128]{1,0:T(8,128)S(1)} collective-permute-done((f32[90,128]{1,0:T(8,128)S(1)}, f32[90,128]{1,0:T(8,128)S(1)}, u32[]{:S(2)}, u32[]{:S(2)}) %collective-permute-start.2) | collective-permute-done | bytes 46112 | tf_op jit(solution)/shard_map/ppermute | solution.py:444
  15.7 0.0 collective-permute-done.3.refs_1_.odd_ref
  15.7 0.2 shard_map.113
  15.9 0.1 collective-permute-start.8
  16.0 1.2 %shard_map.114.smooth_ref = f32[16,1152]{1,0:T(8,128)S(1)} custom-call(f32[16,1152]{1,0:T(8,128)S(1)} %get-tuple-element.31.after_ref.own_ref, f32[90,128]{1,0:T(8,128)S(1)} %collective-permute-done.2.refs_0_.even_ref, f32[90,128]{1,0:T(8,128)S(1)} %collective-permute-done.3.refs_1_.odd_ref, f32[5,40,1152]{2,1,0:T(8,128)S(1)} %get-tuple-element.41.coef_ref), custom_call_target="tpu_custom_call" | custom-call | flops 16384000 | bytes 4096000 | tf_op jit(solution)/shard_map/pallas_call | solution.py:545
  17.3 0.0 collective-permute-done.8.more_ref
  17.4 2.0 %collective-permute-start.9 = (f32[90,128]{1,0:T(8,128)S(1)}, f32[90,128]{1,0:T(8,128)S(1)}, u32[]{:S(2)}, u32[]{:S(2)}) collective-permute-start(f32[90,128]{1,0:T(8,128)S(1)} %get-tuple-element.45), channel_id=1, source_target_pairs={{0,4},{4,0},{8,12},{12,8},{1,5},{5,1},{9,13},{13,9},{2,6},{6,2},{1... | collective-permute-start | bytes 138248 | tf_op jit(solution)/shard_map/ppermute | solution.py:444
  19.4 0.1 collective-permute-start.10
  19.6 2.2 %collective-permute-done.9.even_ref = f32[90,128]{1,0:T(8,128)S(1)} collective-permute-done((f32[90,128]{1,0:T(8,128)S(1)}, f32[90,128]{1,0:T(8,128)S(1)}, u32[]{:S(2)}, u32[]{:S(2)}) %collective-permute-start.9) | collective-permute-done | bytes 46112 | tf_op jit(solution)/shard_map/ppermute | solution.py:444
  21.7 1.2 %shard_map.116.refs_0_ = f32[16,1024]{1,0:T(8,128)S(1)} custom-call(f32[16,1152]{1,0:T(8,128)S(1)} %get-tuple-element.44.own_ref, f32[90,128]{1,0:T(8,128)S(1)} %collective-permute-done.9.even_ref, f32[90,128]{1,0:T(8,128)S(1)} %collective-permute-done.10.odd_ref, f32[5,40,1152]{2,1,0:T(8,128)S(1)} %get-tuple-element.41.coef_ref), custom_call_target="tpu_custom_call" | custom-call | flops 16384000 | bytes 4096000 | tf_op jit(solution)/shard_map/pallas_call | solution.py:556
  23.0 0.9 %collective-permute-start.13 = (f32[16,1024]{1,0:T(8,128)S(1)}, f32[16,1024]{1,0:T(8,128)S(1)}, u32[]{:S(2)}, u32[]{:S(2)}) collective-permute-start(f32[16,1024]{1,0:T(8,128)S(1)} %shard_map.116.refs_0_), channel_id=1, source_target_pairs={{0,2},{1,3},{2,0},{3,1},{4,6},{5,7},{6,4},{7,5},{8,10},{9,11},{10,... | collective-permute-start | bytes 196616 | tf_op jit(solution)/shard_map/ppermute | solution.py:444
  23.9 0.3 collective-permute-start.12
  24.2 1.0 %collective-permute-start.11 = (f32[16,1024]{1,0:T(8,128)S(1)}, f32[16,1024]{1,0:T(8,128)S(1)}, u32[]{:S(2)}, u32[]{:S(2)}) collective-permute-start(f32[16,1024]{1,0:T(8,128)S(1)} %shard_map.116.refs_0_), channel_id=1, source_target_pairs={{0,1},{1,0},{2,3},{3,2},{4,5},{5,4},{6,7},{7,6},{8,9},{9,8},{10,11... | collective-permute-start | bytes 196616 | tf_op jit(solution)/shard_map/ppermute | solution.py:444
  25.2 2.5 %collective-permute-done.13.refs_3_ = f32[16,1024]{1,0:T(8,128)S(1)} collective-permute-done((f32[16,1024]{1,0:T(8,128)S(1)}, f32[16,1024]{1,0:T(8,128)S(1)}, u32[]{:S(2)}, u32[]{:S(2)}) %collective-permute-start.13) | collective-permute-done | bytes 65568 | tf_op jit(solution)/shard_map/ppermute | solution.py:444
  27.8 0.6 %collective-permute-done.12.refs_2_ = f32[16,1024]{1,0:T(8,128)S(1)} collective-permute-done((f32[16,1024]{1,0:T(8,128)S(1)}, f32[16,1024]{1,0:T(8,128)S(1)}, u32[]{:S(2)}, u32[]{:S(2)}) %collective-permute-start.12) | collective-permute-done | bytes 65568 | tf_op jit(solution)/shard_map/ppermute | solution.py:444
  28.3 0.0 collective-permute-done.11.refs_1_
  28.3 0.8 %shard_map.117 = f32[2,16,2048]{2,1,0:T(8,128)} custom-call(f32[2,2,8,128]{3,2,1,0:T(8,128)S(1)} %get-tuple-element.26.response_ref, f32[2,16,2048]{2,1,0:T(8,128)S(1)} %copy-done, f32[16,1024]{1,0:T(8,128)S(1)} %shard_map.116.refs_0_, f32[16,1024]{1,0:T(8,128)S(1)} %collective-permute-done.11.refs_1_, f32[16,1024]{1,0:T(8,128)S(1)} %collective-permute-done.12.refs_2_, ...), custom_call_target="tpu_custom_call" | custom-call | flops 4096000 | bytes 1024000 | tf_op jit(solution)/shard_map/pallas_call | solution.py:564
  (9 shorter events, 0.1 us)
Async XLA Ops:
  1.6 4.2 %collective-permute-start = (f32[16,2048]{1,0:T(8,128)S(1)}, f32[16,2048]{1,0:T(8,128)S(1)}, u32[]{:S(2)}, u32[]{:S(2)}) collective-permute-start(f32[16,2048]{1,0:T(8,128)S(1)} %get-tuple-element.28), channel_id=1, source_target_pairs={{0,1},{1,0},{2,3},{3,2},{4,5},{5,4},{6,7},{7,6},{8,9},{9,8},{10,11... | collective-permute-start | bytes 393224 | tf_op jit(solution)/shard_map/ppermute | solution.py:444
  2.1 10.5 %collective-permute-start.7 = (f32[2,104,128]{2,1,0:T(8,128)S(1)}, f32[2,104,128]{2,1,0:T(8,128)S(1)}, u32[]{:S(2)}, u32[]{:S(2)}) collective-permute-start(f32[2,104,128]{2,1,0:T(8,128)S(1)} %get-tuple-element.38), channel_id=1, source_target_pairs={{0,8},{1,13},{2,10},{3,15},{4,12},{5,9},{6,14},{7,11},{8,0},{9,5},... | collective-permute-start | bytes 319496 | tf_op jit(solution)/shard_map/ppermute | solution.py:467
  5.8 5.0 %collective-permute-start.1 = (f32[16,1152]{1,0:T(8,128)S(1)}, f32[16,1152]{1,0:T(8,128)S(1)}, u32[]{:S(2)}, u32[]{:S(2)}) collective-permute-start(f32[16,1152]{1,0:T(8,128)S(1)} %get-tuple-element.30), channel_id=1, source_target_pairs={{0,2},{1,3},{2,0},{3,1},{4,6},{5,7},{6,4},{7,5},{8,10},{9,11},{10,... | collective-permute-start | bytes 221192 | tf_op jit(solution)/shard_map/ppermute | solution.py:444
  7.4 5.2 %collective-permute-start.6 = (f32[104,128]{1,0:T(8,128)S(1)}, f32[104,128]{1,0:T(8,128)S(1)}, u32[]{:S(2)}, u32[]{:S(2)}) collective-permute-start(f32[104,128]{1,0:T(8,128)S(1)} %get-tuple-element.37), channel_id=1, source_target_pairs={{0,4},{1,5},{2,6},{3,7},{4,0},{5,1},{6,2},{7,3},{8,12},{9,13},{10,... | collective-permute-start | bytes 159752 | tf_op jit(solution)/shard_map/ppermute | solution.py:467
  8.9 6.2 %collective-permute-start.4 = (f32[2,90,128]{2,1,0:T(8,128)S(1)}, f32[2,90,128]{2,1,0:T(8,128)S(1)}, u32[]{:S(2)}, u32[]{:S(2)}) collective-permute-start(f32[2,90,128]{2,1,0:T(8,128)S(1)} %get-tuple-element.34), channel_id=1, source_target_pairs={{0,4},{4,0},{8,12},{12,8},{1,5},{5,1},{9,13},{13,9},{2,6},{6,2},{1... | collective-permute-start | bytes 276488 | tf_op jit(solution)/shard_map/ppermute | solution.py:444
  9.4 5.8 %collective-permute-start.5 = (f32[2,90,128]{2,1,0:T(8,128)S(1)}, f32[2,90,128]{2,1,0:T(8,128)S(1)}, u32[]{:S(2)}, u32[]{:S(2)}) collective-permute-start(f32[2,90,128]{2,1,0:T(8,128)S(1)} %get-tuple-element.35), channel_id=1, source_target_pairs={{0,1},{1,0},{2,3},{3,2},{4,8},{5,9},{6,10},{7,11},{8,4},{9,5},{10,... | collective-permute-start | bytes 276488 | tf_op jit(solution)/shard_map/ppermute | solution.py:455
  10.8 4.8 %collective-permute-start.2 = (f32[90,128]{1,0:T(8,128)S(1)}, f32[90,128]{1,0:T(8,128)S(1)}, u32[]{:S(2)}, u32[]{:S(2)}) collective-permute-start(f32[90,128]{1,0:T(8,128)S(1)} %get-tuple-element.32), channel_id=1, source_target_pairs={{0,4},{4,0},{8,12},{12,8},{1,5},{5,1},{9,13},{13,9},{2,6},{6,2},{1... | collective-permute-start | bytes 138248 | tf_op jit(solution)/shard_map/ppermute | solution.py:444
  12.5 3.1 %collective-permute-start.3 = (f32[90,128]{1,0:T(8,128)S(1)}, f32[90,128]{1,0:T(8,128)S(1)}, u32[]{:S(2)}, u32[]{:S(2)}) collective-permute-start(f32[90,128]{1,0:T(8,128)S(1)} %get-tuple-element.33), channel_id=1, source_target_pairs={{0,1},{1,0},{2,3},{3,2},{4,8},{5,9},{6,10},{7,11},{8,4},{9,5},{10,... | collective-permute-start | bytes 138248 | tf_op jit(solution)/shard_map/ppermute | solution.py:455
  15.9 1.4 %collective-permute-start.8 = (f32[2,16,1152]{2,1,0:T(8,128)S(1)}, f32[2,16,1152]{2,1,0:T(8,128)S(1)}, u32[]{:S(2)}, u32[]{:S(2)}) collective-permute-start(f32[2,16,1152]{2,1,0:T(8,128)S(1)} %get-tuple-element.43), channel_id=1, source_target_pairs={{0,1},{1,0},{2,3},{3,2},{4,5},{5,4},{6,7},{7,6},{8,9},{9,8},{10,11... | collective-permute-start | bytes 442376 | tf_op jit(solution)/shard_map/ppermute | solution.py:444
  16.0 1.3 %copy-start.1 = (s32[16,2048]{1,0:T(8,128)S(1)}, s32[16,2048]{1,0:T(8,128)}, u32[]{:S(2)}) copy-start(s32[16,2048]{1,0:T(8,128)} %mask_ref.1) | copy-start | bytes 393220
  17.4 4.4 %collective-permute-start.9 = (f32[90,128]{1,0:T(8,128)S(1)}, f32[90,128]{1,0:T(8,128)S(1)}, u32[]{:S(2)}, u32[]{:S(2)}) collective-permute-start(f32[90,128]{1,0:T(8,128)S(1)} %get-tuple-element.45), channel_id=1, source_target_pairs={{0,4},{4,0},{8,12},{12,8},{1,5},{5,1},{9,13},{13,9},{2,6},{6,2},{1... | collective-permute-start | bytes 138248 | tf_op jit(solution)/shard_map/ppermute | solution.py:444
  19.4 2.3 %collective-permute-start.10 = (f32[90,128]{1,0:T(8,128)S(1)}, f32[90,128]{1,0:T(8,128)S(1)}, u32[]{:S(2)}, u32[]{:S(2)}) collective-permute-start(f32[90,128]{1,0:T(8,128)S(1)} %get-tuple-element.46), channel_id=1, source_target_pairs={{0,1},{1,0},{2,3},{3,2},{4,8},{5,9},{6,10},{7,11},{8,4},{9,5},{10,... | collective-permute-start | bytes 138248 | tf_op jit(solution)/shard_map/ppermute | solution.py:455
  21.7 6.6 %copy-start = (f32[2,16,2048]{2,1,0:T(8,128)S(1)}, f32[2,16,2048]{2,1,0:T(8,128)}, u32[]{:S(2)}) copy-start(f32[2,16,2048]{2,1,0:T(8,128)} %control_ref.1) | copy-start | bytes 786436
  23.0 4.8 %collective-permute-start.13 = (f32[16,1024]{1,0:T(8,128)S(1)}, f32[16,1024]{1,0:T(8,128)S(1)}, u32[]{:S(2)}, u32[]{:S(2)}) collective-permute-start(f32[16,1024]{1,0:T(8,128)S(1)} %shard_map.116.refs_0_), channel_id=1, source_target_pairs={{0,2},{1,3},{2,0},{3,1},{4,6},{5,7},{6,4},{7,5},{8,10},{9,11},{10,... | collective-permute-start | bytes 196616 | tf_op jit(solution)/shard_map/ppermute | solution.py:444
  23.9 4.4 %collective-permute-start.12 = (f32[16,1024]{1,0:T(8,128)S(1)}, f32[16,1024]{1,0:T(8,128)S(1)}, u32[]{:S(2)}, u32[]{:S(2)}) collective-permute-start(f32[16,1024]{1,0:T(8,128)S(1)} %shard_map.116.refs_0_), channel_id=1, source_target_pairs={{0,3},{1,2},{2,1},{3,0},{4,7},{5,6},{6,5},{7,4},{8,11},{9,10},{10,... | collective-permute-start | bytes 196616 | tf_op jit(solution)/shard_map/ppermute | solution.py:444
  24.2 4.1 %collective-permute-start.11 = (f32[16,1024]{1,0:T(8,128)S(1)}, f32[16,1024]{1,0:T(8,128)S(1)}, u32[]{:S(2)}, u32[]{:S(2)}) collective-permute-start(f32[16,1024]{1,0:T(8,128)S(1)} %shard_map.116.refs_0_), channel_id=1, source_target_pairs={{0,1},{1,0},{2,3},{3,2},{4,5},{5,4},{6,7},{7,6},{8,9},{9,8},{10,11... | collective-permute-start | bytes 196616 | tf_op jit(solution)/shard_map/ppermute | solution.py:444

commit v14 on v13

--- a/solution.py
+++ b/solution.py
@@ -70,8 +70,8 @@
 
 
 def first_kernel(slots, margin, sens_hbm, factor_hbm, control_hbm, kappa_hbm, tile_hbm, row_hbm, sensor_hbm,
-                 value_hbm, weight_hbm, cols_hbm, own_ref, other_ref, response_ref, kappa_ref, even_ref,
-                 odd_ref, *refs):
+                 value_hbm, weight_hbm, cols_hbm, own_ref, other_ref, response_ref, kappa_ref, odd_ref,
+                 *refs):
     chunk_refs = refs[:-11]
     (sens_ref, factor_ref, control_ref, tile_ref, row_ref, sensor_ref, value_ref, weight_ref, cols_ref,
      before_ref, sems) = refs[-11:]
@@ -103,7 +103,8 @@
         out_ref[...] = total
 
     for i in range(2):
-        pack_edges(even_ref.at[i], odd_ref.at[i], kappa_ref[i], margin)
+        even_ref = even_kappa(chunk_refs[-2], slots, odd_ref.shape[1], i)
+        pack_edges(even_ref, odd_ref.at[i], kappa_ref[i], margin)
 
     tiles = lax.axis_size("tile")
     full = tiles // 2 - 1
@@ -149,7 +150,7 @@
         out_ref = chunk_refs[i // 2].at[i % 2] if i < 2 * full else chunk_refs[i - full]
         for part, rows in enumerate(sent):
             out_ref[part * slots : (part + 1) * slots] = rows[i * slots : (i + 1) * slots]
-        out_ref[3 * slots :] = meta
+        out_ref[3 * slots : 3 * slots + 8] = meta
 
 
 def thirds(values):
@@ -275,6 +276,15 @@
         odd_ref[b * margin : (b + 1) * margin] = jnp.where(even, head, tail)
 
 
+def even_kappa(ref, slots, edge_rows, i):
+    return ref.at[pl.ds(3 * slots + 8 + i * (-(-edge_rows // 8) * 8), edge_rows)]
+
+
+def relay_kernel(*refs):
+    for in_ref, out_ref in zip(refs[: len(refs) // 2], refs[len(refs) // 2 :]):
+        out_ref[...] = in_ref[...]
+
+
 def cut_kernel(first_ref, second_ref, mine_ref, *out_refs):
     chip, chips, blocks = my_chip(), chip_count(), first_ref.shape[1] // LANES
     for d, out_ref in enumerate((mine_ref, *out_refs)):
@@ -382,12 +392,13 @@
     return [f[:rows] for f in fields]
 
 
-def faces_kernel(margin, even_ref, odd_ref, kappa_ref, sums_ref, *refs):
+def faces_kernel(margin, slots, shared_ref, odd_ref, kappa_ref, sums_ref, *refs):
     coef_ref, sums_out, one_ref, two_ref = refs[-4:]
     sums_out[...] = sums_ref[...]
     rows = kappa_ref.shape[1]
-    lay_ring(one_ref, kappa_ref[0], even_ref.at[0], odd_ref.at[0], margin)
-    lay_ring(two_ref, kappa_ref[1], even_ref.at[1], odd_ref.at[1], margin)
+    for i, ring_ref in enumerate((one_ref, two_ref)):
+        even_ref = even_kappa(shared_ref, slots, odd_ref.shape[1], i)
+        lay_ring(ring_ref, kappa_ref[i], even_ref, odd_ref.at[i], margin)
     face_weights(coef_ref, one_ref, two_ref, rows, margin)
 
 
@@ -418,7 +429,7 @@
 
 
 def sent_last(members):
-    return [0, 1] + sorted(range(2, members), key=lambda d: -(d % 2))
+    return [0, 1] + sorted(range(2, members), key=lambda d: d % 2)
 
 
 def result_kernel(response_ref, control_ref, *refs):
@@ -444,7 +455,7 @@
     return lax.ppermute(values, axis, [(i, i ^ bit) for i in range(count)])
 
 
-def swap_edges(even, odd):
+def swap_odd(edges):
     tiles, members = lax.axis_size("tile"), lax.axis_size("var")
     pairs = []
     for t in range(tiles):
@@ -452,7 +463,11 @@
         for q in range(members):
             to = other * members + q if 0 <= other < tiles else t * members + (q ^ 1)
             pairs.append((t * members + q, to))
-    return swap(even, "tile", 1), lax.ppermute(odd, ("tile", "var"), pairs)
+    return lax.ppermute(edges, ("tile", "var"), pairs)
+
+
+def swap_edges(even, odd):
+    return swap(even, "tile", 1), swap_odd(odd)
 
 
 def deliver(chunks):
@@ -487,12 +502,14 @@
     edge = jax.ShapeDtypeStruct((margin * size, LANES), F32)
     edge2 = jax.ShapeDtypeStruct((2, *edge.shape), F32)
     half = jax.ShapeDtypeStruct((3 * slots + 8, panel_width), F32)
-    chunks = [jax.ShapeDtypeStruct((2, *half.shape), F32)] * (tiles // 2 - 1) + [half] * 2
+    shared = jax.ShapeDtypeStruct((half.shape[0] + 2 * (-(-edge.shape[0] // 8) * 8), panel_width), F32)
+    chunks_far = [jax.ShapeDtypeStruct((2, *half.shape), F32)] * (tiles // 2 - 1)
+    chunks = chunks_far + [shared, half]
     line = pltpu.VMEM((1, panels), jnp.int32)
 
-    own, other, responses, kappa, kappa_even, kappa_odd, *chunks = call(
+    own, other, responses, kappa, kappa_odd, *chunks = call(
         functools.partial(first_kernel, slots, margin),
-        [field, field, jax.ShapeDtypeStruct((2, var_dev, 8, LANES), F32), view2, edge2, edge2]
+        [field, field, jax.ShapeDtypeStruct((2, var_dev, 8, LANES), F32), view2, edge2]
         + chunks,
         [HBM] * 10,
         [
@@ -516,11 +533,12 @@
         own, swap(other, "var", 1)
     )
     parts = [swap(p, "var", 2 * (d + 1)) for d, p in enumerate(parts)]
-    kappa_even, kappa_odd = swap_edges(kappa_even, kappa_odd)
+    kappa_odd = swap_odd(kappa_odd)
     smooth_in, even, odd = call(
         functools.partial(edges_kernel, margin), [view, edge, edge], [VMEM] * chips, cost=cost(500)
     )(part, *parts)
     even, odd = swap_edges(even, odd)
+    far = call(relay_kernel, chunks_far, [VMEM] * len(chunks_far), cost=cost(270000))(*got[:-2])
     sums, sums_other = call(
         functools.partial(scatter_kernel, slots, blocks),
         [view2, view2],
@@ -532,15 +550,15 @@
             pltpu.SemaphoreType.DMA((1,)),
         ],
         cost=cost(100000),
-    )(smooth_in, got[-2], *got[:-2], got[-1])
+    )(smooth_in, got[-2], *far, got[-1])
     ring = pltpu.VMEM((total, size * LANES), F32)
     coef, sums_other = call(
-        functools.partial(faces_kernel, margin),
+        functools.partial(faces_kernel, margin, slots),
         [jax.ShapeDtypeStruct((5, total, size * LANES), F32), view2],
         [VMEM] * 4 + [AFTER] * 2,
         [ring, ring],
         cost=cost(1000),
-    )(kappa_even, kappa_odd, kappa, sums_other, even, odd)
+    )(got[-2], kappa_odd, kappa, sums_other, even, odd)
     more_sums = swap(sums_other, "var", 1)
     (smooth,) = call(
         functools.partial(smooth_kernel, margin),

time: 29.3 us -> 30.4 us (1.038)
  waiting for transfers between devices: 7.56 us -> 11.5 us
  starting transfers between devices: 13.7 us -> 10.9 us
    ppermute x9 -> x8, starting transfers between devices: 8 us -> 5.21 us  [swap(): return lax.ppermute(values, axis, [(i, i ^ bit) for i in range(count)])]
    ppermute x2, waiting for transfers between devices: 0.64 us -> 2.74 us  [deliver(): got.append(lax.ppermute(chunk, ('tile', 'var'), pairs))]
    ppermute x9 -> x8, waiting for transfers between devices: 6.9 us -> 8.71 us  [swap(): return lax.ppermute(values, axis, [(i, i ^ bit) for i in range(count)])]
  transfers between devices with their start and end apart: 14 -> 13, of which waited for: 6 -> 6; matrix products, arithmetic and copies ran while one was open for 0% -> 0% of each run, Pallas kernels for 13% -> 13%
where the time goes in v14:
time: 30.4 us; the launch traced here: 30.2 us
  waiting for transfers between devices  11.5 us (38%)
  starting transfers between devices  10.9 us (36%)
  Pallas kernels  7.71 us (25%)
    ppermute x8, waiting for transfers between devices, swap(): return lax.ppermute(values, axis, [(i, i ^ bit) for i in range(count)])  8.71 us
    ppermute x2, starting transfers between devices, deliver(): got.append(lax.ppermute(chunk, ('tile', 'var'), pairs))  5.23 us
    ppermute x8, starting transfers between devices, swap(): return lax.ppermute(values, axis, [(i, i ^ bit) for i in range(count)])  5.21 us
    ppermute x2, waiting for transfers between devices, deliver(): got.append(lax.ppermute(chunk, ('tile', 'var'), pairs))  2.74 us
    pallas_call x1, Pallas kernels, local(): call(functools.partial(scatter_kernel, slots, blocks), [view2, view2], [A...  2.57 us
    pallas_call x1, Pallas kernels, local(): call(functools.partial(first_kernel, slots, margin), [field, field, jax.S...  1.59 us
    pallas_call x1, Pallas kernels, local(): call(functools.partial(smooth_kernel, margin), [view], [VMEM] * 4, [ring]...  1.24 us
    pallas_call x1, Pallas kernels, local(): call(functools.partial(spread_kernel, margin), [share], [VMEM] * 4, [ring...  1.23 us
  transfers between devices with their start and end apart: 13, of which 6 were waited for; matrix products, arithmetic and copies ran while one was open for 0% of the time, Pallas kernels for 13%

profile of v14, /device:TPU:0, one launch (start us, length us, event | category | flops | bytes accessed | tf_op | source)
XLA Modules:
  0.0 30.2 jit_solution(13358340605231195395)
XLA Ops:
  0.0 1.6 %shard_map.109 = (f32[16,2048]{1,0:T(8,128)S(1)}, f32[16,2048]{1,0:T(8,128)S(1)}, f32[2,2,8,128]{3,2,1,0:T(8,128)S(1)}, f32[2,16,1152]{2,1,0:T(8,128)S(1)}, f32[...) custom-call(f32[2,8]{1,0:T(2,128)} %sens_hbm.1, ...), custom_call_target="tpu_custom_call" | custom-call | flops 12288000 | bytes 3072000 | tf_op jit(solution)/shard_map/pallas_call | solution.py:510
  1.6 0.5 %collective-permute-start = (f32[16,2048]{1,0:T(8,128)S(1)}, f32[16,2048]{1,0:T(8,128)S(1)}, u32[]{:S(2)}, u32[]{:S(2)}) collective-permute-start(f32[16,2048]{1,0:T(8,128)S(1)} %get-tuple-element.27), channel_id=1, source_target_pairs={{0,1},{1,0},{2,3},{3,2},{4,5},{5,4},{6,7},{7,6},{8,9},{9,8},{10,11... | collective-permute-start | bytes 393224 | tf_op jit(solution)/shard_map/ppermute | solution.py:455
  2.1 3.7 %collective-permute-start.6 = (f32[2,104,128]{2,1,0:T(8,128)S(1)}, f32[2,104,128]{2,1,0:T(8,128)S(1)}, u32[]{:S(2)}, u32[]{:S(2)}) collective-permute-start(f32[2,104,128]{2,1,0:T(8,128)S(1)} %get-tuple-element.36), channel_id=1, source_target_pairs={{0,8},{1,13},{2,10},{3,15},{4,12},{5,9},{6,14},{7,11},{8,0},{9,5},... | collective-permute-start | bytes 319496 | tf_op jit(solution)/shard_map/ppermute | solution.py:482
  5.8 0.0 collective-permute-done.second_ref
  5.8 1.6 %collective-permute-start.1 = (f32[16,1152]{1,0:T(8,128)S(1)}, f32[16,1152]{1,0:T(8,128)S(1)}, u32[]{:S(2)}, u32[]{:S(2)}) collective-permute-start(f32[16,1152]{1,0:T(8,128)S(1)} %get-tuple-element.29), channel_id=1, source_target_pairs={{0,2},{1,3},{2,0},{3,1},{4,6},{5,7},{6,4},{7,5},{8,10},{9,11},{10,... | collective-permute-start | bytes 221192 | tf_op jit(solution)/shard_map/ppermute | solution.py:455
  7.4 1.6 %collective-permute-start.4 = (f32[296,128]{1,0:T(8,128)S(1)}, f32[296,128]{1,0:T(8,128)S(1)}, u32[]{:S(2)}, u32[]{:S(2)}) collective-permute-start(f32[296,128]{1,0:T(8,128)S(1)} %get-tuple-element.33), channel_id=1, source_target_pairs={{0,4},{1,5},{2,6},{3,7},{4,0},{5,1},{6,2},{7,3},{8,12},{9,13},{10,... | collective-permute-start | bytes 454664 | tf_op jit(solution)/shard_map/ppermute | solution.py:482
  8.9 0.0 collective-permute-start.5
  8.9 1.9 %collective-permute-done.1.refs_1_ = f32[16,1152]{1,0:T(8,128)S(1)} collective-permute-done((f32[16,1152]{1,0:T(8,128)S(1)}, f32[16,1152]{1,0:T(8,128)S(1)}, u32[]{:S(2)}, u32[]{:S(2)}) %collective-permute-start.1) | collective-permute-done | bytes 73760 | tf_op jit(solution)/shard_map/ppermute | solution.py:455
  10.8 1.0 %collective-permute-start.2 = (f32[90,128]{1,0:T(8,128)S(1)}, f32[90,128]{1,0:T(8,128)S(1)}, u32[]{:S(2)}, u32[]{:S(2)}) collective-permute-start(f32[90,128]{1,0:T(8,128)S(1)} %get-tuple-element.31), channel_id=1, source_target_pairs={{0,4},{4,0},{8,12},{12,8},{1,5},{5,1},{9,13},{13,9},{2,6},{6,2},{1... | collective-permute-start | bytes 138248 | tf_op jit(solution)/shard_map/ppermute | solution.py:455
  11.9 0.0 collective-permute-start.3
  11.9 0.0 collective-permute-done.6.refs_0_
  11.9 2.7 %collective-permute-done.4.refs_0_.shared_ref = f32[296,128]{1,0:T(8,128)S(1)} collective-permute-done((f32[296,128]{1,0:T(8,128)S(1)}, f32[296,128]{1,0:T(8,128)S(1)}, u32[]{:S(2)}, u32[]{:S(2)}) %collective-permute-start.4) | collective-permute-done | bytes 151584 | tf_op jit(solution)/shard_map/ppermute | solution.py:482
  14.6 2.6 %shard_map.113 = (f32[2,16,1152]{2,1,0:T(8,128)S(1)}, f32[2,16,1152]{2,1,0:T(8,128)S(1)}) custom-call(f32[16,1152]{1,0:T(8,128)S(1)} %get-tuple-element.30.after_ref.own_ref, f32[296,128]{1,0:T(8,128)S(1)} %collective-permute-done.4.refs_0_.shared_ref, f32[2,104,128]{2,1,0:T(8,128)S(1)} %shard_map.112.refs_1_, f32[104,128]{1,0:T(8,128)S(1)} %get-tuple-element.37.refs_2_), custom_call_target="tpu_custom_call" | custom-call | flops 409600000 | bytes 102400000 | tf_op jit(solution)/shard_map/pallas_call | solution.py:542
  17.2 0.0 collective-permute-done.5.odd_ref
  17.2 0.0 collective-permute-done.2.refs_0_.even_ref
  17.2 0.0 collective-permute-done.3.refs_1_.odd_ref
  17.3 0.2 shard_map.114
  17.5 0.1 collective-permute-start.7
  17.6 1.2 %shard_map.115.smooth_ref = f32[16,1152]{1,0:T(8,128)S(1)} custom-call(f32[16,1152]{1,0:T(8,128)S(1)} %get-tuple-element.30.after_ref.own_ref, f32[90,128]{1,0:T(8,128)S(1)} %collective-permute-done.2.refs_0_.even_ref, f32[90,128]{1,0:T(8,128)S(1)} %collective-permute-done.3.refs_1_.odd_ref, f32[5,40,1152]{2,1,0:T(8,128)S(1)} %get-tuple-element.39.coef_ref), custom_call_target="tpu_custom_call" | custom-call | flops 16384000 | bytes 4096000 | tf_op jit(solution)/shard_map/pallas_call | solution.py:563
  18.8 0.1 collective-permute-done.7.more_ref
  19.0 0.1 collective-permute-start.8
  19.0 0.5 %collective-permute-start.9 = (f32[90,128]{1,0:T(8,128)S(1)}, f32[90,128]{1,0:T(8,128)S(1)}, u32[]{:S(2)}, u32[]{:S(2)}) collective-permute-start(f32[90,128]{1,0:T(8,128)S(1)} %get-tuple-element.44), channel_id=1, source_target_pairs={{0,1},{1,0},{2,3},{3,2},{4,8},{5,9},{6,10},{7,11},{8,4},{9,5},{10,... | collective-permute-start | bytes 138248 | tf_op jit(solution)/shard_map/ppermute | solution.py:466
  19.5 3.6 %collective-permute-done.8.even_ref = f32[90,128]{1,0:T(8,128)S(1)} collective-permute-done((f32[90,128]{1,0:T(8,128)S(1)}, f32[90,128]{1,0:T(8,128)S(1)}, u32[]{:S(2)}, u32[]{:S(2)}) %collective-permute-start.8) | collective-permute-done | bytes 46112 | tf_op jit(solution)/shard_map/ppermute | solution.py:455
  23.1 0.0 collective-permute-done.9.odd_ref
  23.1 1.2 %shard_map.117.refs_0_ = f32[16,1024]{1,0:T(8,128)S(1)} custom-call(f32[16,1152]{1,0:T(8,128)S(1)} %get-tuple-element.42.own_ref, f32[90,128]{1,0:T(8,128)S(1)} %collective-permute-done.8.even_ref, f32[90,128]{1,0:T(8,128)S(1)} %collective-permute-done.9.odd_ref, f32[5,40,1152]{2,1,0:T(8,128)S(1)} %get-tuple-element.39.coef_ref), custom_call_target="tpu_custom_call" | custom-call | flops 16384000 | bytes 4096000 | tf_op jit(solution)/shard_map/pallas_call | solution.py:574
  24.4 0.1 collective-permute-start.12
  24.4 1.0 %collective-permute-start.11 = (f32[16,1024]{1,0:T(8,128)S(1)}, f32[16,1024]{1,0:T(8,128)S(1)}, u32[]{:S(2)}, u32[]{:S(2)}) collective-permute-start(f32[16,1024]{1,0:T(8,128)S(1)} %shard_map.117.refs_0_), channel_id=1, source_target_pairs={{0,2},{1,3},{2,0},{3,1},{4,6},{5,7},{6,4},{7,5},{8,10},{9,11},{10,... | collective-permute-start | bytes 196616 | tf_op jit(solution)/shard_map/ppermute | solution.py:455
  25.4 0.9 %collective-permute-start.10 = (f32[16,1024]{1,0:T(8,128)S(1)}, f32[16,1024]{1,0:T(8,128)S(1)}, u32[]{:S(2)}, u32[]{:S(2)}) collective-permute-start(f32[16,1024]{1,0:T(8,128)S(1)} %shard_map.117.refs_0_), channel_id=1, source_target_pairs={{0,1},{1,0},{2,3},{3,2},{4,5},{5,4},{6,7},{7,6},{8,9},{9,8},{10,11... | collective-permute-start | bytes 196616 | tf_op jit(solution)/shard_map/ppermute | solution.py:455
  26.3 2.2 %collective-permute-done.12.refs_3_ = f32[16,1024]{1,0:T(8,128)S(1)} collective-permute-done((f32[16,1024]{1,0:T(8,128)S(1)}, f32[16,1024]{1,0:T(8,128)S(1)}, u32[]{:S(2)}, u32[]{:S(2)}) %collective-permute-start.12) | collective-permute-done | bytes 65568 | tf_op jit(solution)/shard_map/ppermute | solution.py:455
  28.5 0.9 %collective-permute-done.11.refs_2_ = f32[16,1024]{1,0:T(8,128)S(1)} collective-permute-done((f32[16,1024]{1,0:T(8,128)S(1)}, f32[16,1024]{1,0:T(8,128)S(1)}, u32[]{:S(2)}, u32[]{:S(2)}) %collective-permute-start.11) | collective-permute-done | bytes 65568 | tf_op jit(solution)/shard_map/ppermute | solution.py:455
  29.4 0.0 collective-permute-done.10.refs_1_
  29.4 0.8 %shard_map.118 = f32[2,16,2048]{2,1,0:T(8,128)} custom-call(f32[2,2,8,128]{3,2,1,0:T(8,128)S(1)} %get-tuple-element.25.response_ref, f32[2,16,2048]{2,1,0:T(8,128)S(1)} %copy-done, f32[16,1024]{1,0:T(8,128)S(1)} %shard_map.117.refs_0_, f32[16,1024]{1,0:T(8,128)S(1)} %collective-permute-done.10.refs_1_, f32[16,1024]{1,0:T(8,128)S(1)} %collective-permute-done.11.refs_2_, ...), custom_call_target="tpu_custom_call" | custom-call | flops 4096000 | bytes 1024000 | tf_op jit(solution)/shard_map/pallas_call | solution.py:582
  (8 shorter events, 0.1 us)
Async XLA Ops:
  1.6 4.2 %collective-permute-start = (f32[16,2048]{1,0:T(8,128)S(1)}, f32[16,2048]{1,0:T(8,128)S(1)}, u32[]{:S(2)}, u32[]{:S(2)}) collective-permute-start(f32[16,2048]{1,0:T(8,128)S(1)} %get-tuple-element.27), channel_id=1, source_target_pairs={{0,1},{1,0},{2,3},{3,2},{4,5},{5,4},{6,7},{7,6},{8,9},{9,8},{10,11... | collective-permute-start | bytes 393224 | tf_op jit(solution)/shard_map/ppermute | solution.py:455
  2.1 9.8 %collective-permute-start.6 = (f32[2,104,128]{2,1,0:T(8,128)S(1)}, f32[2,104,128]{2,1,0:T(8,128)S(1)}, u32[]{:S(2)}, u32[]{:S(2)}) collective-permute-start(f32[2,104,128]{2,1,0:T(8,128)S(1)} %get-tuple-element.36), channel_id=1, source_target_pairs={{0,8},{1,13},{2,10},{3,15},{4,12},{5,9},{6,14},{7,11},{8,0},{9,5},... | collective-permute-start | bytes 319496 | tf_op jit(solution)/shard_map/ppermute | solution.py:482
  5.8 5.0 %collective-permute-start.1 = (f32[16,1152]{1,0:T(8,128)S(1)}, f32[16,1152]{1,0:T(8,128)S(1)}, u32[]{:S(2)}, u32[]{:S(2)}) collective-permute-start(f32[16,1152]{1,0:T(8,128)S(1)} %get-tuple-element.29), channel_id=1, source_target_pairs={{0,2},{1,3},{2,0},{3,1},{4,6},{5,7},{6,4},{7,5},{8,10},{9,11},{10,... | collective-permute-start | bytes 221192 | tf_op jit(solution)/shard_map/ppermute | solution.py:455
  7.4 7.3 %collective-permute-start.4 = (f32[296,128]{1,0:T(8,128)S(1)}, f32[296,128]{1,0:T(8,128)S(1)}, u32[]{:S(2)}, u32[]{:S(2)}) collective-permute-start(f32[296,128]{1,0:T(8,128)S(1)} %get-tuple-element.33), channel_id=1, source_target_pairs={{0,4},{1,5},{2,6},{3,7},{4,0},{5,1},{6,2},{7,3},{8,12},{9,13},{10,... | collective-permute-start | bytes 454664 | tf_op jit(solution)/shard_map/ppermute | solution.py:482
  8.9 8.3 %collective-permute-start.5 = (f32[2,90,128]{2,1,0:T(8,128)S(1)}, f32[2,90,128]{2,1,0:T(8,128)S(1)}, u32[]{:S(2)}, u32[]{:S(2)}) collective-permute-start(f32[2,90,128]{2,1,0:T(8,128)S(1)} %get-tuple-element.34), channel_id=1, source_target_pairs={{0,1},{1,0},{2,3},{3,2},{4,8},{5,9},{6,10},{7,11},{8,4},{9,5},{10,... | collective-permute-start | bytes 276488 | tf_op jit(solution)/shard_map/ppermute | solution.py:466
  10.8 6.4 %collective-permute-start.2 = (f32[90,128]{1,0:T(8,128)S(1)}, f32[90,128]{1,0:T(8,128)S(1)}, u32[]{:S(2)}, u32[]{:S(2)}) collective-permute-start(f32[90,128]{1,0:T(8,128)S(1)} %get-tuple-element.31), channel_id=1, source_target_pairs={{0,4},{4,0},{8,12},{12,8},{1,5},{5,1},{9,13},{13,9},{2,6},{6,2},{1... | collective-permute-start | bytes 138248 | tf_op jit(solution)/shard_map/ppermute | solution.py:455
  11.9 5.4 %collective-permute-start.3 = (f32[90,128]{1,0:T(8,128)S(1)}, f32[90,128]{1,0:T(8,128)S(1)}, u32[]{:S(2)}, u32[]{:S(2)}) collective-permute-start(f32[90,128]{1,0:T(8,128)S(1)} %get-tuple-element.32), channel_id=1, source_target_pairs={{0,1},{1,0},{2,3},{3,2},{4,8},{5,9},{6,10},{7,11},{8,4},{9,5},{10,... | collective-permute-start | bytes 138248 | tf_op jit(solution)/shard_map/ppermute | solution.py:466
  17.5 1.4 %collective-permute-start.7 = (f32[2,16,1152]{2,1,0:T(8,128)S(1)}, f32[2,16,1152]{2,1,0:T(8,128)S(1)}, u32[]{:S(2)}, u32[]{:S(2)}) collective-permute-start(f32[2,16,1152]{2,1,0:T(8,128)S(1)} %get-tuple-element.41), channel_id=1, source_target_pairs={{0,1},{1,0},{2,3},{3,2},{4,5},{5,4},{6,7},{7,6},{8,9},{9,8},{10,11... | collective-permute-start | bytes 442376 | tf_op jit(solution)/shard_map/ppermute | solution.py:455
  17.6 1.3 %copy-start.1 = (s32[16,2048]{1,0:T(8,128)S(1)}, s32[16,2048]{1,0:T(8,128)}, u32[]{:S(2)}) copy-start(s32[16,2048]{1,0:T(8,128)} %mask_ref.1) | copy-start | bytes 393220
  19.0 4.2 %collective-permute-start.8 = (f32[90,128]{1,0:T(8,128)S(1)}, f32[90,128]{1,0:T(8,128)S(1)}, u32[]{:S(2)}, u32[]{:S(2)}) collective-permute-start(f32[90,128]{1,0:T(8,128)S(1)} %get-tuple-element.43), channel_id=1, source_target_pairs={{0,4},{4,0},{8,12},{12,8},{1,5},{5,1},{9,13},{13,9},{2,6},{6,2},{1... | collective-permute-start | bytes 138248 | tf_op jit(solution)/shard_map/ppermute | solution.py:455
  19.0 4.1 %collective-permute-start.9 = (f32[90,128]{1,0:T(8,128)S(1)}, f32[90,128]{1,0:T(8,128)S(1)}, u32[]{:S(2)}, u32[]{:S(2)}) collective-permute-start(f32[90,128]{1,0:T(8,128)S(1)} %get-tuple-element.44), channel_id=1, source_target_pairs={{0,1},{1,0},{2,3},{3,2},{4,8},{5,9},{6,10},{7,11},{8,4},{9,5},{10,... | collective-permute-start | bytes 138248 | tf_op jit(solution)/shard_map/ppermute | solution.py:466
  23.1 6.3 %copy-start = (f32[2,16,2048]{2,1,0:T(8,128)S(1)}, f32[2,16,2048]{2,1,0:T(8,128)}, u32[]{:S(2)}) copy-start(f32[2,16,2048]{2,1,0:T(8,128)} %control_ref.1) | copy-start | bytes 786436
  24.4 4.2 %collective-permute-start.12 = (f32[16,1024]{1,0:T(8,128)S(1)}, f32[16,1024]{1,0:T(8,128)S(1)}, u32[]{:S(2)}, u32[]{:S(2)}) collective-permute-start(f32[16,1024]{1,0:T(8,128)S(1)} %shard_map.117.refs_0_), channel_id=1, source_target_pairs={{0,3},{1,2},{2,1},{3,0},{4,7},{5,6},{6,5},{7,4},{8,11},{9,10},{10,... | collective-permute-start | bytes 196616 | tf_op jit(solution)/shard_map/ppermute | solution.py:455
  24.4 5.0 %collective-permute-start.11 = (f32[16,1024]{1,0:T(8,128)S(1)}, f32[16,1024]{1,0:T(8,128)S(1)}, u32[]{:S(2)}, u32[]{:S(2)}) collective-permute-start(f32[16,1024]{1,0:T(8,128)S(1)} %shard_map.117.refs_0_), channel_id=1, source_target_pairs={{0,2},{1,3},{2,0},{3,1},{4,6},{5,7},{6,4},{7,5},{8,10},{9,11},{10,... | collective-permute-start | bytes 196616 | tf_op jit(solution)/shard_map/ppermute | solution.py:455
  25.4 4.0 %collective-permute-start.10 = (f32[16,1024]{1,0:T(8,128)S(1)}, f32[16,1024]{1,0:T(8,128)S(1)}, u32[]{:S(2)}, u32[]{:S(2)}) collective-permute-start(f32[16,1024]{1,0:T(8,128)S(1)} %shard_map.117.refs_0_), channel_id=1, source_target_pairs={{0,1},{1,0},{2,3},{3,2},{4,5},{5,4},{6,7},{7,6},{8,9},{9,8},{10,11... | collective-permute-start | bytes 196616 | tf_op jit(solution)/shard_map/ppermute | solution.py:455

commit v15 on v13

--- a/solution.py
+++ b/solution.py
@@ -418,7 +418,7 @@
 
 
 def sent_last(members):
-    return [0, 1] + sorted(range(2, members), key=lambda d: -(d % 2))
+    return [0, 1] + sorted(range(2, members), key=lambda d: d % 2)
 
 
 def result_kernel(response_ref, control_ref, *refs):

time: 29.3 us -> 29.7 us (1.014)
  waiting for transfers between devices: 7.56 us -> 9.15 us
  Pallas kernels: 7.71 us -> 6.91 us
  starting transfers between devices: 13.7 us -> 13.4 us
    ppermute x9, waiting for transfers between devices: 6.9 us -> 8.5 us  [swap(): return lax.ppermute(values, axis, [(i, i ^ bit) for i in range(count)])]
    pallas_call x1, Pallas kernels: 2.57 us -> 1.77 us  [local(): call(functools.partial(scatter_kernel, slots, blocks), [view2, view2], [A...]
    ppermute x9, starting transfers between devices: 8 us -> 7.69 us  [swap(): return lax.ppermute(values, axis, [(i, i ^ bit) for i in range(count)])]
  transfers between devices with their start and end apart: 14 -> 14, of which waited for: 6 -> 7; matrix products, arithmetic and copies ran while one was open for 0% -> 0% of each run, Pallas kernels for 13% -> 10%
where the time goes in v15:
time: 29.7 us; the launch traced here: 29.6 us
  starting transfers between devices  13.4 us (45%)
  waiting for transfers between devices  9.15 us (31%)
  Pallas kernels  6.91 us (23%)
    ppermute x9, waiting for transfers between devices, swap(): return lax.ppermute(values, axis, [(i, i ^ bit) for i in range(count)])  8.5 us
    ppermute x9, starting transfers between devices, swap(): return lax.ppermute(values, axis, [(i, i ^ bit) for i in range(count)])  7.69 us
    ppermute x2, starting transfers between devices, deliver(): got.append(lax.ppermute(chunk, ('tile', 'var'), pairs))  5.23 us
    pallas_call x1, Pallas kernels, local(): call(functools.partial(scatter_kernel, slots, blocks), [view2, view2], [A...  1.77 us
    pallas_call x1, Pallas kernels, local(): call(functools.partial(first_kernel, slots, margin), [field, field, jax.S...  1.58 us
    pallas_call x1, Pallas kernels, local(): call(functools.partial(spread_kernel, margin), [share], [VMEM] * 4, [ring...  1.25 us
    pallas_call x1, Pallas kernels, local(): call(functools.partial(smooth_kernel, margin), [view], [VMEM] * 4, [ring]...  1.25 us
    pallas_call x1, Pallas kernels, local(): call(result_kernel, [jax.ShapeDtypeStruct(control.shape, F32)], [VMEM] *...  0.77 us
  transfers between devices with their start and end apart: 14, of which 7 were waited for; matrix products, arithmetic and copies ran while one was open for 0% of the time, Pallas kernels for 10%

profile of v15, /device:TPU:0, one launch (start us, length us, event | category | flops | bytes accessed | tf_op | source)
XLA Modules:
  0.0 29.6 jit_solution(17728850726928496736)
XLA Ops:
  0.0 1.6 %shard_map.109 = (f32[16,2048]{1,0:T(8,128)S(1)}, f32[16,2048]{1,0:T(8,128)S(1)}, f32[2,2,8,128]{3,2,1,0:T(8,128)S(1)}, f32[2,16,1152]{2,1,0:T(8,128)S(1)}, f32[...) custom-call(f32[2,8]{1,0:T(2,128)} %sens_hbm.1, ...), custom_call_target="tpu_custom_call" | custom-call | flops 12288000 | bytes 3072000 | tf_op jit(solution)/shard_map/pallas_call | solution.py:493
  1.6 0.5 %collective-permute-start = (f32[16,2048]{1,0:T(8,128)S(1)}, f32[16,2048]{1,0:T(8,128)S(1)}, u32[]{:S(2)}, u32[]{:S(2)}) collective-permute-start(f32[16,2048]{1,0:T(8,128)S(1)} %get-tuple-element.28), channel_id=1, source_target_pairs={{0,1},{1,0},{2,3},{3,2},{4,5},{5,4},{6,7},{7,6},{8,9},{9,8},{10,11... | collective-permute-start | bytes 393224 | tf_op jit(solution)/shard_map/ppermute | solution.py:444
  2.1 3.7 %collective-permute-start.7 = (f32[2,104,128]{2,1,0:T(8,128)S(1)}, f32[2,104,128]{2,1,0:T(8,128)S(1)}, u32[]{:S(2)}, u32[]{:S(2)}) collective-permute-start(f32[2,104,128]{2,1,0:T(8,128)S(1)} %get-tuple-element.38), channel_id=1, source_target_pairs={{0,8},{1,13},{2,10},{3,15},{4,12},{5,9},{6,14},{7,11},{8,0},{9,5},... | collective-permute-start | bytes 319496 | tf_op jit(solution)/shard_map/ppermute | solution.py:467
  5.8 0.0 collective-permute-done.second_ref
  5.8 1.6 %collective-permute-start.1 = (f32[16,1152]{1,0:T(8,128)S(1)}, f32[16,1152]{1,0:T(8,128)S(1)}, u32[]{:S(2)}, u32[]{:S(2)}) collective-permute-start(f32[16,1152]{1,0:T(8,128)S(1)} %get-tuple-element.30), channel_id=1, source_target_pairs={{0,2},{1,3},{2,0},{3,1},{4,6},{5,7},{6,4},{7,5},{8,10},{9,11},{10,... | collective-permute-start | bytes 221192 | tf_op jit(solution)/shard_map/ppermute | solution.py:444
  7.4 1.6 %collective-permute-start.6 = (f32[104,128]{1,0:T(8,128)S(1)}, f32[104,128]{1,0:T(8,128)S(1)}, u32[]{:S(2)}, u32[]{:S(2)}) collective-permute-start(f32[104,128]{1,0:T(8,128)S(1)} %get-tuple-element.37), channel_id=1, source_target_pairs={{0,4},{1,5},{2,6},{3,7},{4,0},{5,1},{6,2},{7,3},{8,12},{9,13},{10,... | collective-permute-start | bytes 159752 | tf_op jit(solution)/shard_map/ppermute | solution.py:467
  8.9 0.4 %collective-permute-start.4 = (f32[2,90,128]{2,1,0:T(8,128)S(1)}, f32[2,90,128]{2,1,0:T(8,128)S(1)}, u32[]{:S(2)}, u32[]{:S(2)}) collective-permute-start(f32[2,90,128]{2,1,0:T(8,128)S(1)} %get-tuple-element.34), channel_id=1, source_target_pairs={{0,4},{4,0},{8,12},{12,8},{1,5},{5,1},{9,13},{13,9},{2,6},{6,2},{1... | collective-permute-start | bytes 276488 | tf_op jit(solution)/shard_map/ppermute | solution.py:444
  9.4 0.3 %collective-permute-start.5 = (f32[2,90,128]{2,1,0:T(8,128)S(1)}, f32[2,90,128]{2,1,0:T(8,128)S(1)}, u32[]{:S(2)}, u32[]{:S(2)}) collective-permute-start(f32[2,90,128]{2,1,0:T(8,128)S(1)} %get-tuple-element.35), channel_id=1, source_target_pairs={{0,1},{1,0},{2,3},{3,2},{4,8},{5,9},{6,10},{7,11},{8,4},{9,5},{10,... | collective-permute-start | bytes 276488 | tf_op jit(solution)/shard_map/ppermute | solution.py:455
  9.7 1.1 %collective-permute-done.1.refs_1_ = f32[16,1152]{1,0:T(8,128)S(1)} collective-permute-done((f32[16,1152]{1,0:T(8,128)S(1)}, f32[16,1152]{1,0:T(8,128)S(1)}, u32[]{:S(2)}, u32[]{:S(2)}) %collective-permute-start.1) | collective-permute-done | bytes 73760 | tf_op jit(solution)/shard_map/ppermute | solution.py:444
  10.8 1.1 %collective-permute-start.2 = (f32[90,128]{1,0:T(8,128)S(1)}, f32[90,128]{1,0:T(8,128)S(1)}, u32[]{:S(2)}, u32[]{:S(2)}) collective-permute-start(f32[90,128]{1,0:T(8,128)S(1)} %get-tuple-element.32), channel_id=1, source_target_pairs={{0,4},{4,0},{8,12},{12,8},{1,5},{5,1},{9,13},{13,9},{2,6},{6,2},{1... | collective-permute-start | bytes 138248 | tf_op jit(solution)/shard_map/ppermute | solution.py:444
  11.9 0.6 %collective-permute-done.6.refs_0_ = f32[104,128]{1,0:T(8,128)S(1)} collective-permute-done((f32[104,128]{1,0:T(8,128)S(1)}, f32[104,128]{1,0:T(8,128)S(1)}, u32[]{:S(2)}, u32[]{:S(2)}) %collective-permute-start.6) | collective-permute-done | bytes 53280 | tf_op jit(solution)/shard_map/ppermute | solution.py:467
  12.5 0.0 collective-permute-start.3
  12.6 0.0 collective-permute-done.7.refs_1_
  12.6 1.8 %shard_map.112 = (f32[2,16,1152]{2,1,0:T(8,128)S(1)}, f32[2,16,1152]{2,1,0:T(8,128)S(1)}) custom-call(f32[16,1152]{1,0:T(8,128)S(1)} %get-tuple-element.31.after_ref.own_ref, f32[104,128]{1,0:T(8,128)S(1)} %collective-permute-done.6.refs_0_, f32[2,104,128]{2,1,0:T(8,128)S(1)} %collective-permute-done.7.refs_1_, f32[104,128]{1,0:T(8,128)S(1)} %get-tuple-element.39.refs_2_), custom_call_target="tpu_custom_call" | custom-call | flops 409600000 | bytes 102400000 | tf_op jit(solution)/shard_map/pallas_call | solution.py:524
  14.3 0.3 %collective-permute-done.4.even_ref = f32[2,90,128]{2,1,0:T(8,128)S(1)} collective-permute-done((f32[2,90,128]{2,1,0:T(8,128)S(1)}, f32[2,90,128]{2,1,0:T(8,128)S(1)}, u32[]{:S(2)}, u32[]{:S(2)}) %collective-permute-start.4) | collective-permute-done | bytes 92192 | tf_op jit(solution)/shard_map/ppermute | solution.py:444
  14.6 1.0 %collective-permute-done.2.refs_0_.even_ref = f32[90,128]{1,0:T(8,128)S(1)} collective-permute-done((f32[90,128]{1,0:T(8,128)S(1)}, f32[90,128]{1,0:T(8,128)S(1)}, u32[]{:S(2)}, u32[]{:S(2)}) %collective-permute-start.2) | collective-permute-done | bytes 46112 | tf_op jit(solution)/shard_map/ppermute | solution.py:444
  15.7 0.0 collective-permute-done.3.refs_1_.odd_ref
  15.7 0.2 shard_map.113
  15.9 0.1 collective-permute-start.8
  16.0 1.2 %shard_map.114.smooth_ref = f32[16,1152]{1,0:T(8,128)S(1)} custom-call(f32[16,1152]{1,0:T(8,128)S(1)} %get-tuple-element.31.after_ref.own_ref, f32[90,128]{1,0:T(8,128)S(1)} %collective-permute-done.2.refs_0_.even_ref, f32[90,128]{1,0:T(8,128)S(1)} %collective-permute-done.3.refs_1_.odd_ref, f32[5,40,1152]{2,1,0:T(8,128)S(1)} %get-tuple-element.41.coef_ref), custom_call_target="tpu_custom_call" | custom-call | flops 16384000 | bytes 4096000 | tf_op jit(solution)/shard_map/pallas_call | solution.py:545
  17.3 0.0 collective-permute-done.8.more_ref
  17.4 2.0 %collective-permute-start.9 = (f32[90,128]{1,0:T(8,128)S(1)}, f32[90,128]{1,0:T(8,128)S(1)}, u32[]{:S(2)}, u32[]{:S(2)}) collective-permute-start(f32[90,128]{1,0:T(8,128)S(1)} %get-tuple-element.45), channel_id=1, source_target_pairs={{0,4},{4,0},{8,12},{12,8},{1,5},{5,1},{9,13},{13,9},{2,6},{6,2},{1... | collective-permute-start | bytes 138248 | tf_op jit(solution)/shard_map/ppermute | solution.py:444
  19.4 0.1 collective-permute-start.10
  19.6 2.2 %collective-permute-done.9.even_ref = f32[90,128]{1,0:T(8,128)S(1)} collective-permute-done((f32[90,128]{1,0:T(8,128)S(1)}, f32[90,128]{1,0:T(8,128)S(1)}, u32[]{:S(2)}, u32[]{:S(2)}) %collective-permute-start.9) | collective-permute-done | bytes 46112 | tf_op jit(solution)/shard_map/ppermute | solution.py:444
  21.7 1.2 %shard_map.116.refs_0_ = f32[16,1024]{1,0:T(8,128)S(1)} custom-call(f32[16,1152]{1,0:T(8,128)S(1)} %get-tuple-element.44.own_ref, f32[90,128]{1,0:T(8,128)S(1)} %collective-permute-done.9.even_ref, f32[90,128]{1,0:T(8,128)S(1)} %collective-permute-done.10.odd_ref, f32[5,40,1152]{2,1,0:T(8,128)S(1)} %get-tuple-element.41.coef_ref), custom_call_target="tpu_custom_call" | custom-call | flops 16384000 | bytes 4096000 | tf_op jit(solution)/shard_map/pallas_call | solution.py:556
  23.0 0.3 %collective-permute-start.13 = (f32[16,1024]{1,0:T(8,128)S(1)}, f32[16,1024]{1,0:T(8,128)S(1)}, u32[]{:S(2)}, u32[]{:S(2)}) collective-permute-start(f32[16,1024]{1,0:T(8,128)S(1)} %shard_map.116.refs_0_), channel_id=1, source_target_pairs={{0,3},{1,2},{2,1},{3,0},{4,7},{5,6},{6,5},{7,4},{8,11},{9,10},{10,... | collective-permute-start | bytes 196616 | tf_op jit(solution)/shard_map/ppermute | solution.py:444
  23.3 1.1 %collective-permute-start.12 = (f32[16,1024]{1,0:T(8,128)S(1)}, f32[16,1024]{1,0:T(8,128)S(1)}, u32[]{:S(2)}, u32[]{:S(2)}) collective-permute-start(f32[16,1024]{1,0:T(8,128)S(1)} %shard_map.116.refs_0_), channel_id=1, source_target_pairs={{0,2},{1,3},{2,0},{3,1},{4,6},{5,7},{6,4},{7,5},{8,10},{9,11},{10,... | collective-permute-start | bytes 196616 | tf_op jit(solution)/shard_map/ppermute | solution.py:444
  24.5 0.4 %collective-permute-start.11 = (f32[16,1024]{1,0:T(8,128)S(1)}, f32[16,1024]{1,0:T(8,128)S(1)}, u32[]{:S(2)}, u32[]{:S(2)}) collective-permute-start(f32[16,1024]{1,0:T(8,128)S(1)} %shard_map.116.refs_0_), channel_id=1, source_target_pairs={{0,1},{1,0},{2,3},{3,2},{4,5},{5,4},{6,7},{7,6},{8,9},{9,8},{10,11... | collective-permute-start | bytes 196616 | tf_op jit(solution)/shard_map/ppermute | solution.py:444
  24.9 2.5 %collective-permute-done.13.refs_3_ = f32[16,1024]{1,0:T(8,128)S(1)} collective-permute-done((f32[16,1024]{1,0:T(8,128)S(1)}, f32[16,1024]{1,0:T(8,128)S(1)}, u32[]{:S(2)}, u32[]{:S(2)}) %collective-permute-start.13) | collective-permute-done | bytes 65568 | tf_op jit(solution)/shard_map/ppermute | solution.py:444
  27.4 1.3 %collective-permute-done.12.refs_2_ = f32[16,1024]{1,0:T(8,128)S(1)} collective-permute-done((f32[16,1024]{1,0:T(8,128)S(1)}, f32[16,1024]{1,0:T(8,128)S(1)}, u32[]{:S(2)}, u32[]{:S(2)}) %collective-permute-start.12) | collective-permute-done | bytes 65568 | tf_op jit(solution)/shard_map/ppermute | solution.py:444
  28.8 0.0 collective-permute-done.11.refs_1_
  28.8 0.8 %shard_map.117 = f32[2,16,2048]{2,1,0:T(8,128)} custom-call(f32[2,2,8,128]{3,2,1,0:T(8,128)S(1)} %get-tuple-element.26.response_ref, f32[2,16,2048]{2,1,0:T(8,128)S(1)} %copy-done, f32[16,1024]{1,0:T(8,128)S(1)} %shard_map.116.refs_0_, f32[16,1024]{1,0:T(8,128)S(1)} %collective-permute-done.11.refs_1_, f32[16,1024]{1,0:T(8,128)S(1)} %collective-permute-done.12.refs_2_, ...), custom_call_target="tpu_custom_call" | custom-call | flops 4096000 | bytes 1024000 | tf_op jit(solution)/shard_map/pallas_call | solution.py:564
  (9 shorter events, 0.1 us)
Async XLA Ops:
  1.6 4.2 %collective-permute-start = (f32[16,2048]{1,0:T(8,128)S(1)}, f32[16,2048]{1,0:T(8,128)S(1)}, u32[]{:S(2)}, u32[]{:S(2)}) collective-permute-start(f32[16,2048]{1,0:T(8,128)S(1)} %get-tuple-element.28), channel_id=1, source_target_pairs={{0,1},{1,0},{2,3},{3,2},{4,5},{5,4},{6,7},{7,6},{8,9},{9,8},{10,11... | collective-permute-start | bytes 393224 | tf_op jit(solution)/shard_map/ppermute | solution.py:444
  2.1 10.5 %collective-permute-start.7 = (f32[2,104,128]{2,1,0:T(8,128)S(1)}, f32[2,104,128]{2,1,0:T(8,128)S(1)}, u32[]{:S(2)}, u32[]{:S(2)}) collective-permute-start(f32[2,104,128]{2,1,0:T(8,128)S(1)} %get-tuple-element.38), channel_id=1, source_target_pairs={{0,8},{1,13},{2,10},{3,15},{4,12},{5,9},{6,14},{7,11},{8,0},{9,5},... | collective-permute-start | bytes 319496 | tf_op jit(solution)/shard_map/ppermute | solution.py:467
  5.8 5.0 %collective-permute-start.1 = (f32[16,1152]{1,0:T(8,128)S(1)}, f32[16,1152]{1,0:T(8,128)S(1)}, u32[]{:S(2)}, u32[]{:S(2)}) collective-permute-start(f32[16,1152]{1,0:T(8,128)S(1)} %get-tuple-element.30), channel_id=1, source_target_pairs={{0,2},{1,3},{2,0},{3,1},{4,6},{5,7},{6,4},{7,5},{8,10},{9,11},{10,... | collective-permute-start | bytes 221192 | tf_op jit(solution)/shard_map/ppermute | solution.py:444
  7.4 5.2 %collective-permute-start.6 = (f32[104,128]{1,0:T(8,128)S(1)}, f32[104,128]{1,0:T(8,128)S(1)}, u32[]{:S(2)}, u32[]{:S(2)}) collective-permute-start(f32[104,128]{1,0:T(8,128)S(1)} %get-tuple-element.37), channel_id=1, source_target_pairs={{0,4},{1,5},{2,6},{3,7},{4,0},{5,1},{6,2},{7,3},{8,12},{9,13},{10,... | collective-permute-start | bytes 159752 | tf_op jit(solution)/shard_map/ppermute | solution.py:467
  8.9 5.7 %collective-permute-start.4 = (f32[2,90,128]{2,1,0:T(8,128)S(1)}, f32[2,90,128]{2,1,0:T(8,128)S(1)}, u32[]{:S(2)}, u32[]{:S(2)}) collective-permute-start(f32[2,90,128]{2,1,0:T(8,128)S(1)} %get-tuple-element.34), channel_id=1, source_target_pairs={{0,4},{4,0},{8,12},{12,8},{1,5},{5,1},{9,13},{13,9},{2,6},{6,2},{1... | collective-permute-start | bytes 276488 | tf_op jit(solution)/shard_map/ppermute | solution.py:444
  9.4 5.3 %collective-permute-start.5 = (f32[2,90,128]{2,1,0:T(8,128)S(1)}, f32[2,90,128]{2,1,0:T(8,128)S(1)}, u32[]{:S(2)}, u32[]{:S(2)}) collective-permute-start(f32[2,90,128]{2,1,0:T(8,128)S(1)} %get-tuple-element.35), channel_id=1, source_target_pairs={{0,1},{1,0},{2,3},{3,2},{4,8},{5,9},{6,10},{7,11},{8,4},{9,5},{10,... | collective-permute-start | bytes 276488 | tf_op jit(solution)/shard_map/ppermute | solution.py:455
  10.8 4.8 %collective-permute-start.2 = (f32[90,128]{1,0:T(8,128)S(1)}, f32[90,128]{1,0:T(8,128)S(1)}, u32[]{:S(2)}, u32[]{:S(2)}) collective-permute-start(f32[90,128]{1,0:T(8,128)S(1)} %get-tuple-element.32), channel_id=1, source_target_pairs={{0,4},{4,0},{8,12},{12,8},{1,5},{5,1},{9,13},{13,9},{2,6},{6,2},{1... | collective-permute-start | bytes 138248 | tf_op jit(solution)/shard_map/ppermute | solution.py:444
  12.5 3.1 %collective-permute-start.3 = (f32[90,128]{1,0:T(8,128)S(1)}, f32[90,128]{1,0:T(8,128)S(1)}, u32[]{:S(2)}, u32[]{:S(2)}) collective-permute-start(f32[90,128]{1,0:T(8,128)S(1)} %get-tuple-element.33), channel_id=1, source_target_pairs={{0,1},{1,0},{2,3},{3,2},{4,8},{5,9},{6,10},{7,11},{8,4},{9,5},{10,... | collective-permute-start | bytes 138248 | tf_op jit(solution)/shard_map/ppermute | solution.py:455
  15.9 1.4 %collective-permute-start.8 = (f32[2,16,1152]{2,1,0:T(8,128)S(1)}, f32[2,16,1152]{2,1,0:T(8,128)S(1)}, u32[]{:S(2)}, u32[]{:S(2)}) collective-permute-start(f32[2,16,1152]{2,1,0:T(8,128)S(1)} %get-tuple-element.43), channel_id=1, source_target_pairs={{0,1},{1,0},{2,3},{3,2},{4,5},{5,4},{6,7},{7,6},{8,9},{9,8},{10,11... | collective-permute-start | bytes 442376 | tf_op jit(solution)/shard_map/ppermute | solution.py:444
  16.0 1.3 %copy-start.1 = (s32[16,2048]{1,0:T(8,128)S(1)}, s32[16,2048]{1,0:T(8,128)}, u32[]{:S(2)}) copy-start(s32[16,2048]{1,0:T(8,128)} %mask_ref.1) | copy-start | bytes 393220
  17.4 4.4 %collective-permute-start.9 = (f32[90,128]{1,0:T(8,128)S(1)}, f32[90,128]{1,0:T(8,128)S(1)}, u32[]{:S(2)}, u32[]{:S(2)}) collective-permute-start(f32[90,128]{1,0:T(8,128)S(1)} %get-tuple-element.45), channel_id=1, source_target_pairs={{0,4},{4,0},{8,12},{12,8},{1,5},{5,1},{9,13},{13,9},{2,6},{6,2},{1... | collective-permute-start | bytes 138248 | tf_op jit(solution)/shard_map/ppermute | solution.py:444
  19.4 2.3 %collective-permute-start.10 = (f32[90,128]{1,0:T(8,128)S(1)}, f32[90,128]{1,0:T(8,128)S(1)}, u32[]{:S(2)}, u32[]{:S(2)}) collective-permute-start(f32[90,128]{1,0:T(8,128)S(1)} %get-tuple-element.46), channel_id=1, source_target_pairs={{0,1},{1,0},{2,3},{3,2},{4,8},{5,9},{6,10},{7,11},{8,4},{9,5},{10,... | collective-permute-start | bytes 138248 | tf_op jit(solution)/shard_map/ppermute | solution.py:455
  21.7 7.1 %copy-start = (f32[2,16,2048]{2,1,0:T(8,128)S(1)}, f32[2,16,2048]{2,1,0:T(8,128)}, u32[]{:S(2)}) copy-start(f32[2,16,2048]{2,1,0:T(8,128)} %control_ref.1) | copy-start | bytes 786436
  23.0 4.5 %collective-permute-start.13 = (f32[16,1024]{1,0:T(8,128)S(1)}, f32[16,1024]{1,0:T(8,128)S(1)}, u32[]{:S(2)}, u32[]{:S(2)}) collective-permute-start(f32[16,1024]{1,0:T(8,128)S(1)} %shard_map.116.refs_0_), channel_id=1, source_target_pairs={{0,3},{1,2},{2,1},{3,0},{4,7},{5,6},{6,5},{7,4},{8,11},{9,10},{10,... | collective-permute-start | bytes 196616 | tf_op jit(solution)/shard_map/ppermute | solution.py:444
  23.3 5.5 %collective-permute-start.12 = (f32[16,1024]{1,0:T(8,128)S(1)}, f32[16,1024]{1,0:T(8,128)S(1)}, u32[]{:S(2)}, u32[]{:S(2)}) collective-permute-start(f32[16,1024]{1,0:T(8,128)S(1)} %shard_map.116.refs_0_), channel_id=1, source_target_pairs={{0,2},{1,3},{2,0},{3,1},{4,6},{5,7},{6,4},{7,5},{8,10},{9,11},{10,... | collective-permute-start | bytes 196616 | tf_op jit(solution)/shard_map/ppermute | solution.py:444
  24.5 4.3 %collective-permute-start.11 = (f32[16,1024]{1,0:T(8,128)S(1)}, f32[16,1024]{1,0:T(8,128)S(1)}, u32[]{:S(2)}, u32[]{:S(2)}) collective-permute-start(f32[16,1024]{1,0:T(8,128)S(1)} %shard_map.116.refs_0_), channel_id=1, source_target_pairs={{0,1},{1,0},{2,3},{3,2},{4,5},{5,4},{6,7},{7,6},{8,9},{9,8},{10,11... | collective-permute-start | bytes 196616 | tf_op jit(solution)/shard_map/ppermute | solution.py:444

commit v16 on v13

--- a/solution.py
+++ b/solution.py
@@ -391,7 +391,7 @@
     face_weights(coef_ref, one_ref, two_ref, rows, margin)
 
 
-def smooth_kernel(margin, own_ref, even_ref, odd_ref, coef_ref, out_ref, ring_ref):
+def smooth_kernel(margin, own_ref, odd_ref, even_ref, coef_ref, out_ref, ring_ref):
     rows = own_ref.shape[0]
     lay_ring(ring_ref, own_ref[...], even_ref, odd_ref, margin)
     for j, field in enumerate(diffuse(ring_ref, coef_ref, rows, margin)):
@@ -540,7 +540,7 @@
         [VMEM] * 4 + [AFTER] * 2,
         [ring, ring],
         cost=cost(1000),
-    )(kappa_even, kappa_odd, kappa, sums_other, even, odd)
+    )(kappa_even, kappa_odd, kappa, sums_other, odd, even)
     more_sums = swap(sums_other, "var", 1)
     (smooth,) = call(
         functools.partial(smooth_kernel, margin),
@@ -548,7 +548,7 @@
         [VMEM] * 4,
         [ring],
         cost=cost(4000),
-    )(smooth_in, even, odd, coef)
+    )(smooth_in, odd, even, coef)
     adjoint, even, odd = call(
         functools.partial(adjoint_kernel, margin), [view, edge, edge], [VMEM] * 4, cost=cost(500)
     )(smooth, land_mask, sums, more_sums)

time: 29.3 us -> 30.1 us (1.027)
  waiting for transfers between devices: 7.56 us -> 8.86 us
  starting transfers between devices: 13.7 us -> 13 us
    ppermute x9, starting transfers between devices: 8 us -> 6.89 us  [swap(): return lax.ppermute(values, axis, [(i, i ^ bit) for i in range(count)])]
    ppermute x2, waiting for transfers between devices: 0.64 us -> 1.32 us  [deliver(): got.append(lax.ppermute(chunk, ('tile', 'var'), pairs))]
    ppermute x9, waiting for transfers between devices: 6.9 us -> 7.53 us  [swap(): return lax.ppermute(values, axis, [(i, i ^ bit) for i in range(count)])]
    ppermute x3, starting transfers between devices: 0.51 us -> 0.86 us  [swap_edges(): return (swap(even, 'tile', 1), lax.ppermute(odd, ('tile', 'var'), pairs))]
  transfers between devices with their start and end apart: 14 -> 14, of which waited for: 6 -> 7; matrix products, arithmetic and copies ran while one was open for 0% -> 0% of each run, Pallas kernels for 13% -> 13%
where the time goes in v16:
time: 30.1 us; the launch traced here: 29.7 us
  starting transfers between devices  13 us (43%)
  waiting for transfers between devices  8.86 us (29%)
  Pallas kernels  7.72 us (26%)
    ppermute x9, waiting for transfers between devices, swap(): return lax.ppermute(values, axis, [(i, i ^ bit) for i in range(count)])  7.53 us
    ppermute x9, starting transfers between devices, swap(): return lax.ppermute(values, axis, [(i, i ^ bit) for i in range(count)])  6.89 us
    ppermute x2, starting transfers between devices, deliver(): got.append(lax.ppermute(chunk, ('tile', 'var'), pairs))  5.23 us
    pallas_call x1, Pallas kernels, local(): call(functools.partial(scatter_kernel, slots, blocks), [view2, view2], [A...  2.57 us
    pallas_call x1, Pallas kernels, local(): call(functools.partial(first_kernel, slots, margin), [field, field, jax.S...  1.58 us
    ppermute x2, waiting for transfers between devices, deliver(): got.append(lax.ppermute(chunk, ('tile', 'var'), pairs))  1.32 us
    pallas_call x1, Pallas kernels, local(): call(functools.partial(smooth_kernel, margin), [view], [VMEM] * 4, [ring]...  1.25 us
    pallas_call x1, Pallas kernels, local(): call(functools.partial(spread_kernel, margin), [share], [VMEM] * 4, [ring...  1.25 us
  transfers between devices with their start and end apart: 14, of which 7 were waited for; matrix products, arithmetic and copies ran while one was open for 0% of the time, Pallas kernels for 13%

profile of v16, /device:TPU:0, one launch (start us, length us, event | category | flops | bytes accessed | tf_op | source)
XLA Modules:
  0.0 29.7 jit_solution(14917111264489558115)
XLA Ops:
  0.0 1.6 %shard_map.109 = (f32[16,2048]{1,0:T(8,128)S(1)}, f32[16,2048]{1,0:T(8,128)S(1)}, f32[2,2,8,128]{3,2,1,0:T(8,128)S(1)}, f32[2,16,1152]{2,1,0:T(8,128)S(1)}, f32[...) custom-call(f32[2,8]{1,0:T(2,128)} %sens_hbm.1, ...), custom_call_target="tpu_custom_call" | custom-call | flops 12288000 | bytes 3072000 | tf_op jit(solution)/shard_map/pallas_call | solution.py:493
  1.6 0.5 %collective-permute-start = (f32[16,2048]{1,0:T(8,128)S(1)}, f32[16,2048]{1,0:T(8,128)S(1)}, u32[]{:S(2)}, u32[]{:S(2)}) collective-permute-start(f32[16,2048]{1,0:T(8,128)S(1)} %get-tuple-element.28), channel_id=1, source_target_pairs={{0,1},{1,0},{2,3},{3,2},{4,5},{5,4},{6,7},{7,6},{8,9},{9,8},{10,11... | collective-permute-start | bytes 393224 | tf_op jit(solution)/shard_map/ppermute | solution.py:444
  2.1 3.7 %collective-permute-start.7 = (f32[2,104,128]{2,1,0:T(8,128)S(1)}, f32[2,104,128]{2,1,0:T(8,128)S(1)}, u32[]{:S(2)}, u32[]{:S(2)}) collective-permute-start(f32[2,104,128]{2,1,0:T(8,128)S(1)} %get-tuple-element.38), channel_id=1, source_target_pairs={{0,8},{1,13},{2,10},{3,15},{4,12},{5,9},{6,14},{7,11},{8,0},{9,5},... | collective-permute-start | bytes 319496 | tf_op jit(solution)/shard_map/ppermute | solution.py:467
  5.8 0.0 collective-permute-done.second_ref
  5.8 1.6 %collective-permute-start.1 = (f32[16,1152]{1,0:T(8,128)S(1)}, f32[16,1152]{1,0:T(8,128)S(1)}, u32[]{:S(2)}, u32[]{:S(2)}) collective-permute-start(f32[16,1152]{1,0:T(8,128)S(1)} %get-tuple-element.30), channel_id=1, source_target_pairs={{0,2},{1,3},{2,0},{3,1},{4,6},{5,7},{6,4},{7,5},{8,10},{9,11},{10,... | collective-permute-start | bytes 221192 | tf_op jit(solution)/shard_map/ppermute | solution.py:444
  7.4 1.6 %collective-permute-start.6 = (f32[104,128]{1,0:T(8,128)S(1)}, f32[104,128]{1,0:T(8,128)S(1)}, u32[]{:S(2)}, u32[]{:S(2)}) collective-permute-start(f32[104,128]{1,0:T(8,128)S(1)} %get-tuple-element.37), channel_id=1, source_target_pairs={{0,4},{1,5},{2,6},{3,7},{4,0},{5,1},{6,2},{7,3},{8,12},{9,13},{10,... | collective-permute-start | bytes 159752 | tf_op jit(solution)/shard_map/ppermute | solution.py:467
  8.9 0.4 %collective-permute-start.4 = (f32[2,90,128]{2,1,0:T(8,128)S(1)}, f32[2,90,128]{2,1,0:T(8,128)S(1)}, u32[]{:S(2)}, u32[]{:S(2)}) collective-permute-start(f32[2,90,128]{2,1,0:T(8,128)S(1)} %get-tuple-element.34), channel_id=1, source_target_pairs={{0,4},{4,0},{8,12},{12,8},{1,5},{5,1},{9,13},{13,9},{2,6},{6,2},{1... | collective-permute-start | bytes 276488 | tf_op jit(solution)/shard_map/ppermute | solution.py:444
  9.4 0.3 %collective-permute-start.5 = (f32[2,90,128]{2,1,0:T(8,128)S(1)}, f32[2,90,128]{2,1,0:T(8,128)S(1)}, u32[]{:S(2)}, u32[]{:S(2)}) collective-permute-start(f32[2,90,128]{2,1,0:T(8,128)S(1)} %get-tuple-element.35), channel_id=1, source_target_pairs={{0,1},{1,0},{2,3},{3,2},{4,8},{5,9},{6,10},{7,11},{8,4},{9,5},{10,... | collective-permute-start | bytes 276488 | tf_op jit(solution)/shard_map/ppermute | solution.py:455
  9.7 1.1 %collective-permute-done.1.refs_1_ = f32[16,1152]{1,0:T(8,128)S(1)} collective-permute-done((f32[16,1152]{1,0:T(8,128)S(1)}, f32[16,1152]{1,0:T(8,128)S(1)}, u32[]{:S(2)}, u32[]{:S(2)}) %collective-permute-start.1) | collective-permute-done | bytes 73760 | tf_op jit(solution)/shard_map/ppermute | solution.py:444
  10.8 0.4 %collective-permute-start.2 = (f32[90,128]{1,0:T(8,128)S(1)}, f32[90,128]{1,0:T(8,128)S(1)}, u32[]{:S(2)}, u32[]{:S(2)}) collective-permute-start(f32[90,128]{1,0:T(8,128)S(1)} %get-tuple-element.32), channel_id=1, source_target_pairs={{0,1},{1,0},{2,3},{3,2},{4,8},{5,9},{6,10},{7,11},{8,4},{9,5},{10,... | collective-permute-start | bytes 138248 | tf_op jit(solution)/shard_map/ppermute | solution.py:455
  11.2 1.3 %collective-permute-done.6.refs_0_ = f32[104,128]{1,0:T(8,128)S(1)} collective-permute-done((f32[104,128]{1,0:T(8,128)S(1)}, f32[104,128]{1,0:T(8,128)S(1)}, u32[]{:S(2)}, u32[]{:S(2)}) %collective-permute-start.6) | collective-permute-done | bytes 53280 | tf_op jit(solution)/shard_map/ppermute | solution.py:467
  12.5 1.0 %collective-permute-start.3 = (f32[90,128]{1,0:T(8,128)S(1)}, f32[90,128]{1,0:T(8,128)S(1)}, u32[]{:S(2)}, u32[]{:S(2)}) collective-permute-start(f32[90,128]{1,0:T(8,128)S(1)} %get-tuple-element.33), channel_id=1, source_target_pairs={{0,4},{4,0},{8,12},{12,8},{1,5},{5,1},{9,13},{13,9},{2,6},{6,2},{1... | collective-permute-start | bytes 138248 | tf_op jit(solution)/shard_map/ppermute | solution.py:444
  13.5 0.0 collective-permute-done.7.refs_1_
  13.6 2.6 %shard_map.112 = (f32[2,16,1152]{2,1,0:T(8,128)S(1)}, f32[2,16,1152]{2,1,0:T(8,128)S(1)}) custom-call(f32[16,1152]{1,0:T(8,128)S(1)} %get-tuple-element.31.after_ref.own_ref, f32[104,128]{1,0:T(8,128)S(1)} %collective-permute-done.6.refs_0_, f32[2,104,128]{2,1,0:T(8,128)S(1)} %collective-permute-done.7.refs_1_, f32[104,128]{1,0:T(8,128)S(1)} %get-tuple-element.39.refs_2_), custom_call_target="tpu_custom_call" | custom-call | flops 409600000 | bytes 102400000 | tf_op jit(solution)/shard_map/pallas_call | solution.py:524
  16.1 0.0 collective-permute-done.5.odd_ref
  16.2 0.0 collective-permute-done.2.refs_0_.odd_ref
  16.2 0.5 %collective-permute-done.3.refs_1_.even_ref = f32[90,128]{1,0:T(8,128)S(1)} collective-permute-done((f32[90,128]{1,0:T(8,128)S(1)}, f32[90,128]{1,0:T(8,128)S(1)}, u32[]{:S(2)}, u32[]{:S(2)}) %collective-permute-start.3) | collective-permute-done | bytes 46112 | tf_op jit(solution)/shard_map/ppermute | solution.py:444
  16.6 0.2 shard_map.113
  16.8 0.1 collective-permute-start.8
  16.9 0.0 copy-start.1
  16.9 1.3 %shard_map.114.smooth_ref = f32[16,1152]{1,0:T(8,128)S(1)} custom-call(f32[16,1152]{1,0:T(8,128)S(1)} %get-tuple-element.31.after_ref.own_ref, f32[90,128]{1,0:T(8,128)S(1)} %collective-permute-done.2.refs_0_.odd_ref, f32[90,128]{1,0:T(8,128)S(1)} %collective-permute-done.3.refs_1_.even_ref, f32[5,40,1152]{2,1,0:T(8,128)S(1)} %get-tuple-element.41.coef_ref), custom_call_target="tpu_custom_call" | custom-call | flops 16384000 | bytes 4096000 | tf_op jit(solution)/shard_map/pallas_call | solution.py:545
  18.2 0.1 collective-permute-done.8.more_ref
  18.3 1.1 %collective-permute-start.9 = (f32[90,128]{1,0:T(8,128)S(1)}, f32[90,128]{1,0:T(8,128)S(1)}, u32[]{:S(2)}, u32[]{:S(2)}) collective-permute-start(f32[90,128]{1,0:T(8,128)S(1)} %get-tuple-element.45), channel_id=1, source_target_pairs={{0,4},{4,0},{8,12},{12,8},{1,5},{5,1},{9,13},{13,9},{2,6},{6,2},{1... | collective-permute-start | bytes 138248 | tf_op jit(solution)/shard_map/ppermute | solution.py:444
  19.4 0.1 collective-permute-start.10
  19.6 2.9 %collective-permute-done.9.even_ref = f32[90,128]{1,0:T(8,128)S(1)} collective-permute-done((f32[90,128]{1,0:T(8,128)S(1)}, f32[90,128]{1,0:T(8,128)S(1)}, u32[]{:S(2)}, u32[]{:S(2)}) %collective-permute-start.9) | collective-permute-done | bytes 46112 | tf_op jit(solution)/shard_map/ppermute | solution.py:444
  22.5 1.2 %shard_map.116.refs_0_ = f32[16,1024]{1,0:T(8,128)S(1)} custom-call(f32[16,1152]{1,0:T(8,128)S(1)} %get-tuple-element.44.own_ref, f32[90,128]{1,0:T(8,128)S(1)} %collective-permute-done.9.even_ref, f32[90,128]{1,0:T(8,128)S(1)} %collective-permute-done.10.odd_ref, f32[5,40,1152]{2,1,0:T(8,128)S(1)} %get-tuple-element.41.coef_ref), custom_call_target="tpu_custom_call" | custom-call | flops 16384000 | bytes 4096000 | tf_op jit(solution)/shard_map/pallas_call | solution.py:556
  23.7 0.8 %collective-permute-start.13 = (f32[16,1024]{1,0:T(8,128)S(1)}, f32[16,1024]{1,0:T(8,128)S(1)}, u32[]{:S(2)}, u32[]{:S(2)}) collective-permute-start(f32[16,1024]{1,0:T(8,128)S(1)} %shard_map.116.refs_0_), channel_id=1, source_target_pairs={{0,2},{1,3},{2,0},{3,1},{4,6},{5,7},{6,4},{7,5},{8,10},{9,11},{10,... | collective-permute-start | bytes 196616 | tf_op jit(solution)/shard_map/ppermute | solution.py:444
  24.5 0.0 collective-permute-start.12
  24.5 1.4 %collective-permute-start.11 = (f32[16,1024]{1,0:T(8,128)S(1)}, f32[16,1024]{1,0:T(8,128)S(1)}, u32[]{:S(2)}, u32[]{:S(2)}) collective-permute-start(f32[16,1024]{1,0:T(8,128)S(1)} %shard_map.116.refs_0_), channel_id=1, source_target_pairs={{0,1},{1,0},{2,3},{3,2},{4,5},{5,4},{6,7},{7,6},{8,9},{9,8},{10,11... | collective-permute-start | bytes 196616 | tf_op jit(solution)/shard_map/ppermute | solution.py:444
  25.9 2.7 %collective-permute-done.13.refs_3_ = f32[16,1024]{1,0:T(8,128)S(1)} collective-permute-done((f32[16,1024]{1,0:T(8,128)S(1)}, f32[16,1024]{1,0:T(8,128)S(1)}, u32[]{:S(2)}, u32[]{:S(2)}) %collective-permute-start.13) | collective-permute-done | bytes 65568 | tf_op jit(solution)/shard_map/ppermute | solution.py:444
  28.7 0.2 collective-permute-done.12.refs_2_
  28.9 0.8 %shard_map.117 = f32[2,16,2048]{2,1,0:T(8,128)} custom-call(f32[2,2,8,128]{3,2,1,0:T(8,128)S(1)} %get-tuple-element.26.response_ref, f32[2,16,2048]{2,1,0:T(8,128)S(1)} %copy-done, f32[16,1024]{1,0:T(8,128)S(1)} %shard_map.116.refs_0_, f32[16,1024]{1,0:T(8,128)S(1)} %collective-permute-done.11.refs_1_, f32[16,1024]{1,0:T(8,128)S(1)} %collective-permute-done.12.refs_2_, ...), custom_call_target="tpu_custom_call" | custom-call | flops 4096000 | bytes 1024000 | tf_op jit(solution)/shard_map/pallas_call | solution.py:564
  (9 shorter events, 0.1 us)
Async XLA Ops:
  1.6 4.2 %collective-permute-start = (f32[16,2048]{1,0:T(8,128)S(1)}, f32[16,2048]{1,0:T(8,128)S(1)}, u32[]{:S(2)}, u32[]{:S(2)}) collective-permute-start(f32[16,2048]{1,0:T(8,128)S(1)} %get-tuple-element.28), channel_id=1, source_target_pairs={{0,1},{1,0},{2,3},{3,2},{4,5},{5,4},{6,7},{7,6},{8,9},{9,8},{10,11... | collective-permute-start | bytes 393224 | tf_op jit(solution)/shard_map/ppermute | solution.py:444
  2.1 11.4 %collective-permute-start.7 = (f32[2,104,128]{2,1,0:T(8,128)S(1)}, f32[2,104,128]{2,1,0:T(8,128)S(1)}, u32[]{:S(2)}, u32[]{:S(2)}) collective-permute-start(f32[2,104,128]{2,1,0:T(8,128)S(1)} %get-tuple-element.38), channel_id=1, source_target_pairs={{0,8},{1,13},{2,10},{3,15},{4,12},{5,9},{6,14},{7,11},{8,0},{9,5},... | collective-permute-start | bytes 319496 | tf_op jit(solution)/shard_map/ppermute | solution.py:467
  5.8 5.0 %collective-permute-start.1 = (f32[16,1152]{1,0:T(8,128)S(1)}, f32[16,1152]{1,0:T(8,128)S(1)}, u32[]{:S(2)}, u32[]{:S(2)}) collective-permute-start(f32[16,1152]{1,0:T(8,128)S(1)} %get-tuple-element.30), channel_id=1, source_target_pairs={{0,2},{1,3},{2,0},{3,1},{4,6},{5,7},{6,4},{7,5},{8,10},{9,11},{10,... | collective-permute-start | bytes 221192 | tf_op jit(solution)/shard_map/ppermute | solution.py:444
  7.4 5.2 %collective-permute-start.6 = (f32[104,128]{1,0:T(8,128)S(1)}, f32[104,128]{1,0:T(8,128)S(1)}, u32[]{:S(2)}, u32[]{:S(2)}) collective-permute-start(f32[104,128]{1,0:T(8,128)S(1)} %get-tuple-element.37), channel_id=1, source_target_pairs={{0,4},{1,5},{2,6},{3,7},{4,0},{5,1},{6,2},{7,3},{8,12},{9,13},{10,... | collective-permute-start | bytes 159752 | tf_op jit(solution)/shard_map/ppermute | solution.py:467
  8.9 7.2 %collective-permute-start.4 = (f32[2,90,128]{2,1,0:T(8,128)S(1)}, f32[2,90,128]{2,1,0:T(8,128)S(1)}, u32[]{:S(2)}, u32[]{:S(2)}) collective-permute-start(f32[2,90,128]{2,1,0:T(8,128)S(1)} %get-tuple-element.34), channel_id=1, source_target_pairs={{0,4},{4,0},{8,12},{12,8},{1,5},{5,1},{9,13},{13,9},{2,6},{6,2},{1... | collective-permute-start | bytes 276488 | tf_op jit(solution)/shard_map/ppermute | solution.py:444
  9.4 6.8 %collective-permute-start.5 = (f32[2,90,128]{2,1,0:T(8,128)S(1)}, f32[2,90,128]{2,1,0:T(8,128)S(1)}, u32[]{:S(2)}, u32[]{:S(2)}) collective-permute-start(f32[2,90,128]{2,1,0:T(8,128)S(1)} %get-tuple-element.35), channel_id=1, source_target_pairs={{0,1},{1,0},{2,3},{3,2},{4,8},{5,9},{6,10},{7,11},{8,4},{9,5},{10,... | collective-permute-start | bytes 276488 | tf_op jit(solution)/shard_map/ppermute | solution.py:455
  10.8 5.3 %collective-permute-start.2 = (f32[90,128]{1,0:T(8,128)S(1)}, f32[90,128]{1,0:T(8,128)S(1)}, u32[]{:S(2)}, u32[]{:S(2)}) collective-permute-start(f32[90,128]{1,0:T(8,128)S(1)} %get-tuple-element.32), channel_id=1, source_target_pairs={{0,1},{1,0},{2,3},{3,2},{4,8},{5,9},{6,10},{7,11},{8,4},{9,5},{10,... | collective-permute-start | bytes 138248 | tf_op jit(solution)/shard_map/ppermute | solution.py:455
  12.5 4.1 %collective-permute-start.3 = (f32[90,128]{1,0:T(8,128)S(1)}, f32[90,128]{1,0:T(8,128)S(1)}, u32[]{:S(2)}, u32[]{:S(2)}) collective-permute-start(f32[90,128]{1,0:T(8,128)S(1)} %get-tuple-element.33), channel_id=1, source_target_pairs={{0,4},{4,0},{8,12},{12,8},{1,5},{5,1},{9,13},{13,9},{2,6},{6,2},{1... | collective-permute-start | bytes 138248 | tf_op jit(solution)/shard_map/ppermute | solution.py:444
  16.8 1.4 %collective-permute-start.8 = (f32[2,16,1152]{2,1,0:T(8,128)S(1)}, f32[2,16,1152]{2,1,0:T(8,128)S(1)}, u32[]{:S(2)}, u32[]{:S(2)}) collective-permute-start(f32[2,16,1152]{2,1,0:T(8,128)S(1)} %get-tuple-element.43), channel_id=1, source_target_pairs={{0,1},{1,0},{2,3},{3,2},{4,5},{5,4},{6,7},{7,6},{8,9},{9,8},{10,11... | collective-permute-start | bytes 442376 | tf_op jit(solution)/shard_map/ppermute | solution.py:444
  16.9 1.4 %copy-start.1 = (s32[16,2048]{1,0:T(8,128)S(1)}, s32[16,2048]{1,0:T(8,128)}, u32[]{:S(2)}) copy-start(s32[16,2048]{1,0:T(8,128)} %mask_ref.1) | copy-start | bytes 393220
  18.3 4.2 %collective-permute-start.9 = (f32[90,128]{1,0:T(8,128)S(1)}, f32[90,128]{1,0:T(8,128)S(1)}, u32[]{:S(2)}, u32[]{:S(2)}) collective-permute-start(f32[90,128]{1,0:T(8,128)S(1)} %get-tuple-element.45), channel_id=1, source_target_pairs={{0,4},{4,0},{8,12},{12,8},{1,5},{5,1},{9,13},{13,9},{2,6},{6,2},{1... | collective-permute-start | bytes 138248 | tf_op jit(solution)/shard_map/ppermute | solution.py:444
  19.4 3.1 %collective-permute-start.10 = (f32[90,128]{1,0:T(8,128)S(1)}, f32[90,128]{1,0:T(8,128)S(1)}, u32[]{:S(2)}, u32[]{:S(2)}) collective-permute-start(f32[90,128]{1,0:T(8,128)S(1)} %get-tuple-element.46), channel_id=1, source_target_pairs={{0,1},{1,0},{2,3},{3,2},{4,8},{5,9},{6,10},{7,11},{8,4},{9,5},{10,... | collective-permute-start | bytes 138248 | tf_op jit(solution)/shard_map/ppermute | solution.py:455
  22.5 6.4 %copy-start = (f32[2,16,2048]{2,1,0:T(8,128)S(1)}, f32[2,16,2048]{2,1,0:T(8,128)}, u32[]{:S(2)}) copy-start(f32[2,16,2048]{2,1,0:T(8,128)} %control_ref.1) | copy-start | bytes 786436
  23.7 4.9 %collective-permute-start.13 = (f32[16,1024]{1,0:T(8,128)S(1)}, f32[16,1024]{1,0:T(8,128)S(1)}, u32[]{:S(2)}, u32[]{:S(2)}) collective-permute-start(f32[16,1024]{1,0:T(8,128)S(1)} %shard_map.116.refs_0_), channel_id=1, source_target_pairs={{0,2},{1,3},{2,0},{3,1},{4,6},{5,7},{6,4},{7,5},{8,10},{9,11},{10,... | collective-permute-start | bytes 196616 | tf_op jit(solution)/shard_map/ppermute | solution.py:444
  24.5 4.4 %collective-permute-start.12 = (f32[16,1024]{1,0:T(8,128)S(1)}, f32[16,1024]{1,0:T(8,128)S(1)}, u32[]{:S(2)}, u32[]{:S(2)}) collective-permute-start(f32[16,1024]{1,0:T(8,128)S(1)} %shard_map.116.refs_0_), channel_id=1, source_target_pairs={{0,3},{1,2},{2,1},{3,0},{4,7},{5,6},{6,5},{7,4},{8,11},{9,10},{10,... | collective-permute-start | bytes 196616 | tf_op jit(solution)/shard_map/ppermute | solution.py:444
  24.5 4.4 %collective-permute-start.11 = (f32[16,1024]{1,0:T(8,128)S(1)}, f32[16,1024]{1,0:T(8,128)S(1)}, u32[]{:S(2)}, u32[]{:S(2)}) collective-permute-start(f32[16,1024]{1,0:T(8,128)S(1)} %shard_map.116.refs_0_), channel_id=1, source_target_pairs={{0,1},{1,0},{2,3},{3,2},{4,5},{5,4},{6,7},{7,6},{8,9},{9,8},{10,11... | collective-permute-start | bytes 196616 | tf_op jit(solution)/shard_map/ppermute | solution.py:444

commit v17 on v13

--- a/solution.py
+++ b/solution.py
@@ -526,7 +526,7 @@
         [view2, view2],
         [AFTER] + [VMEM] * len(got),
         [
-            pltpu.VMEM((2 * rows * 2 * padded_blocks(size), LANES), F32),
+            pltpu.VMEM(((2 * rows + 1) * 2 * padded_blocks(size), LANES), F32),
             pltpu.SMEM((8 * tiles, LANES), jnp.int32),
             pltpu.VMEM((8 * tiles, LANES), jnp.int32),
             pltpu.SemaphoreType.DMA((1,)),

time: 29.3 us -> 29.3 us (level)
  waiting for transfers between devices: 7.56 us -> 8.38 us
  Pallas kernels: 7.71 us -> 6.91 us
    ppermute x9, waiting for transfers between devices: 6.9 us -> 7.73 us  [swap(): return lax.ppermute(values, axis, [(i, i ^ bit) for i in range(count)])]
    pallas_call x1, Pallas kernels: 2.57 us -> 1.76 us  [local(): call(functools.partial(scatter_kernel, slots, blocks), [view2, view2], [A...]
  transfers between devices with their start and end apart: 14 -> 14, of which waited for: 6 -> 7; matrix products, arithmetic and copies ran while one was open for 0% -> 0% of each run, Pallas kernels for 13% -> 10%
where the time goes in v17:
time: 29.3 us; the launch traced here: 29.1 us
  starting transfers between devices  13.7 us (47%)
  waiting for transfers between devices  8.38 us (29%)
  Pallas kernels  6.91 us (24%)
    ppermute x9, starting transfers between devices, swap(): return lax.ppermute(values, axis, [(i, i ^ bit) for i in range(count)])  8 us
    ppermute x9, waiting for transfers between devices, swap(): return lax.ppermute(values, axis, [(i, i ^ bit) for i in range(count)])  7.73 us
    ppermute x2, starting transfers between devices, deliver(): got.append(lax.ppermute(chunk, ('tile', 'var'), pairs))  5.23 us
    pallas_call x1, Pallas kernels, local(): call(functools.partial(scatter_kernel, slots, blocks), [view2, view2], [A...  1.76 us
    pallas_call x1, Pallas kernels, local(): call(functools.partial(first_kernel, slots, margin), [field, field, jax.S...  1.58 us
    pallas_call x1, Pallas kernels, local(): call(functools.partial(spread_kernel, margin), [share], [VMEM] * 4, [ring...  1.25 us
    pallas_call x1, Pallas kernels, local(): call(functools.partial(smooth_kernel, margin), [view], [VMEM] * 4, [ring]...  1.25 us
    pallas_call x1, Pallas kernels, local(): call(result_kernel, [jax.ShapeDtypeStruct(control.shape, F32)], [VMEM] *...  0.77 us
  transfers between devices with their start and end apart: 14, of which 7 were waited for; matrix products, arithmetic and copies ran while one was open for 0% of the time, Pallas kernels for 10%

profile of v17, /device:TPU:0, one launch (start us, length us, event | category | flops | bytes accessed | tf_op | source)
XLA Modules:
  0.0 29.1 jit_solution(411833272296146383)
XLA Ops:
  0.0 1.6 %shard_map.109 = (f32[16,2048]{1,0:T(8,128)S(1)}, f32[16,2048]{1,0:T(8,128)S(1)}, f32[2,2,8,128]{3,2,1,0:T(8,128)S(1)}, f32[2,16,1152]{2,1,0:T(8,128)S(1)}, f32[...) custom-call(f32[2,8]{1,0:T(2,128)} %sens_hbm.1, ...), custom_call_target="tpu_custom_call" | custom-call | flops 12288000 | bytes 3072000 | tf_op jit(solution)/shard_map/pallas_call | solution.py:493
  1.6 0.5 %collective-permute-start = (f32[16,2048]{1,0:T(8,128)S(1)}, f32[16,2048]{1,0:T(8,128)S(1)}, u32[]{:S(2)}, u32[]{:S(2)}) collective-permute-start(f32[16,2048]{1,0:T(8,128)S(1)} %get-tuple-element.28), channel_id=1, source_target_pairs={{0,1},{1,0},{2,3},{3,2},{4,5},{5,4},{6,7},{7,6},{8,9},{9,8},{10,11... | collective-permute-start | bytes 393224 | tf_op jit(solution)/shard_map/ppermute | solution.py:444
  2.1 3.7 %collective-permute-start.7 = (f32[2,104,128]{2,1,0:T(8,128)S(1)}, f32[2,104,128]{2,1,0:T(8,128)S(1)}, u32[]{:S(2)}, u32[]{:S(2)}) collective-permute-start(f32[2,104,128]{2,1,0:T(8,128)S(1)} %get-tuple-element.38), channel_id=1, source_target_pairs={{0,8},{1,13},{2,10},{3,15},{4,12},{5,9},{6,14},{7,11},{8,0},{9,5},... | collective-permute-start | bytes 319496 | tf_op jit(solution)/shard_map/ppermute | solution.py:467
  5.8 1.6 %collective-permute-start.1 = (f32[16,1152]{1,0:T(8,128)S(1)}, f32[16,1152]{1,0:T(8,128)S(1)}, u32[]{:S(2)}, u32[]{:S(2)}) collective-permute-start(f32[16,1152]{1,0:T(8,128)S(1)} %get-tuple-element.30), channel_id=1, source_target_pairs={{0,2},{1,3},{2,0},{3,1},{4,6},{5,7},{6,4},{7,5},{8,10},{9,11},{10,... | collective-permute-start | bytes 221192 | tf_op jit(solution)/shard_map/ppermute | solution.py:444
  7.4 1.6 %collective-permute-start.6 = (f32[104,128]{1,0:T(8,128)S(1)}, f32[104,128]{1,0:T(8,128)S(1)}, u32[]{:S(2)}, u32[]{:S(2)}) collective-permute-start(f32[104,128]{1,0:T(8,128)S(1)} %get-tuple-element.37), channel_id=1, source_target_pairs={{0,4},{1,5},{2,6},{3,7},{4,0},{5,1},{6,2},{7,3},{8,12},{9,13},{10,... | collective-permute-start | bytes 159752 | tf_op jit(solution)/shard_map/ppermute | solution.py:467
  8.9 0.4 %collective-permute-start.4 = (f32[2,90,128]{2,1,0:T(8,128)S(1)}, f32[2,90,128]{2,1,0:T(8,128)S(1)}, u32[]{:S(2)}, u32[]{:S(2)}) collective-permute-start(f32[2,90,128]{2,1,0:T(8,128)S(1)} %get-tuple-element.34), channel_id=1, source_target_pairs={{0,4},{4,0},{8,12},{12,8},{1,5},{5,1},{9,13},{13,9},{2,6},{6,2},{1... | collective-permute-start | bytes 276488 | tf_op jit(solution)/shard_map/ppermute | solution.py:444
  9.4 0.3 %collective-permute-start.5 = (f32[2,90,128]{2,1,0:T(8,128)S(1)}, f32[2,90,128]{2,1,0:T(8,128)S(1)}, u32[]{:S(2)}, u32[]{:S(2)}) collective-permute-start(f32[2,90,128]{2,1,0:T(8,128)S(1)} %get-tuple-element.35), channel_id=1, source_target_pairs={{0,1},{1,0},{2,3},{3,2},{4,8},{5,9},{6,10},{7,11},{8,4},{9,5},{10,... | collective-permute-start | bytes 276488 | tf_op jit(solution)/shard_map/ppermute | solution.py:455
  9.7 1.1 %collective-permute-done.1.refs_1_ = f32[16,1152]{1,0:T(8,128)S(1)} collective-permute-done((f32[16,1152]{1,0:T(8,128)S(1)}, f32[16,1152]{1,0:T(8,128)S(1)}, u32[]{:S(2)}, u32[]{:S(2)}) %collective-permute-start.1) | collective-permute-done | bytes 73760 | tf_op jit(solution)/shard_map/ppermute | solution.py:444
  10.8 1.1 %collective-permute-start.2 = (f32[90,128]{1,0:T(8,128)S(1)}, f32[90,128]{1,0:T(8,128)S(1)}, u32[]{:S(2)}, u32[]{:S(2)}) collective-permute-start(f32[90,128]{1,0:T(8,128)S(1)} %get-tuple-element.32), channel_id=1, source_target_pairs={{0,4},{4,0},{8,12},{12,8},{1,5},{5,1},{9,13},{13,9},{2,6},{6,2},{1... | collective-permute-start | bytes 138248 | tf_op jit(solution)/shard_map/ppermute | solution.py:444
  11.9 0.6 %collective-permute-done.6.refs_0_ = f32[104,128]{1,0:T(8,128)S(1)} collective-permute-done((f32[104,128]{1,0:T(8,128)S(1)}, f32[104,128]{1,0:T(8,128)S(1)}, u32[]{:S(2)}, u32[]{:S(2)}) %collective-permute-start.6) | collective-permute-done | bytes 53280 | tf_op jit(solution)/shard_map/ppermute | solution.py:467
  12.5 0.0 collective-permute-start.3
  12.6 0.0 collective-permute-done.7.refs_1_
  12.6 1.8 %shard_map.112 = (f32[2,16,1152]{2,1,0:T(8,128)S(1)}, f32[2,16,1152]{2,1,0:T(8,128)S(1)}) custom-call(f32[16,1152]{1,0:T(8,128)S(1)} %get-tuple-element.31.after_ref.own_ref, f32[104,128]{1,0:T(8,128)S(1)} %collective-permute-done.6.refs_0_, f32[2,104,128]{2,1,0:T(8,128)S(1)} %collective-permute-done.7.refs_1_, f32[104,128]{1,0:T(8,128)S(1)} %get-tuple-element.39.refs_2_), custom_call_target="tpu_custom_call" | custom-call | flops 409600000 | bytes 102400000 | tf_op jit(solution)/shard_map/pallas_call | solution.py:524
  14.3 0.3 %collective-permute-done.4.even_ref = f32[2,90,128]{2,1,0:T(8,128)S(1)} collective-permute-done((f32[2,90,128]{2,1,0:T(8,128)S(1)}, f32[2,90,128]{2,1,0:T(8,128)S(1)}, u32[]{:S(2)}, u32[]{:S(2)}) %collective-permute-start.4) | collective-permute-done | bytes 92192 | tf_op jit(solution)/shard_map/ppermute | solution.py:444
  14.6 0.0 collective-permute-done.5.odd_ref
  14.6 1.0 %collective-permute-done.2.refs_0_.even_ref = f32[90,128]{1,0:T(8,128)S(1)} collective-permute-done((f32[90,128]{1,0:T(8,128)S(1)}, f32[90,128]{1,0:T(8,128)S(1)}, u32[]{:S(2)}, u32[]{:S(2)}) %collective-permute-start.2) | collective-permute-done | bytes 46112 | tf_op jit(solution)/shard_map/ppermute | solution.py:444
  15.7 0.0 collective-permute-done.3.refs_1_.odd_ref
  15.7 0.2 shard_map.113
  15.9 0.1 collective-permute-start.8
  16.0 1.2 %shard_map.114.smooth_ref = f32[16,1152]{1,0:T(8,128)S(1)} custom-call(f32[16,1152]{1,0:T(8,128)S(1)} %get-tuple-element.31.after_ref.own_ref, f32[90,128]{1,0:T(8,128)S(1)} %collective-permute-done.2.refs_0_.even_ref, f32[90,128]{1,0:T(8,128)S(1)} %collective-permute-done.3.refs_1_.odd_ref, f32[5,40,1152]{2,1,0:T(8,128)S(1)} %get-tuple-element.41.coef_ref), custom_call_target="tpu_custom_call" | custom-call | flops 16384000 | bytes 4096000 | tf_op jit(solution)/shard_map/pallas_call | solution.py:545
  17.3 0.0 collective-permute-done.8.more_ref
  17.4 2.0 %collective-permute-start.9 = (f32[90,128]{1,0:T(8,128)S(1)}, f32[90,128]{1,0:T(8,128)S(1)}, u32[]{:S(2)}, u32[]{:S(2)}) collective-permute-start(f32[90,128]{1,0:T(8,128)S(1)} %get-tuple-element.45), channel_id=1, source_target_pairs={{0,4},{4,0},{8,12},{12,8},{1,5},{5,1},{9,13},{13,9},{2,6},{6,2},{1... | collective-permute-start | bytes 138248 | tf_op jit(solution)/shard_map/ppermute | solution.py:444
  19.4 0.1 collective-permute-start.10
  19.6 2.2 %collective-permute-done.9.even_ref = f32[90,128]{1,0:T(8,128)S(1)} collective-permute-done((f32[90,128]{1,0:T(8,128)S(1)}, f32[90,128]{1,0:T(8,128)S(1)}, u32[]{:S(2)}, u32[]{:S(2)}) %collective-permute-start.9) | collective-permute-done | bytes 46112 | tf_op jit(solution)/shard_map/ppermute | solution.py:444
  21.7 1.2 %shard_map.116.refs_0_ = f32[16,1024]{1,0:T(8,128)S(1)} custom-call(f32[16,1152]{1,0:T(8,128)S(1)} %get-tuple-element.44.own_ref, f32[90,128]{1,0:T(8,128)S(1)} %collective-permute-done.9.even_ref, f32[90,128]{1,0:T(8,128)S(1)} %collective-permute-done.10.odd_ref, f32[5,40,1152]{2,1,0:T(8,128)S(1)} %get-tuple-element.41.coef_ref), custom_call_target="tpu_custom_call" | custom-call | flops 16384000 | bytes 4096000 | tf_op jit(solution)/shard_map/pallas_call | solution.py:556
  23.0 0.9 %collective-permute-start.13 = (f32[16,1024]{1,0:T(8,128)S(1)}, f32[16,1024]{1,0:T(8,128)S(1)}, u32[]{:S(2)}, u32[]{:S(2)}) collective-permute-start(f32[16,1024]{1,0:T(8,128)S(1)} %shard_map.116.refs_0_), channel_id=1, source_target_pairs={{0,2},{1,3},{2,0},{3,1},{4,6},{5,7},{6,4},{7,5},{8,10},{9,11},{10,... | collective-permute-start | bytes 196616 | tf_op jit(solution)/shard_map/ppermute | solution.py:444
  23.9 0.3 collective-permute-start.12
  24.2 1.0 %collective-permute-start.11 = (f32[16,1024]{1,0:T(8,128)S(1)}, f32[16,1024]{1,0:T(8,128)S(1)}, u32[]{:S(2)}, u32[]{:S(2)}) collective-permute-start(f32[16,1024]{1,0:T(8,128)S(1)} %shard_map.116.refs_0_), channel_id=1, source_target_pairs={{0,1},{1,0},{2,3},{3,2},{4,5},{5,4},{6,7},{7,6},{8,9},{9,8},{10,11... | collective-permute-start | bytes 196616 | tf_op jit(solution)/shard_map/ppermute | solution.py:444
  25.2 2.5 %collective-permute-done.13.refs_3_ = f32[16,1024]{1,0:T(8,128)S(1)} collective-permute-done((f32[16,1024]{1,0:T(8,128)S(1)}, f32[16,1024]{1,0:T(8,128)S(1)}, u32[]{:S(2)}, u32[]{:S(2)}) %collective-permute-start.13) | collective-permute-done | bytes 65568 | tf_op jit(solution)/shard_map/ppermute | solution.py:444
  27.8 0.6 %collective-permute-done.12.refs_2_ = f32[16,1024]{1,0:T(8,128)S(1)} collective-permute-done((f32[16,1024]{1,0:T(8,128)S(1)}, f32[16,1024]{1,0:T(8,128)S(1)}, u32[]{:S(2)}, u32[]{:S(2)}) %collective-permute-start.12) | collective-permute-done | bytes 65568 | tf_op jit(solution)/shard_map/ppermute | solution.py:444
  28.3 0.0 collective-permute-done.11.refs_1_
  28.3 0.8 %shard_map.117 = f32[2,16,2048]{2,1,0:T(8,128)} custom-call(f32[2,2,8,128]{3,2,1,0:T(8,128)S(1)} %get-tuple-element.26.response_ref, f32[2,16,2048]{2,1,0:T(8,128)S(1)} %copy-done, f32[16,1024]{1,0:T(8,128)S(1)} %shard_map.116.refs_0_, f32[16,1024]{1,0:T(8,128)S(1)} %collective-permute-done.11.refs_1_, f32[16,1024]{1,0:T(8,128)S(1)} %collective-permute-done.12.refs_2_, ...), custom_call_target="tpu_custom_call" | custom-call | flops 4096000 | bytes 1024000 | tf_op jit(solution)/shard_map/pallas_call | solution.py:564
  (9 shorter events, 0.1 us)
Async XLA Ops:
  1.6 4.2 %collective-permute-start = (f32[16,2048]{1,0:T(8,128)S(1)}, f32[16,2048]{1,0:T(8,128)S(1)}, u32[]{:S(2)}, u32[]{:S(2)}) collective-permute-start(f32[16,2048]{1,0:T(8,128)S(1)} %get-tuple-element.28), channel_id=1, source_target_pairs={{0,1},{1,0},{2,3},{3,2},{4,5},{5,4},{6,7},{7,6},{8,9},{9,8},{10,11... | collective-permute-start | bytes 393224 | tf_op jit(solution)/shard_map/ppermute | solution.py:444
  2.1 10.5 %collective-permute-start.7 = (f32[2,104,128]{2,1,0:T(8,128)S(1)}, f32[2,104,128]{2,1,0:T(8,128)S(1)}, u32[]{:S(2)}, u32[]{:S(2)}) collective-permute-start(f32[2,104,128]{2,1,0:T(8,128)S(1)} %get-tuple-element.38), channel_id=1, source_target_pairs={{0,8},{1,13},{2,10},{3,15},{4,12},{5,9},{6,14},{7,11},{8,0},{9,5},... | collective-permute-start | bytes 319496 | tf_op jit(solution)/shard_map/ppermute | solution.py:467
  5.8 5.0 %collective-permute-start.1 = (f32[16,1152]{1,0:T(8,128)S(1)}, f32[16,1152]{1,0:T(8,128)S(1)}, u32[]{:S(2)}, u32[]{:S(2)}) collective-permute-start(f32[16,1152]{1,0:T(8,128)S(1)} %get-tuple-element.30), channel_id=1, source_target_pairs={{0,2},{1,3},{2,0},{3,1},{4,6},{5,7},{6,4},{7,5},{8,10},{9,11},{10,... | collective-permute-start | bytes 221192 | tf_op jit(solution)/shard_map/ppermute | solution.py:444
  7.4 5.2 %collective-permute-start.6 = (f32[104,128]{1,0:T(8,128)S(1)}, f32[104,128]{1,0:T(8,128)S(1)}, u32[]{:S(2)}, u32[]{:S(2)}) collective-permute-start(f32[104,128]{1,0:T(8,128)S(1)} %get-tuple-element.37), channel_id=1, source_target_pairs={{0,4},{1,5},{2,6},{3,7},{4,0},{5,1},{6,2},{7,3},{8,12},{9,13},{10,... | collective-permute-start | bytes 159752 | tf_op jit(solution)/shard_map/ppermute | solution.py:467
  8.9 5.7 %collective-permute-start.4 = (f32[2,90,128]{2,1,0:T(8,128)S(1)}, f32[2,90,128]{2,1,0:T(8,128)S(1)}, u32[]{:S(2)}, u32[]{:S(2)}) collective-permute-start(f32[2,90,128]{2,1,0:T(8,128)S(1)} %get-tuple-element.34), channel_id=1, source_target_pairs={{0,4},{4,0},{8,12},{12,8},{1,5},{5,1},{9,13},{13,9},{2,6},{6,2},{1... | collective-permute-start | bytes 276488 | tf_op jit(solution)/shard_map/ppermute | solution.py:444
  9.4 5.3 %collective-permute-start.5 = (f32[2,90,128]{2,1,0:T(8,128)S(1)}, f32[2,90,128]{2,1,0:T(8,128)S(1)}, u32[]{:S(2)}, u32[]{:S(2)}) collective-permute-start(f32[2,90,128]{2,1,0:T(8,128)S(1)} %get-tuple-element.35), channel_id=1, source_target_pairs={{0,1},{1,0},{2,3},{3,2},{4,8},{5,9},{6,10},{7,11},{8,4},{9,5},{10,... | collective-permute-start | bytes 276488 | tf_op jit(solution)/shard_map/ppermute | solution.py:455
  10.8 4.8 %collective-permute-start.2 = (f32[90,128]{1,0:T(8,128)S(1)}, f32[90,128]{1,0:T(8,128)S(1)}, u32[]{:S(2)}, u32[]{:S(2)}) collective-permute-start(f32[90,128]{1,0:T(8,128)S(1)} %get-tuple-element.32), channel_id=1, source_target_pairs={{0,4},{4,0},{8,12},{12,8},{1,5},{5,1},{9,13},{13,9},{2,6},{6,2},{1... | collective-permute-start | bytes 138248 | tf_op jit(solution)/shard_map/ppermute | solution.py:444
  12.5 3.1 %collective-permute-start.3 = (f32[90,128]{1,0:T(8,128)S(1)}, f32[90,128]{1,0:T(8,128)S(1)}, u32[]{:S(2)}, u32[]{:S(2)}) collective-permute-start(f32[90,128]{1,0:T(8,128)S(1)} %get-tuple-element.33), channel_id=1, source_target_pairs={{0,1},{1,0},{2,3},{3,2},{4,8},{5,9},{6,10},{7,11},{8,4},{9,5},{10,... | collective-permute-start | bytes 138248 | tf_op jit(solution)/shard_map/ppermute | solution.py:455
  15.9 1.4 %collective-permute-start.8 = (f32[2,16,1152]{2,1,0:T(8,128)S(1)}, f32[2,16,1152]{2,1,0:T(8,128)S(1)}, u32[]{:S(2)}, u32[]{:S(2)}) collective-permute-start(f32[2,16,1152]{2,1,0:T(8,128)S(1)} %get-tuple-element.43), channel_id=1, source_target_pairs={{0,1},{1,0},{2,3},{3,2},{4,5},{5,4},{6,7},{7,6},{8,9},{9,8},{10,11... | collective-permute-start | bytes 442376 | tf_op jit(solution)/shard_map/ppermute | solution.py:444
  16.0 1.3 %copy-start.1 = (s32[16,2048]{1,0:T(8,128)S(1)}, s32[16,2048]{1,0:T(8,128)}, u32[]{:S(2)}) copy-start(s32[16,2048]{1,0:T(8,128)} %mask_ref.1) | copy-start | bytes 393220
  17.4 4.4 %collective-permute-start.9 = (f32[90,128]{1,0:T(8,128)S(1)}, f32[90,128]{1,0:T(8,128)S(1)}, u32[]{:S(2)}, u32[]{:S(2)}) collective-permute-start(f32[90,128]{1,0:T(8,128)S(1)} %get-tuple-element.45), channel_id=1, source_target_pairs={{0,4},{4,0},{8,12},{12,8},{1,5},{5,1},{9,13},{13,9},{2,6},{6,2},{1... | collective-permute-start | bytes 138248 | tf_op jit(solution)/shard_map/ppermute | solution.py:444
  19.4 2.3 %collective-permute-start.10 = (f32[90,128]{1,0:T(8,128)S(1)}, f32[90,128]{1,0:T(8,128)S(1)}, u32[]{:S(2)}, u32[]{:S(2)}) collective-permute-start(f32[90,128]{1,0:T(8,128)S(1)} %get-tuple-element.46), channel_id=1, source_target_pairs={{0,1},{1,0},{2,3},{3,2},{4,8},{5,9},{6,10},{7,11},{8,4},{9,5},{10,... | collective-permute-start | bytes 138248 | tf_op jit(solution)/shard_map/ppermute | solution.py:455
  21.7 6.6 %copy-start = (f32[2,16,2048]{2,1,0:T(8,128)S(1)}, f32[2,16,2048]{2,1,0:T(8,128)}, u32[]{:S(2)}) copy-start(f32[2,16,2048]{2,1,0:T(8,128)} %control_ref.1) | copy-start | bytes 786436
  23.0 4.8 %collective-permute-start.13 = (f32[16,1024]{1,0:T(8,128)S(1)}, f32[16,1024]{1,0:T(8,128)S(1)}, u32[]{:S(2)}, u32[]{:S(2)}) collective-permute-start(f32[16,1024]{1,0:T(8,128)S(1)} %shard_map.116.refs_0_), channel_id=1, source_target_pairs={{0,2},{1,3},{2,0},{3,1},{4,6},{5,7},{6,4},{7,5},{8,10},{9,11},{10,... | collective-permute-start | bytes 196616 | tf_op jit(solution)/shard_map/ppermute | solution.py:444
  23.9 4.4 %collective-permute-start.12 = (f32[16,1024]{1,0:T(8,128)S(1)}, f32[16,1024]{1,0:T(8,128)S(1)}, u32[]{:S(2)}, u32[]{:S(2)}) collective-permute-start(f32[16,1024]{1,0:T(8,128)S(1)} %shard_map.116.refs_0_), channel_id=1, source_target_pairs={{0,3},{1,2},{2,1},{3,0},{4,7},{5,6},{6,5},{7,4},{8,11},{9,10},{10,... | collective-permute-start | bytes 196616 | tf_op jit(solution)/shard_map/ppermute | solution.py:444
  24.2 4.1 %collective-permute-start.11 = (f32[16,1024]{1,0:T(8,128)S(1)}, f32[16,1024]{1,0:T(8,128)S(1)}, u32[]{:S(2)}, u32[]{:S(2)}) collective-permute-start(f32[16,1024]{1,0:T(8,128)S(1)} %shard_map.116.refs_0_), channel_id=1, source_target_pairs={{0,1},{1,0},{2,3},{3,2},{4,5},{5,4},{6,7},{7,6},{8,9},{9,8},{10,11... | collective-permute-start | bytes 196616 | tf_op jit(solution)/shard_map/ppermute | solution.py:444

commit v18 on v17

--- a/solution.py
+++ b/solution.py
@@ -275,6 +275,11 @@
         odd_ref[b * margin : (b + 1) * margin] = jnp.where(even, head, tail)
 
 
+def relay_kernel(*refs):
+    for in_ref, out_ref in zip(refs[: len(refs) // 2], refs[len(refs) // 2 :]):
+        out_ref[...] = in_ref[...]
+
+
 def cut_kernel(first_ref, second_ref, mine_ref, *out_refs):
     chip, chips, blocks = my_chip(), chip_count(), first_ref.shape[1] // LANES
     for d, out_ref in enumerate((mine_ref, *out_refs)):
@@ -487,7 +492,8 @@
     edge = jax.ShapeDtypeStruct((margin * size, LANES), F32)
     edge2 = jax.ShapeDtypeStruct((2, *edge.shape), F32)
     half = jax.ShapeDtypeStruct((3 * slots + 8, panel_width), F32)
-    chunks = [jax.ShapeDtypeStruct((2, *half.shape), F32)] * (tiles // 2 - 1) + [half] * 2
+    far_shapes = [jax.ShapeDtypeStruct((2, *half.shape), F32)] * (tiles // 2 - 1)
+    chunks = far_shapes + [half] * 2
     line = pltpu.VMEM((1, panels), jnp.int32)
 
     own, other, responses, kappa, kappa_even, kappa_odd, *chunks = call(
@@ -521,6 +527,7 @@
         functools.partial(edges_kernel, margin), [view, edge, edge], [VMEM] * chips, cost=cost(500)
     )(part, *parts)
     even, odd = swap_edges(even, odd)
+    far = call(relay_kernel, far_shapes, [VMEM] * len(far_shapes), cost=cost(270000))(*got[:-2])
     sums, sums_other = call(
         functools.partial(scatter_kernel, slots, blocks),
         [view2, view2],
@@ -532,7 +539,7 @@
             pltpu.SemaphoreType.DMA((1,)),
         ],
         cost=cost(100000),
-    )(smooth_in, got[-2], *got[:-2], got[-1])
+    )(smooth_in, got[-2], *far, got[-1])
     ring = pltpu.VMEM((total, size * LANES), F32)
     coef, sums_other = call(
         functools.partial(faces_kernel, margin),

time: 29.3 us -> 29.2 us (level)
  Pallas kernels: 6.91 us -> 7.74 us
  starting transfers between devices: 13.7 us -> 13.1 us
    pallas_call x1, Pallas kernels: 1.76 us -> 2.59 us  [local(): call(functools.partial(scatter_kernel, slots, blocks), [view2, view2], [A...]
    ppermute x9, starting transfers between devices: 8 us -> 7.35 us  [swap(): return lax.ppermute(values, axis, [(i, i ^ bit) for i in range(count)])]
  transfers between devices with their start and end apart: 14 -> 14, of which waited for: 7 -> 6; matrix products, arithmetic and copies ran while one was open for 0% -> 0% of each run, Pallas kernels for 10% -> 13%
where the time goes in v18:
time: 29.2 us; the launch traced here: 29 us
  starting transfers between devices  13.1 us (45%)
  waiting for transfers between devices  8.13 us (28%)
  Pallas kernels  7.74 us (27%)
    ppermute x9, waiting for transfers between devices, swap(): return lax.ppermute(values, axis, [(i, i ^ bit) for i in range(count)])  7.5 us
    ppermute x9, starting transfers between devices, swap(): return lax.ppermute(values, axis, [(i, i ^ bit) for i in range(count)])  7.35 us
    ppermute x2, starting transfers between devices, deliver(): got.append(lax.ppermute(chunk, ('tile', 'var'), pairs))  5.23 us
    pallas_call x1, Pallas kernels, local(): call(functools.partial(scatter_kernel, slots, blocks), [view2, view2], [A...  2.59 us
    pallas_call x1, Pallas kernels, local(): call(functools.partial(first_kernel, slots, margin), [field, field, jax.S...  1.58 us
    pallas_call x1, Pallas kernels, local(): call(functools.partial(spread_kernel, margin), [share], [VMEM] * 4, [ring...  1.25 us
    pallas_call x1, Pallas kernels, local(): call(functools.partial(smooth_kernel, margin), [view], [VMEM] * 4, [ring]...  1.25 us
    pallas_call x1, Pallas kernels, local(): call(result_kernel, [jax.ShapeDtypeStruct(control.shape, F32)], [VMEM] *...  0.77 us
  transfers between devices with their start and end apart: 14, of which 6 were waited for; matrix products, arithmetic and copies ran while one was open for 0% of the time, Pallas kernels for 13%

profile of v18, /device:TPU:0, one launch (start us, length us, event | category | flops | bytes accessed | tf_op | source)
XLA Modules:
  0.0 29.0 jit_solution(171228541053887209)
XLA Ops:
  0.0 1.6 %shard_map.109 = (f32[16,2048]{1,0:T(8,128)S(1)}, f32[16,2048]{1,0:T(8,128)S(1)}, f32[2,2,8,128]{3,2,1,0:T(8,128)S(1)}, f32[2,16,1152]{2,1,0:T(8,128)S(1)}, f32[...) custom-call(f32[2,8]{1,0:T(2,128)} %sens_hbm.1, ...), custom_call_target="tpu_custom_call" | custom-call | flops 12288000 | bytes 3072000 | tf_op jit(solution)/shard_map/pallas_call | solution.py:499
  1.6 0.5 %collective-permute-start = (f32[16,2048]{1,0:T(8,128)S(1)}, f32[16,2048]{1,0:T(8,128)S(1)}, u32[]{:S(2)}, u32[]{:S(2)}) collective-permute-start(f32[16,2048]{1,0:T(8,128)S(1)} %get-tuple-element.28), channel_id=1, source_target_pairs={{0,1},{1,0},{2,3},{3,2},{4,5},{5,4},{6,7},{7,6},{8,9},{9,8},{10,11... | collective-permute-start | bytes 393224 | tf_op jit(solution)/shard_map/ppermute | solution.py:449
  2.1 3.7 %collective-permute-start.7 = (f32[2,104,128]{2,1,0:T(8,128)S(1)}, f32[2,104,128]{2,1,0:T(8,128)S(1)}, u32[]{:S(2)}, u32[]{:S(2)}) collective-permute-start(f32[2,104,128]{2,1,0:T(8,128)S(1)} %get-tuple-element.38), channel_id=1, source_target_pairs={{0,8},{1,13},{2,10},{3,15},{4,12},{5,9},{6,14},{7,11},{8,0},{9,5},... | collective-permute-start | bytes 319496 | tf_op jit(solution)/shard_map/ppermute | solution.py:472
  5.8 0.0 collective-permute-done.second_ref
  5.8 1.6 %collective-permute-start.1 = (f32[16,1152]{1,0:T(8,128)S(1)}, f32[16,1152]{1,0:T(8,128)S(1)}, u32[]{:S(2)}, u32[]{:S(2)}) collective-permute-start(f32[16,1152]{1,0:T(8,128)S(1)} %get-tuple-element.30), channel_id=1, source_target_pairs={{0,2},{1,3},{2,0},{3,1},{4,6},{5,7},{6,4},{7,5},{8,10},{9,11},{10,... | collective-permute-start | bytes 221192 | tf_op jit(solution)/shard_map/ppermute | solution.py:449
  7.4 1.6 %collective-permute-start.6 = (f32[104,128]{1,0:T(8,128)S(1)}, f32[104,128]{1,0:T(8,128)S(1)}, u32[]{:S(2)}, u32[]{:S(2)}) collective-permute-start(f32[104,128]{1,0:T(8,128)S(1)} %get-tuple-element.37), channel_id=1, source_target_pairs={{0,4},{1,5},{2,6},{3,7},{4,0},{5,1},{6,2},{7,3},{8,12},{9,13},{10,... | collective-permute-start | bytes 159752 | tf_op jit(solution)/shard_map/ppermute | solution.py:472
  8.9 0.4 %collective-permute-start.4 = (f32[2,90,128]{2,1,0:T(8,128)S(1)}, f32[2,90,128]{2,1,0:T(8,128)S(1)}, u32[]{:S(2)}, u32[]{:S(2)}) collective-permute-start(f32[2,90,128]{2,1,0:T(8,128)S(1)} %get-tuple-element.34), channel_id=1, source_target_pairs={{0,4},{4,0},{8,12},{12,8},{1,5},{5,1},{9,13},{13,9},{2,6},{6,2},{1... | collective-permute-start | bytes 276488 | tf_op jit(solution)/shard_map/ppermute | solution.py:449
  9.4 0.3 %collective-permute-start.5 = (f32[2,90,128]{2,1,0:T(8,128)S(1)}, f32[2,90,128]{2,1,0:T(8,128)S(1)}, u32[]{:S(2)}, u32[]{:S(2)}) collective-permute-start(f32[2,90,128]{2,1,0:T(8,128)S(1)} %get-tuple-element.35), channel_id=1, source_target_pairs={{0,1},{1,0},{2,3},{3,2},{4,8},{5,9},{6,10},{7,11},{8,4},{9,5},{10,... | collective-permute-start | bytes 276488 | tf_op jit(solution)/shard_map/ppermute | solution.py:460
  9.7 1.1 %collective-permute-done.1.refs_1_ = f32[16,1152]{1,0:T(8,128)S(1)} collective-permute-done((f32[16,1152]{1,0:T(8,128)S(1)}, f32[16,1152]{1,0:T(8,128)S(1)}, u32[]{:S(2)}, u32[]{:S(2)}) %collective-permute-start.1) | collective-permute-done | bytes 73760 | tf_op jit(solution)/shard_map/ppermute | solution.py:449
  10.8 1.1 %collective-permute-start.2 = (f32[90,128]{1,0:T(8,128)S(1)}, f32[90,128]{1,0:T(8,128)S(1)}, u32[]{:S(2)}, u32[]{:S(2)}) collective-permute-start(f32[90,128]{1,0:T(8,128)S(1)} %get-tuple-element.32), channel_id=1, source_target_pairs={{0,4},{4,0},{8,12},{12,8},{1,5},{5,1},{9,13},{13,9},{2,6},{6,2},{1... | collective-permute-start | bytes 138248 | tf_op jit(solution)/shard_map/ppermute | solution.py:449
  11.9 0.0 collective-permute-done.7.refs_0_
  11.9 0.0 collective-permute-start.3
  11.9 0.6 %collective-permute-done.6.refs_0_ = f32[104,128]{1,0:T(8,128)S(1)} collective-permute-done((f32[104,128]{1,0:T(8,128)S(1)}, f32[104,128]{1,0:T(8,128)S(1)}, u32[]{:S(2)}, u32[]{:S(2)}) %collective-permute-start.6) | collective-permute-done | bytes 53280 | tf_op jit(solution)/shard_map/ppermute | solution.py:472
  12.5 2.6 %shard_map.113 = (f32[2,16,1152]{2,1,0:T(8,128)S(1)}, f32[2,16,1152]{2,1,0:T(8,128)S(1)}) custom-call(f32[16,1152]{1,0:T(8,128)S(1)} %get-tuple-element.31.after_ref.own_ref, f32[104,128]{1,0:T(8,128)S(1)} %collective-permute-done.6.refs_0_, f32[2,104,128]{2,1,0:T(8,128)S(1)} %shard_map.112.refs_1_, f32[104,128]{1,0:T(8,128)S(1)} %get-tuple-element.39.refs_2_), custom_call_target="tpu_custom_call" | custom-call | flops 409600000 | bytes 102400000 | tf_op jit(solution)/shard_map/pallas_call | solution.py:531
  15.1 0.0 collective-permute-done.4.even_ref
  15.1 0.0 collective-permute-done.5.odd_ref
  15.2 0.5 %collective-permute-done.2.refs_0_.even_ref = f32[90,128]{1,0:T(8,128)S(1)} collective-permute-done((f32[90,128]{1,0:T(8,128)S(1)}, f32[90,128]{1,0:T(8,128)S(1)}, u32[]{:S(2)}, u32[]{:S(2)}) %collective-permute-start.2) | collective-permute-done | bytes 46112 | tf_op jit(solution)/shard_map/ppermute | solution.py:449
  15.7 0.0 collective-permute-done.3.refs_1_.odd_ref
  15.7 0.2 shard_map.114
  15.9 0.1 collective-permute-start.8
  16.0 1.2 %shard_map.115.smooth_ref = f32[16,1152]{1,0:T(8,128)S(1)} custom-call(f32[16,1152]{1,0:T(8,128)S(1)} %get-tuple-element.31.after_ref.own_ref, f32[90,128]{1,0:T(8,128)S(1)} %collective-permute-done.2.refs_0_.even_ref, f32[90,128]{1,0:T(8,128)S(1)} %collective-permute-done.3.refs_1_.odd_ref, f32[5,40,1152]{2,1,0:T(8,128)S(1)} %get-tuple-element.41.coef_ref), custom_call_target="tpu_custom_call" | custom-call | flops 16384000 | bytes 4096000 | tf_op jit(solution)/shard_map/pallas_call | solution.py:552
  17.3 0.0 collective-permute-done.8.more_ref
  17.4 1.4 %collective-permute-start.9 = (f32[90,128]{1,0:T(8,128)S(1)}, f32[90,128]{1,0:T(8,128)S(1)}, u32[]{:S(2)}, u32[]{:S(2)}) collective-permute-start(f32[90,128]{1,0:T(8,128)S(1)} %get-tuple-element.45), channel_id=1, source_target_pairs={{0,4},{4,0},{8,12},{12,8},{1,5},{5,1},{9,13},{13,9},{2,6},{6,2},{1... | collective-permute-start | bytes 138248 | tf_op jit(solution)/shard_map/ppermute | solution.py:449
  18.8 0.1 collective-permute-start.10
  18.9 2.6 %collective-permute-done.9.even_ref = f32[90,128]{1,0:T(8,128)S(1)} collective-permute-done((f32[90,128]{1,0:T(8,128)S(1)}, f32[90,128]{1,0:T(8,128)S(1)}, u32[]{:S(2)}, u32[]{:S(2)}) %collective-permute-start.9) | collective-permute-done | bytes 46112 | tf_op jit(solution)/shard_map/ppermute | solution.py:449
  21.5 0.0 collective-permute-done.10.odd_ref
  21.5 1.2 %shard_map.117.refs_0_ = f32[16,1024]{1,0:T(8,128)S(1)} custom-call(f32[16,1152]{1,0:T(8,128)S(1)} %get-tuple-element.44.own_ref, f32[90,128]{1,0:T(8,128)S(1)} %collective-permute-done.9.even_ref, f32[90,128]{1,0:T(8,128)S(1)} %collective-permute-done.10.odd_ref, f32[5,40,1152]{2,1,0:T(8,128)S(1)} %get-tuple-element.41.coef_ref), custom_call_target="tpu_custom_call" | custom-call | flops 16384000 | bytes 4096000 | tf_op jit(solution)/shard_map/pallas_call | solution.py:563
  22.8 1.1 %collective-permute-start.13 = (f32[16,1024]{1,0:T(8,128)S(1)}, f32[16,1024]{1,0:T(8,128)S(1)}, u32[]{:S(2)}, u32[]{:S(2)}) collective-permute-start(f32[16,1024]{1,0:T(8,128)S(1)} %shard_map.117.refs_0_), channel_id=1, source_target_pairs={{0,2},{1,3},{2,0},{3,1},{4,6},{5,7},{6,4},{7,5},{8,10},{9,11},{10,... | collective-permute-start | bytes 196616 | tf_op jit(solution)/shard_map/ppermute | solution.py:449
  23.9 1.1 %collective-permute-start.11 = (f32[16,1024]{1,0:T(8,128)S(1)}, f32[16,1024]{1,0:T(8,128)S(1)}, u32[]{:S(2)}, u32[]{:S(2)}) collective-permute-start(f32[16,1024]{1,0:T(8,128)S(1)} %shard_map.117.refs_0_), channel_id=1, source_target_pairs={{0,1},{1,0},{2,3},{3,2},{4,5},{5,4},{6,7},{7,6},{8,9},{9,8},{10,11... | collective-permute-start | bytes 196616 | tf_op jit(solution)/shard_map/ppermute | solution.py:449
  25.0 2.4 %collective-permute-done.13.refs_3_ = f32[16,1024]{1,0:T(8,128)S(1)} collective-permute-done((f32[16,1024]{1,0:T(8,128)S(1)}, f32[16,1024]{1,0:T(8,128)S(1)}, u32[]{:S(2)}, u32[]{:S(2)}) %collective-permute-start.13) | collective-permute-done | bytes 65568 | tf_op jit(solution)/shard_map/ppermute | solution.py:449
  27.4 0.9 %collective-permute-done.12.refs_2_ = f32[16,1024]{1,0:T(8,128)S(1)} collective-permute-done((f32[16,1024]{1,0:T(8,128)S(1)}, f32[16,1024]{1,0:T(8,128)S(1)}, u32[]{:S(2)}, u32[]{:S(2)}) %collective-permute-start.12) | collective-permute-done | bytes 65568 | tf_op jit(solution)/shard_map/ppermute | solution.py:449
  28.2 0.8 %shard_map.118 = f32[2,16,2048]{2,1,0:T(8,128)} custom-call(f32[2,2,8,128]{3,2,1,0:T(8,128)S(1)} %get-tuple-element.26.response_ref, f32[2,16,2048]{2,1,0:T(8,128)S(1)} %copy-done, f32[16,1024]{1,0:T(8,128)S(1)} %shard_map.117.refs_0_, f32[16,1024]{1,0:T(8,128)S(1)} %collective-permute-done.11.refs_1_, f32[16,1024]{1,0:T(8,128)S(1)} %collective-permute-done.12.refs_2_, ...), custom_call_target="tpu_custom_call" | custom-call | flops 4096000 | bytes 1024000 | tf_op jit(solution)/shard_map/pallas_call | solution.py:571
  (10 shorter events, 0.1 us)
Async XLA Ops:
  1.6 4.2 %collective-permute-start = (f32[16,2048]{1,0:T(8,128)S(1)}, f32[16,2048]{1,0:T(8,128)S(1)}, u32[]{:S(2)}, u32[]{:S(2)}) collective-permute-start(f32[16,2048]{1,0:T(8,128)S(1)} %get-tuple-element.28), channel_id=1, source_target_pairs={{0,1},{1,0},{2,3},{3,2},{4,5},{5,4},{6,7},{7,6},{8,9},{9,8},{10,11... | collective-permute-start | bytes 393224 | tf_op jit(solution)/shard_map/ppermute | solution.py:449
  2.1 9.8 %collective-permute-start.7 = (f32[2,104,128]{2,1,0:T(8,128)S(1)}, f32[2,104,128]{2,1,0:T(8,128)S(1)}, u32[]{:S(2)}, u32[]{:S(2)}) collective-permute-start(f32[2,104,128]{2,1,0:T(8,128)S(1)} %get-tuple-element.38), channel_id=1, source_target_pairs={{0,8},{1,13},{2,10},{3,15},{4,12},{5,9},{6,14},{7,11},{8,0},{9,5},... | collective-permute-start | bytes 319496 | tf_op jit(solution)/shard_map/ppermute | solution.py:472
  5.8 5.0 %collective-permute-start.1 = (f32[16,1152]{1,0:T(8,128)S(1)}, f32[16,1152]{1,0:T(8,128)S(1)}, u32[]{:S(2)}, u32[]{:S(2)}) collective-permute-start(f32[16,1152]{1,0:T(8,128)S(1)} %get-tuple-element.30), channel_id=1, source_target_pairs={{0,2},{1,3},{2,0},{3,1},{4,6},{5,7},{6,4},{7,5},{8,10},{9,11},{10,... | collective-permute-start | bytes 221192 | tf_op jit(solution)/shard_map/ppermute | solution.py:449
  7.4 5.2 %collective-permute-start.6 = (f32[104,128]{1,0:T(8,128)S(1)}, f32[104,128]{1,0:T(8,128)S(1)}, u32[]{:S(2)}, u32[]{:S(2)}) collective-permute-start(f32[104,128]{1,0:T(8,128)S(1)} %get-tuple-element.37), channel_id=1, source_target_pairs={{0,4},{1,5},{2,6},{3,7},{4,0},{5,1},{6,2},{7,3},{8,12},{9,13},{10,... | collective-permute-start | bytes 159752 | tf_op jit(solution)/shard_map/ppermute | solution.py:472
  8.9 6.2 %collective-permute-start.4 = (f32[2,90,128]{2,1,0:T(8,128)S(1)}, f32[2,90,128]{2,1,0:T(8,128)S(1)}, u32[]{:S(2)}, u32[]{:S(2)}) collective-permute-start(f32[2,90,128]{2,1,0:T(8,128)S(1)} %get-tuple-element.34), channel_id=1, source_target_pairs={{0,4},{4,0},{8,12},{12,8},{1,5},{5,1},{9,13},{13,9},{2,6},{6,2},{1... | collective-permute-start | bytes 276488 | tf_op jit(solution)/shard_map/ppermute | solution.py:449
  9.4 5.8 %collective-permute-start.5 = (f32[2,90,128]{2,1,0:T(8,128)S(1)}, f32[2,90,128]{2,1,0:T(8,128)S(1)}, u32[]{:S(2)}, u32[]{:S(2)}) collective-permute-start(f32[2,90,128]{2,1,0:T(8,128)S(1)} %get-tuple-element.35), channel_id=1, source_target_pairs={{0,1},{1,0},{2,3},{3,2},{4,8},{5,9},{6,10},{7,11},{8,4},{9,5},{10,... | collective-permute-start | bytes 276488 | tf_op jit(solution)/shard_map/ppermute | solution.py:460
  10.8 4.8 %collective-permute-start.2 = (f32[90,128]{1,0:T(8,128)S(1)}, f32[90,128]{1,0:T(8,128)S(1)}, u32[]{:S(2)}, u32[]{:S(2)}) collective-permute-start(f32[90,128]{1,0:T(8,128)S(1)} %get-tuple-element.32), channel_id=1, source_target_pairs={{0,4},{4,0},{8,12},{12,8},{1,5},{5,1},{9,13},{13,9},{2,6},{6,2},{1... | collective-permute-start | bytes 138248 | tf_op jit(solution)/shard_map/ppermute | solution.py:449
  11.9 3.8 %collective-permute-start.3 = (f32[90,128]{1,0:T(8,128)S(1)}, f32[90,128]{1,0:T(8,128)S(1)}, u32[]{:S(2)}, u32[]{:S(2)}) collective-permute-start(f32[90,128]{1,0:T(8,128)S(1)} %get-tuple-element.33), channel_id=1, source_target_pairs={{0,1},{1,0},{2,3},{3,2},{4,8},{5,9},{6,10},{7,11},{8,4},{9,5},{10,... | collective-permute-start | bytes 138248 | tf_op jit(solution)/shard_map/ppermute | solution.py:460
  15.9 1.4 %collective-permute-start.8 = (f32[2,16,1152]{2,1,0:T(8,128)S(1)}, f32[2,16,1152]{2,1,0:T(8,128)S(1)}, u32[]{:S(2)}, u32[]{:S(2)}) collective-permute-start(f32[2,16,1152]{2,1,0:T(8,128)S(1)} %get-tuple-element.43), channel_id=1, source_target_pairs={{0,1},{1,0},{2,3},{3,2},{4,5},{5,4},{6,7},{7,6},{8,9},{9,8},{10,11... | collective-permute-start | bytes 442376 | tf_op jit(solution)/shard_map/ppermute | solution.py:449
  16.0 1.3 %copy-start.1 = (s32[16,2048]{1,0:T(8,128)S(1)}, s32[16,2048]{1,0:T(8,128)}, u32[]{:S(2)}) copy-start(s32[16,2048]{1,0:T(8,128)} %mask_ref.1) | copy-start | bytes 393220
  17.4 4.2 %collective-permute-start.9 = (f32[90,128]{1,0:T(8,128)S(1)}, f32[90,128]{1,0:T(8,128)S(1)}, u32[]{:S(2)}, u32[]{:S(2)}) collective-permute-start(f32[90,128]{1,0:T(8,128)S(1)} %get-tuple-element.45), channel_id=1, source_target_pairs={{0,4},{4,0},{8,12},{12,8},{1,5},{5,1},{9,13},{13,9},{2,6},{6,2},{1... | collective-permute-start | bytes 138248 | tf_op jit(solution)/shard_map/ppermute | solution.py:449
  18.8 2.7 %collective-permute-start.10 = (f32[90,128]{1,0:T(8,128)S(1)}, f32[90,128]{1,0:T(8,128)S(1)}, u32[]{:S(2)}, u32[]{:S(2)}) collective-permute-start(f32[90,128]{1,0:T(8,128)S(1)} %get-tuple-element.46), channel_id=1, source_target_pairs={{0,1},{1,0},{2,3},{3,2},{4,8},{5,9},{6,10},{7,11},{8,4},{9,5},{10,... | collective-permute-start | bytes 138248 | tf_op jit(solution)/shard_map/ppermute | solution.py:460
  21.5 6.7 %copy-start = (f32[2,16,2048]{2,1,0:T(8,128)S(1)}, f32[2,16,2048]{2,1,0:T(8,128)}, u32[]{:S(2)}) copy-start(f32[2,16,2048]{2,1,0:T(8,128)} %control_ref.1) | copy-start | bytes 786436
  22.8 4.6 %collective-permute-start.13 = (f32[16,1024]{1,0:T(8,128)S(1)}, f32[16,1024]{1,0:T(8,128)S(1)}, u32[]{:S(2)}, u32[]{:S(2)}) collective-permute-start(f32[16,1024]{1,0:T(8,128)S(1)} %shard_map.117.refs_0_), channel_id=1, source_target_pairs={{0,2},{1,3},{2,0},{3,1},{4,6},{5,7},{6,4},{7,5},{8,10},{9,11},{10,... | collective-permute-start | bytes 196616 | tf_op jit(solution)/shard_map/ppermute | solution.py:449
  23.9 4.3 %collective-permute-start.12 = (f32[16,1024]{1,0:T(8,128)S(1)}, f32[16,1024]{1,0:T(8,128)S(1)}, u32[]{:S(2)}, u32[]{:S(2)}) collective-permute-start(f32[16,1024]{1,0:T(8,128)S(1)} %shard_map.117.refs_0_), channel_id=1, source_target_pairs={{0,3},{1,2},{2,1},{3,0},{4,7},{5,6},{6,5},{7,4},{8,11},{9,10},{10,... | collective-permute-start | bytes 196616 | tf_op jit(solution)/shard_map/ppermute | solution.py:449
  23.9 4.3 %collective-permute-start.11 = (f32[16,1024]{1,0:T(8,128)S(1)}, f32[16,1024]{1,0:T(8,128)S(1)}, u32[]{:S(2)}, u32[]{:S(2)}) collective-permute-start(f32[16,1024]{1,0:T(8,128)S(1)} %shard_map.117.refs_0_), channel_id=1, source_target_pairs={{0,1},{1,0},{2,3},{3,2},{4,5},{5,4},{6,7},{7,6},{8,9},{9,8},{10,11... | collective-permute-start | bytes 196616 | tf_op jit(solution)/shard_map/ppermute | solution.py:449
